TPU v7x, 32 devices: a whole 2x2x4 slice. The times are simulated.
32 devices in a mesh: fsdp: 4 (over z), ctx: 4 (over x, core), tp: 2 (over y).
Axes of the slice: x: 2, y: 2, z: 4, core: 2. Of those that a mesh axis runs over, the one named last changes fastest.
Arguments:
- inputs: bfloat16 [8192, 1536], P(('fsdp', 'ctx')), may hold values from -6 to 6
- cotangent: bfloat16 [8192, 1536], P(('fsdp', 'ctx', 'tp')), may hold values from -6 to 6
- routes: int32 [8192, 8], P(('fsdp', 'ctx')), may hold values from 0 to 31, all different within a row; in each aligned block of 256 rows (0 to 255, 256 to 511, ...) at most 96 rows name the same one
- segment_ids: int32 [4, 2048], P('fsdp'), may hold values from 0 to 12, as said below
- parents: int32 [4, 13], P('fsdp'), may hold values from 0 to 11, as said below
- w_qkv: float32 [1536, 2560], P(('fsdp', 'ctx'), 'tp'), may hold values from -0.15625 to 0.15625
- w_out: float32 [1536, 1536], P('tp', ('fsdp', 'ctx')), may hold values from -1.25 to 1.25
- w_router: float32 [1536, 32], P(('fsdp', 'ctx')), may hold values from -0.15625 to 0.15625
- w_gate_up: float32 [32, 1536, 1024], P(('fsdp', 'tp'), 'ctx'), may hold values from -0.15625 to 0.15625
- w_down: float32 [32, 512, 1536], P(('fsdp', 'tp'), None, 'ctx'), may hold values from -0.25 to 0.25
- gain_attn: float32 [1536], P(('fsdp', 'ctx')), may hold values from 0.5 to 1.5
- gain_moe: float32 [1536], P(('fsdp', 'ctx')), may hold values from 0.5 to 1.5
- row_qkv: float32 [1536], replicated, may hold values from 27 to 9830, as said below
- col_qkv: float32 [2560], replicated, may hold values from 163 to 1638
- row_out: float32 [1536], replicated, may hold values from 163 to 1638
- col_out: float32 [1536], replicated, may hold values from 27 to 9830, as said below
- row_router: float32 [1536], replicated, may hold values from 27 to 9830, as said below
- col_router: float32 [32], replicated, may hold values from 163 to 1638
- row_gate_up: float32 [32, 1536], replicated, may hold values from 27 to 9830, as said below
- col_gate_up: float32 [32, 1024], replicated, may hold values from 27 to 9830, as said below
- row_down: float32 [32, 512], replicated, may hold values from 1 to 491, as said below
- col_down: float32 [32, 1536], replicated, may hold values from 1 to 491, as said below
- second_attn: float32 [1536], P(('fsdp', 'ctx')), may hold values from 27 to 9830, as said below
- second_moe: float32 [1536], P(('fsdp', 'ctx')), may hold values from 27 to 9830, as said below
Outputs:
- layer_out: bfloat16 [8192, 1536], P(('fsdp', 'ctx', 'tp'))
- grad_inputs: float32 [8192, 1536], P(('fsdp', 'ctx'))
- aux_loss: float32 [], replicated
- grad_qkv: float32 [1536, 2560], P(('fsdp', 'ctx'), 'tp')
- grad_out: float32 [1536, 1536], P('tp', ('fsdp', 'ctx'))
- grad_router: float32 [1536, 32], P(('fsdp', 'ctx'))
- grad_gate_up: float32 [32, 1536, 1024], P(('fsdp', 'tp'), 'ctx')
- grad_down: float32 [32, 512, 1536], P(('fsdp', 'tp'), None, 'ctx')
- grad_gain_attn: float32 [1536], P(('fsdp', 'ctx'))
- grad_gain_moe: float32 [1536], P(('fsdp', 'ctx'))
- new_qkv: float32 [1536, 2560], P(('fsdp', 'ctx'), 'tp')
- new_out: float32 [1536, 1536], P('tp', ('fsdp', 'ctx'))
- new_router: float32 [1536, 32], P(('fsdp', 'ctx'))
- new_gate_up: float32 [32, 1536, 1024], P(('fsdp', 'tp'), 'ctx')
- new_down: float32 [32, 512, 1536], P(('fsdp', 'tp'), None, 'ctx')
- new_gain_attn: float32 [1536], P(('fsdp', 'ctx'))
- new_gain_moe: float32 [1536], P(('fsdp', 'ctx'))
- copy_qkv: bfloat16 [1536, 2560], P(('fsdp', 'ctx'), 'tp')
- copy_out: bfloat16 [1536, 1536], P('tp', ('fsdp', 'ctx'))
- copy_router: bfloat16 [1536, 32], P(('fsdp', 'ctx'))
- copy_gate_up: bfloat16 [32, 1536, 1024], P(('fsdp', 'tp'), 'ctx')
- copy_down: bfloat16 [32, 512, 1536], P(('fsdp', 'tp'), None, 'ctx')
- copy_gain_attn: bfloat16 [1536], P(('fsdp', 'ctx'))
- copy_gain_moe: bfloat16 [1536], P(('fsdp', 'ctx'))
- row_qkv_new: float32 [1536], replicated
- col_qkv_new: float32 [2560], replicated
- row_out_new: float32 [1536], replicated
- col_out_new: float32 [1536], replicated
- row_router_new: float32 [1536], replicated
- col_router_new: float32 [32], replicated
- row_gate_up_new: float32 [32, 1536], replicated
- col_gate_up_new: float32 [32, 1024], replicated
- row_down_new: float32 [32, 512], replicated
- col_down_new: float32 [32, 1536], replicated
- second_attn_new: float32 [1536], P(('fsdp', 'ctx'))
- second_moe_new: float32 [1536], P(('fsdp', 'ctx'))
- update_rms: float32 [7], replicated
Inputs may be any that keep to these rules, and one draw needn't show every extreme that they name: `segment_ids`: in each tree the segment number never falls along the tokens; segment 0 holds exactly the first 819 tokens, and every segment holds at least one token. parents[r, 0] = 0; for s >= 1 the parent of segment s is smaller than s; the parent of segment 13 - 1 is 11. `routes`: within each aligned block of 256 rows no expert is named by more than 96 rows. `row_qkv`: positive. `col_out`: positive. `row_router`: positive. `row_gate_up`: positive. `col_gate_up`: positive. `row_down`: positive. `col_down`: positive. `second_attn`: positive. `second_moe`: positive.
All inputs are finite; a program needn't handle non-finite values.
Results may differ from a plain program's by a relative error of at most 0.015.
The roundings to bfloat16 on the way count: a program that leaves them out, or rounds other values in their place, can miss the bound.
Values may be sent and summed in bfloat16 or wider, within the bound.
No kernel may reach another device: no remote copies, remote signals or barrier semaphores. Data moves between devices by JAX's collectives and lax.ppermute only.
A program may use at most 320 MiB of HBM per device.

v0:
```python
import jax
import jax.numpy as jnp
from jax import lax
from jax.sharding import PartitionSpec as P

D = 1536
HEADS = 24
KV_HEADS = 8
HEAD = 64
FFE = 512
TOPK = 8
EXPERTS = 32
NSEG = 13


norm_eps = 1e-05
decay = 0.5
floor_sq = 1e-30
rate = 0.25
clip_rms = 0.05
aux_weight = 1.0
highest = lax.Precision.HIGHEST


def rms_norm(values, gain):
    return values * lax.rsqrt(jnp.mean(values * values, axis=-1, keepdims=True) + norm_eps) * gain


def ancestry(parent_row):
    seg_labels = jnp.arange(NSEG, dtype=jnp.int32)
    table = jnp.maximum(
        (seg_labels[:, None] == seg_labels[None, :]).astype(jnp.float32),
        (parent_row[:, None] == seg_labels[None, :]).astype(jnp.float32),
    )
    for sweep in range(NSEG.bit_length()):
        table = jnp.max(table[:, :, None] * table[None, :, :], axis=1)
    return table


def visible(segments, parent_row, start, count):
    table = ancestry(parent_row)
    seg_labels = jnp.arange(NSEG, dtype=jnp.int32)
    own_segments = lax.dynamic_slice_in_dim(segments, start, count, 0)
    query_hot = (own_segments[:, None] == seg_labels[None, :]).astype(jnp.float32)
    key_hot = (segments[None, :] == seg_labels[:, None]).astype(jnp.float32)
    reach = jnp.dot(jnp.dot(query_hot, table, precision=highest), key_hot, precision=highest)
    rows_at = start + jnp.arange(count, dtype=jnp.int32)
    cols_at = jnp.arange(segments.shape[0], dtype=jnp.int32)
    return (reach > 0.5) & (cols_at[None, :] <= rows_at[:, None])


def placed(piece, full_shape, offsets):
    starts = tuple((jnp.asarray(offset, jnp.int32) for offset in offsets))
    return lax.dynamic_update_slice(jnp.zeros(full_shape, jnp.float32), piece, starts)


def per_device(
    inputs,
    cotangent,
    routes,
    segment_ids,
    parents,
    w_qkv,
    w_out,
    w_router,
    w_gate_up,
    w_down,
    gain_attn,
    gain_moe,
    row_qkv,
    col_qkv,
    row_out,
    col_out,
    row_router,
    col_router,
    row_gate_up,
    col_gate_up,
    row_down,
    col_down,
    second_attn,
    second_moe,
):
    tp_count = lax.axis_size("tp")
    ctx_count = lax.axis_size("ctx")
    fsdp_count = lax.axis_size("fsdp")
    tp_index = lax.axis_index("tp")
    ctx_index = lax.axis_index("ctx")
    fsdp_index = lax.axis_index("fsdp")
    flat_index = fsdp_index * ctx_count + ctx_index
    owner_index = fsdp_index * tp_count + tp_index
    keep_once = (tp_index == 0).astype(jnp.float32)
    tok_rows = inputs.shape[0]
    half_rows = tok_rows // tp_count
    tree_len = segment_ids.shape[1]
    tokens_all = tok_rows * fsdp_count * ctx_count
    capacity = half_rows * TOPK * 3 // (2 * EXPERTS)
    groups = fsdp_count * tp_count
    local_experts = EXPERTS // groups
    q_heads = HEADS // tp_count
    kv_local = KV_HEADS // tp_count
    group_size = HEADS // KV_HEADS
    scale = HEAD ** (-0.5)
    dense_rows = w_qkv.shape[0]
    qkv_cols = w_qkv.shape[1]
    ctx_rows = w_gate_up.shape[1]
    labels = jnp.arange(EXPERTS, dtype=jnp.int32)
    slot_block = local_experts * capacity
    halves = routes.reshape(tp_count, half_rows, TOPK)
    counts_half = jnp.sum((halves[..., None] == labels).astype(jnp.float32), axis=(1, 2))
    qkv_full, out_full, router_full, gain1_full, gain2_full, counts_all = (
        lax.all_gather(w_qkv.astype(jnp.bfloat16), ("fsdp", "ctx"), axis=0, tiled=True),
        lax.all_gather(w_out.astype(jnp.bfloat16), ("fsdp", "ctx"), axis=1, tiled=True),
        lax.all_gather(w_router.astype(jnp.bfloat16), ("fsdp", "ctx"), axis=0, tiled=True),
        lax.all_gather(gain_attn.astype(jnp.bfloat16), ("fsdp", "ctx"), axis=0, tiled=True),
        lax.all_gather(gain_moe.astype(jnp.bfloat16), ("fsdp", "ctx"), axis=0, tiled=True),
        lax.all_gather(counts_half.astype(jnp.bfloat16), ("fsdp", "ctx"), axis=0, tiled=True),
    )
    fraction = jnp.sum(counts_all.astype(jnp.float32), axis=0) / (tokens_all * TOPK)
    gain_one = gain1_full.astype(jnp.float32)
    gain_two = gain2_full.astype(jnp.float32)
    inputs_f32 = inputs.astype(jnp.float32)
    normed_attn, norm_attn_back = jax.vjp(rms_norm, inputs_f32, gain_one)
    act1 = normed_attn.astype(jnp.bfloat16)
    qkv = jnp.dot(act1, qkv_full, preferred_element_type=jnp.float32).astype(jnp.bfloat16)
    query = qkv[:, : q_heads * HEAD].reshape(tok_rows, q_heads, HEAD)
    keyval = qkv[:, q_heads * HEAD :]
    gate_up_all, down_all, keyval_all = (
        lax.all_gather(w_gate_up.astype(jnp.bfloat16), "ctx", axis=1, tiled=True),
        lax.all_gather(w_down.astype(jnp.bfloat16), "ctx", axis=2, tiled=True),
        lax.all_gather(keyval, "ctx", axis=0, tiled=True),
    )
    keys = keyval_all[:, : kv_local * HEAD].reshape(tree_len, kv_local, HEAD)
    values = keyval_all[:, kv_local * HEAD :].reshape(tree_len, kv_local, HEAD)
    allowed = visible(segment_ids[0], parents[0], ctx_index * tok_rows, tok_rows)
    outs_list = []
    log_totals = []
    for kv_index in range(kv_local):
        query_group = query[:, kv_index * group_size : (kv_index + 1) * group_size]
        scores = (
            jnp.einsum(
                "qgd,kd->gqk", query_group, keys[:, kv_index], preferred_element_type=jnp.float32
            )
            * scale
        )
        masked = jnp.where(allowed[None], scores, -1e30)
        row_max = jnp.max(masked, axis=-1, keepdims=True)
        exp_scores = jnp.exp(masked - row_max)
        row_total = jnp.sum(exp_scores, axis=-1, keepdims=True)
        prob_low = (exp_scores / row_total).astype(jnp.bfloat16)
        log_totals.append(row_max + jnp.log(row_total))
        outs_list.append(
            jnp.einsum(
                "gqk,kd->qgd", prob_low, values[:, kv_index], preferred_element_type=jnp.float32
            )
        )
    attended = (
        jnp.concatenate(outs_list, axis=1).reshape(tok_rows, q_heads * HEAD).astype(jnp.bfloat16)
    )
    attn_part = jnp.dot(attended, out_full, preferred_element_type=jnp.float32)
    attn = lax.psum(attn_part, "tp")
    x_one = inputs_f32 + attn
    half = lax.dynamic_slice_in_dim(x_one, tp_index * half_rows, half_rows, 0)
    normed_moe, norm_moe_back = jax.vjp(rms_norm, half, gain_two)
    act2 = normed_moe.astype(jnp.bfloat16)
    logits = jnp.dot(act2, router_full, preferred_element_type=jnp.float32)
    my_routes = lax.dynamic_slice_in_dim(routes, tp_index * half_rows, half_rows, 0)
    route_hot = (my_routes[..., None] == labels).astype(jnp.float32)

    def router_terms(logit_values):
        probs_all = jax.nn.softmax(logit_values, axis=-1)
        chosen = jnp.sum(route_hot * logit_values[:, None, :], axis=-1)
        return (probs_all, jax.nn.softmax(chosen, axis=-1))

    (router_probs, combine), router_back = jax.vjp(router_terms, logits)
    flat_hot = route_hot.reshape(half_rows * TOPK, EXPERTS).astype(jnp.int32)
    rank_all = jnp.cumsum(flat_hot, axis=0) - flat_hot
    slot_rank = jnp.sum(rank_all * flat_hot, axis=1)
    dest = my_routes.reshape(-1) * capacity + slot_rank
    slot_ids = jnp.arange(half_rows * TOPK, dtype=jnp.int32)
    source_slot = jnp.zeros((EXPERTS * capacity,), jnp.int32).at[dest].set(slot_ids)
    filled = jnp.zeros((EXPERTS * capacity,), jnp.bool_).at[dest].set(True)
    send_rows = jnp.where(filled[:, None], act2[source_slot // TOPK], jnp.zeros((), jnp.bfloat16))
    received = lax.all_to_all(
        send_rows.reshape(groups, slot_block, D),
        ("fsdp", "tp"),
        split_axis=0,
        concat_axis=0,
        tiled=True,
    )
    received = received.reshape(groups, local_experts, capacity, D)
    gate_up = jnp.einsum(
        "secd,edf->secf", received, gate_up_all, preferred_element_type=jnp.float32
    )
    gate = gate_up[..., :FFE]
    up_part = gate_up[..., FFE:]
    hidden = (jax.nn.silu(gate) * up_part).astype(jnp.bfloat16)
    expert_out = jnp.einsum(
        "secf,efd->secd", hidden, down_all, preferred_element_type=jnp.float32
    ).astype(jnp.bfloat16)
    returned = lax.all_to_all(
        expert_out.reshape(groups, slot_block, D),
        ("fsdp", "tp"),
        split_axis=0,
        concat_axis=0,
        tiled=True,
    )
    returned = returned.reshape(EXPERTS * capacity, D)
    picked = returned[dest].astype(jnp.float32).reshape(half_rows, TOPK, D)
    moe = jnp.sum(picked * combine[..., None], axis=1)
    layer_out = (half + moe).astype(jnp.bfloat16)
    grad_half = cotangent.astype(jnp.float32)
    d_combine = jnp.sum(picked * grad_half[:, None, :], axis=-1)
    d_slot = (
        (combine[..., None] * grad_half[:, None, :])
        .reshape(half_rows * TOPK, D)
        .astype(jnp.bfloat16)
    )
    d_send = jnp.where(filled[:, None], d_slot[source_slot], jnp.zeros((), jnp.bfloat16))
    d_received = lax.all_to_all(
        d_send.reshape(groups, slot_block, D),
        ("fsdp", "tp"),
        split_axis=0,
        concat_axis=0,
        tiled=True,
    )
    d_received = d_received.reshape(groups, local_experts, capacity, D)
    gate_back, up_back, hidden_back = (gate, up_part, hidden)
    d_hidden = jnp.einsum(
        "secd,efd->secf", d_received, down_all, preferred_element_type=jnp.float32
    )
    g_down_local = jnp.einsum(
        "secf,secd->efd", hidden_back, d_received, preferred_element_type=jnp.float32
    )
    silu_product, silu_back = jax.vjp(
        lambda gate_in, up_in: jax.nn.silu(gate_in) * up_in, gate_back, up_back
    )
    d_gate, d_up = silu_back(d_hidden)
    d_gate_up = jnp.concatenate([d_gate, d_up], axis=-1).astype(jnp.bfloat16)
    d_rows = jnp.einsum(
        "secf,edf->secd", d_gate_up, gate_up_all, preferred_element_type=jnp.float32
    ).astype(jnp.bfloat16)
    g_gate_up_local = jnp.einsum(
        "secd,secf->edf", received, d_gate_up, preferred_element_type=jnp.float32
    )
    d_back = lax.all_to_all(
        d_rows.reshape(groups, slot_block, D),
        ("fsdp", "tp"),
        split_axis=0,
        concat_axis=0,
        tiled=True,
    )
    d_back = d_back.reshape(EXPERTS * capacity, D)
    d_act2 = jnp.sum(d_back[dest].astype(jnp.float32).reshape(half_rows, TOPK, D), axis=1)
    d_probs_aux = jnp.broadcast_to(aux_weight * EXPERTS * fraction, router_probs.shape)
    d_logits = router_back((d_probs_aux, d_combine))[0].astype(jnp.bfloat16)
    g_router_part = jnp.einsum("td,te->de", act2, d_logits, preferred_element_type=jnp.float32)
    d_act2 = d_act2 + jnp.einsum(
        "te,de->td", d_logits, router_full, preferred_element_type=jnp.float32
    )
    d_half, d_gain_two = norm_moe_back(d_act2)
    d_x1_half = grad_half + d_half
    d_x1, router_parts, gain2_parts = (
        lax.all_gather(d_x1_half, "tp", axis=0, tiled=True),
        lax.all_gather(g_router_part[None], "tp", axis=0, tiled=True),
        lax.all_gather(d_gain_two[None], "tp", axis=0, tiled=True),
    )
    g_router_sum = jnp.sum(router_parts, axis=0)
    g_gain2_sum = jnp.sum(gain2_parts, axis=0)
    d_x1_low = d_x1.astype(jnp.bfloat16)
    g_out_local = jnp.einsum("tq,td->qd", attended, d_x1_low, preferred_element_type=jnp.float32)
    d_attended = jnp.einsum(
        "td,qd->tq", d_x1_low, out_full, preferred_element_type=jnp.float32
    ).astype(jnp.bfloat16)
    d_attended = d_attended.reshape(tok_rows, q_heads, HEAD)
    d_query_list = []
    d_key_list = []
    d_value_list = []
    for kv_index in range(kv_local):
        query_group = query[:, kv_index * group_size : (kv_index + 1) * group_size]
        d_out_group = d_attended[:, kv_index * group_size : (kv_index + 1) * group_size]
        scores = (
            jnp.einsum(
                "qgd,kd->gqk", query_group, keys[:, kv_index], preferred_element_type=jnp.float32
            )
            * scale
        )
        masked = jnp.where(allowed[None], scores, -1e30)
        prob_full = jnp.exp(masked - log_totals[kv_index])
        prob_low = prob_full.astype(jnp.bfloat16)
        d_prob = jnp.einsum(
            "qgd,kd->gqk", d_out_group, values[:, kv_index], preferred_element_type=jnp.float32
        )
        delta = jnp.sum(prob_full * d_prob, axis=-1, keepdims=True)
        d_scores = (prob_full * (d_prob - delta)).astype(jnp.bfloat16)
        d_query_list.append(
            jnp.einsum(
                "gqk,kd->qgd", d_scores, keys[:, kv_index], preferred_element_type=jnp.float32
            )
            * scale
        )
        d_key_list.append(
            jnp.einsum("gqk,qgd->kd", d_scores, query_group, preferred_element_type=jnp.float32)
            * scale
        )
        d_value_list.append(
            jnp.einsum("gqk,qgd->kd", prob_low, d_out_group, preferred_element_type=jnp.float32)
        )
    d_keys = jnp.stack(d_key_list, axis=1).reshape(tree_len, kv_local * HEAD)
    d_values = jnp.stack(d_value_list, axis=1).reshape(tree_len, kv_local * HEAD)
    d_keyval = jnp.concatenate([d_keys, d_values], axis=-1)
    g_gate_up, g_down, d_keyval_own = (
        lax.psum_scatter(g_gate_up_local, "ctx", scatter_dimension=1, tiled=True),
        lax.psum_scatter(g_down_local, "ctx", scatter_dimension=2, tiled=True),
        lax.psum_scatter(d_keyval, "ctx", scatter_dimension=0, tiled=True),
    )
    d_query = jnp.concatenate(d_query_list, axis=1).reshape(tok_rows, q_heads * HEAD)
    d_qkv = jnp.concatenate([d_query, d_keyval_own], axis=-1).astype(jnp.bfloat16)
    g_qkv_local = jnp.einsum("td,tc->dc", act1, d_qkv, preferred_element_type=jnp.float32)
    d_act1_part = jnp.einsum("tc,dc->td", d_qkv, qkv_full, preferred_element_type=jnp.float32)
    d_act1 = lax.psum(d_act1_part, "tp")
    d_inputs_attn, d_gain_one = norm_attn_back(d_act1)
    grad_inputs = d_x1 + d_inputs_attn
    g_qkv, g_out, g_router, g_gain1, g_gain2 = (
        lax.psum_scatter(g_qkv_local, ("fsdp", "ctx"), scatter_dimension=0, tiled=True),
        lax.psum_scatter(g_out_local, ("fsdp", "ctx"), scatter_dimension=1, tiled=True),
        lax.psum_scatter(g_router_sum, ("fsdp", "ctx"), scatter_dimension=0, tiled=True),
        lax.psum_scatter(d_gain_one, ("fsdp", "ctx"), scatter_dimension=0, tiled=True),
        lax.psum_scatter(g_gain2_sum, ("fsdp", "ctx"), scatter_dimension=0, tiled=True),
    )
    sq_qkv = g_qkv * g_qkv
    sq_out = g_out * g_out
    sq_router = g_router * g_router
    sq_gate_up = g_gate_up * g_gate_up
    sq_down = g_down * g_down
    expert_start = owner_index * local_experts
    moment_parts = (
        placed(jnp.sum(sq_qkv, axis=1), (D,), (flat_index * dense_rows,)),
        placed(jnp.sum(sq_qkv, axis=0), (qkv_cols * tp_count,), (tp_index * qkv_cols,)),
        placed(jnp.sum(sq_out, axis=1), (HEADS * HEAD,), (tp_index * q_heads * HEAD,)),
        placed(jnp.sum(sq_out, axis=0), (D,), (flat_index * dense_rows,)),
        placed(jnp.sum(sq_router, axis=1) * keep_once, (D,), (flat_index * dense_rows,)),
        jnp.sum(sq_router, axis=0) * keep_once,
        placed(jnp.sum(sq_gate_up, axis=2), (EXPERTS, D), (expert_start, ctx_index * ctx_rows)),
        placed(jnp.sum(sq_gate_up, axis=1), (EXPERTS, 2 * FFE), (expert_start, 0)),
        placed(jnp.sum(sq_down, axis=2), (EXPERTS, FFE), (expert_start, 0)),
        placed(jnp.sum(sq_down, axis=1), (EXPERTS, D), (expert_start, ctx_index * ctx_rows)),
        jnp.sum(router_probs, axis=0),
    )
    (
        tot_row_qkv,
        tot_col_qkv,
        tot_row_out,
        tot_col_out,
        tot_row_router,
        tot_col_router,
        tot_row_gu,
        tot_col_gu,
        tot_row_down,
        tot_col_down,
        prob_totals,
    ) = lax.psum(
        (
            moment_parts[0],
            moment_parts[1],
            moment_parts[2],
            moment_parts[3],
            moment_parts[4],
            moment_parts[5],
            moment_parts[6],
            moment_parts[7],
            moment_parts[8],
            moment_parts[9],
            moment_parts[10],
        ),
        ("fsdp", "ctx", "tp"),
    )
    qkv_width = (HEADS + 2 * KV_HEADS) * HEAD
    row_qkv_new = decay * row_qkv + (1.0 - decay) * (tot_row_qkv / qkv_width + floor_sq)
    col_qkv_new = decay * col_qkv + (1.0 - decay) * (tot_col_qkv / D + floor_sq)
    row_out_new = decay * row_out + (1.0 - decay) * (tot_row_out / D + floor_sq)
    col_out_new = decay * col_out + (1.0 - decay) * (tot_col_out / (HEADS * HEAD) + floor_sq)
    row_router_new = decay * row_router + (1.0 - decay) * (tot_row_router / EXPERTS + floor_sq)
    col_router_new = decay * col_router + (1.0 - decay) * (tot_col_router / D + floor_sq)
    row_gu_new = decay * row_gate_up + (1.0 - decay) * (tot_row_gu / (2 * FFE) + floor_sq)
    col_gu_new = decay * col_gate_up + (1.0 - decay) * (tot_col_gu / D + floor_sq)
    row_down_new = decay * row_down + (1.0 - decay) * (tot_row_down / D + floor_sq)
    col_down_new = decay * col_down + (1.0 - decay) * (tot_col_down / FFE + floor_sq)
    aux_loss = EXPERTS * jnp.sum(fraction * prob_totals / tokens_all)
    rows_here = lax.dynamic_slice_in_dim(row_qkv_new, flat_index * dense_rows, dense_rows, 0)
    cols_here = lax.dynamic_slice_in_dim(col_qkv_new, tp_index * qkv_cols, qkv_cols, 0)
    change_qkv = g_qkv * lax.rsqrt(rows_here[:, None] * cols_here[None, :] / jnp.mean(row_qkv_new))
    rows_here = lax.dynamic_slice_in_dim(row_out_new, tp_index * q_heads * HEAD, q_heads * HEAD, 0)
    cols_here = lax.dynamic_slice_in_dim(col_out_new, flat_index * dense_rows, dense_rows, 0)
    change_out = g_out * lax.rsqrt(rows_here[:, None] * cols_here[None, :] / jnp.mean(row_out_new))
    rows_here = lax.dynamic_slice_in_dim(row_router_new, flat_index * dense_rows, dense_rows, 0)
    change_router = g_router * lax.rsqrt(
        rows_here[:, None] * col_router_new[None, :] / jnp.mean(row_router_new)
    )
    start_pair = (
        jnp.asarray(expert_start, jnp.int32),
        jnp.asarray(ctx_index * ctx_rows, jnp.int32),
    )
    zero_start = jnp.asarray(0, jnp.int32)
    rows_gu = lax.dynamic_slice(row_gu_new, start_pair, (local_experts, ctx_rows))
    cols_gu = lax.dynamic_slice(col_gu_new, (start_pair[0], zero_start), (local_experts, 2 * FFE))
    mean_gu = lax.dynamic_slice_in_dim(
        jnp.mean(row_gu_new, axis=-1), expert_start, local_experts, 0
    )
    change_gate_up = g_gate_up * lax.rsqrt(
        rows_gu[:, :, None] * cols_gu[:, None, :] / mean_gu[:, None, None]
    )
    rows_dn = lax.dynamic_slice(row_down_new, (start_pair[0], zero_start), (local_experts, FFE))
    cols_dn = lax.dynamic_slice(col_down_new, start_pair, (local_experts, ctx_rows))
    mean_dn = lax.dynamic_slice_in_dim(
        jnp.mean(row_down_new, axis=-1), expert_start, local_experts, 0
    )
    change_down = g_down * lax.rsqrt(
        rows_dn[:, :, None] * cols_dn[:, None, :] / mean_dn[:, None, None]
    )
    second_attn_new = decay * second_attn + (1.0 - decay) * (g_gain1 * g_gain1 + floor_sq)
    second_moe_new = decay * second_moe + (1.0 - decay) * (g_gain2 * g_gain2 + floor_sq)
    change_gain1 = g_gain1 * lax.rsqrt(second_attn_new)
    change_gain2 = g_gain2 * lax.rsqrt(second_moe_new)
    square_sums = jnp.stack(
        [
            jnp.sum(change_qkv * change_qkv),
            jnp.sum(change_out * change_out),
            keep_once * jnp.sum(change_router * change_router),
            jnp.sum(change_gate_up * change_gate_up),
            jnp.sum(change_down * change_down),
            keep_once * jnp.sum(change_gain1 * change_gain1),
            keep_once * jnp.sum(change_gain2 * change_gain2),
        ]
    )
    master_sums = jnp.stack(
        [
            jnp.sum(w_qkv * w_qkv),
            jnp.sum(w_out * w_out),
            keep_once * jnp.sum(w_router * w_router),
            jnp.sum(w_gate_up * w_gate_up),
            jnp.sum(w_down * w_down),
            keep_once * jnp.sum(gain_attn * gain_attn),
            keep_once * jnp.sum(gain_moe * gain_moe),
        ]
    )
    square_totals, master_totals = lax.psum((square_sums, master_sums), ("fsdp", "ctx", "tp"))
    entries = jnp.array(
        [
            D * qkv_width,
            HEADS * HEAD * D,
            D * EXPERTS,
            EXPERTS * D * 2 * FFE,
            EXPERTS * FFE * D,
            D,
            D,
        ],
        jnp.float32,
    )
    update_rms = jnp.sqrt(square_totals / entries)
    weight_rms = jnp.sqrt(master_totals / entries)
    step_scale = rate * weight_rms / jnp.maximum(clip_rms, update_rms)
    new_qkv = w_qkv - step_scale[0] * change_qkv
    new_out = w_out - step_scale[1] * change_out
    new_router = w_router - step_scale[2] * change_router
    new_gate_up = w_gate_up - step_scale[3] * change_gate_up
    new_down = w_down - step_scale[4] * change_down
    new_gain1 = gain_attn - step_scale[5] * change_gain1
    new_gain2 = gain_moe - step_scale[6] * change_gain2
    return (
        layer_out,
        grad_inputs,
        aux_loss,
        g_qkv,
        g_out,
        g_router,
        g_gate_up,
        g_down,
        g_gain1,
        g_gain2,
        new_qkv,
        new_out,
        new_router,
        new_gate_up,
        new_down,
        new_gain1,
        new_gain2,
        new_qkv.astype(jnp.bfloat16),
        new_out.astype(jnp.bfloat16),
        new_router.astype(jnp.bfloat16),
        new_gate_up.astype(jnp.bfloat16),
        new_down.astype(jnp.bfloat16),
        new_gain1.astype(jnp.bfloat16),
        new_gain2.astype(jnp.bfloat16),
        row_qkv_new,
        col_qkv_new,
        row_out_new,
        col_out_new,
        row_router_new,
        col_router_new,
        row_gu_new,
        col_gu_new,
        row_down_new,
        col_down_new,
        second_attn_new,
        second_moe_new,
        update_rms,
    )


def solution(mesh):
    placed = (
        P(("fsdp", "ctx"), None),
        P(("fsdp", "ctx", "tp"), None),
        P(("fsdp", "ctx"), None),
        P("fsdp", None),
        P("fsdp", None),
        P(("fsdp", "ctx"), "tp"),
        P("tp", ("fsdp", "ctx")),
        P(("fsdp", "ctx"), None),
        P(("fsdp", "tp"), "ctx", None),
        P(("fsdp", "tp"), None, "ctx"),
        P(("fsdp", "ctx")),
        P(("fsdp", "ctx")),
        P(),
        P(),
        P(),
        P(),
        P(),
        P(),
        P(),
        P(),
        P(),
        P(),
        P(("fsdp", "ctx")),
        P(("fsdp", "ctx")),
    )
    return jax.shard_map(
        per_device,
        mesh=mesh,
        in_specs=placed,
        out_specs=(
            P(("fsdp", "ctx", "tp"), None),
            P(("fsdp", "ctx"), None),
            P(),
            P(("fsdp", "ctx"), "tp"),
            P("tp", ("fsdp", "ctx")),
            P(("fsdp", "ctx"), None),
            P(("fsdp", "tp"), "ctx", None),
            P(("fsdp", "tp"), None, "ctx"),
            P(("fsdp", "ctx")),
            P(("fsdp", "ctx")),
            P(("fsdp", "ctx"), "tp"),
            P("tp", ("fsdp", "ctx")),
            P(("fsdp", "ctx"), None),
            P(("fsdp", "tp"), "ctx", None),
            P(("fsdp", "tp"), None, "ctx"),
            P(("fsdp", "ctx")),
            P(("fsdp", "ctx")),
            P(("fsdp", "ctx"), "tp"),
            P("tp", ("fsdp", "ctx")),
            P(("fsdp", "ctx"), None),
            P(("fsdp", "tp"), "ctx", None),
            P(("fsdp", "tp"), None, "ctx"),
            P(("fsdp", "ctx")),
            P(("fsdp", "ctx")),
            P(),
            P(),
            P(),
            P(),
            P(),
            P(),
            P(),
            P(),
            P(),
            P(),
            P(("fsdp", "ctx")),
            P(("fsdp", "ctx")),
            P(),
        ),
        check_vma=False,
    )
```

profile of v0, /device:TPU:0, one launch (start us, length us, event | category | flops | bytes accessed | tf_op | source)
XLA Modules:
  0.0 2309.2 jit_solution(2645736006619030169)
XLA Ops:
  15.0 36.2 %all-reduce.8 = (bf16[1536]{0:T(1024)(128)(2,1)S(1)}, bf16[1536]{0:T(1024)(128)(2,1)S(1)}) all-reduce(bf16[1536]{0:T(1024)(128)(2,1)S(1)} %dynamic-update-slice, bf16[1536]{0:T(1024)(128)(2,1)S(1)} %dynamic-update-slice.1), channel_id=1, replica_groups=mesh['fsdp'=4,'ctx'=4,'tp'=2] {'fsdp','ctx'}, use_global_device_ids=true, to_apply=%add | all-reduce | flops 3072 | bytes 12288
  53.6 8.9 all-gather.12.cloned.1.call-done
  76.7 13.3 all-gather.14.cloned.1.call-done
  93.3 7.3 fusion.169
  100.6 5.9 fusion.170
  106.5 5.8 fusion.171
  113.8 6.9 fusion.22
  120.8 6.1 fusion.104
  130.9 6.3 fusion.103
  139.8 6.8 fusion.172
  146.7 6.2 fusion.19
  168.7 20.4 all-gather.2
  189.6 9.1 reduce-window.6
  199.5 8.1 scatter_custom_fusion.1
  207.6 9.5 scatter_custom_fusion
  217.2 33.9 %all-reduce.13.cloned.1.call-done = f32[512,1536]{1,0:T(8,128)} async-done(((f32[512,1536]{1,0:T(8,128)}), f32[512,1536]{1,0:T(8,128)}) %all-reduce.13.cloned.1.call-update) | async-done | bytes 3145744 | tf_op jit(solution)/shard_map/psum | solution.py:160
  257.5 14.8 gather_fusion
  276.1 22.9 gather_fusion.2
  299.1 14.3 broadcast_select_fusion
  318.5 8.7 multiply_reduce_fusion.1
  327.2 197.1 %all-to-all-done = bf16[8,384,1536]{2,1,0:T(8,128)(2,1)} async-done(((bf16[8,384,1536]{2,1,0:T(8,128)(2,1)}), bf16[8,384,1536]{2,1,0:T(8,128)(2,1)}, u32[]{:S(2)}, u32[]{:S(2)}) %all-to-all-start) | async-done | bytes 9437216 | tf_op jit(solution)/shard_map/all_to_all | solution.py:183
  532.2 18.4 fusion.61
  550.6 29.4 %all-gather.20.cloned.1.call-done = bf16[4,512,1536]{2,1,0:T(8,128)(2,1)} async-done(((bf16[4,512,384]{2,1,0:T(8,128)(2,1)}), bf16[4,512,1536]{2,1,0:T(8,128)(2,1)}) %all-gather.20.cloned.1.call-update) | async-done | bytes 6291472 | tf_op jit(solution)/shard_map/all_gather | solution.py:129
  580.0 154.6 %all-to-all-done.2 = bf16[8,384,1536]{2,1,0:T(8,128)(2,1)} async-done(((bf16[8,384,1536]{2,1,0:T(8,128)(2,1)}), bf16[8,384,1536]{2,1,0:T(8,128)(2,1)}, u32[]{:S(2)}, u32[]{:S(2)}) %all-to-all-start.2) | async-done | bytes 9437216 | tf_op jit(solution)/shard_map/all_to_all | solution.py:219
  734.6 15.0 fusion.39
  749.6 18.4 convert_bitcast_fusion
  768.0 8.2 copy.224
  781.3 10.2 convert_bitcast_fusion.1
  791.4 8.4 copy.219
  799.8 185.8 %all-to-all-done.3 = bf16[8,384,1536]{2,1,0:T(8,128)(2,1)} async-done(((bf16[8,384,1536]{2,1,0:T(8,128)(2,1)}), bf16[8,384,1536]{2,1,0:T(8,128)(2,1)}, u32[]{:S(2)}, u32[]{:S(2)}) %all-to-all-start.3) | async-done | bytes 9437216 | tf_op jit(solution)/shard_map/all_to_all | solution.py:245
  991.0 167.0 %all-gather.3 = bf16[16,2,32]{2,1,0:T(2,128)(2,1)S(1)} all-gather(bf16[1,2,32]{2,1,0:T(2,128)(2,1)S(1)} %bitcast.365), channel_id=1, replica_groups=mesh['fsdp'=4,'ctx'=4,'tp'=2] {'fsdp','ctx'}, dimensions={0}, use_global_device_ids=true | all-gather | bytes 2176 | tf_op jit(solution)/shard_map/all_gather | solution.py:116
  1159.9 18.6 gather_fusion.3
  1178.4 8.1 convert_reduce_fusion
  1186.5 8.9 all-to-all-done.1
  1195.4 18.3 gather_fusion.1
  1213.7 9.6 fusion.1
  1233.6 81.5 %all-gather.22.cloned.1.call-done = f32[512,1536]{1,0:T(8,128)} async-done(((f32[256,1536]{1,0:T(8,128)}), f32[512,1536]{1,0:T(8,128)}) %all-gather.22.cloned.1.call-update) | async-done | bytes 3145744 | tf_op jit(solution)/shard_map/all_gather | solution.py:263
  1319.4 6.8 fusion.85
  1326.2 8.9 fusion.2
  1337.2 5.8 fusion.5
  1345.2 5.8 fusion.8
  1350.9 6.6 fusion.76
  1357.5 8.5 fusion.11
  1366.0 12.6 fusion.4
  1383.4 9.5 fusion.7
  1397.8 10.5 fusion.10
  1413.1 6.7 fusion.13
  1425.0 7.3 all-gather
  1434.4 12.4 fusion.34
  1470.7 6.1 fusion.106
  1477.0 5.6 fusion.105
  1482.8 19.2 convolution_bitcast_fusion
  1512.3 17.8 reduce-scatter.19.cloned.1.call-done
  1531.2 100.2 %reduce-scatter.17.cloned.1.call-done = f32[4,512,384]{2,1,0:T(8,128)} async-done(((f32[4,512,1536]{2,1,0:T(8,128)}), f32[4,512,384]{2,1,0:T(8,128)}) %reduce-scatter.17.cloned.1.call-update) | async-done | bytes 3145744 | tf_op jit(solution)/shard_map/reduce_scatter | solution.py:313
  1637.1 74.8 %reduce-scatter.13.cloned.1.call-done = f32[768,96]{0,1:T(8,128)} async-done(((f32[768,1536]{0,1:T(8,128)}), f32[768,96]{0,1:T(8,128)}) %reduce-scatter.13.cloned.1.call-update) | async-done | bytes 294928 | tf_op jit(solution)/shard_map/reduce_scatter | solution.py:325
  1713.6 85.9 %all-reduce.15.cloned.1.call-done = f32[512,1536]{1,0:T(8,128)} async-done(((f32[512,1536]{1,0:T(8,128)}), f32[512,1536]{1,0:T(8,128)}) %all-reduce.15.cloned.1.call-update) | async-done | bytes 3145744 | tf_op jit(solution)/shard_map/psum | solution.py:320
  1802.4 62.3 %all-reduce.7 = (f32[1536]{0:T(1024)S(1)}, f32[1536]{0:T(1024)S(1)}) all-reduce(f32[1536]{0:T(1024)S(1)} %get-tuple-element.41, f32[1536]{0:T(1024)S(1)} %reduce_sum.591), channel_id=10, replica_groups=mesh['fsdp'=4,'ctx'=4,'tp'=2] {'fsdp','ctx'}, use_global_device_ids=true, to_apply=%region_51.52.clone | all-reduce | flops 3072 | bytes 24576
  1867.3 5.4 fusion.67
  1872.7 27.8 %reduce-scatter.11.cloned.1.call-done = f32[96,1280]{1,0:T(8,128)} async-done(((f32[1536,1280]{1,0:T(8,128)}), f32[96,1280]{1,0:T(8,128)}) %reduce-scatter.11.cloned.1.call-update) | async-done | bytes 491536 | tf_op jit(solution)/shard_map/reduce_scatter | solution.py:324
  1902.3 41.4 %all-reduce.5 = (f32[1536]{0:T(1024)S(1)}, f32[2560]{0:T(1024)S(1)}, f32[1536]{0:T(1024)S(1)}, f32[1536]{0:T(1024)S(1)}, f32[1536]{0:T(1024)S(1)}, /*index=5*/f32[32]{0:T(128)S(1)}) all-reduce(f32[1536]{0:T(1024)S(1)} %dynamic_update_slice.27, ...), channel_id=1, replica_groups=mesh['fsdp'=4,'ctx'=4,'tp'=2] {'fsdp','ctx','tp'}, use_global_device_ids=true, to_apply=%region_64.65 | all-reduce | flops 8736 | bytes 69888 | tf_op jit(solution)/shard_map/psum | solution.py:361
  1948.7 135.1 %reduce-scatter.15.cloned.1.call-done = f32[4,384,1024]{2,1,0:T(8,128)} async-done(((f32[4,1536,1024]{2,1,0:T(8,128)}), f32[4,384,1024]{2,1,0:T(8,128)}) %reduce-scatter.15.cloned.1.call-update) | async-done | bytes 6291472 | tf_op jit(solution)/shard_map/reduce_scatter | solution.py:312
  2094.9 125.4 %all-reduce.17.cloned.1.call-done = (f32[32,1536]{1,0:T(8,128)}, f32[32,1024]{1,0:T(8,128)}, f32[32,512]{1,0:T(8,128)}, f32[32,1536]{1,0:T(8,128)}) async-done(((f32[32,1536]{1,0:T(8,128)}, f32[32,1024]{1,0:T(8,128)}, f32[32,512]{1,0:T(8,128)}, f32[32,1536]{1,0:T(8,128)}), (f32[32,1536]{1,0:T(8,128)}, f32[32,1024]{1,0:T(8,128)}, f32[32,512]{1,0:T(8,128)}, ...) | async-done | bytes 589840 | tf_op jit(solution)/shard_map/psum | solution.py:361
  2233.9 40.6 %all-reduce.4 = (f32[32]{0:T(128)S(1)}, f32[7]{0:T(128)S(1)}, f32[7]{0:T(128)S(1)}) all-reduce(f32[32]{0:T(128)} %get-tuple-element.51, f32[7]{0:T(128)} %stack.95, f32[7]{0:T(128)S(1)} %stack.103), channel_id=1, replica_groups=mesh['fsdp'=4,'ctx'=4,'tp'=2] {'fsdp','ctx','tp'}, use_global_device_ids=true, to_apply=%region_42.43 | all-reduce | flops 46 | bytes 368 | tf_op jit(solution)/shard_map/psum | solution.py:361
  2289.4 8.5 fusion.157
  (471 shorter events, 218.0 us)
Async XLA Ops:
  7.2 55.3 %all-gather.12.cloned.1.call-start = ((), (), s32[]{:S(2)}) async-start(), calls=%async_computation.10 | async-start | bytes 4177920 | tf_op jit(solution)/shard_map/all_gather | solution.py:111
  9.9 80.2 %all-gather.14.cloned.1.call-start = ((), (), s32[]{:S(2)}) async-start(), calls=%async_computation.11 | async-start | bytes 2621440 | tf_op jit(solution)/shard_map/all_gather | solution.py:130
  51.2 16.2 copy-start.43
  53.6 16.6 copy-start.99
  68.3 91.8 %all-gather.16.cloned.1.call-start = ((), (), s32[]{:S(2)}) async-start(), calls=%async_computation.12 | async-start | bytes 2506752 | tf_op jit(solution)/shard_map/all_gather | solution.py:112
  69.6 181.4 %all-reduce.13.cloned.1.call-start = ((), (), s32[]{:S(2)}) async-start(), calls=%async_computation.13 | async-start | bytes 6291456 | tf_op jit(solution)/shard_map/psum | solution.py:160
  76.7 29.8 %copy-start.19 = (bf16[512,768]{0,1:T(8,128)(2,1)}, bf16[512,768]{0,1:T(8,128)(2,1)S(1)}, u32[]{:S(2)}) copy-start(bf16[512,768]{0,1:T(8,128)(2,1)S(1)} %copy.208) | copy-start | bytes 2359300
  93.3 46.5 %copy-start.17 = (bf16[2048,256]{0,1:T(8,128)(2,1)}, bf16[2048,256]{0,1:T(8,128)(2,1)S(1)}, u32[]{:S(2)}) copy-start(bf16[2048,256]{0,1:T(8,128)(2,1)S(1)} %copy.207) | copy-start | bytes 3145732
  100.6 20.1 copy-start.50
  106.5 24.4 %copy-start.52 = (f32[3,512]{1,0:T(4,128)}, f32[3,512]{1,0:T(4,128)S(1)}, u32[]{:S(2)}) copy-start(f32[3,512]{1,0:T(4,128)S(1)} %get-tuple-element.144) | copy-start | bytes 18436
  112.3 40.6 %copy-start.54 = (f32[3,512]{1,0:T(4,128)}, f32[3,512]{1,0:T(4,128)S(1)}, u32[]{:S(2)}) copy-start(f32[3,512]{1,0:T(4,128)S(1)} %get-tuple-element.146) | copy-start | bytes 18436
  113.8 41.5 %copy-start.15 = (bf16[2048,256]{0,1:T(8,128)(2,1)}, bf16[2048,256]{0,1:T(8,128)(2,1)S(1)}, u32[]{:S(2)}) copy-start(bf16[2048,256]{0,1:T(8,128)(2,1)S(1)} %copy.205) | copy-start | bytes 3145732
  167.4 88.1 %copy-start.41 = (s32[256,8]{0,1:T(8,128)}, s32[256,8]{0,1:T(8,128)S(1)}, u32[]{:S(2)}) copy-start(s32[256,8]{0,1:T(8,128)S(1)} %get-tuple-element.105) | copy-start | bytes 24580
  167.8 86.8 %copy-start.39 = (f32[1536]{0:T(1024)}, f32[1536]{0:T(1024)S(1)}, u32[]{:S(2)}) copy-start(f32[1536]{0:T(1024)S(1)} %convert_element_type.223) | copy-start | bytes 18436
  168.0 104.3 %copy-start.9 = (f32[256,1536]{1,0:T(8,128)}, f32[256,1536]{1,0:T(8,128)S(1)}, u32[]{:S(2)}) copy-start(f32[256,1536]{1,0:T(8,128)S(1)} %convert_element_type.234) | copy-start | bytes 4718596
  189.2 66.9 %copy-start.28 = (bf16[1536,32]{0,1:T(8,128)(2,1)}, bf16[1536,32]{0,1:T(8,128)(2,1)S(1)}, u32[]{:S(2)}) copy-start(bf16[1536,32]{0,1:T(8,128)(2,1)S(1)} %reshape.529) | copy-start | bytes 294916
  199.5 53.7 %copy-start.67 = (s32[2048,1]{0,1:T(1,128)}, s32[2048,1]{0,1:T(1,128)S(1)}, u32[]{:S(2)}) copy-start(s32[2048,1]{0,1:T(1,128)S(1)} %compare_select_fusion) | copy-start | bytes 24580
  254.5 17.7 copy-start
  313.4 210.9 %all-to-all-start = ((bf16[8,384,1536]{2,1,0:T(8,128)(2,1)}), bf16[8,384,1536]{2,1,0:T(8,128)(2,1)}, u32[]{:S(2)}, u32[]{:S(2)}) async-start(bf16[8,384,1536]{2,1,0:T(8,128)(2,1)} %get-tuple-element.128), calls=%async_computation | async-start | bytes 18874368 | tf_op jit(solution)/shard_map/all_to_all | solution.py:183
  318.5 213.7 %all-gather.18.cloned.1.call-start = ((), (), s32[]{:S(2)}) async-start(), calls=%async_computation.14 | async-start | bytes 15728640 | tf_op jit(solution)/shard_map/all_gather | solution.py:128
  524.3 210.3 %all-to-all-start.2 = ((bf16[8,384,1536]{2,1,0:T(8,128)(2,1)}), bf16[8,384,1536]{2,1,0:T(8,128)(2,1)}, u32[]{:S(2)}, u32[]{:S(2)}) async-start(bf16[8,384,1536]{2,1,0:T(8,128)(2,1)} %get-tuple-element.127), calls=%async_computation.2 | async-start | bytes 18874368 | tf_op jit(solution)/shard_map/all_to_all | solution.py:219
  529.6 50.4 %all-gather.20.cloned.1.call-start = ((), (), s32[]{:S(2)}) async-start(), calls=%async_computation.15 | async-start | bytes 7864320 | tf_op jit(solution)/shard_map/all_gather | solution.py:129
  749.6 31.7 %copy-start.103 = (bf16[8,4,96,512]{3,2,0,1:T(8,128)(2,1)}, bf16[8,4,96,512]{3,2,0,1:T(8,128)(2,1)S(1)}, u32[]{:S(2)}) copy-start(bf16[8,4,96,512]{3,2,0,1:T(8,128)(2,1)S(1)} %get-tuple-element.110) | copy-start | bytes 9437188
  776.1 209.4 %all-to-all-start.3 = ((bf16[8,384,1536]{2,1,0:T(8,128)(2,1)}), bf16[8,384,1536]{2,1,0:T(8,128)(2,1)}, u32[]{:S(2)}, u32[]{:S(2)}) async-start(bf16[8,384,1536]{2,1,0:T(8,128)(2,1)} %bitcast.316), calls=%async_computation.3 | async-start | bytes 18874368 | tf_op jit(solution)/shard_map/all_to_all | solution.py:245
  985.6 172.4 %copy-start.68 = (s32[2048,1]{0,1:T(1,128)S(1)}, s32[2048,1]{0,1:T(1,128)}, u32[]{:S(2)}) copy-start(s32[2048,1]{0,1:T(1,128)} %copy-done.67) | copy-start | bytes 24580
  985.6 172.5 %copy-start.31 = (f32[256,32]{0,1:T(8,128)S(1)}, f32[256,32]{0,1:T(8,128)}, u32[]{:S(2)}) copy-start(f32[256,32]{0,1:T(8,128)} %copy-done.30) | copy-start | bytes 98308
  985.6 172.5 %copy-start.79 = (f32[256]{0:T(256)S(1)}, f32[256]{0:T(256)}, u32[]{:S(2)}) copy-start(f32[256]{0:T(256)} %get-tuple-element.150) | copy-start | bytes 3076
  985.6 173.7 %copy-start.78 = (f32[256]{0:T(256)S(1)}, f32[256]{0:T(256)}, u32[]{:S(2)}) copy-start(f32[256]{0:T(256)} %copy-done.77) | copy-start | bytes 3076
  985.6 209.8 %all-to-all-start.1 = ((bf16[8,384,1536]{2,1,0:T(8,128)(2,1)}), bf16[8,384,1536]{2,1,0:T(8,128)(2,1)}, u32[]{:S(2)}, u32[]{:S(2)}) async-start(bf16[8,384,1536]{2,1,0:T(8,128)(2,1)} %bitcast.315), calls=%async_computation.1 | async-start | bytes 18874368 | tf_op jit(solution)/shard_map/all_to_all | solution.py:200
  990.8 324.3 %all-gather.22.cloned.1.call-start = ((), (), s32[]{:S(2)}) async-start(), calls=%async_computation.16 | async-start | bytes 4718592 | tf_op jit(solution)/shard_map/all_gather | solution.py:263
  1158.0 20.4 copy-start.98
  1158.0 20.4 copy-start.94
  1158.1 20.3 copy-start.76
  1195.4 18.3 copy-start.10
  1195.4 18.3 copy-start.24
  1233.4 236.0 %reduce-scatter.9.cloned.1.call-start = ((), (), s32[]{:S(2)}) async-start(), calls=%async_computation.17 | async-start | bytes 5242880 | tf_op jit(solution)/shard_map/reduce_scatter | solution.py:314
  1424.8 105.4 %reduce-scatter.19.cloned.1.call-start = ((), (), s32[]{:S(2)}) async-start(), calls=%async_computation.23 | async-start | bytes 835584
  1434.3 197.1 %reduce-scatter.17.cloned.1.call-start = ((), (), s32[]{:S(2)}) async-start(), calls=%async_computation.22 | async-start | bytes 15728640 | tf_op jit(solution)/shard_map/reduce_scatter | solution.py:313
  1446.8 265.0 %reduce-scatter.13.cloned.1.call-start = ((), (), s32[]{:S(2)}) async-start(), calls=%async_computation.20 | async-start | bytes 5013504 | tf_op jit(solution)/shard_map/reduce_scatter | solution.py:325
  1453.4 346.1 %all-reduce.15.cloned.1.call-start = ((), (), s32[]{:S(2)}) async-start(), calls=%async_computation.18 | async-start | bytes 6291456 | tf_op jit(solution)/shard_map/psum | solution.py:320
  1476.9 423.6 %reduce-scatter.11.cloned.1.call-start = ((), (), s32[]{:S(2)}) async-start(), calls=%async_computation.19 | async-start | bytes 8355840 | tf_op jit(solution)/shard_map/reduce_scatter | solution.py:324
  1482.6 601.2 %reduce-scatter.15.cloned.1.call-start = ((), (), s32[]{:S(2)}) async-start(), calls=%async_computation.21 | async-start | bytes 31457280 | tf_op jit(solution)/shard_map/reduce_scatter | solution.py:312
  1502.0 362.8 %copy-start.100 = (f32[96]{0:T(128)S(1)}, f32[96]{0:T(128)}, u32[]{:S(2)}) copy-start(f32[96]{0:T(128)} %param.48) | copy-start | bytes 1156
  1502.0 362.7 %copy-start.101 = (f32[96]{0:T(128)S(1)}, f32[96]{0:T(128)}, u32[]{:S(2)}) copy-start(f32[96]{0:T(128)} %param.47) | copy-start | bytes 1156
  1502.0 365.2 %copy-start.73 = (f32[512]{0:T(512)S(1)}, f32[512]{0:T(512)}, u32[]{:S(2)}) copy-start(f32[512]{0:T(512)} %copy-done.72) | copy-start | bytes 6148
  1502.0 718.2 %all-reduce.17.cloned.1.call-start = ((), (), s32[]{:S(2)}) async-start(), calls=%async_computation.24 | async-start | bytes 1179648 | tf_op jit(solution)/shard_map/psum | solution.py:361
  1531.0 746.6 %copy-start.35 = (f32[96,32]{0,1:T(8,128)}, f32[96,32]{0,1:T(8,128)S(1)}, u32[]{:S(2)}) copy-start(f32[96,32]{0,1:T(8,128)S(1)} %copy.263) | copy-start | bytes 36868
  1637.1 235.6 %copy-start.34 = (f32[32,512]{1,0:T(8,128)}, f32[32,512]{1,0:T(8,128)S(1)}, u32[]{:S(2)}) copy-start(f32[32,512]{1,0:T(8,128)S(1)} %constant_dynamic-update-slice_fusion) | copy-start | bytes 196612
  1802.4 141.3 %copy-start.80 = (f32[2560]{0:T(1024)S(1)}, f32[2560]{0:T(1024)}, u32[]{:S(2)}) copy-start(f32[2560]{0:T(1024)} %param.38) | copy-start | bytes 30724
  1802.4 141.4 %copy-start.82 = (f32[1536]{0:T(1024)S(1)}, f32[1536]{0:T(1024)}, u32[]{:S(2)}) copy-start(f32[1536]{0:T(1024)} %param.37) | copy-start | bytes 18436
  1802.4 141.4 %copy-start.83 = (f32[1536]{0:T(1024)S(1)}, f32[1536]{0:T(1024)}, u32[]{:S(2)}) copy-start(f32[1536]{0:T(1024)} %param.40) | copy-start | bytes 18436
  1802.4 142.8 %copy-start.84 = (f32[1536]{0:T(1024)S(1)}, f32[1536]{0:T(1024)}, u32[]{:S(2)}) copy-start(f32[1536]{0:T(1024)} %param.41) | copy-start | bytes 18436
  1802.4 142.8 %copy-start.85 = (f32[1536]{0:T(1024)S(1)}, f32[1536]{0:T(1024)}, u32[]{:S(2)}) copy-start(f32[1536]{0:T(1024)} %param.39) | copy-start | bytes 18436
  1802.4 144.9 %copy-start.102 = (f32[32]{0:T(128)S(1)}, f32[32]{0:T(128)}, u32[]{:S(2)}) copy-start(f32[32]{0:T(128)} %param.42) | copy-start | bytes 388
  1872.7 219.6 %copy-start.22 = (f32[768,96]{0,1:T(8,128)S(1)}, f32[768,96]{0,1:T(8,128)}, u32[]{:S(2)}) copy-start(f32[768,96]{0,1:T(8,128)} %reduce-scatter.13.cloned.1.call-done) | copy-start | bytes 884740
  1943.7 285.7 %copy-start.49 = (f32[2560]{0:T(1024)}, f32[2560]{0:T(1024)S(1)}, u32[]{:S(2)}) copy-start(f32[2560]{0:T(1024)S(1)} %add_multiply_fusion.4) | copy-start | bytes 30724
  1944.4 285.0 %copy-start.86 = (f32[1536]{0:T(1024)}, f32[1536]{0:T(1024)S(1)}, u32[]{:S(2)}) copy-start(f32[1536]{0:T(1024)S(1)} %get-tuple-element.103) | copy-start | bytes 18436
  1944.5 278.4 %copy-start.89 = (f32[96]{0:T(128)}, f32[96]{0:T(128)S(1)}, u32[]{:S(2)}) copy-start(f32[96]{0:T(128)S(1)} %dynamic_slice.45) | copy-start | bytes 1156
  1945.8 283.6 %copy-start.74 = (f32[1536]{0:T(1024)}, f32[1536]{0:T(1024)S(1)}, u32[]{:S(2)}) copy-start(f32[1536]{0:T(1024)S(1)} %get-tuple-element.162) | copy-start | bytes 18436
  1946.5 276.3 %copy-start.90 = (f32[96]{0:T(128)}, f32[96]{0:T(128)S(1)}, u32[]{:S(2)}) copy-start(f32[96]{0:T(128)S(1)} %dynamic_slice.48) | copy-start | bytes 1156
  1947.3 276.7 %copy-start.96 = (f32[96]{0:T(128)}, f32[96]{0:T(128)S(1)}, u32[]{:S(2)}) copy-start(f32[96]{0:T(128)S(1)} %dynamic_slice.49) | copy-start | bytes 1156
  1947.3 276.7 %copy-start.95 = (f32[32]{0:T(128)}, f32[32]{0:T(128)S(1)}, u32[]{:S(2)}) copy-start(f32[32]{0:T(128)S(1)} %add_multiply_fusion.12) | copy-start | bytes 388
  2087.3 142.1 %copy-start.4 = (f32[4,512,384]{2,1,0:T(8,128)S(1)}, f32[4,512,384]{2,1,0:T(8,128)}, u32[]{:S(2)}) copy-start(f32[4,512,384]{2,1,0:T(8,128)} %reduce-scatter.17.cloned.1.call-done) | copy-start | bytes 9437188
  2092.3 185.4 %copy-start.46 = (f32[96,32]{0,1:T(8,128)S(1)}, f32[96,32]{0,1:T(8,128)}, u32[]{:S(2)}) copy-start(f32[96,32]{0,1:T(8,128)} %param.32) | copy-start | bytes 36868
  (78 other events, 537.0 us)
Sparse Core Ops, SparseCore 0:
  10.9 51.5 all-gather.11
  68.4 21.6 all-gather.13
  92.9 42.2 all-gather.15
  165.4 85.5 all-reduce.12
  327.3 83.3 all-gather.17
  532.3 47.5 all-gather.19
  1233.5 81.5 all-gather.21
  1424.9 44.4 reduce-scatter.8
  1473.5 56.5 reduce-scatter.18
  1533.3 98.0 reduce-scatter.16
  1636.4 75.4 reduce-scatter.12
  1714.6 84.8 all-reduce.14
  1804.6 95.8 reduce-scatter.10
  1903.7 180.0 reduce-scatter.14
  2092.4 127.8 all-reduce.16
where the time goes:
time: 2320 us; the launch traced here: 2310 us
  waiting for transfers between devices  1290 us (56%)
  blocking collectives  380 us (16%)
  matrix products  247 us (11%)
  other arithmetic  198 us (9%)
  local copies, waits for them, and re-layouts  152 us (7%)
  between operations  25.1 us (1%)
    all_to_all x1, waiting for transfers between devices, per_device(): lax.all_to_all(send_rows.reshape(groups, slot_block, D), ('fsdp', 'tp'),...  197 us
    all_to_all x1, waiting for transfers between devices, per_device(): lax.all_to_all(d_rows.reshape(groups, slot_block, D), ('fsdp', 'tp'), spl...  186 us
    all_gather x1, blocking collectives, per_device(): lax.all_gather(counts_half.astype(jnp.bfloat16), ('fsdp', 'ctx'), axis=0,...  167 us
    all_to_all x1, waiting for transfers between devices, per_device(): lax.all_to_all(d_send.reshape(groups, slot_block, D), ('fsdp', 'tp'), spl...  155 us
    reduce_scatter x1, waiting for transfers between devices, per_device(): lax.psum_scatter(g_gate_up_local, 'ctx', scatter_dimension=1, tiled=True)  135 us
    psum x1, waiting for transfers between devices, per_device(): lax.psum((moment_parts[0], moment_parts[1], moment_parts[2], moment_parts...  125 us
    reduce_scatter x1, waiting for transfers between devices, per_device(): lax.psum_scatter(g_down_local, 'ctx', scatter_dimension=2, tiled=True)  100 us
    unnamed x2, blocking collectives  98.5 us
  transfers between devices with their start and end apart: 19, of which 17 were waited for; matrix products, arithmetic and copies ran while one was open for 12% of the time, Pallas kernels for 0%

commit v1 on v0

v1 whole, which is shorter than its diff:
```python
import jax
import jax.numpy as jnp
from jax import lax
from jax.sharding import PartitionSpec as P

D = 1536
HEADS = 24
KV_HEADS = 8
HEAD = 64
FFE = 512
TOPK = 8
EXPERTS = 32
NSEG = 13

norm_eps = 1e-05
decay = 0.5
floor_sq = 1e-30
rate = 0.25
clip_rms = 0.05
aux_weight = 1.0
bf16 = jnp.bfloat16
f32 = jnp.float32
EVERY = ("fsdp", "ctx", "tp")


def dot(spec, left, right):
    return jnp.einsum(spec, left, right, preferred_element_type=f32)


def exchange(values, axes):
    return lax.all_to_all(values, axes, split_axis=0, concat_axis=0, tiled=True)


def share(vector, count):
    return exchange(jnp.broadcast_to(vector[None], (count,) + vector.shape), EVERY)


def inv_rms(values):
    return lax.rsqrt(jnp.mean(values * values, axis=-1, keepdims=True) + norm_eps)


def norm_backward(values, inv, gain, d_out):
    normed = values * inv
    scaled = d_out * gain
    d_values = inv * (scaled - normed * jnp.mean(scaled * normed, axis=-1, keepdims=True))
    return d_values, normed


def ancestry(parent_row):
    seg_labels = jnp.arange(NSEG, dtype=jnp.int32)
    table = jnp.maximum(
        (seg_labels[:, None] == seg_labels[None, :]).astype(f32),
        (parent_row[:, None] == seg_labels[None, :]).astype(f32),
    )
    for sweep in range(NSEG.bit_length()):
        table = jnp.max(table[:, :, None] * table[None, :, :], axis=1)
    return table


def attention_forward(query, key, value, allowed, blocks):
    rows = query.shape[0] // blocks
    outs, logs = [], []
    for b in range(blocks):
        seen = (b + 1) * rows
        mine = slice(b * rows, seen)
        scores = dot("qgd,kd->gqk", query[mine], key[:seen]) * HEAD ** (-0.5)
        masked = jnp.where(allowed[None, mine, :seen], scores, -1e30)
        row_max = jnp.max(masked, axis=-1, keepdims=True)
        exp_scores = jnp.exp(masked - row_max)
        row_total = jnp.sum(exp_scores, axis=-1, keepdims=True)
        prob_low = (exp_scores / row_total).astype(bf16)
        logs.append(row_max + jnp.log(row_total))
        outs.append(dot("gqk,kd->qgd", prob_low, value[:seen]))
    return jnp.concatenate(outs, axis=0).astype(bf16), logs


def attention_backward(query, key, value, allowed, logs, d_out):
    blocks = len(logs)
    rows = query.shape[0] // blocks
    scale = HEAD ** (-0.5)
    d_key = jnp.zeros(key.shape, f32)
    d_value = jnp.zeros(key.shape, f32)
    d_queries = []
    for b in range(blocks):
        seen = (b + 1) * rows
        mine = slice(b * rows, seen)
        scores = dot("qgd,kd->gqk", query[mine], key[:seen]) * scale
        masked = jnp.where(allowed[None, mine, :seen], scores, -1e30)
        prob_full = jnp.exp(masked - logs[b])
        d_prob = dot("qgd,kd->gqk", d_out[mine], value[:seen])
        delta = jnp.sum(prob_full * d_prob, axis=-1, keepdims=True)
        d_scores = (prob_full * (d_prob - delta)).astype(bf16)
        d_queries.append(dot("gqk,kd->qgd", d_scores, key[:seen]) * scale)
        d_key = d_key.at[:seen].add(dot("gqk,qgd->kd", d_scores, query[mine]) * scale)
        d_value = d_value.at[:seen].add(dot("gqk,qgd->kd", prob_full.astype(bf16), d_out[mine]))
    return jnp.concatenate(d_queries, axis=0), d_key, d_value


def per_device(
    inputs,
    cotangent,
    routes,
    segment_ids,
    parents,
    w_qkv,
    w_out,
    w_router,
    w_gate_up,
    w_down,
    gain_attn,
    gain_moe,
    row_qkv,
    col_qkv,
    row_out,
    col_out,
    row_router,
    col_router,
    row_gate_up,
    col_gate_up,
    row_down,
    col_down,
    second_attn,
    second_moe,
):
    tp_count = lax.axis_size("tp")
    ctx_count = lax.axis_size("ctx")
    fsdp_count = lax.axis_size("fsdp")
    count = tp_count * ctx_count * fsdp_count
    tp_index = lax.axis_index("tp")
    ctx_index = lax.axis_index("ctx")
    fsdp_index = lax.axis_index("fsdp")
    flat_index = fsdp_index * ctx_count + ctx_index
    owner_index = fsdp_index * tp_count + tp_index
    keep_once = (tp_index == 0).astype(f32)
    tok_rows = inputs.shape[0]
    half_rows = tok_rows // tp_count
    tree_len = segment_ids.shape[1]
    tokens_all = tok_rows * fsdp_count * ctx_count
    capacity = half_rows * TOPK * 3 // (2 * EXPERTS)
    groups = fsdp_count * tp_count
    local_experts = EXPERTS // groups
    q_own = HEADS // (tp_count * ctx_count)
    kv_own = KV_HEADS // (tp_count * ctx_count)
    group_size = HEADS // KV_HEADS
    q_cols = q_own * HEAD
    kv_cols = kv_own * HEAD
    own_cols = q_cols + 2 * kv_cols
    dense_rows = w_qkv.shape[0]
    qkv_cols = w_qkv.shape[1]
    dense_parts = fsdp_count * ctx_count
    ctx_rows = w_gate_up.shape[1]
    labels = jnp.arange(EXPERTS, dtype=jnp.int32)

    def by_ctx(columns):
        q_end = ctx_count * q_cols
        k_end = q_end + ctx_count * kv_cols
        lead = columns.shape[:-1]
        return jnp.concatenate(
            [
                columns[..., :q_end].reshape(lead + (ctx_count, q_cols)),
                columns[..., q_end:k_end].reshape(lead + (ctx_count, kv_cols)),
                columns[..., k_end:].reshape(lead + (ctx_count, kv_cols)),
            ],
            axis=-1,
        )

    def from_ctx(columns):
        lead = columns.shape[:-2]
        return jnp.concatenate(
            [
                columns[..., :q_cols].reshape(lead + (-1,)),
                columns[..., q_cols : q_cols + kv_cols].reshape(lead + (-1,)),
                columns[..., q_cols + kv_cols :].reshape(lead + (-1,)),
            ],
            axis=-1,
        )

    w_qkv_low = w_qkv.astype(bf16)
    w_grouped = by_ctx(w_qkv_low)
    extras = jnp.concatenate(
        [gain_attn.astype(bf16)[:, None], gain_moe.astype(bf16)[:, None], w_router.astype(bf16)],
        axis=1,
    )
    w_send = jnp.concatenate(
        [
            jnp.moveaxis(w_grouped, 1, 0),
            jnp.broadcast_to(extras[None], (ctx_count,) + extras.shape),
        ],
        axis=-1,
    )
    w_send = jnp.broadcast_to(w_send[None], (fsdp_count,) + w_send.shape)
    w_got = exchange(w_send.reshape((dense_parts,) + w_send.shape[2:]), ("fsdp", "ctx"))
    w_got = w_got.reshape(D, own_cols + 2 + EXPERTS)
    tree_inputs = lax.all_gather(inputs, "ctx", axis=0, tiled=True).astype(f32)
    w_own = w_got[:, :own_cols]
    gain_one = w_got[:, own_cols].astype(f32)
    gain_two = w_got[:, own_cols + 1].astype(f32)
    router_full = w_got[:, own_cols + 2 :]

    my_routes = lax.dynamic_slice_in_dim(routes, tp_index * half_rows, half_rows, 0)
    hit = jnp.sum((my_routes[..., None] == labels).astype(f32), axis=1)
    master_sums = jnp.stack(
        [
            jnp.sum(w_qkv * w_qkv),
            jnp.sum(w_out * w_out),
            keep_once * jnp.sum(w_router * w_router),
            jnp.sum(w_gate_up * w_gate_up),
            jnp.sum(w_down * w_down),
            keep_once * jnp.sum(gain_attn * gain_attn),
            keep_once * jnp.sum(gain_moe * gain_moe),
        ]
    )
    early = jnp.sum(share(jnp.concatenate([jnp.sum(hit, axis=0), master_sums]), count), axis=0)
    fraction = early[:EXPERTS] / (tokens_all * TOPK)
    master_totals = early[EXPERTS:]
    before = (
        jnp.arange(half_rows, dtype=jnp.int32)[:, None]
        < jnp.arange(half_rows, dtype=jnp.int32)[None, :]
    ).astype(bf16)
    rank = dot("te,tu->eu", hit.astype(bf16), before)
    rank = jnp.where(hit.T > 0.5, rank, -1.0)
    ranks = exchange(rank.reshape(groups, local_experts, half_rows), ("fsdp", "tp"))
    grad_rows = lax.all_gather(cotangent, ("fsdp", "tp"), axis=0, tiled=True)
    grad_rows = grad_rows.reshape(groups, half_rows, D)
    gate_up_all = lax.all_gather(w_gate_up.astype(bf16), "ctx", axis=1, tiled=True)
    down_all = lax.all_gather(w_down.astype(bf16), "ctx", axis=2, tiled=True)
    out_t = lax.all_gather(w_out.astype(bf16).T, ("tp", "fsdp", "ctx"), axis=0, tiled=True)
    out_t = out_t.reshape(tp_count, D, w_out.shape[0])
    qkv_full = lax.all_gather(
        w_grouped.reshape(dense_rows, qkv_cols), ("tp", "fsdp", "ctx"), axis=0, tiled=True
    ).reshape(tp_count, D, qkv_cols)

    act1 = (tree_inputs * inv_rms(tree_inputs) * gain_one).astype(bf16)
    qkv = dot("td,dc->tc", act1, w_own).astype(bf16)
    query = qkv[:, :q_cols].reshape(tree_len, kv_own, group_size, HEAD)
    keys = qkv[:, q_cols : q_cols + kv_cols].reshape(tree_len, kv_own, HEAD)
    values = qkv[:, q_cols + kv_cols :].reshape(tree_len, kv_own, HEAD)
    seg_hot = (segment_ids[0][:, None] == jnp.arange(NSEG, dtype=jnp.int32)).astype(bf16)
    reach = dot("qs,ks->qk", dot("qs,su->qu", seg_hot, ancestry(parents[0]).astype(bf16)).astype(bf16), seg_hot)
    positions = jnp.arange(tree_len, dtype=jnp.int32)
    allowed = (reach > 0.5) & (positions[None, :] <= positions[:, None])
    blocks = 4
    outs, logs = [], []
    for h in range(kv_own):
        out_h, log_h = attention_forward(query[:, h], keys[:, h], values[:, h], allowed, blocks)
        outs.append(out_h)
        logs.append(log_h)
    attended_own = jnp.concatenate(outs, axis=1).reshape(tree_len, q_cols)
    attended = exchange(attended_own, ("ctx", "tp")).reshape(ctx_count, tp_count, half_rows, q_cols)
    attended = attended.transpose(2, 1, 0, 3).reshape(half_rows, tp_count, ctx_count * q_cols)
    inputs_half = lax.dynamic_slice_in_dim(inputs, tp_index * half_rows, half_rows, 0).astype(f32)
    x_one = inputs_half + dot("rtk,tdk->rd", attended, out_t)

    inv_two = inv_rms(x_one)
    act2 = (x_one * inv_two * gain_two).astype(bf16)
    rows = lax.all_gather(act2, ("fsdp", "tp"), axis=0, tiled=True).reshape(groups, half_rows, D)
    logits = dot("td,de->te", act2, router_full)
    router_probs = jax.nn.softmax(logits, axis=-1)
    combine = jax.nn.softmax(jnp.where(hit > 0.5, logits, -jnp.inf), axis=-1)
    weights = exchange(combine.T.reshape(groups, local_experts, half_rows), ("fsdp", "tp"))

    slots = jnp.arange(capacity, dtype=f32)
    chosen = ranks[:, :, None, :] == slots[None, None, :, None]
    pick = chosen.astype(bf16)
    slot_weight = jnp.sum(jnp.where(chosen, weights[:, :, None, :], 0.0), axis=-1)
    x_e = dot("sert,std->serd", pick, rows).astype(bf16)
    c_e = dot("sert,std->serd", pick, grad_rows)
    gate_up = dot("serd,edf->serf", x_e, gate_up_all)
    gate = gate_up[..., :FFE]
    up = gate_up[..., FFE:]
    sig = jax.nn.sigmoid(gate)
    hidden = (gate * sig * up).astype(bf16)
    expert_out = dot("serf,efd->serd", hidden, down_all).astype(bf16)
    d_slot_out = jnp.sum(c_e * expert_out.astype(f32), axis=-1)
    d_slot = (slot_weight[..., None] * c_e).astype(bf16)
    d_hidden = dot("serd,efd->serf", d_slot, down_all)
    g_down_local = dot("serf,serd->efd", hidden, d_slot)
    d_gate = d_hidden * up * sig * (1.0 + gate * (1.0 - sig))
    d_up = d_hidden * gate * sig
    d_gate_up = jnp.concatenate([d_gate, d_up], axis=-1).astype(bf16)
    d_row = dot("serf,edf->serd", d_gate_up, gate_up_all).astype(bf16)
    g_gate_up_local = dot("serd,serf->edf", x_e, d_gate_up)
    d_sum = dot("sert,serd->std", pick, d_row).astype(bf16)
    weighted = (slot_weight[..., None] * expert_out.astype(f32)).astype(bf16)
    moe_sum = dot("sert,serd->std", pick, weighted).astype(bf16)
    d_combine_own = jnp.sum(jnp.where(chosen, d_slot_out[..., None], 0.0), axis=2)
    d_combine = exchange(d_combine_own, ("fsdp", "tp")).reshape(EXPERTS, half_rows).T
    d_act2 = lax.psum_scatter(
        d_sum.reshape(groups * half_rows, D), ("fsdp", "tp"), scatter_dimension=0, tiled=True
    ).astype(f32)
    moe = lax.psum_scatter(
        moe_sum.reshape(groups * half_rows, D), ("fsdp", "tp"), scatter_dimension=0, tiled=True
    ).astype(f32)
    layer_out = (x_one + moe).astype(bf16)
    g_gate_up = lax.psum_scatter(
        g_gate_up_local.astype(bf16), "ctx", scatter_dimension=1, tiled=True
    ).astype(f32)
    g_down = lax.psum_scatter(
        g_down_local.astype(bf16), "ctx", scatter_dimension=2, tiled=True
    ).astype(f32)

    aux_grad = aux_weight * EXPERTS * fraction
    d_logits = combine * (d_combine - jnp.sum(combine * d_combine, axis=-1, keepdims=True))
    d_logits = d_logits + router_probs * (
        aux_grad - jnp.sum(router_probs * aux_grad, axis=-1, keepdims=True)
    )
    d_logits = d_logits.astype(bf16)
    d_act2 = d_act2 + dot("te,de->td", d_logits, router_full)
    d_half, normed_two = norm_backward(x_one, inv_two, gain_two, d_act2)
    d_x1_half = cotangent.astype(f32) + d_half
    d_x1_low = d_x1_half.astype(bf16)
    g_small = jnp.concatenate(
        [dot("te,td->ed", d_logits, act2), jnp.sum(d_act2 * normed_two, axis=0)[None]], axis=0
    )
    g_small = jnp.moveaxis(g_small.reshape(EXPERTS + 1, dense_parts, dense_rows), 1, 0)
    g_small = jnp.broadcast_to(g_small[:, None], (dense_parts, tp_count) + g_small.shape[1:])
    g_small = exchange(g_small.reshape((count,) + g_small.shape[2:]), EVERY)
    g_small = jnp.sum(g_small, axis=0)
    g_router = g_small[:EXPERTS].T
    g_gain2 = g_small[EXPERTS]

    d_attended = dot("rd,tdk->rtk", d_x1_low, out_t).astype(bf16)
    d_attended = d_attended.reshape(half_rows, tp_count, ctx_count, q_cols).transpose(2, 1, 0, 3)
    d_attended = exchange(d_attended.reshape(tree_len, q_cols), ("ctx", "tp"))
    d_attended = d_attended.reshape(tree_len, kv_own, group_size, HEAD)
    d_q, d_k, d_v = [], [], []
    for h in range(kv_own):
        dq_h, dk_h, dv_h = attention_backward(
            query[:, h], keys[:, h], values[:, h], allowed, logs[h], d_attended[:, h]
        )
        d_q.append(dq_h.reshape(tree_len, -1))
        d_k.append(dk_h)
        d_v.append(dv_h)
    d_qkv = jnp.concatenate(d_q + d_k + d_v, axis=1).astype(bf16)
    g_qkv_part = dot("td,tc->dc", act1, d_qkv).astype(bf16)
    g_qkv_got = exchange(g_qkv_part.reshape(dense_parts, dense_rows, own_cols), ("fsdp", "ctx"))
    g_qkv_got = g_qkv_got.reshape(fsdp_count, ctx_count, dense_rows, own_cols).astype(f32)
    g_qkv = from_ctx(jnp.moveaxis(jnp.sum(g_qkv_got, axis=0), 0, 1))
    d_qkv_send = jnp.broadcast_to(
        d_qkv.reshape(ctx_count, 1, tok_rows, own_cols), (ctx_count, tp_count, tok_rows, own_cols)
    )
    d_qkv_all = exchange(d_qkv_send.reshape(-1, tok_rows, own_cols), ("ctx", "tp"))
    d_qkv_all = d_qkv_all.reshape(ctx_count, tp_count, tok_rows, own_cols)
    d_qkv_all = d_qkv_all.transpose(2, 1, 0, 3).reshape(tok_rows, tp_count, qkv_cols)
    d_act1 = dot("rtc,tdc->rd", d_qkv_all, qkv_full)
    own_inputs = inputs.astype(f32)
    d_inputs_attn, _ = norm_backward(own_inputs, inv_rms(own_inputs), gain_one, d_act1)
    d_x1 = lax.all_gather(d_x1_half, "tp", axis=0, tiled=True)
    grad_inputs = d_x1 + d_inputs_attn

    attended_t = attended.transpose(1, 0, 2)
    attended_pair = exchange(attended_t, "tp").reshape(tok_rows, -1)
    d_x1_pair = d_x1.astype(bf16)
    g_out_part = dot("td,tq->dq", d_x1_pair, attended_pair).astype(bf16)
    g_out_got = exchange(g_out_part.reshape(dense_parts, dense_rows, -1), ("fsdp", "ctx"))
    g_out = jnp.sum(g_out_got.astype(f32), axis=0).T

    sq_out = g_out * g_out
    sq_router = g_router * g_router
    out_rows = w_out.shape[0]
    first = jnp.concatenate(
        [
            jnp.sum(sq_out, axis=1),
            jnp.sum(sq_out, axis=0),
            jnp.sum(sq_router, axis=1),
            jnp.sum(sq_router, axis=0),
            jnp.sum(router_probs, axis=0),
        ]
    )
    first = share(first, count).reshape(dense_parts, tp_count, -1)
    at = [out_rows, out_rows + dense_rows, out_rows + 2 * dense_rows]
    at.append(at[-1] + EXPERTS)
    tot_row_out = jnp.sum(first[..., : at[0]], axis=0).reshape(-1)
    tot_col_out = jnp.sum(first[..., at[0] : at[1]], axis=1).reshape(-1)
    tot_row_router = first[:, 0, at[1] : at[2]].reshape(-1)
    tot_col_router = jnp.sum(first[:, 0, at[2] : at[3]], axis=0)
    prob_totals = jnp.sum(first[..., at[3] :], axis=(0, 1))

    sq_gate_up = g_gate_up * g_gate_up
    sq_down = g_down * g_down
    expert_parts = jnp.concatenate(
        [
            jnp.sum(sq_gate_up, axis=2),
            jnp.sum(sq_down, axis=1),
            jnp.sum(sq_gate_up, axis=1),
            jnp.sum(sq_down, axis=2),
        ],
        axis=1,
    )
    expert_got = share(expert_parts, count).reshape(
        fsdp_count, ctx_count, tp_count, local_experts, -1
    )
    split_rows = expert_got[..., : 2 * ctx_rows].transpose(0, 2, 3, 1, 4)
    summed = jnp.sum(expert_got[..., 2 * ctx_rows :], axis=1).reshape(EXPERTS, -1)
    tot_row_gu = split_rows[..., :ctx_rows].reshape(EXPERTS, D)
    tot_col_down = split_rows[..., ctx_rows:].reshape(EXPERTS, D)
    tot_col_gu = summed[:, : 2 * FFE]
    tot_row_down = summed[:, 2 * FFE :]

    sq_qkv = g_qkv * g_qkv
    gain_part = jnp.sum(g_qkv * w_qkv_low.astype(f32), axis=1) / gain_attn.astype(bf16).astype(f32)
    second = jnp.concatenate([jnp.sum(sq_qkv, axis=1), gain_part, jnp.sum(sq_qkv, axis=0)])
    second = share(second, count).reshape(dense_parts, tp_count, -1)
    tot_row_qkv = jnp.sum(second[..., :dense_rows], axis=1).reshape(-1)
    g_gain1_all = jnp.sum(second[..., dense_rows : 2 * dense_rows], axis=1)
    g_gain1 = lax.dynamic_index_in_dim(g_gain1_all, flat_index, 0, keepdims=False)
    tot_col_qkv = jnp.sum(second[..., 2 * dense_rows :], axis=0).reshape(-1)

    qkv_width = (HEADS + 2 * KV_HEADS) * HEAD
    row_qkv_new = decay * row_qkv + (1.0 - decay) * (tot_row_qkv / qkv_width + floor_sq)
    col_qkv_new = decay * col_qkv + (1.0 - decay) * (tot_col_qkv / D + floor_sq)
    row_out_new = decay * row_out + (1.0 - decay) * (tot_row_out / D + floor_sq)
    col_out_new = decay * col_out + (1.0 - decay) * (tot_col_out / (HEADS * HEAD) + floor_sq)
    row_router_new = decay * row_router + (1.0 - decay) * (tot_row_router / EXPERTS + floor_sq)
    col_router_new = decay * col_router + (1.0 - decay) * (tot_col_router / D + floor_sq)
    row_gu_new = decay * row_gate_up + (1.0 - decay) * (tot_row_gu / (2 * FFE) + floor_sq)
    col_gu_new = decay * col_gate_up + (1.0 - decay) * (tot_col_gu / D + floor_sq)
    row_down_new = decay * row_down + (1.0 - decay) * (tot_row_down / D + floor_sq)
    col_down_new = decay * col_down + (1.0 - decay) * (tot_col_down / FFE + floor_sq)
    aux_loss = EXPERTS * jnp.sum(fraction * prob_totals / tokens_all)

    expert_start = owner_index * local_experts
    rows_here = lax.dynamic_slice_in_dim(row_qkv_new, flat_index * dense_rows, dense_rows, 0)
    cols_here = lax.dynamic_slice_in_dim(col_qkv_new, tp_index * qkv_cols, qkv_cols, 0)
    change_qkv = g_qkv * lax.rsqrt(rows_here[:, None] * cols_here[None, :] / jnp.mean(row_qkv_new))
    rows_here = lax.dynamic_slice_in_dim(row_out_new, tp_index * out_rows, out_rows, 0)
    cols_here = lax.dynamic_slice_in_dim(col_out_new, flat_index * dense_rows, dense_rows, 0)
    change_out = g_out * lax.rsqrt(rows_here[:, None] * cols_here[None, :] / jnp.mean(row_out_new))
    rows_here = lax.dynamic_slice_in_dim(row_router_new, flat_index * dense_rows, dense_rows, 0)
    change_router = g_router * lax.rsqrt(
        rows_here[:, None] * col_router_new[None, :] / jnp.mean(row_router_new)
    )
    start_pair = (
        jnp.asarray(expert_start, jnp.int32),
        jnp.asarray(ctx_index * ctx_rows, jnp.int32),
    )
    zero_start = jnp.asarray(0, jnp.int32)
    rows_gu = lax.dynamic_slice(row_gu_new, start_pair, (local_experts, ctx_rows))
    cols_gu = lax.dynamic_slice(col_gu_new, (start_pair[0], zero_start), (local_experts, 2 * FFE))
    mean_gu = lax.dynamic_slice_in_dim(
        jnp.mean(row_gu_new, axis=-1), expert_start, local_experts, 0
    )
    change_gate_up = g_gate_up * lax.rsqrt(
        rows_gu[:, :, None] * cols_gu[:, None, :] / mean_gu[:, None, None]
    )
    rows_dn = lax.dynamic_slice(row_down_new, (start_pair[0], zero_start), (local_experts, FFE))
    cols_dn = lax.dynamic_slice(col_down_new, start_pair, (local_experts, ctx_rows))
    mean_dn = lax.dynamic_slice_in_dim(
        jnp.mean(row_down_new, axis=-1), expert_start, local_experts, 0
    )
    change_down = g_down * lax.rsqrt(
        rows_dn[:, :, None] * cols_dn[:, None, :] / mean_dn[:, None, None]
    )
    second_attn_new = decay * second_attn + (1.0 - decay) * (g_gain1 * g_gain1 + floor_sq)
    second_moe_new = decay * second_moe + (1.0 - decay) * (g_gain2 * g_gain2 + floor_sq)
    change_gain1 = g_gain1 * lax.rsqrt(second_attn_new)
    change_gain2 = g_gain2 * lax.rsqrt(second_moe_new)
    square_sums = jnp.stack(
        [
            jnp.sum(change_qkv * change_qkv),
            jnp.sum(change_out * change_out),
            keep_once * jnp.sum(change_router * change_router),
            jnp.sum(change_gate_up * change_gate_up),
            jnp.sum(change_down * change_down),
            keep_once * jnp.sum(change_gain1 * change_gain1),
            keep_once * jnp.sum(change_gain2 * change_gain2),
        ]
    )
    square_totals = jnp.sum(share(square_sums, count), axis=0)
    entries = jnp.array(
        [
            D * qkv_width,
            HEADS * HEAD * D,
            D * EXPERTS,
            EXPERTS * D * 2 * FFE,
            EXPERTS * FFE * D,
            D,
            D,
        ],
        f32,
    )
    update_rms = jnp.sqrt(square_totals / entries)
    weight_rms = jnp.sqrt(master_totals / entries)
    step_scale = rate * weight_rms / jnp.maximum(clip_rms, update_rms)
    new_qkv = w_qkv - step_scale[0] * change_qkv
    new_out = w_out - step_scale[1] * change_out
    new_router = w_router - step_scale[2] * change_router
    new_gate_up = w_gate_up - step_scale[3] * change_gate_up
    new_down = w_down - step_scale[4] * change_down
    new_gain1 = gain_attn - step_scale[5] * change_gain1
    new_gain2 = gain_moe - step_scale[6] * change_gain2
    return (
        layer_out,
        grad_inputs,
        aux_loss,
        g_qkv,
        g_out,
        g_router,
        g_gate_up,
        g_down,
        g_gain1,
        g_gain2,
        new_qkv,
        new_out,
        new_router,
        new_gate_up,
        new_down,
        new_gain1,
        new_gain2,
        new_qkv.astype(bf16),
        new_out.astype(bf16),
        new_router.astype(bf16),
        new_gate_up.astype(bf16),
        new_down.astype(bf16),
        new_gain1.astype(bf16),
        new_gain2.astype(bf16),
        row_qkv_new,
        col_qkv_new,
        row_out_new,
        col_out_new,
        row_router_new,
        col_router_new,
        row_gu_new,
        col_gu_new,
        row_down_new,
        col_down_new,
        second_attn_new,
        second_moe_new,
        update_rms,
    )


def solution(mesh):
    placed = (
        P(("fsdp", "ctx"), None),
        P(("fsdp", "ctx", "tp"), None),
        P(("fsdp", "ctx"), None),
        P("fsdp", None),
        P("fsdp", None),
        P(("fsdp", "ctx"), "tp"),
        P("tp", ("fsdp", "ctx")),
        P(("fsdp", "ctx"), None),
        P(("fsdp", "tp"), "ctx", None),
        P(("fsdp", "tp"), None, "ctx"),
        P(("fsdp", "ctx")),
        P(("fsdp", "ctx")),
        P(),
        P(),
        P(),
        P(),
        P(),
        P(),
        P(),
        P(),
        P(),
        P(),
        P(("fsdp", "ctx")),
        P(("fsdp", "ctx")),
    )
    return jax.shard_map(
        per_device,
        mesh=mesh,
        in_specs=placed,
        out_specs=(
            P(("fsdp", "ctx", "tp"), None),
            P(("fsdp", "ctx"), None),
            P(),
            P(("fsdp", "ctx"), "tp"),
            P("tp", ("fsdp", "ctx")),
            P(("fsdp", "ctx"), None),
            P(("fsdp", "tp"), "ctx", None),
            P(("fsdp", "tp"), None, "ctx"),
            P(("fsdp", "ctx")),
            P(("fsdp", "ctx")),
            P(("fsdp", "ctx"), "tp"),
            P("tp", ("fsdp", "ctx")),
            P(("fsdp", "ctx"), None),
            P(("fsdp", "tp"), "ctx", None),
            P(("fsdp", "tp"), None, "ctx"),
            P(("fsdp", "ctx")),
            P(("fsdp", "ctx")),
            P(("fsdp", "ctx"), "tp"),
            P("tp", ("fsdp", "ctx")),
            P(("fsdp", "ctx"), None),
            P(("fsdp", "tp"), "ctx", None),
            P(("fsdp", "tp"), None, "ctx"),
            P(("fsdp", "ctx")),
            P(("fsdp", "ctx")),
            P(),
            P(),
            P(),
            P(),
            P(),
            P(),
            P(),
            P(),
            P(),
            P(),
            P(("fsdp", "ctx")),
            P(("fsdp", "ctx")),
            P(),
        ),
        check_vma=False,
    )
```

time: 2320 us -> 1290 us (0.56)
  waiting for transfers between devices: 1290 us -> 646 us
  blocking collectives: 380 us -> 20.9 us
  starting transfers between devices: 21.9 us -> 70.7 us
  other arithmetic: 198 us -> 162 us
  local copies, waits for them, and re-layouts: 152 us -> 124 us
    all_to_all x4 -> x14, waiting for transfers between devices: 546 us -> 151 us  [exchange(): return lax.all_to_all(values, axes, split_axis=0, concat_axis=0, tiled=True)]
    psum x3 -> x0, waiting for transfers between devices: 245 us -> none  [the longest x1 125 us: per_device(): lax.psum((moment_parts[0], moment_parts[1], moment_parts[2], moment_parts...]
    all_gather x4 -> x0, blocking collectives: 199 us -> none  [the longest x1 167 us: per_device(): lax.all_gather(counts_half.astype(jnp.bfloat16), ('fsdp', 'ctx'), axis=0,...]
    all_gather x6 -> x8, waiting for transfers between devices: 133 us -> 275 us  [the longest x1 90.4 us: per_device(): grad_rows = lax.all_gather(cotangent, ('fsdp', 'tp'), axis=0, tiled=True)]
    reduce_scatter x5 -> x3, waiting for transfers between devices: 342 us -> 218 us  [the longest x1 118 us: per_device(): lax.psum_scatter(moe_sum.reshape(groups * half_rows, D), ('fsdp', 'tp'),...]
    unnamed x2 -> x0, blocking collectives: 98.5 us -> none
    psum x2 -> x0, blocking collectives: 82 us -> none  [per_device(): lax.psum((moment_parts[0], moment_parts[1], moment_parts[2], moment_parts...]
    gather x4 -> x0, local copies, waits for them, and re-layouts: 74.5 us -> none  [the longest x1 22.9 us: per_device(): d_slot[source_slot]]
  transfers between devices with their start and end apart: 19 -> 26, of which waited for: 17 -> 18; matrix products, arithmetic and copies ran while one was open for 12% -> 32% of each run, Pallas kernels for 0% -> 0%
where the time goes in v1:
time: 1290 us; the launch traced here: 1280 us
  waiting for transfers between devices  646 us (50%)
  matrix products  233 us (18%)
  other arithmetic  162 us (13%)
  local copies, waits for them, and re-layouts  124 us (10%)
  starting transfers between devices  70.7 us (5%)
  between operations  24.2 us (2%)
  blocking collectives  20.9 us (2%)
    dot_general x44, matrix products, dot(): return jnp.einsum(spec, left, right, preferred_element_type=f32)  233 us
    all_to_all x14, waiting for transfers between devices, exchange(): return lax.all_to_all(values, axes, split_axis=0, concat_axis=0, tiled=True)  151 us
    reduce_scatter x1, waiting for transfers between devices, per_device(): lax.psum_scatter(moe_sum.reshape(groups * half_rows, D), ('fsdp', 'tp'),...  118 us
    reduce_scatter x1, waiting for transfers between devices, per_device(): lax.psum_scatter(d_sum.reshape(groups * half_rows, D), ('fsdp', 'tp'), sc...  99.8 us
    all_gather x1, waiting for transfers between devices, per_device(): grad_rows = lax.all_gather(cotangent, ('fsdp', 'tp'), axis=0, tiled=True)  90.4 us
    all_gather x1, waiting for transfers between devices, per_device(): lax.all_gather(w_gate_up.astype(bf16), 'ctx', axis=1, tiled=True)  73.7 us
    all_to_all x14, starting transfers between devices, exchange(): return lax.all_to_all(values, axes, split_axis=0, concat_axis=0, tiled=True)  70.2 us
    all_gather x1, waiting for transfers between devices, per_device(): lax.all_gather(act2, ('fsdp', 'tp'), axis=0, tiled=True)  51.3 us
  transfers between devices with their start and end apart: 26, of which 18 were waited for; matrix products, arithmetic and copies ran while one was open for 32% of the time, Pallas kernels for 0%

profile of v1, /device:TPU:0, one launch (start us, length us, event | category | flops | bytes accessed | tf_op | source)
XLA Modules:
  0.0 1279.6 jit_solution(14556916121845740593)
XLA Ops:
  15.8 7.4 all-to-all-start
  25.0 7.0 fusion.2
  44.1 4.3 all-to-all-done
  48.9 22.5 %all-gather.9.cloned.1.call-done = bf16[2048,1536]{1,0:T(8,128)(2,1)} async-done(((bf16[512,1536]{1,0:T(8,128)(2,1)}), bf16[2048,1536]{1,0:T(8,128)(2,1)}) %all-gather.9.cloned.1.call-update) | async-done | bytes 6291472 | tf_op jit(solution)/shard_map/all_gather | solution.py:194
  71.4 4.2 fusion.3
  90.3 3.8 fusion.206
  98.3 5.6 fusion.123
  108.4 3.5 all-to-all-start.1
  112.0 14.6 %all-to-all-done.1 = bf16[8,256,192]{1,2,0:T(8,128)(2,1)S(1)} async-done(((bf16[8,256,192]{1,2,0:T(8,128)(2,1)}), bf16[8,256,192]{1,2,0:T(8,128)(2,1)S(1)}, u32[]{:S(2)}, u32[]{:S(2)}) %all-to-all-start.1) | async-done | bytes 786464 | tf_op jit(solution)/shard_map/all_to_all | solution.py:31
  127.6 13.7 %all-gather.11.cloned.1.call-done = bf16[3072,768]{1,0:T(8,128)(2,1)} async-done(((bf16[96,768]{1,0:T(8,128)(2,1)}), bf16[3072,768]{1,0:T(8,128)(2,1)}) %all-gather.11.cloned.1.call-update) | async-done | bytes 4718608 | tf_op jit(solution)/shard_map/all_gather | solution.py:227
  141.3 4.1 multiply_reduce_fusion.10
  146.6 8.5 multiply_reduce_fusion.1
  155.1 5.4 multiply_reduce_fusion.5
  166.7 11.2 all_to_all.89
  185.1 5.4 all-to-all-done.2
  193.9 51.3 %all-gather.13.cloned.1.call-done = bf16[2048,1536]{1,0:T(8,128)(2,1)} async-done(((bf16[256,1536]{1,0:T(8,128)(2,1)}), bf16[2048,1536]{1,0:T(8,128)(2,1)}) %all-gather.13.cloned.1.call-update) | async-done | bytes 6291472 | tf_op jit(solution)/shard_map/all_gather | solution.py:256
  245.2 8.6 convolution_convert_fusion
  253.8 73.7 %all-gather.15.cloned.1.call-done = bf16[4,1536,1024]{2,1,0:T(8,128)(2,1)} async-done(((bf16[4,384,1024]{2,1,0:T(8,128)(2,1)}), bf16[4,1536,1024]{2,1,0:T(8,128)(2,1)}) %all-gather.15.cloned.1.call-update) | async-done | bytes 12582928 | tf_op jit(solution)/shard_map/all_gather | solution.py:225
  327.6 18.2 %fusion.53 = f32[8,4,96,1024]{3,2,0,1:T(8,128)} fusion(bf16[4,1536,1024]{2,1,0:T(8,128)(2,1)} %all-gather.15.cloned.1.call-done, bf16[8,4,96,1536]{3,2,1,0:T(8,128)(2,1)} %convolution_convert_fusion), kind=kOutput, calls=%fused_computation.89 | convolution fusion | flops 9663676416 | bytes 34603008 | tf_op jit(solution)/shard_map/serd,edf->serf/dot_general | solution.py:27
  345.8 6.9 multiply_convert_fusion.1
  352.7 23.2 %all-gather.17.cloned.1.call-done = bf16[4,512,1536]{2,1,0:T(8,128)(2,1)} async-done(((bf16[4,512,384]{2,1,0:T(8,128)(2,1)}), bf16[4,512,1536]{2,1,0:T(8,128)(2,1)}) %all-gather.17.cloned.1.call-update) | async-done | bytes 6291472 | tf_op jit(solution)/shard_map/all_gather | solution.py:226
  375.9 10.7 convolution_convert_fusion.1
  386.6 90.4 %all-gather.19.cloned.1.call-done = bf16[2048,1536]{1,0:T(8,128)(2,1)} async-done(((bf16[256,1536]{1,0:T(8,128)(2,1)}), bf16[2048,1536]{1,0:T(8,128)(2,1)}) %all-gather.19.cloned.1.call-update) | async-done | bytes 6291472 | tf_op jit(solution)/shard_map/all_gather | solution.py:223
  477.0 12.2 fusion.1
  490.6 18.6 %fusion.33 = (bf16[8,4,96,512]{3,2,0,1:T(8,128)(2,1)}, bf16[8,4,96,512]{3,2,0,1:T(8,128)(2,1)}) fusion(f32[8,4,96,1024]{3,2,0,1:T(8,128)} %fusion.53, bf16[4,512,1536]{2,1,0:T(8,128)(2,1)} %all-gather.17.cloned.1.call-done, f32[8,4,96,1536]{3,2,0,1:T(8,128)} %get-tuple-element.560, f32[8,4,96]{2,0,1:T(8,128)S(1)} %copy.497), kind=kOutput, calls=%fused_computation.61 | convolution fusion | flops 4861722624 | bytes 44052480 | tf_op jit(solution)/shard_map/serd,efd->serf/dot_general | solution.py:27
  509.1 19.1 %bitcast_convert_fusion.2 = bf16[8,256,1536]{2,1,0:T(8,128)(2,1)} fusion(f32[8,4,256]{2,1,0:T(4,128)S(1)} %all-to-all-done.2, bf16[4,1536,1024]{2,1,0:T(8,128)(2,1)} %all-gather.15.cloned.1.call-done, bf16[8,4,96,512]{3,2,0,1:T(8,128)(2,1)} %get-tuple-element.508, bf16[8,4,96,512]{3,2,0,1:T(8,128)(2,1)} %get-tuple-element.507), kind=kOutput, calls=%fused_computation.21 | convolution fusion | flops 12096110592 | bytes 25198592 | tf_op jit(solution)/shard_map/sert,serd->std/dot_general | solution.py:27
  528.3 7.9 bitcast_convert_fusion.3
  536.4 9.7 all_to_all.90
  546.1 99.8 %reduce-scatter.9.cloned.1.call-done = bf16[256,1536]{1,0:T(8,128)(2,1)} async-done(((bf16[2048,1536]{1,0:T(8,128)(2,1)}), bf16[256,1536]{1,0:T(8,128)(2,1)}) %reduce-scatter.9.cloned.1.call-update) | async-done | bytes 786448 | tf_op jit(solution)/shard_map/reduce_scatter | solution.py:288
  648.7 118.5 %reduce-scatter.7.cloned.1.call-done = bf16[256,1536]{1,0:T(8,128)(2,1)} async-done(((bf16[2048,1536]{1,0:T(8,128)(2,1)}), bf16[256,1536]{1,0:T(8,128)(2,1)}) %reduce-scatter.7.cloned.1.call-update) | async-done | bytes 786448 | tf_op jit(solution)/shard_map/reduce_scatter | solution.py:291
  770.6 13.0 %bitcast_convert_fusion.1 = bf16[4,512,1536]{2,1,0:T(8,128)(2,1)} fusion(bf16[8,4,96,512]{3,2,0,1:T(8,128)(2,1)} %multiply_convert_fusion.1, f32[8,4,96,1536]{3,2,0,1:T(8,128)} %get-tuple-element.560, f32[8,4,96]{2,0,1:T(8,128)S(1)} %copy.497), kind=kOutput, calls=%fused_computation.15 | convolution fusion | flops 4844421120 | bytes 28323840 | tf_op jit(solution)/shard_map/serf,serd->efd/dot_general | solution.py:27
  783.6 11.2 copy.578
  794.8 8.1 copy.595
  804.9 16.2 %bitcast_convert_fusion = bf16[4,1536,1024]{2,1,0:T(8,128)(2,1)} fusion(bf16[8,4,96,1536]{3,2,1,0:T(8,128)(2,1)} %convolution_convert_fusion, bf16[8,4,96,512]{3,2,0,1:T(8,128)(2,1)} %get-tuple-element.508, bf16[8,4,96,512]{3,2,0,1:T(8,128)(2,1)S(1)} %copy-done.25), kind=kOutput, calls=%fused_computation | convolution fusion | flops 9682550784 | bytes 28311552 | tf_op jit(solution)/shard_map/serd,serf->edf/dot_general | solution.py:27
  822.6 4.9 convolution_convert_fusion.6
  832.1 4.2 all-to-all-start.6
  838.2 18.0 %all-to-all-done.6 = bf16[8,256,192]{1,2,0:T(8,128)(2,1)} async-done(((bf16[8,256,192]{1,2,0:T(8,128)(2,1)}), bf16[8,256,192]{1,2,0:T(8,128)(2,1)}, u32[]{:S(2)}, u32[]{:S(2)}) %all-to-all-start.6) | async-done | bytes 786464 | tf_op jit(solution)/shard_map/all_to_all | solution.py:31
  856.2 4.7 all-to-all-start.8
  882.2 5.6 fusion.28
  887.8 4.7 fusion.30
  894.9 7.0 fusion.15
  901.9 11.2 fusion.17
  913.0 3.7 fusion.120
  916.8 10.3 fusion.8
  928.2 7.8 fusion.10
  953.4 3.7 all-to-all-start.12
  957.8 24.3 %all-to-all-done.12 = bf16[16,96,320]{2,1,0:T(8,128)(2,1)S(1)} async-done(((bf16[16,96,320]{2,1,0:T(8,128)(2,1)}), bf16[16,96,320]{2,1,0:T(8,128)(2,1)S(1)}, u32[]{:S(2)}, u32[]{:S(2)}) %all-to-all-start.12) | async-done | bytes 983072 | tf_op jit(solution)/shard_map/all_to_all | solution.py:31
  983.0 7.9 all-to-all-start.10
  992.0 16.6 %all-to-all-done.10 = f32[32,33,96]{2,1,0:T(8,128)} async-done(((f32[32,33,96]{2,1,0:T(8,128)}), f32[32,33,96]{2,1,0:T(8,128)}, u32[]{:S(2)}, u32[]{:S(2)}) %all-to-all-start.10) | async-done | bytes 405536 | tf_op jit(solution)/shard_map/all_to_all | solution.py:31
  1009.5 3.7 all-to-all-start.13
  1015.4 7.5 all-to-all-done.13
  1024.6 4.4 all-to-all-start.7
  1030.9 4.7 convolution_convert_fusion.2
  1035.6 53.1 %all-to-all-done.7 = bf16[8,512,320]{1,2,0:T(8,128)(2,1)} async-done(((bf16[8,512,320]{1,2,0:T(8,128)(2,1)}), bf16[8,512,320]{1,2,0:T(8,128)(2,1)}, u32[]{:S(2)}, u32[]{:S(2)}) %all-to-all-start.7) | async-done | bytes 2621472 | tf_op jit(solution)/shard_map/all_to_all | solution.py:31
  1088.7 4.8 all-to-all-start.9
  1130.9 10.6 fusion.61
  1148.4 9.3 all-to-all-start.11
  1157.8 5.6 multiply_reduce_fusion.3
  1168.2 3.7 all-to-all-start.14
  1172.0 5.6 fusion.64
  1216.9 4.8 multiply_reduce_fusion
  1228.0 6.1 all-to-all-start.15
  1236.0 5.0 all-to-all-done.15
  1256.2 8.6 fusion.190
  (537 shorter events, 244.7 us)
Async XLA Ops:
  7.2 155.9 %copy-start = (s32[512,8]{0,1:T(8,128)S(1)}, s32[512,8]{0,1:T(8,128)}, u32[]{:S(2)}) copy-start(s32[512,8]{0,1:T(8,128)} %param.47) | copy-start | bytes 49156
  7.2 64.1 %all-gather.9.cloned.1.call-start = ((), (), s32[]{:S(2)}) async-start(), calls=%async_computation.20 | async-start | bytes 7864320 | tf_op jit(solution)/shard_map/all_gather | solution.py:194
  8.0 15.2 %copy-start.38 = (f32[768,96]{0,1:T(8,128)S(1)}, f32[768,96]{0,1:T(8,128)}, u32[]{:S(2)}) copy-start(f32[768,96]{0,1:T(8,128)} %param.51) | copy-start | bytes 884740
  8.0 16.5 %copy-start.119 = (s32[1,13]{1,0:T(1,128)S(1)}, s32[1,13]{1,0:T(1,128)}, u32[]{:S(2)}) copy-start(s32[1,13]{1,0:T(1,128)} %param.49) | copy-start | bytes 160
  8.0 17.0 %copy-start.124 = (s32[1,2048]{1,0:T(1,128)S(1)}, s32[1,2048]{1,0:T(1,128)}, u32[]{:S(2)}) copy-start(s32[1,2048]{1,0:T(1,128)} %param.48) | copy-start | bytes 24580
  9.3 22.7 %copy-start.16 = (f32[96,1280]{0,1:T(8,128)}, f32[96,1280]{0,1:T(8,128)S(1)}, u32[]{:S(2)}) copy-start(f32[96,1280]{0,1:T(8,128)S(1)} %copy.484) | copy-start | bytes 1474564
  15.8 32.6 %all-to-all-start = ((bf16[16,96,354]{2,1,0:T(8,128)(2,1)}), bf16[16,96,354]{2,1,0:T(8,128)(2,1)S(1)}, u32[]{:S(2)}, u32[]{:S(2)}) async-start(bf16[16,96,354]{2,1,0:T(8,128)(2,1)} %bitcast.6), calls=%async_computation | async-start | bytes 2359296 | tf_op jit(solution)/shard_map/all_to_all | solution.py:31
  23.1 118.2 %all-gather.11.cloned.1.call-start = ((), (), s32[]{:S(2)}) async-start(), calls=%async_computation.21 | async-start | bytes 4866048 | tf_op jit(solution)/shard_map/all_gather | solution.py:227
  48.4 31.0 %copy-start.18 = (bf16[16,96,354]{2,1,0:T(8,128)(2,1)}, bf16[16,96,354]{2,1,0:T(8,128)(2,1)S(1)}, u32[]{:S(2)}) copy-start(bf16[16,96,354]{2,1,0:T(8,128)(2,1)S(1)} %all-to-all-done) | copy-start | bytes 3262468
  48.9 30.4 %copy-start.101 = (f32[1536]{0:T(1024)}, f32[1536]{0:T(1024)S(1)}, u32[]{:S(2)}) copy-start(f32[1536]{0:T(1024)S(1)} %get-tuple-element.452) | copy-start | bytes 18436
  107.4 33.9 %copy-start.10 = (bf16[512,1536]{1,0:T(8,128)(2,1)S(1)}, bf16[512,1536]{1,0:T(8,128)(2,1)}, u32[]{:S(2)}) copy-start(bf16[512,1536]{1,0:T(8,128)(2,1)} %param.45) | copy-start | bytes 4718596
  108.4 18.2 %all-to-all-start.1 = ((bf16[8,256,192]{1,2,0:T(8,128)(2,1)}), bf16[8,256,192]{1,2,0:T(8,128)(2,1)S(1)}, u32[]{:S(2)}, u32[]{:S(2)}) async-start(bf16[8,256,192]{1,2,0:T(8,128)(2,1)} %bitcast.423), calls=%async_computation.1 | async-start | bytes 1572864 | tf_op jit(solution)/shard_map/all_to_all | solution.py:31
  112.0 133.3 %all-gather.13.cloned.1.call-start = ((), (), s32[]{:S(2)}) async-start(), calls=%async_computation.22 | async-start | bytes 7077888 | tf_op jit(solution)/shard_map/all_gather | solution.py:256
  146.5 181.0 %all-gather.15.cloned.1.call-start = ((), (), s32[]{:S(2)}) async-start(), calls=%async_computation.23 | async-start | bytes 15728640 | tf_op jit(solution)/shard_map/all_gather | solution.py:225
  155.1 22.8 %copy-start.13 = (bf16[256,1536]{1,0:T(8,128)(2,1)S(1)}, bf16[256,1536]{1,0:T(8,128)(2,1)}, u32[]{:S(2)}) copy-start(bf16[256,1536]{1,0:T(8,128)(2,1)} %multiply_convert_fusion.4) | copy-start | bytes 2359300
  155.1 220.8 %all-gather.17.cloned.1.call-start = ((), (), s32[]{:S(2)}) async-start(), calls=%async_computation.24 | async-start | bytes 7864320 | tf_op jit(solution)/shard_map/all_gather | solution.py:226
  160.6 316.4 %all-gather.19.cloned.1.call-start = ((), (), s32[]{:S(2)}) async-start(), calls=%async_computation.26 | async-start | bytes 7077888 | tf_op jit(solution)/shard_map/all_gather | solution.py:223
  177.9 468.0 %copy-start.106 = (f32[32]{0:T(128)}, f32[32]{0:T(128)S(1)}, u32[]{:S(2)}) copy-start(f32[32]{0:T(128)S(1)} %slice_multiply_fusion.5) | copy-start | bytes 388
  179.6 466.4 %copy-start.34 = (f32[256,32]{0,1:T(8,128)}, f32[256,32]{0,1:T(8,128)S(1)}, u32[]{:S(2)}) copy-start(f32[256,32]{0,1:T(8,128)S(1)} %get-tuple-element.558) | copy-start | bytes 98308
  179.6 466.4 %copy-start.92 = (f32[256]{0:T(256)}, f32[256]{0:T(256)S(1)}, u32[]{:S(2)}) copy-start(f32[256]{0:T(256)S(1)} %get-tuple-element.557) | copy-start | bytes 3076
  179.6 466.3 %copy-start.69 = (f32[256]{0:T(256)}, f32[256]{0:T(256)S(1)}, u32[]{:S(2)}) copy-start(f32[256]{0:T(256)S(1)} %get-tuple-element.464) | copy-start | bytes 3076
  179.6 466.3 %copy-start.95 = (f32[256]{0:T(256)}, f32[256]{0:T(256)S(1)}, u32[]{:S(2)}) copy-start(f32[256]{0:T(256)S(1)} %get-tuple-element.463) | copy-start | bytes 3076
  180.4 10.1 all-to-all-start.2
  184.4 461.5 %copy-start.90 = (f32[256]{0:T(256)}, f32[256]{0:T(256)S(1)}, u32[]{:S(2)}) copy-start(f32[256]{0:T(256)S(1)} %get-tuple-element.462) | copy-start | bytes 3076
  184.4 461.6 %copy-start.99 = (f32[256]{0:T(256)}, f32[256]{0:T(256)S(1)}, u32[]{:S(2)}) copy-start(f32[256]{0:T(256)S(1)} %get-tuple-element.461) | copy-start | bytes 3076
  190.5 298.7 %all-to-all-start.3 = ((f32[8,4,256]{2,1,0:T(4,128)}), f32[8,4,256]{2,1,0:T(4,128)S(1)}, u32[]{:S(2)}, u32[]{:S(2)}) async-start(f32[8,4,256]{2,1,0:T(4,128)} %reshape.704), calls=%async_computation.3 | async-start | bytes 65536 | tf_op jit(solution)/shard_map/all_to_all | solution.py:31
  193.9 452.1 %reduce-scatter.9.cloned.1.call-start = ((), (), s32[]{:S(2)}) async-start(), calls=%async_computation.27 | async-start | bytes 7077888 | tf_op jit(solution)/shard_map/reduce_scatter | solution.py:288
  528.3 238.9 %reduce-scatter.7.cloned.1.call-start = ((), (), s32[]{:S(2)}) async-start(), calls=%async_computation.25 | async-start | bytes 7077888 | tf_op jit(solution)/shard_map/reduce_scatter | solution.py:291
  536.3 494.5 %all-gather.21.cloned.1.call-start = ((), (), s32[]{:S(2)}) async-start(), calls=%async_computation.28 | async-start | bytes 4718592 | tf_op jit(solution)/shard_map/all_gather | solution.py:348
  546.1 224.5 %copy-start.51 = (f32[32,256]{1,0:T(8,128)}, f32[32,256]{1,0:T(8,128)S(1)}, u32[]{:S(2)}) copy-start(f32[32,256]{1,0:T(8,128)S(1)} %reshape.709) | copy-start | bytes 98308
  546.1 224.4 %copy-start.97 = (f32[256]{0:T(256)}, f32[256]{0:T(256)S(1)}, u32[]{:S(2)}) copy-start(f32[256]{0:T(256)S(1)} %fusion.161) | copy-start | bytes 3076
  770.6 323.6 %reduce-scatter.13.cloned.1.call-start = ((), (), s32[]{:S(2)}) async-start(), calls=%async_computation.31 | async-start | bytes 7864320
  802.9 328.0 %all-gather.23.cloned.1.call-start = ((), (), s32[]{:S(2)}) async-start(), calls=%async_computation.29 | async-start | bytes 8110080 | tf_op jit(solution)/shard_map/all_gather | solution.py:229
  804.7 353.0 %reduce-scatter.11.cloned.1.call-start = ((), (), s32[]{:S(2)}) async-start(), calls=%async_computation.30 | async-start | bytes 15728640 | tf_op jit(solution)/shard_map/reduce_scatter | solution.py:295
  822.5 13.8 %copy-start.73 = (f32[3,512]{1,0:T(4,128)S(1)}, f32[3,512]{1,0:T(4,128)}, u32[]{:S(2)}) copy-start(f32[3,512]{1,0:T(4,128)} %copy-done.72) | copy-start | bytes 18436
  822.5 13.8 %copy-start.75 = (f32[3,512]{1,0:T(4,128)S(1)}, f32[3,512]{1,0:T(4,128)}, u32[]{:S(2)}) copy-start(f32[3,512]{1,0:T(4,128)} %copy-done.74) | copy-start | bytes 18436
  822.5 14.4 %copy-start.77 = (f32[3,512]{1,0:T(4,128)S(1)}, f32[3,512]{1,0:T(4,128)}, u32[]{:S(2)}) copy-start(f32[3,512]{1,0:T(4,128)} %copy-done.76) | copy-start | bytes 18436
  822.5 14.4 %copy-start.79 = (f32[3,512]{1,0:T(4,128)S(1)}, f32[3,512]{1,0:T(4,128)}, u32[]{:S(2)}) copy-start(f32[3,512]{1,0:T(4,128)} %copy-done.78) | copy-start | bytes 18436
  822.5 15.0 %copy-start.81 = (f32[3,512]{1,0:T(4,128)S(1)}, f32[3,512]{1,0:T(4,128)}, u32[]{:S(2)}) copy-start(f32[3,512]{1,0:T(4,128)} %copy-done.80) | copy-start | bytes 18436
  822.5 15.0 %copy-start.83 = (f32[3,512]{1,0:T(4,128)S(1)}, f32[3,512]{1,0:T(4,128)}, u32[]{:S(2)}) copy-start(f32[3,512]{1,0:T(4,128)} %copy-done.82) | copy-start | bytes 18436
  822.5 15.6 %copy-start.85 = (f32[3,512]{1,0:T(4,128)S(1)}, f32[3,512]{1,0:T(4,128)}, u32[]{:S(2)}) copy-start(f32[3,512]{1,0:T(4,128)} %copy-done.84) | copy-start | bytes 18436
  822.5 15.6 %copy-start.87 = (f32[3,512]{1,0:T(4,128)S(1)}, f32[3,512]{1,0:T(4,128)}, u32[]{:S(2)}) copy-start(f32[3,512]{1,0:T(4,128)} %copy-done.86) | copy-start | bytes 18436
  827.4 37.4 %copy-start.6 = (f32[3,512,512]{1,2,0:T(8,128)S(1)}, f32[3,512,512]{1,2,0:T(8,128)}, u32[]{:S(2)}) copy-start(f32[3,512,512]{1,2,0:T(8,128)} %copy-done.5) | copy-start | bytes 9437188
  832.1 24.1 %all-to-all-start.6 = ((bf16[8,256,192]{1,2,0:T(8,128)(2,1)}), bf16[8,256,192]{1,2,0:T(8,128)(2,1)}, u32[]{:S(2)}, u32[]{:S(2)}) async-start(bf16[8,256,192]{1,2,0:T(8,128)(2,1)} %bitcast.462), calls=%async_computation.8 | async-start | bytes 1572864 | tf_op jit(solution)/shard_map/all_to_all | solution.py:31
  856.2 97.2 %all-to-all-start.8 = ((bf16[2,256,768]{1,2,0:T(8,128)(2,1)}), bf16[2,256,768]{1,2,0:T(8,128)(2,1)}, u32[]{:S(2)}, u32[]{:S(2)}) async-start(bf16[2,256,768]{1,2,0:T(8,128)(2,1)} %bitcast.459), calls=%async_computation.10 | async-start | bytes 1572864 | tf_op jit(solution)/shard_map/all_to_all | solution.py:31
  913.0 14.0 %slice-start = ((s8[12582912]{0:T(1024)(128)(4,1)}), s8[4194304]{0:T(1024)(128)(4,1)S(1)}, s32[]{:S(2)}) async-start(s8[12582912]{0:T(1024)(128)(4,1)} %bitcast.425), calls=%async_computation.32 | async-start | bytes 8388608
  916.7 22.8 %slice-start.13 = ((s8[4718592]{0:T(1024)(128)(4,1)}), s8[4194304]{0:T(1024)(128)(4,1)S(1)}, s32[]{:S(2)}) async-start(s8[4718592]{0:T(1024)(128)(4,1)} %bitcast.435), calls=%async_computation.45 | async-start | bytes 8388608
  953.4 28.8 %all-to-all-start.12 = ((bf16[16,96,320]{2,1,0:T(8,128)(2,1)}), bf16[16,96,320]{2,1,0:T(8,128)(2,1)S(1)}, u32[]{:S(2)}, u32[]{:S(2)}) async-start(bf16[16,96,320]{2,1,0:T(8,128)(2,1)} %bitcast.454), calls=%async_computation.14 | async-start | bytes 2359296 | tf_op jit(solution)/shard_map/all_to_all | solution.py:31
  957.2 34.5 %copy-start.17 = (f32[96,1280]{0,1:T(8,128)S(1)}, f32[96,1280]{0,1:T(8,128)}, u32[]{:S(2)}) copy-start(f32[96,1280]{0,1:T(8,128)} %copy-done.16) | copy-start | bytes 1474564
  957.7 34.3 %copy-start.121 = (f32[96]{0:T(128)S(1)}, f32[96]{0:T(128)}, u32[]{:S(2)}) copy-start(f32[96]{0:T(128)} %param.55) | copy-start | bytes 1156
  957.8 55.6 %copy-start.40 = (bf16[2048,64]{0,1:T(8,128)(2,1)S(1)}, bf16[2048,64]{0,1:T(8,128)(2,1)}, u32[]{:S(2)}) copy-start(bf16[2048,64]{0,1:T(8,128)(2,1)} %copy-done.39) | copy-start | bytes 786436
  983.0 30.6 %copy-start.24 = (bf16[2048,3,64]{0,2,1:T(8,128)(2,1)S(1)}, bf16[2048,3,64]{0,2,1:T(8,128)(2,1)}, u32[]{:S(2)}) copy-start(bf16[2048,3,64]{0,2,1:T(8,128)(2,1)} %copy-done.23) | copy-start | bytes 2359300
  983.0 25.7 %all-to-all-start.10 = ((f32[32,33,96]{2,1,0:T(8,128)}), f32[32,33,96]{2,1,0:T(8,128)}, u32[]{:S(2)}, u32[]{:S(2)}) async-start(f32[32,33,96]{2,1,0:T(8,128)} %bitcast.103), calls=%async_computation.12 | async-start | bytes 1310720 | tf_op jit(solution)/shard_map/all_to_all | solution.py:31
  991.3 22.1 %copy-start.28 = (f32[96,4,64]{0,2,1:T(8,128)}, f32[96,4,64]{0,2,1:T(8,128)S(1)}, u32[]{:S(2)}) copy-start(f32[96,4,64]{0,2,1:T(8,128)S(1)} %copy.534) | copy-start | bytes 294916
  991.5 22.7 %copy-start.29 = (f32[96,4,64]{0,2,1:T(8,128)}, f32[96,4,64]{0,2,1:T(8,128)S(1)}, u32[]{:S(2)}) copy-start(f32[96,4,64]{0,2,1:T(8,128)S(1)} %copy.533) | copy-start | bytes 294916
  1009.5 13.4 %all-to-all-start.13 = ((f32[32,1,1472]{2,1,0:T(1,128)}), f32[32,1,1472]{2,1,0:T(1,128)}, u32[]{:S(2)}, u32[]{:S(2)}) async-start(f32[32,1,1472]{2,1,0:T(1,128)} %broadcast_in_dim.140), calls=%async_computation.16 | async-start | bytes 393216 | tf_op jit(solution)/shard_map/all_to_all | solution.py:31
  1015.4 13.6 %copy-start.11 = (bf16[512,1536]{1,0:T(8,128)(2,1)S(1)}, bf16[512,1536]{1,0:T(8,128)(2,1)}, u32[]{:S(2)}) copy-start(bf16[512,1536]{1,0:T(8,128)(2,1)} %param.45) | copy-start | bytes 4718596
  1024.6 64.1 %all-to-all-start.7 = ((bf16[8,512,320]{1,2,0:T(8,128)(2,1)}), bf16[8,512,320]{1,2,0:T(8,128)(2,1)}, u32[]{:S(2)}, u32[]{:S(2)}) async-start(bf16[8,512,320]{1,2,0:T(8,128)(2,1)} %bitcast.440), calls=%async_computation.9 | async-start | bytes 5242880 | tf_op jit(solution)/shard_map/all_to_all | solution.py:31
  1088.7 53.4 %all-to-all-start.9 = ((bf16[16,96,768]{2,1,0:T(8,128)(2,1)}), bf16[16,96,768]{2,1,0:T(8,128)(2,1)}, u32[]{:S(2)}, u32[]{:S(2)}) async-start(bf16[16,96,768]{2,1,0:T(8,128)(2,1)} %bitcast.100), calls=%async_computation.11 | async-start | bytes 4718592 | tf_op jit(solution)/shard_map/all_to_all | solution.py:31
  1102.1 162.7 %copy-start.9 = (f32[4,512,384]{2,1,0:T(8,128)}, f32[4,512,384]{2,1,0:T(8,128)S(1)}, u32[]{:S(2)}) copy-start(f32[4,512,384]{2,1,0:T(8,128)S(1)} %get-tuple-element.498) | copy-start | bytes 9437188
  1108.1 146.0 %copy-start.56 = (f32[96,32]{0,1:T(8,128)}, f32[96,32]{0,1:T(8,128)S(1)}, u32[]{:S(2)}) copy-start(f32[96,32]{0,1:T(8,128)S(1)} %get-tuple-element.505) | copy-start | bytes 36868
  1148.4 17.9 %all-to-all-start.11 = ((f32[32,1,1024]{2,1,0:T(1,128)}), f32[32,1,1024]{2,1,0:T(1,128)}, u32[]{:S(2)}, u32[]{:S(2)}) async-start(f32[32,1,1024]{2,1,0:T(1,128)} %broadcast_in_dim.139), calls=%async_computation.13 | async-start | bytes 262144 | tf_op jit(solution)/shard_map/all_to_all | solution.py:31
  1168.2 36.2 %all-to-all-start.14 = ((f32[32,4,2304]{2,1,0:T(4,128)}), f32[32,4,2304]{2,1,0:T(4,128)}, u32[]{:S(2)}, u32[]{:S(2)}) async-start(f32[32,4,2304]{2,1,0:T(4,128)} %broadcast_in_dim.141), calls=%async_computation.17 | async-start | bytes 2359296 | tf_op jit(solution)/shard_map/all_to_all | solution.py:31
  1228.0 13.0 %all-to-all-start.15 = ((f32[32,1,7]{2,1,0:T(1,128)}), f32[32,1,7]{2,1,0:T(1,128)}, u32[]{:S(2)}, u32[]{:S(2)}) async-start(f32[32,1,7]{2,1,0:T(1,128)} %broadcast_in_dim.142), calls=%async_computation.18 | async-start | bytes 32768 | tf_op jit(solution)/shard_map/all_to_all | solution.py:31
  (104 other events, 563.7 us)
Sparse Core Ops, SparseCore 0:
  9.6 61.7 all-gather.8
  74.8 66.3 all-gather.10
  146.6 98.5 all-gather.12
  247.2 80.2 all-gather.14
  329.5 46.2 all-gather.16
  377.9 99.0 all-gather.18
  528.4 117.4 reduce-scatter.8
  650.1 117.0 reduce-scatter.6
  770.7 44.0 all-gather.20
  817.1 66.0 reduce-scatter.12
  887.1 73.6 all-gather.22
  963.4 135.0 reduce-scatter.10

commit v2 on v1

--- a/solution.py
+++ b/solution.py
@@ -1,6 +1,10 @@
+import functools
+
 import jax
 import jax.numpy as jnp
 from jax import lax
+from jax.experimental import pallas as pl
+from jax.experimental.pallas import tpu as pltpu
 from jax.sharding import PartitionSpec as P
 
 D = 1536
@@ -21,6 +25,9 @@
 bf16 = jnp.bfloat16
 f32 = jnp.float32
 EVERY = ("fsdp", "ctx", "tp")
+NT = (((1,), (1,)), ((), ()))
+NN = (((1,), (0,)), ((), ()))
+TN = (((0,), (0,)), ((), ()))
 
 
 def dot(spec, left, right):
@@ -57,43 +64,323 @@
     return table
 
 
-def attention_forward(query, key, value, allowed, blocks):
-    rows = query.shape[0] // blocks
-    outs, logs = [], []
-    for b in range(blocks):
-        seen = (b + 1) * rows
-        mine = slice(b * rows, seen)
-        scores = dot("qgd,kd->gqk", query[mine], key[:seen]) * HEAD ** (-0.5)
-        masked = jnp.where(allowed[None, mine, :seen], scores, -1e30)
-        row_max = jnp.max(masked, axis=-1, keepdims=True)
-        exp_scores = jnp.exp(masked - row_max)
-        row_total = jnp.sum(exp_scores, axis=-1, keepdims=True)
-        prob_low = (exp_scores / row_total).astype(bf16)
-        logs.append(row_max + jnp.log(row_total))
-        outs.append(dot("gqk,kd->qgd", prob_low, value[:seen]))
-    return jnp.concatenate(outs, axis=0).astype(bf16), logs
-
-
-def attention_backward(query, key, value, allowed, logs, d_out):
-    blocks = len(logs)
-    rows = query.shape[0] // blocks
-    scale = HEAD ** (-0.5)
-    d_key = jnp.zeros(key.shape, f32)
-    d_value = jnp.zeros(key.shape, f32)
-    d_queries = []
-    for b in range(blocks):
-        seen = (b + 1) * rows
-        mine = slice(b * rows, seen)
-        scores = dot("qgd,kd->gqk", query[mine], key[:seen]) * scale
-        masked = jnp.where(allowed[None, mine, :seen], scores, -1e30)
-        prob_full = jnp.exp(masked - logs[b])
-        d_prob = dot("qgd,kd->gqk", d_out[mine], value[:seen])
-        delta = jnp.sum(prob_full * d_prob, axis=-1, keepdims=True)
-        d_scores = (prob_full * (d_prob - delta)).astype(bf16)
-        d_queries.append(dot("gqk,kd->qgd", d_scores, key[:seen]) * scale)
-        d_key = d_key.at[:seen].add(dot("gqk,qgd->kd", d_scores, query[mine]) * scale)
-        d_value = d_value.at[:seen].add(dot("gqk,qgd->kd", prob_full.astype(bf16), d_out[mine]))
-    return jnp.concatenate(d_queries, axis=0), d_key, d_value
+def partner(values, axis, bits, count):
+    return lax.ppermute(values, axis, [(i, i ^ bits) for i in range(count)])
+
+
+def after(values, *others):
+    return lax.optimization_barrier((values,) + others)[0]
+
+
+def xor_order(values, axis, index):
+    shape = values.shape
+    bit = 1
+    while bit < shape[axis]:
+        halves = values.reshape(shape[:axis] + (-1, 2, bit) + shape[axis + 1 :])
+        swapped = jnp.flip(halves, axis + 1)
+        values = jnp.where((index // bit) % 2 == 1, swapped, halves).reshape(shape)
+        bit *= 2
+    return values
+
+
+def in_order(mine, other, bit, axis):
+    first = jnp.where(bit == 0, mine, other)
+    second = jnp.where(bit == 0, other, mine)
+    return jnp.stack([first, second], axis=axis)
+
+
+def mm(left, right, dims):
+    return lax.dot_general(left, right, dims, preferred_element_type=f32)
+
+
+def forward_kernel(q_ref, k_ref, vt_ref, out_ref, log_ref, acc_ref, top_ref, sum_ref):
+    step = pl.program_id(0)
+    heads, rows, wide = q_ref.shape
+    query = q_ref[...].reshape(heads * rows, wide)
+    acc_ref[...] = jnp.zeros_like(acc_ref)
+    top_ref[...] = jnp.full(top_ref.shape, -3e38, f32)
+    sum_ref[...] = jnp.zeros_like(sum_ref)
+
+    def chunk(j, diagonal):
+        at = pl.ds(pl.multiple_of(j * rows, rows), rows)
+        scores = mm(k_ref[at, :], query, NT)
+        if diagonal:
+            key_at = lax.broadcasted_iota(jnp.int32, (rows, rows), 0)
+            query_at = lax.broadcasted_iota(jnp.int32, (rows, rows), 1)
+            later = jnp.where(key_at > query_at, -1e30, 0.0)
+            scores = scores + jnp.concatenate([later] * heads, axis=1)
+        top_old = top_ref[...]
+        top = jnp.maximum(top_old, jnp.max(scores, axis=0, keepdims=True))
+        probs = jnp.exp(scores - top)
+        shrink = jnp.exp(top_old - top)
+        sum_ref[...] = sum_ref[...] * shrink + jnp.sum(probs, axis=0, keepdims=True)
+        acc_ref[...] = acc_ref[...] * shrink + mm(vt_ref[:, at], probs.astype(bf16), NN)
+        top_ref[...] = top
+
+    chunk(step, True)
+
+    @pl.loop(0, step)
+    def _(j):
+        chunk(j, False)
+
+    total = sum_ref[...]
+    log_ref[...] = (top_ref[...] + jnp.log(total))[None]
+    out = (acc_ref[...] / total).T.astype(bf16)
+    out_ref[...] = out.reshape(heads, rows, HEAD)
+
+
+def attention_forward(query, key, value_t, rows):
+    heads, length, wide = query.shape
+    steps = length // rows
+    return pl.pallas_call(
+        forward_kernel,
+        out_shape=(
+            jax.ShapeDtypeStruct((heads, length, HEAD), bf16),
+            jax.ShapeDtypeStruct((steps, 1, heads * rows), f32),
+        ),
+        grid=(steps,),
+        in_specs=[
+            pl.BlockSpec((heads, rows, wide), lambda i: (0, i, 0)),
+            pl.BlockSpec((length, wide), lambda i: (0, 0)),
+            pl.BlockSpec((HEAD, length), lambda i: (0, 0)),
+        ],
+        out_specs=(
+            pl.BlockSpec((heads, rows, HEAD), lambda i: (0, i, 0)),
+            pl.BlockSpec((1, 1, heads * rows), lambda i: (i, 0, 0)),
+        ),
+        scratch_shapes=[
+            pltpu.VMEM((HEAD, heads * rows), f32),
+            pltpu.VMEM((1, heads * rows), f32),
+            pltpu.VMEM((1, heads * rows), f32),
+        ],
+        compiler_params=pltpu.CompilerParams(vmem_limit_bytes=40 * 2**20),
+        cost_estimate=pl.CostEstimate(
+            flops=3 * heads * length * length * 128, bytes_accessed=8 * 2**20, transcendentals=0
+        ),
+    )(query, key, value_t)
+
+
+def backward_kernel(
+    q_ref, k_ref, kt_ref, v_ref, do_ref, log_ref, delta_ref, dq_ref, dk_ref, dv_ref, acc_ref
+):
+    step = pl.program_id(0)
+    heads, rows, wide = q_ref.shape
+    query = q_ref[...].reshape(heads * rows, wide)
+    d_out = do_ref[...].reshape(heads * rows, HEAD)
+    logs = log_ref[0]
+    delta = delta_ref[0]
+
+    @pl.when(step == 0)
+    def _():
+        dk_ref[...] = jnp.zeros_like(dk_ref)
+        dv_ref[...] = jnp.zeros_like(dv_ref)
+
+    acc_ref[...] = jnp.zeros_like(acc_ref)
+
+    def chunk(j, diagonal):
+        at = pl.ds(pl.multiple_of(j * rows, rows), rows)
+        scores = mm(k_ref[at, :], query, NT)
+        if diagonal:
+            key_at = lax.broadcasted_iota(jnp.int32, (rows, rows), 0)
+            query_at = lax.broadcasted_iota(jnp.int32, (rows, rows), 1)
+            later = jnp.where(key_at > query_at, -1e30, 0.0)
+            scores = scores + jnp.concatenate([later] * heads, axis=1)
+        probs = jnp.exp(scores - logs)
+        d_probs = mm(v_ref[at, :], d_out, NT)
+        d_scores = (probs * (d_probs - delta)).astype(bf16)
+        dv_ref[at, :] += mm(probs.astype(bf16), d_out, NN)
+        dk_ref[at, :] += mm(d_scores, query, NN)
+        acc_ref[...] += mm(kt_ref[:, at], d_scores, NN)
+
+    chunk(step, True)
+
+    @pl.loop(0, step)
+    def _(j):
+        chunk(j, False)
+
+    out = (acc_ref[...] * HEAD ** (-0.5)).T.astype(bf16)
+    dq_ref[...] = out.reshape(heads, rows, HEAD)
+
+
+def attention_backward(query, key, key_t, value, d_out, logs, delta):
+    heads, length, wide = query.shape
+    steps = logs.shape[0]
+    rows = length // steps
+    return pl.pallas_call(
+        backward_kernel,
+        out_shape=(
+            jax.ShapeDtypeStruct((heads, length, HEAD), bf16),
+            jax.ShapeDtypeStruct((length, wide), f32),
+            jax.ShapeDtypeStruct((length, HEAD), f32),
+        ),
+        grid=(steps,),
+        in_specs=[
+            pl.BlockSpec((heads, rows, wide), lambda i: (0, i, 0)),
+            pl.BlockSpec((length, wide), lambda i: (0, 0)),
+            pl.BlockSpec((HEAD, length), lambda i: (0, 0)),
+            pl.BlockSpec((length, HEAD), lambda i: (0, 0)),
+            pl.BlockSpec((heads, rows, HEAD), lambda i: (0, i, 0)),
+            pl.BlockSpec((1, 1, heads * rows), lambda i: (i, 0, 0)),
+            pl.BlockSpec((1, 1, heads * rows), lambda i: (i, 0, 0)),
+        ],
+        out_specs=(
+            pl.BlockSpec((heads, rows, HEAD), lambda i: (0, i, 0)),
+            pl.BlockSpec((length, wide), lambda i: (0, 0)),
+            pl.BlockSpec((length, HEAD), lambda i: (0, 0)),
+        ),
+        scratch_shapes=[pltpu.VMEM((HEAD, heads * rows), f32)],
+        compiler_params=pltpu.CompilerParams(vmem_limit_bytes=40 * 2**20),
+        cost_estimate=pl.CostEstimate(
+            flops=8 * heads * length * length * 128, bytes_accessed=8 * 2**20, transcendentals=0
+        ),
+    )(query, key, key_t, value, d_out, logs, delta)
+
+
+def slot_kernel(sources, *refs):
+    row_refs, cot_refs = refs[:sources], refs[sources : 2 * sources]
+    rank_ref, weight_ref, gu_ref, down_ref = refs[2 * sources : 2 * sources + 4]
+    x_ref, hid_ref, ds_ref, dgu_ref, dcomb_ref = refs[2 * sources + 4 : 2 * sources + 9]
+    moe_refs = refs[2 * sources + 9 : 3 * sources + 9]
+    dsum_refs = refs[3 * sources + 9 : 4 * sources + 9]
+    moe_acc, dsum_acc = refs[4 * sources + 9 :]
+    expert = pl.program_id(0)
+    tokens, width = row_refs[0].shape
+    cap = x_ref.shape[1] // sources
+
+    @pl.when(expert == 0)
+    def _():
+        moe_acc[...] = jnp.zeros_like(moe_acc)
+        dsum_acc[...] = jnp.zeros_like(dsum_acc)
+
+    slots = lax.broadcasted_iota(jnp.int32, (cap, tokens), 0).astype(f32)
+    chosen, picks, cots, slot_weights = [], [], [], []
+    for s in range(sources):
+        hit = rank_ref[0, s : s + 1, :] == slots
+        pick = jnp.where(hit, 1.0, 0.0).astype(bf16)
+        chosen.append(hit)
+        picks.append(pick)
+        x_ref[0, s * cap : (s + 1) * cap, :] = mm(pick, row_refs[s][...], NN).astype(bf16)
+        cots.append(mm(pick, cot_refs[s][...], NN))
+        slot_weights.append(
+            jnp.sum(jnp.where(hit, weight_ref[0, s : s + 1, :], 0.0), axis=1, keepdims=True)
+        )
+    x_rows = x_ref[0]
+    cot = jnp.concatenate(cots, axis=0)
+    slot_weight = jnp.concatenate(slot_weights, axis=0)
+    gate_up = mm(x_rows, gu_ref[0], NN)
+    gate = gate_up[:, :FFE]
+    up = gate_up[:, FFE:]
+    sig = 1.0 / (1.0 + jnp.exp(-gate))
+    silu = gate * sig
+    hidden = (silu * up).astype(bf16)
+    hid_ref[0] = hidden
+    expert_out = mm(hidden, down_ref[0], NN).astype(bf16).astype(f32)
+    d_slot = (slot_weight * cot).astype(bf16)
+    ds_ref[0] = d_slot
+    d_comb = jnp.sum(cot * expert_out, axis=1, keepdims=True)
+    weighted = (slot_weight * expert_out).astype(bf16)
+    d_hidden = mm(d_slot, down_ref[0], NT)
+    d_gate = (d_hidden * up * sig * (1.0 + gate * (1.0 - sig))).astype(bf16)
+    d_up = (d_hidden * silu).astype(bf16)
+    dgu_ref[0, :, :FFE] = d_gate
+    dgu_ref[0, :, FFE:] = d_up
+    d_row = mm(dgu_ref[0], gu_ref[0], NT).astype(bf16)
+    for s in range(sources):
+        part = slice(s * cap, (s + 1) * cap)
+        moe_acc[s] += mm(picks[s], weighted[part], TN)
+        dsum_acc[s] += mm(picks[s], d_row[part], TN)
+        dcomb_ref[0, s : s + 1, :] = jnp.sum(
+            jnp.where(chosen[s], d_comb[part], 0.0), axis=0, keepdims=True
+        )
+
+    @pl.when(expert == pl.num_programs(0) - 1)
+    def _():
+        for s in range(sources):
+            moe_refs[s][...] = moe_acc[s].astype(bf16)
+            dsum_refs[s][...] = dsum_acc[s].astype(bf16)
+
+
+def expert_slot(rows, cots, ranks, weights, gate_up, down, cap):
+    sources = len(rows)
+    tokens, width = rows[0].shape
+    experts = gate_up.shape[0]
+    held = sources * cap
+    each = lambda *shape: pl.BlockSpec((1,) + shape, lambda e: (e,) + (0,) * len(shape))
+    fixed = pl.BlockSpec((tokens, width), lambda e: (0, 0))
+    token_out = jax.ShapeDtypeStruct((tokens, width), bf16)
+    got = pl.pallas_call(
+        functools.partial(slot_kernel, sources),
+        out_shape=(
+            jax.ShapeDtypeStruct((experts, held, width), bf16),
+            jax.ShapeDtypeStruct((experts, held, FFE), bf16),
+            jax.ShapeDtypeStruct((experts, held, width), bf16),
+            jax.ShapeDtypeStruct((experts, held, 2 * FFE), bf16),
+            jax.ShapeDtypeStruct((experts, sources, tokens), f32),
+        )
+        + (token_out,) * (2 * sources),
+        grid=(experts,),
+        in_specs=[fixed] * (2 * sources)
+        + [
+            each(sources, tokens),
+            each(sources, tokens),
+            each(width, 2 * FFE),
+            each(FFE, width),
+        ],
+        out_specs=(
+            each(held, width),
+            each(held, FFE),
+            each(held, width),
+            each(held, 2 * FFE),
+            each(sources, tokens),
+        )
+        + (fixed,) * (2 * sources),
+        scratch_shapes=[
+            pltpu.VMEM((sources, tokens, width), f32),
+            pltpu.VMEM((sources, tokens, width), f32),
+        ],
+        compiler_params=pltpu.CompilerParams(vmem_limit_bytes=56 * 2**20),
+        cost_estimate=pl.CostEstimate(
+            flops=experts * held * width * FFE * 12,
+            bytes_accessed=experts * FFE * width * 6 + 8 * held * width * experts,
+            transcendentals=0,
+        ),
+    )(*rows, *cots, ranks, weights, gate_up, down)
+    return got[:5], got[5 : 5 + sources], got[5 + sources :]
+
+
+def grads_kernel(parts, *refs):
+    x_refs, dgu_refs = refs[:parts], refs[parts : 2 * parts]
+    hid_refs, ds_refs = refs[2 * parts : 3 * parts], refs[3 * parts : 4 * parts]
+    gu_ref, down_ref = refs[4 * parts :]
+    join = lambda many: jnp.concatenate([r[0] for r in many], axis=0)
+    gu_ref[0] = mm(join(x_refs), join(dgu_refs), TN).astype(bf16)
+    down_ref[0] = mm(join(hid_refs), join(ds_refs), TN).astype(bf16)
+
+
+def expert_grads(xs, dgus, hids, dss):
+    parts = len(xs)
+    experts, _, width = xs[0].shape
+    spec = lambda a: pl.BlockSpec((1,) + a.shape[1:], lambda e: (e, 0, 0))
+    many = [*xs, *dgus, *hids, *dss]
+    return pl.pallas_call(
+        functools.partial(grads_kernel, parts),
+        out_shape=(
+            jax.ShapeDtypeStruct((experts, width, 2 * FFE), bf16),
+            jax.ShapeDtypeStruct((experts, FFE, width), bf16),
+        ),
+        grid=(experts,),
+        in_specs=[spec(a) for a in many],
+        out_specs=(
+            pl.BlockSpec((1, width, 2 * FFE), lambda e: (e, 0, 0)),
+            pl.BlockSpec((1, FFE, width), lambda e: (e, 0, 0)),
+        ),
+        compiler_params=pltpu.CompilerParams(vmem_limit_bytes=56 * 2**20),
+        cost_estimate=pl.CostEstimate(
+            flops=6 * experts * width * FFE * sum(a.shape[1] for a in xs),
+            bytes_accessed=experts * width * FFE * 6 + 30 * 2**20,
+            transcendentals=0,
+        ),
+    )(*many)
 
 
 def per_device(
@@ -191,7 +478,15 @@
     w_send = jnp.broadcast_to(w_send[None], (fsdp_count,) + w_send.shape)
     w_got = exchange(w_send.reshape((dense_parts,) + w_send.shape[2:]), ("fsdp", "ctx"))
     w_got = w_got.reshape(D, own_cols + 2 + EXPERTS)
-    tree_inputs = lax.all_gather(inputs, "ctx", axis=0, tiled=True).astype(f32)
+    parts = inputs[None]
+    arrived = parts
+    bit = ctx_count // 2
+    while bit:
+        other = partner(parts, "ctx", bit, ctx_count)
+        arrived = other if bit == ctx_count // 2 else arrived
+        parts = in_order(parts, other, (ctx_index // bit) % 2, 1).reshape((-1,) + inputs.shape)
+        bit //= 2
+    tree_inputs = parts.reshape(tree_len, D).astype(f32)
     w_own = w_got[:, :own_cols]
     gain_one = w_got[:, own_cols].astype(f32)
     gain_two = w_got[:, own_cols + 1].astype(f32)
@@ -199,6 +494,8 @@
 
     my_routes = lax.dynamic_slice_in_dim(routes, tp_index * half_rows, half_rows, 0)
     hit = jnp.sum((my_routes[..., None] == labels).astype(f32), axis=1)
+    counts = jnp.sum(share(jnp.sum(hit, axis=0), count), axis=0)
+    fraction = counts / (tokens_all * TOPK)
     master_sums = jnp.stack(
         [
             jnp.sum(w_qkv * w_qkv),
@@ -210,9 +507,6 @@
             keep_once * jnp.sum(gain_moe * gain_moe),
         ]
     )
-    early = jnp.sum(share(jnp.concatenate([jnp.sum(hit, axis=0), master_sums]), count), axis=0)
-    fraction = early[:EXPERTS] / (tokens_all * TOPK)
-    master_totals = early[EXPERTS:]
     before = (
         jnp.arange(half_rows, dtype=jnp.int32)[:, None]
         < jnp.arange(half_rows, dtype=jnp.int32)[None, :]
@@ -220,32 +514,59 @@
     rank = dot("te,tu->eu", hit.astype(bf16), before)
     rank = jnp.where(hit.T > 0.5, rank, -1.0)
     ranks = exchange(rank.reshape(groups, local_experts, half_rows), ("fsdp", "tp"))
-    grad_rows = lax.all_gather(cotangent, ("fsdp", "tp"), axis=0, tiled=True)
-    grad_rows = grad_rows.reshape(groups, half_rows, D)
-    gate_up_all = lax.all_gather(w_gate_up.astype(bf16), "ctx", axis=1, tiled=True)
-    down_all = lax.all_gather(w_down.astype(bf16), "ctx", axis=2, tiled=True)
-    out_t = lax.all_gather(w_out.astype(bf16).T, ("tp", "fsdp", "ctx"), axis=0, tiled=True)
-    out_t = out_t.reshape(tp_count, D, w_out.shape[0])
+    ranks = ranks.reshape(fsdp_count, tp_count, local_experts, half_rows)
+
+    def relative(values):
+        return xor_order(xor_order(values, 0, fsdp_index), 1, tp_index)
+
+    ranks = relative(ranks)
+
+    def spread(block):
+        near = [block] + [partner(block, "fsdp", j, fsdp_count) for j in range(1, fsdp_count)]
+        return [[b] + [partner(b, "tp", y, tp_count) for y in range(1, tp_count)] for b in near]
+
+    grad_slots = spread(after(cotangent, w_got))
+    gate_up_low = after(w_gate_up.astype(bf16), arrived)
+    down_low = after(w_down.astype(bf16), arrived)
+    gate_up_all = lax.all_gather(gate_up_low, "ctx", axis=1, tiled=True)
+    down_all = lax.all_gather(down_low, "ctx", axis=2, tiled=True)
+    out_rows = w_out.shape[0]
+    out_t = jnp.broadcast_to(w_out.astype(bf16).T, (dense_parts, dense_rows, out_rows))
+    out_t = exchange(after(out_t, w_got), ("fsdp", "ctx")).reshape(1, D, out_rows)
+    other = partner(out_t, "tp", 1, tp_count)
+    out_t = in_order(out_t, other, tp_index, 1).reshape(tp_count, D, out_rows)
     qkv_full = lax.all_gather(
-        w_grouped.reshape(dense_rows, qkv_cols), ("tp", "fsdp", "ctx"), axis=0, tiled=True
+        after(w_grouped, down_all).reshape(dense_rows, qkv_cols), ("tp", "fsdp", "ctx"), axis=0, tiled=True
     ).reshape(tp_count, D, qkv_cols)
 
     act1 = (tree_inputs * inv_rms(tree_inputs) * gain_one).astype(bf16)
     qkv = dot("td,dc->tc", act1, w_own).astype(bf16)
-    query = qkv[:, :q_cols].reshape(tree_len, kv_own, group_size, HEAD)
-    keys = qkv[:, q_cols : q_cols + kv_cols].reshape(tree_len, kv_own, HEAD)
-    values = qkv[:, q_cols + kv_cols :].reshape(tree_len, kv_own, HEAD)
+    query = (qkv[:, :q_cols] * HEAD ** (-0.5)).reshape(tree_len, kv_own, group_size, HEAD)
+    query = query.transpose(1, 2, 0, 3)
+    keys = qkv[:, q_cols : q_cols + kv_cols].reshape(tree_len, kv_own, HEAD).transpose(1, 0, 2)
+    values = qkv[:, q_cols + kv_cols :].reshape(tree_len, kv_own, HEAD).transpose(1, 0, 2)
     seg_hot = (segment_ids[0][:, None] == jnp.arange(NSEG, dtype=jnp.int32)).astype(bf16)
-    reach = dot("qs,ks->qk", dot("qs,su->qu", seg_hot, ancestry(parents[0]).astype(bf16)).astype(bf16), seg_hot)
-    positions = jnp.arange(tree_len, dtype=jnp.int32)
-    allowed = (reach > 0.5) & (positions[None, :] <= positions[:, None])
-    blocks = 4
+    hidden_from = (1.0 - ancestry(parents[0])) * -1e30
+    barred = dot("qs,su->qu", seg_hot, hidden_from.astype(bf16)).astype(bf16)
+    lanes = 2 * HEAD
+    spare = lanes - HEAD - NSEG
+    barred = jnp.pad(barred, ((0, 0), (0, spare)))
+    seg_hot = jnp.pad(seg_hot, ((0, 0), (0, spare)))
+    query = jnp.concatenate(
+        [query, jnp.broadcast_to(barred, query.shape[:2] + barred.shape)], axis=-1
+    )
+    keys_wide = jnp.concatenate(
+        [keys, jnp.broadcast_to(seg_hot, (kv_own,) + seg_hot.shape)], axis=-1
+    )
+    step_rows = half_rows
+    steps = tree_len // step_rows
     outs, logs = [], []
     for h in range(kv_own):
-        out_h, log_h = attention_forward(query[:, h], keys[:, h], values[:, h], allowed, blocks)
+        out_h, log_h = attention_forward(query[h], keys_wide[h], values[h].T, step_rows)
         outs.append(out_h)
         logs.append(log_h)
-    attended_own = jnp.concatenate(outs, axis=1).reshape(tree_len, q_cols)
+    attended_heads = jnp.concatenate(outs, axis=0)
+    attended_own = attended_heads.transpose(1, 0, 2).reshape(tree_len, q_cols)
     attended = exchange(attended_own, ("ctx", "tp")).reshape(ctx_count, tp_count, half_rows, q_cols)
     attended = attended.transpose(2, 1, 0, 3).reshape(half_rows, tp_count, ctx_count * q_cols)
     inputs_half = lax.dynamic_slice_in_dim(inputs, tp_index * half_rows, half_rows, 0).astype(f32)
@@ -253,50 +574,58 @@
 
     inv_two = inv_rms(x_one)
     act2 = (x_one * inv_two * gain_two).astype(bf16)
-    rows = lax.all_gather(act2, ("fsdp", "tp"), axis=0, tiled=True).reshape(groups, half_rows, D)
+    row_slots = spread(act2)
     logits = dot("td,de->te", act2, router_full)
     router_probs = jax.nn.softmax(logits, axis=-1)
     combine = jax.nn.softmax(jnp.where(hit > 0.5, logits, -jnp.inf), axis=-1)
     weights = exchange(combine.T.reshape(groups, local_experts, half_rows), ("fsdp", "tp"))
 
-    slots = jnp.arange(capacity, dtype=f32)
-    chosen = ranks[:, :, None, :] == slots[None, None, :, None]
-    pick = chosen.astype(bf16)
-    slot_weight = jnp.sum(jnp.where(chosen, weights[:, :, None, :], 0.0), axis=-1)
-    x_e = dot("sert,std->serd", pick, rows).astype(bf16)
-    c_e = dot("sert,std->serd", pick, grad_rows)
-    gate_up = dot("serd,edf->serf", x_e, gate_up_all)
-    gate = gate_up[..., :FFE]
-    up = gate_up[..., FFE:]
-    sig = jax.nn.sigmoid(gate)
-    hidden = (gate * sig * up).astype(bf16)
-    expert_out = dot("serf,efd->serd", hidden, down_all).astype(bf16)
-    d_slot_out = jnp.sum(c_e * expert_out.astype(f32), axis=-1)
-    d_slot = (slot_weight[..., None] * c_e).astype(bf16)
-    d_hidden = dot("serd,efd->serf", d_slot, down_all)
-    g_down_local = dot("serf,serd->efd", hidden, d_slot)
-    d_gate = d_hidden * up * sig * (1.0 + gate * (1.0 - sig))
-    d_up = d_hidden * gate * sig
-    d_gate_up = jnp.concatenate([d_gate, d_up], axis=-1).astype(bf16)
-    d_row = dot("serf,edf->serd", d_gate_up, gate_up_all).astype(bf16)
-    g_gate_up_local = dot("serd,serf->edf", x_e, d_gate_up)
-    d_sum = dot("sert,serd->std", pick, d_row).astype(bf16)
-    weighted = (slot_weight[..., None] * expert_out.astype(f32)).astype(bf16)
-    moe_sum = dot("sert,serd->std", pick, weighted).astype(bf16)
-    d_combine_own = jnp.sum(jnp.where(chosen, d_slot_out[..., None], 0.0), axis=2)
-    d_combine = exchange(d_combine_own, ("fsdp", "tp")).reshape(EXPERTS, half_rows).T
-    d_act2 = lax.psum_scatter(
-        d_sum.reshape(groups * half_rows, D), ("fsdp", "tp"), scatter_dimension=0, tiled=True
-    ).astype(f32)
-    moe = lax.psum_scatter(
-        moe_sum.reshape(groups * half_rows, D), ("fsdp", "tp"), scatter_dimension=0, tiled=True
-    ).astype(f32)
-    layer_out = (x_one + moe).astype(bf16)
+    weights = weights.reshape(fsdp_count, tp_count, local_experts, half_rows)
+    weights = relative(weights)
+    kept, d_combines, moe_parts, d_parts = [], [], [], []
+    for chunk in [[j] for j in range(fsdp_count)]:
+        rows = [r for j in chunk for r in row_slots[j]]
+        cots = [c for j in chunk for c in grad_slots[j]]
+        pieces = lambda a: a[chunk[0] : chunk[-1] + 1].reshape(-1, local_experts, half_rows)
+        held, moe_out, d_out = expert_slot(
+            rows,
+            cots,
+            pieces(ranks).transpose(1, 0, 2),
+            pieces(weights).transpose(1, 0, 2),
+            gate_up_all,
+            down_all,
+            capacity,
+        )
+        kept.append(held[:4])
+        d_combines.append(held[4])
+        for n, j in enumerate(chunk):
+            moe_parts.append(moe_out[n * tp_count : (n + 1) * tp_count])
+            d_parts.append(d_out[n * tp_count : (n + 1) * tp_count])
+
+    def collect(parts):
+        total = 0.0
+        for j in range(fsdp_count):
+            block = parts[j][0].astype(f32)
+            for y in range(1, tp_count):
+                block = block + partner(parts[j][y], "tp", y, tp_count).astype(f32)
+            if j:
+                block = partner(block.astype(bf16), "fsdp", j, fsdp_count).astype(f32)
+            total = total + block
+        return total
+
+    d_combine = jnp.concatenate(d_combines, axis=1).transpose(1, 0, 2)
+    d_combine = d_combine.reshape(fsdp_count, tp_count, local_experts, half_rows)
+    d_combine = relative(d_combine).reshape(groups, local_experts, half_rows)
+    d_combine = exchange(d_combine, ("fsdp", "tp")).reshape(EXPERTS, half_rows).T
+    d_act2 = collect(d_parts)
+    g_gate_up_local, g_down_local = expert_grads(
+        [k[0] for k in kept], [k[3] for k in kept], [k[1] for k in kept], [k[2] for k in kept]
+    )
     g_gate_up = lax.psum_scatter(
-        g_gate_up_local.astype(bf16), "ctx", scatter_dimension=1, tiled=True
+        g_gate_up_local, "ctx", scatter_dimension=1, tiled=True
     ).astype(f32)
     g_down = lax.psum_scatter(
-        g_down_local.astype(bf16), "ctx", scatter_dimension=2, tiled=True
+        g_down_local, "ctx", scatter_dimension=2, tiled=True
     ).astype(f32)
 
     aux_grad = aux_weight * EXPERTS * fraction
@@ -322,16 +651,21 @@
     d_attended = dot("rd,tdk->rtk", d_x1_low, out_t).astype(bf16)
     d_attended = d_attended.reshape(half_rows, tp_count, ctx_count, q_cols).transpose(2, 1, 0, 3)
     d_attended = exchange(d_attended.reshape(tree_len, q_cols), ("ctx", "tp"))
-    d_attended = d_attended.reshape(tree_len, kv_own, group_size, HEAD)
+    late_parts = [[after(p, d_attended) for p in part] for part in moe_parts]
+    d_heads = d_attended.reshape(tree_len, q_own, HEAD).transpose(1, 0, 2)
+    delta = jnp.sum(d_heads.astype(f32) * attended_heads.astype(f32), axis=-1)
+    delta = delta.reshape(kv_own, group_size, steps, step_rows).transpose(0, 2, 1, 3)
+    delta = delta.reshape(kv_own, steps, 1, group_size * step_rows)
+    d_heads = d_heads.reshape(kv_own, group_size, tree_len, HEAD)
     d_q, d_k, d_v = [], [], []
     for h in range(kv_own):
         dq_h, dk_h, dv_h = attention_backward(
-            query[:, h], keys[:, h], values[:, h], allowed, logs[h], d_attended[:, h]
+            query[h], keys_wide[h], keys[h].T, values[h], d_heads[h], logs[h], delta[h]
         )
-        d_q.append(dq_h.reshape(tree_len, -1))
-        d_k.append(dk_h)
-        d_v.append(dv_h)
-    d_qkv = jnp.concatenate(d_q + d_k + d_v, axis=1).astype(bf16)
+        d_q.append(dq_h.transpose(1, 0, 2).reshape(tree_len, -1))
+        d_k.append(dk_h[:, :HEAD].astype(bf16))
+        d_v.append(dv_h.astype(bf16))
+    d_qkv = jnp.concatenate(d_q + d_k + d_v, axis=1)
     g_qkv_part = dot("td,tc->dc", act1, d_qkv).astype(bf16)
     g_qkv_got = exchange(g_qkv_part.reshape(dense_parts, dense_rows, own_cols), ("fsdp", "ctx"))
     g_qkv_got = g_qkv_got.reshape(fsdp_count, ctx_count, dense_rows, own_cols).astype(f32)
@@ -345,7 +679,10 @@
     d_act1 = dot("rtc,tdc->rd", d_qkv_all, qkv_full)
     own_inputs = inputs.astype(f32)
     d_inputs_attn, _ = norm_backward(own_inputs, inv_rms(own_inputs), gain_one, d_act1)
-    d_x1 = lax.all_gather(d_x1_half, "tp", axis=0, tiled=True)
+    d_x1_own = after(d_x1_half, d_attended)[None]
+    other = partner(d_x1_own, "tp", 1, tp_count)
+    d_x1 = in_order(d_x1_own, other, tp_index, 1).reshape(tok_rows, D)
+    layer_out = (x_one + collect(late_parts)).astype(bf16)
     grad_inputs = d_x1 + d_inputs_attn
 
     attended_t = attended.transpose(1, 0, 2)
@@ -357,7 +694,6 @@
 
     sq_out = g_out * g_out
     sq_router = g_router * g_router
-    out_rows = w_out.shape[0]
     first = jnp.concatenate(
         [
             jnp.sum(sq_out, axis=1),
@@ -365,6 +701,7 @@
             jnp.sum(sq_router, axis=1),
             jnp.sum(sq_router, axis=0),
             jnp.sum(router_probs, axis=0),
+            master_sums,
         ]
     )
     first = share(first, count).reshape(dense_parts, tp_count, -1)
@@ -374,7 +711,9 @@
     tot_col_out = jnp.sum(first[..., at[0] : at[1]], axis=1).reshape(-1)
     tot_row_router = first[:, 0, at[1] : at[2]].reshape(-1)
     tot_col_router = jnp.sum(first[:, 0, at[2] : at[3]], axis=0)
-    prob_totals = jnp.sum(first[..., at[3] :], axis=(0, 1))
+    last_totals = jnp.sum(first[..., at[3] :], axis=(0, 1))
+    prob_totals = last_totals[:EXPERTS]
+    master_totals = last_totals[EXPERTS:]
 
     sq_gate_up = g_gate_up * g_gate_up
     sq_down = g_down * g_down

time: 1290 us -> 1110 us (0.86)
  waiting for transfers between devices: 646 us -> 426 us
  matrix products: 233 us -> 38.8 us
  Pallas kernels: 0 us -> 162 us
  starting transfers between devices: 70.7 us -> 149 us
    all_gather x8 -> x3, waiting for transfers between devices: 275 us -> 0.04 us  [the longest x1 0.02 us: per_device(): down_all = lax.all_gather(down_low, 'ctx', axis=2, tiled=True)]
    reduce_scatter x3 -> x1, waiting for transfers between devices: 218 us -> 0.02 us  [per_device(): lax.psum_scatter(g_gate_up_local, 'ctx', scatter_dimension=1, tiled=True)]
    dot_general x44 -> x11, matrix products: 233 us -> 38.8 us  [dot(): return jnp.einsum(spec, left, right, preferred_element_type=f32)]
    pallas_call x0 -> x7, Pallas kernels: none -> 162 us  [the longest x4 93.2 us: expert_slot(): pl.pallas_call(functools.partial(slot_kernel, sources), out_shape=(jax.Sh...]
    ppermute x0 -> x32, waiting for transfers between devices: none -> 141 us  [partner(): return lax.ppermute(values, axis, [(i, i ^ bits) for i in range(count)])]
    all_to_all x14 -> x16, waiting for transfers between devices: 151 us -> 284 us  [exchange(): return lax.all_to_all(values, axes, split_axis=0, concat_axis=0, tiled=True)]
    ppermute x0 -> x32, starting transfers between devices: none -> 50.1 us  [partner(): return lax.ppermute(values, axis, [(i, i ^ bits) for i in range(count)])]
    all_to_all x14 -> x16, starting transfers between devices: 70.2 us -> 98.7 us  [exchange(): return lax.all_to_all(values, axes, split_axis=0, concat_axis=0, tiled=True)]
  transfers between devices with their start and end apart: 26 -> 53, of which waited for: 18 -> 21; matrix products, arithmetic and copies ran while one was open for 32% -> 23% of each run, Pallas kernels for 0% -> 15%
where the time goes in v2:
time: 1110 us
  waiting for transfers between devices  426 us (38%)
  other arithmetic  164 us (15%)
  Pallas kernels  162 us (15%)
  starting transfers between devices  149 us (13%)
  local copies, waits for them, and re-layouts  117 us (11%)
  matrix products  38.8 us (3%)
  blocking collectives  25.1 us (2%)
  between operations  23.6 us (2%)
    all_to_all x16, waiting for transfers between devices, exchange(): return lax.all_to_all(values, axes, split_axis=0, concat_axis=0, tiled=True)  284 us
    ppermute x32, waiting for transfers between devices, partner(): return lax.ppermute(values, axis, [(i, i ^ bits) for i in range(count)])  141 us
    all_to_all x16, starting transfers between devices, exchange(): return lax.all_to_all(values, axes, split_axis=0, concat_axis=0, tiled=True)  98.7 us
    pallas_call x4, Pallas kernels, expert_slot(): pl.pallas_call(functools.partial(slot_kernel, sources), out_shape=(jax.Sh...  93.2 us
    ppermute x32, starting transfers between devices, partner(): return lax.ppermute(values, axis, [(i, i ^ bits) for i in range(count)])  50.1 us
    unnamed x221, local copies, waits for them, and re-layouts  43.5 us
    dot_general x11, matrix products, dot(): return jnp.einsum(spec, left, right, preferred_element_type=f32)  38.8 us
    pallas_call x1, Pallas kernels, attention_forward(): pl.pallas_call(forward_kernel, out_shape=(jax.ShapeDtypeStruct((heads, le...  25.2 us
  transfers between devices with their start and end apart: 53, of which 21 were waited for; matrix products, arithmetic and copies ran while one was open for 23% of the time, Pallas kernels for 15%

profile of v2, /device:TPU:0, one launch (start us, length us, event | category | flops | bytes accessed | tf_op | source)
XLA Modules:
  0.0 1106.0 jit_solution(8858839509797810492)
XLA Ops:
  10.3 5.3 multiply_reduce_fusion.6
  15.6 29.4 %collective-permute-done = bf16[1,512,1536]{2,1,0:T(8,128)(2,1)} collective-permute-done((bf16[1,512,1536]{2,1,0:T(8,128)(2,1)}, bf16[1,512,1536]{2,1,0:T(8,128)(2,1)}, u32[]{:S(2)}, u32[]{:S(2)}) %collective-permute-start) | collective-permute-done | bytes 1572896 | tf_op jit(solution)/shard_map/ppermute | solution.py:68
  45.1 8.5 multiply_reduce_fusion.2
  64.0 6.3 all-to-all-start
  74.5 21.0 %all-to-all-done = bf16[16,96,354]{2,1,0:T(8,128)(2,1)S(1)} async-done(((bf16[16,96,354]{2,1,0:T(8,128)(2,1)}), bf16[16,96,354]{2,1,0:T(8,128)(2,1)S(1)}, u32[]{:S(2)}, u32[]{:S(2)}) %all-to-all-start) | async-done | bytes 1087520 | tf_op jit(solution)/shard_map/all_to_all | solution.py:38
  98.2 7.6 all-to-all-start.2
  116.9 7.4 maximum_convert_fusion
  124.3 8.5 fusion.1
  132.8 6.2 convolution_convert_fusion.1
  139.0 12.7 %all-to-all-done.2 = bf16[16,96,768]{2,1,0:T(8,128)(2,1)} async-done(((bf16[16,96,768]{2,1,0:T(8,128)(2,1)}), bf16[16,96,768]{2,1,0:T(8,128)(2,1)}, u32[]{:S(2)}, u32[]{:S(2)}) %all-to-all-start.2) | async-done | bytes 2359328 | tf_op jit(solution)/shard_map/all_to_all | solution.py:38
  152.4 12.2 %all-to-all-start.6 = ((f32[32,1,32]{2,1,0:T(1,128)}), f32[32,1,32]{2,1,0:T(1,128)S(1)}, u32[]{:S(2)}, u32[]{:S(2)}) async-start(f32[32,1,32]{2,1,0:T(1,128)} %broadcast_in_dim.59), calls=%async_computation.6 | async-start | bytes 32768 | tf_op jit(solution)/shard_map/all_to_all | solution.py:38
  173.3 25.2 %shard_map.528 = (bf16[3,2048,64]{2,1,0:T(8,128)(2,1)S(1)}, f32[8,1,768]{2,1,0:T(1,128)S(1)}) custom-call(bf16[3,2048,128]{2,1,0:T(8,128)(2,1)S(1)} %maximum_bitcast_fusion.8.q_ref, bf16[2048,128]{1,0:T(8,128)(2,1)S(1)} %maximum_bitcast_fusion.12.k_ref, bf16[64,2048]{1,0:T(8,128)(2,1)S(1)} %copy.482.vt_ref), custom_call_target="tpu_custom_call" | custom-call | flops 4831838208 | bytes 8388608 | tf_op jit(solution)/shard_map/pallas_call | solution.py:135
  200.4 4.0 all-to-all-start.1
  204.4 3.4 collective-permute-start.20
  207.9 20.1 %all-to-all-done.1 = bf16[8,256,192]{1,2,0:T(8,128)(2,1)S(1)} async-done(((bf16[8,256,192]{1,2,0:T(8,128)(2,1)}), bf16[8,256,192]{1,2,0:T(8,128)(2,1)S(1)}, u32[]{:S(2)}, u32[]{:S(2)}) %all-to-all-start.1) | async-done | bytes 786464 | tf_op jit(solution)/shard_map/all_to_all | solution.py:38
  236.4 3.4 collective-permute-start.18
  242.5 3.4 all-to-all-start.3
  247.2 101.3 %all-to-all-done.3 = f32[8,4,256]{2,1,0:T(4,128)S(1)} async-done(((f32[8,4,256]{2,1,0:T(4,128)}), f32[8,4,256]{2,1,0:T(4,128)S(1)}, u32[]{:S(2)}, u32[]{:S(2)}) %all-to-all-start.3) | async-done | bytes 32800 | tf_op jit(solution)/shard_map/all_to_all | solution.py:38
  348.4 3.7 all-to-all-start.4
  361.5 28.2 %collective-permute-done.8.refs_2_ = bf16[256,1536]{1,0:T(8,128)(2,1)} collective-permute-done((bf16[256,1536]{1,0:T(8,128)(2,1)}, bf16[256,1536]{1,0:T(8,128)(2,1)}, u32[]{:S(2)}, u32[]{:S(2)}) %collective-permute-start.8) | collective-permute-done | bytes 786464 | tf_op jit(solution)/shard_map/ppermute | solution.py:68
  394.6 10.5 collective-permute-done.6.refs_0_
  407.1 23.2 %shard_map.532 = (bf16[4,192,1536]{2,1,0:T(8,128)(2,1)}, bf16[4,192,512]{2,1,0:T(8,128)(2,1)}, bf16[4,192,1536]{2,1,0:T(8,128)(2,1)}, bf16[4,192,1024]{2,1,0:T(8...) custom-call(bf16[256,1536]{1,0:T(8,128)(2,1)} %collective-permute-do, ...), custom_call_target="tpu_custom_call" | custom-call | flops 7247757312 | bytes 28311552 | tf_op jit(solution)/shard_map/pallas_call | solution.py:311
  432.0 23.3 %shard_map.531 = (bf16[4,192,1536]{2,1,0:T(8,128)(2,1)}, bf16[4,192,512]{2,1,0:T(8,128)(2,1)}, bf16[4,192,1536]{2,1,0:T(8,128)(2,1)}, bf16[4,192,1024]{2,1,0:T(8...) custom-call(bf16[256,1536]{1,0:T(8,128)(2,1)} %collective-permute-do, ...), custom_call_target="tpu_custom_call" | custom-call | flops 7247757312 | bytes 28311552 | tf_op jit(solution)/shard_map/pallas_call | solution.py:311
  455.3 6.0 collective-permute-done.9.refs_3_
  461.3 16.9 %collective-permute-done.7.refs_1_ = bf16[256,1536]{1,0:T(8,128)(2,1)} collective-permute-done((bf16[256,1536]{1,0:T(8,128)(2,1)}, bf16[256,1536]{1,0:T(8,128)(2,1)}, u32[]{:S(2)}, u32[]{:S(2)}) %collective-permute-start.7) | collective-permute-done | bytes 786464 | tf_op jit(solution)/shard_map/ppermute | solution.py:68
  478.2 23.4 %shard_map.530 = (bf16[4,192,1536]{2,1,0:T(8,128)(2,1)}, bf16[4,192,512]{2,1,0:T(8,128)(2,1)}, bf16[4,192,1536]{2,1,0:T(8,128)(2,1)}, bf16[4,192,1024]{2,1,0:T(8...) custom-call(bf16[256,1536]{1,0:T(8,128)(2,1)} %collective-permute-do, ...), custom_call_target="tpu_custom_call" | custom-call | flops 7247757312 | bytes 28311552 | tf_op jit(solution)/shard_map/pallas_call | solution.py:311
  502.5 23.3 %shard_map.529 = (bf16[4,192,1536]{2,1,0:T(8,128)(2,1)}, bf16[4,192,512]{2,1,0:T(8,128)(2,1)}, bf16[4,192,1536]{2,1,0:T(8,128)(2,1)}, bf16[4,192,1024]{2,1,0:T(8...) custom-call(bf16[256,1536]{1,0:T(8,128)(2,1)} %multiply_convert_fusi, ...), custom_call_target="tpu_custom_call" | custom-call | flops 7247757312 | bytes 28311552 | tf_op jit(solution)/shard_map/pallas_call | solution.py:311
  525.8 19.9 %shard_map.534 = (bf16[4,1536,1024]{2,1,0:T(8,128)(2,1)}, bf16[4,512,1536]{2,1,0:T(8,128)(2,1)}) custom-call(bf16[4,192,1536]{2,1,0:T(8,128)(2,1)} %get-tuple-element.133.refs_0_, bf16[4,192,1536]{2,1,0:T(8,128)(2,1)} %get-tuple-element.134.refs_1_, bf16[4,192,1536]{2,1,0:T(8,128)(2,1)} %get-tuple-element.135.refs_2_, ...), custom_call_target="tpu_custom_call" | custom-call | flops 14495514624 | bytes 50331648 | tf_op jit(solution)/shard_map/pallas_call | solution.py:365
  545.7 11.4 %copy.538 = bf16[4,512,1536]{1,0,2:T(4,128)(2,1)} copy(bf16[4,512,1536]{2,1,0:T(8,128)(2,1)} %get-tuple-element.150) | data formatting | bytes 12582912
  557.1 8.2 copy.561
  570.3 16.4 %collective-permute-done.22 = bf16[256,1536]{1,0:T(8,128)(2,1)S(1)} collective-permute-done((bf16[256,1536]{1,0:T(8,128)(2,1)}, bf16[256,1536]{1,0:T(8,128)(2,1)S(1)}, u32[]{:S(2)}, u32[]{:S(2)}) %collective-permute-start.22) | collective-permute-done | bytes 786464 | tf_op jit(solution)/shard_map/ppermute | solution.py:68
  589.2 3.7 collective-permute-start.23
  592.8 10.7 collective-permute-done.16
  606.0 13.0 %collective-permute-done.10 = bf16[256,1536]{1,0:T(8,128)(2,1)S(1)} collective-permute-done((bf16[256,1536]{1,0:T(8,128)(2,1)}, bf16[256,1536]{1,0:T(8,128)(2,1)S(1)}, u32[]{:S(2)}, u32[]{:S(2)}) %collective-permute-start.10) | collective-permute-done | bytes 786464 | tf_op jit(solution)/shard_map/ppermute | solution.py:68
  621.3 25.1 %all_to_all.100 = f32[8,4,256]{2,1,0:T(4,128)S(1)} all-to-all(f32[8,4,256]{2,1,0:T(4,128)S(1)} %bitcast.334), channel_id=1, replica_groups=mesh['fsdp'=4,'ctx'=4,'tp'=2] {'fsdp','tp'}, dimensions={0} | all-to-all | bytes 65536 | tf_op jit(solution)/shard_map/all_to_all | solution.py:38
  653.7 4.1 fusion.14
  660.2 3.5 all-to-all-start.7
  663.9 20.1 %all-to-all-done.7 = bf16[8,256,192]{1,2,0:T(8,128)(2,1)S(1)} async-done(((bf16[8,256,192]{1,2,0:T(8,128)(2,1)}), bf16[8,256,192]{1,2,0:T(8,128)(2,1)S(1)}, u32[]{:S(2)}, u32[]{:S(2)}) %all-to-all-start.7) | async-done | bytes 786464 | tf_op jit(solution)/shard_map/all_to_all | solution.py:38
  684.0 4.3 all-to-all-start.9
  695.3 4.1 all-to-all-done.9
  701.2 3.7 all-to-all-start.11
  708.5 24.2 %shard_map.533 = (bf16[3,2048,64]{2,1,0:T(8,128)(2,1)S(1)}, f32[2048,128]{1,0:T(8,128)S(1)}, f32[2048,64]{1,0:T(8,128)S(1)}) custom-call(bf16[3,2048,128]{2,1,0:T(8,128)(2,1)S(1)} %copy-done.3, bf16[2048,128]{1,0:T(8,128)(2,1)S(1)} %copy-done.5, bf16[64,2048]{1,0:T(8,128)(2,1)S(1)} %copy.499.kt_ref, bf16[2048,64]{1,0:T(8,128)(2,1)S(1)} %copy-done.6, ...), custom_call_target="tpu_custom_call" | custom-call | flops 12884901888 | bytes 8388608 | tf_op jit(solution)/shard_map/pallas_call | solution.py:209
  733.9 5.9 convolution_convert_fusion.2
  742.3 6.0 all-to-all-start.13
  777.3 7.4 all-to-all-start.14
  787.1 3.6 collective-permute-start.30
  790.7 73.4 %all-to-all-done.14 = f32[32,1,1472]{2,1,0:T(1,128)S(1)} async-done(((f32[32,1,1472]{2,1,0:T(1,128)}), f32[32,1,1472]{2,1,0:T(1,128)S(1)}, u32[]{:S(2)}, u32[]{:S(2)}) %all-to-all-start.14) | async-done | bytes 188448 | tf_op jit(solution)/shard_map/all_to_all | solution.py:38
  865.9 4.7 all-to-all-start.8
  885.8 16.2 %all-to-all-done.8 = bf16[8,512,320]{1,2,0:T(8,128)(2,1)} async-done(((bf16[8,512,320]{1,2,0:T(8,128)(2,1)}), bf16[8,512,320]{1,2,0:T(8,128)(2,1)}, u32[]{:S(2)}, u32[]{:S(2)}) %all-to-all-start.8) | async-done | bytes 2621472 | tf_op jit(solution)/shard_map/all_to_all | solution.py:38
  902.0 5.6 all-to-all-start.10
  907.6 3.4 pad_maximum_fusion
  911.1 10.2 collective-permute-done.26
  930.6 3.4 copy.505
  934.1 10.3 fusion.5
  944.9 8.4 all-to-all-done.10
  959.6 14.3 %all-to-all-start.12 = ((f32[32,1,1031]{2,1,0:T(1,128)}), f32[32,1,1031]{2,1,0:T(1,128)}, u32[]{:S(2)}, u32[]{:S(2)}) async-start(f32[32,1,1031]{2,1,0:T(1,128)} %broadcast_in_dim.64), calls=%async_computation.12 | async-start | bytes 294912 | tf_op jit(solution)/shard_map/all_to_all | solution.py:38
  981.3 6.7 multiply_reduce_fusion.4
  990.5 6.1 all-to-all-start.15
  996.6 5.7 fusion.8
  1044.5 4.8 multiply_reduce_fusion.1
  1055.4 5.9 all-to-all-start.16
  1063.3 5.2 all-to-all-done.16
  1082.9 8.5 fusion.73
  1091.5 3.4 fusion.72
  (500 shorter events, 246.6 us)
Async XLA Ops:
  7.2 63.1 %copy-start = (s32[512,8]{0,1:T(8,128)S(1)}, s32[512,8]{0,1:T(8,128)}, u32[]{:S(2)}) copy-start(s32[512,8]{0,1:T(8,128)} %param.27) | copy-start | bytes 49156
  7.2 104.7 %all-gather.6.cloned.1.call-start = ((), (), s32[]{:S(2)}) async-start(), calls=%async_computation.20 | async-start | bytes 7864320 | tf_op jit(solution)/shard_map/all_gather | solution.py:532
  7.3 37.7 %collective-permute-start = (bf16[1,512,1536]{2,1,0:T(8,128)(2,1)}, bf16[1,512,1536]{2,1,0:T(8,128)(2,1)}, u32[]{:S(2)}, u32[]{:S(2)}) collective-permute-start(bf16[1,512,1536]{2,1,0:T(8,128)(2,1)} %bitcast.287), channel_id=1, source_target_pairs={{0,4},{2,6},{4,0},{6,2},{1,5},{3,7},{5,1},{7,3},{8,12},{10,14},{12... | collective-permute-start | bytes 4718600 | tf_op jit(solution)/shard_map/ppermute | solution.py:68
  45.0 362.1 %all-gather.4.cloned.1.call-start = ((), (), s32[]{:S(2)}) async-start(), calls=%async_computation.19 | async-start | bytes 15728640 | tf_op jit(solution)/shard_map/all_gather | solution.py:531
  59.1 53.7 %collective-permute-start.1 = (bf16[2,512,1536]{2,1,0:T(8,128)(2,1)}, bf16[2,512,1536]{2,1,0:T(8,128)(2,1)}, u32[]{:S(2)}, u32[]{:S(2)}) collective-permute-start(bf16[2,512,1536]{2,1,0:T(8,128)(2,1)} %maximum_bitcast_fusion.1), channel_id=1, source_target_pairs={{0,2},{2,0},{4,6},{6,4},{1,3},{3,1},{5,7},{7,5},{8,10},{10,8},{12,... | collective-permute-start | bytes 9437192 | tf_op jit(solution)/shard_map/ppermute | solution.py:68
  64.0 31.5 %all-to-all-start = ((bf16[16,96,354]{2,1,0:T(8,128)(2,1)}), bf16[16,96,354]{2,1,0:T(8,128)(2,1)S(1)}, u32[]{:S(2)}, u32[]{:S(2)}) async-start(bf16[16,96,354]{2,1,0:T(8,128)(2,1)} %bitcast.300), calls=%async_computation | async-start | bytes 2359296 | tf_op jit(solution)/shard_map/all_to_all | solution.py:38
  98.2 53.5 %all-to-all-start.2 = ((bf16[16,96,768]{2,1,0:T(8,128)(2,1)}), bf16[16,96,768]{2,1,0:T(8,128)(2,1)}, u32[]{:S(2)}, u32[]{:S(2)}) async-start(bf16[16,96,768]{2,1,0:T(8,128)(2,1)} %broadcast_in_dim.55), calls=%async_computation.2 | async-start | bytes 4718592 | tf_op jit(solution)/shard_map/all_to_all | solution.py:38
  105.8 828.3 %all-gather.8.cloned.1.call-start = ((), (), s32[]{:S(2)}) async-start(), calls=%async_computation.21 | async-start | bytes 8110080 | tf_op jit(solution)/shard_map/all_gather | solution.py:538
  139.0 27.4 %copy-start.26 = (bf16[2048,320]{1,0:T(8,128)(2,1)}, bf16[2048,320]{1,0:T(8,128)(2,1)S(1)}, u32[]{:S(2)}) copy-start(bf16[2048,320]{1,0:T(8,128)(2,1)S(1)} %convolution_convert_fusion.1) | copy-start | bytes 3932164
  152.4 48.1 %all-to-all-start.6 = ((f32[32,1,32]{2,1,0:T(1,128)}), f32[32,1,32]{2,1,0:T(1,128)S(1)}, u32[]{:S(2)}, u32[]{:S(2)}) async-start(f32[32,1,32]{2,1,0:T(1,128)} %broadcast_in_dim.59), calls=%async_computation.6 | async-start | bytes 32768 | tf_op jit(solution)/shard_map/all_to_all | solution.py:38
  164.6 64.3 %collective-permute-start.2 = (bf16[1,1536,768]{2,1,0:T(8,128)(2,1)}, bf16[1,1536,768]{2,1,0:T(8,128)(2,1)}, u32[]{:S(2)}, u32[]{:S(2)}) collective-permute-start(bf16[1,1536,768]{2,1,0:T(8,128)(2,1)} %bitcast.30), channel_id=1, source_target_pairs={{0,1},{1,0},{2,3},{3,2},{4,5},{5,4},{6,7},{7,6},{8,9},{9,8},{10,11... | collective-permute-start | bytes 7077896 | tf_op jit(solution)/shard_map/ppermute | solution.py:68
  173.3 25.2 %copy-start.2 = (bf16[3,2048,128]{2,1,0:T(8,128)(2,1)}, bf16[3,2048,128]{2,1,0:T(8,128)(2,1)S(1)}, u32[]{:S(2)}) copy-start(bf16[3,2048,128]{2,1,0:T(8,128)(2,1)S(1)} %maximum_bitcast_fusion.8.q_ref) | copy-start | bytes 4718596
  200.4 27.5 %all-to-all-start.1 = ((bf16[8,256,192]{1,2,0:T(8,128)(2,1)}), bf16[8,256,192]{1,2,0:T(8,128)(2,1)S(1)}, u32[]{:S(2)}, u32[]{:S(2)}) async-start(bf16[8,256,192]{1,2,0:T(8,128)(2,1)} %copy.484), calls=%async_computation.1 | async-start | bytes 1572864 | tf_op jit(solution)/shard_map/all_to_all | solution.py:38
  204.4 27.3 %copy-start.99 = (f32[32]{0:T(128)}, f32[32]{0:T(128)S(1)}, u32[]{:S(2)}) copy-start(f32[32]{0:T(128)S(1)} %reduce_sum.529) | copy-start | bytes 388
  204.4 149.7 %collective-permute-start.20 = (bf16[256,1536]{1,0:T(8,128)(2,1)}, bf16[256,1536]{1,0:T(8,128)(2,1)}, u32[]{:S(2)}, u32[]{:S(2)}) collective-permute-start(bf16[256,1536]{1,0:T(8,128)(2,1)} %refs_2_), channel_id=1, source_target_pairs={{0,24},{8,16},{16,8},{24,0},{1,25},{9,17},{17,9},{25,1},{2,26},{10... | collective-permute-start | bytes 2359304 | tf_op jit(solution)/shard_map/ppermute | solution.py:68
  207.9 151.6 %collective-permute-start.14 = (bf16[256,1536]{1,0:T(8,128)(2,1)}, bf16[256,1536]{1,0:T(8,128)(2,1)}, u32[]{:S(2)}, u32[]{:S(2)}) collective-permute-start(bf16[256,1536]{1,0:T(8,128)(2,1)} %refs_2_), channel_id=1, source_target_pairs={{0,16},{8,24},{16,0},{24,8},{1,17},{9,25},{17,1},{25,9},{2,18},{10... | collective-permute-start | bytes 2359304 | tf_op jit(solution)/shard_map/ppermute | solution.py:68
  235.1 415.8 %copy-start.8 = (f32[256,1536]{1,0:T(8,128)}, f32[256,1536]{1,0:T(8,128)S(1)}, u32[]{:S(2)}) copy-start(f32[256,1536]{1,0:T(8,128)S(1)} %get-tuple-element.594) | copy-start | bytes 4718596
  236.4 123.3 %collective-permute-start.18 = (bf16[256,1536]{1,0:T(8,128)(2,1)}, bf16[256,1536]{1,0:T(8,128)(2,1)}, u32[]{:S(2)}, u32[]{:S(2)}) collective-permute-start(bf16[256,1536]{1,0:T(8,128)(2,1)} %multiply_convert_fusion.refs_0_), channel_id=1, source_target_pairs={{0,24},{8,16},{16,8},{24,0},{1,25},{9,17},{17,9},{25,1},{2,26},{10... | collective-permute-start | bytes 2359304 | tf_op jit(solution)/shard_map/ppermute | solution.py:68
  242.5 105.9 %all-to-all-start.3 = ((f32[8,4,256]{2,1,0:T(4,128)}), f32[8,4,256]{2,1,0:T(4,128)S(1)}, u32[]{:S(2)}, u32[]{:S(2)}) async-start(f32[8,4,256]{2,1,0:T(4,128)} %reshape.511), calls=%async_computation.3 | async-start | bytes 65536 | tf_op jit(solution)/shard_map/all_to_all | solution.py:38
  348.4 10.7 all-to-all-start.4
  352.1 621.8 %reduce-scatter.7.cloned.1.call-start = ((), (), s32[]{:S(2)}) async-start(), calls=%async_computation.23 | async-start | bytes 7864320
  352.2 37.5 %collective-permute-start.8 = (bf16[256,1536]{1,0:T(8,128)(2,1)}, bf16[256,1536]{1,0:T(8,128)(2,1)}, u32[]{:S(2)}, u32[]{:S(2)}) collective-permute-start(bf16[256,1536]{1,0:T(8,128)(2,1)} %refs_2_), channel_id=1, source_target_pairs={{0,8},{8,0},{16,24},{24,16},{1,9},{9,1},{17,25},{25,17},{2,10},{10... | collective-permute-start | bytes 2359304 | tf_op jit(solution)/shard_map/ppermute | solution.py:68
  354.2 38.5 %collective-permute-start.21 = (bf16[256,1536]{1,0:T(8,128)(2,1)}, bf16[256,1536]{1,0:T(8,128)(2,1)}, u32[]{:S(2)}, u32[]{:S(2)}) collective-permute-start(bf16[256,1536]{1,0:T(8,128)(2,1)} %collective-permute-done.20.refs_2_), channel_id=1, source_target_pairs={{0,1},{1,0},{2,3},{3,2},{4,5},{5,4},{6,7},{7,6},{8,9},{9,8},{10,11... | collective-permute-start | bytes 2359304 | tf_op jit(solution)/shard_map/ppermute | solution.py:68
  355.6 36.4 %collective-permute-start.12 = (bf16[256,1536]{1,0:T(8,128)(2,1)}, bf16[256,1536]{1,0:T(8,128)(2,1)}, u32[]{:S(2)}, u32[]{:S(2)}) collective-permute-start(bf16[256,1536]{1,0:T(8,128)(2,1)} %multiply_convert_fusion.refs_0_), channel_id=1, source_target_pairs={{0,16},{8,24},{16,0},{24,8},{1,17},{9,25},{17,1},{25,9},{2,18},{10... | collective-permute-start | bytes 2359304 | tf_op jit(solution)/shard_map/ppermute | solution.py:68
  359.4 45.7 %collective-permute-start.6 = (bf16[256,1536]{1,0:T(8,128)(2,1)}, bf16[256,1536]{1,0:T(8,128)(2,1)}, u32[]{:S(2)}, u32[]{:S(2)}) collective-permute-start(bf16[256,1536]{1,0:T(8,128)(2,1)} %multiply_convert_fusion.refs_0_), channel_id=1, source_target_pairs={{0,8},{8,0},{16,24},{24,16},{1,9},{9,1},{17,25},{25,17},{2,10},{10... | collective-permute-start | bytes 2359304 | tf_op jit(solution)/shard_map/ppermute | solution.py:68
  359.7 47.0 %collective-permute-start.19 = (bf16[256,1536]{1,0:T(8,128)(2,1)}, bf16[256,1536]{1,0:T(8,128)(2,1)}, u32[]{:S(2)}, u32[]{:S(2)}) collective-permute-start(bf16[256,1536]{1,0:T(8,128)(2,1)} %collective-permute-done.18.refs_0_), channel_id=1, source_target_pairs={{0,1},{1,0},{2,3},{3,2},{4,5},{5,4},{6,7},{7,6},{8,9},{9,8},{10,11... | collective-permute-start | bytes 2359304 | tf_op jit(solution)/shard_map/ppermute | solution.py:68
  389.7 40.7 %collective-permute-start.15 = (bf16[256,1536]{1,0:T(8,128)(2,1)}, bf16[256,1536]{1,0:T(8,128)(2,1)}, u32[]{:S(2)}, u32[]{:S(2)}) collective-permute-start(bf16[256,1536]{1,0:T(8,128)(2,1)} %collective-permute-done.14.refs_2_), channel_id=1, source_target_pairs={{0,1},{1,0},{2,3},{3,2},{4,5},{5,4},{6,7},{7,6},{8,9},{9,8},{10,11... | collective-permute-start | bytes 2359304 | tf_op jit(solution)/shard_map/ppermute | solution.py:68
  392.0 40.0 %collective-permute-start.13 = (bf16[256,1536]{1,0:T(8,128)(2,1)}, bf16[256,1536]{1,0:T(8,128)(2,1)}, u32[]{:S(2)}, u32[]{:S(2)}) collective-permute-start(bf16[256,1536]{1,0:T(8,128)(2,1)} %collective-permute-done.12.refs_0_), channel_id=1, source_target_pairs={{0,1},{1,0},{2,3},{3,2},{4,5},{5,4},{6,7},{7,6},{8,9},{9,8},{10,11... | collective-permute-start | bytes 2359304 | tf_op jit(solution)/shard_map/ppermute | solution.py:68
  392.6 109.0 %collective-permute-start.4 = (bf16[256,1536]{1,0:T(8,128)(2,1)}, bf16[256,1536]{1,0:T(8,128)(2,1)}, u32[]{:S(2)}, u32[]{:S(2)}) collective-permute-start(bf16[256,1536]{1,0:T(8,128)(2,1)} %refs_2_), channel_id=1, source_target_pairs={{0,1},{1,0},{2,3},{3,2},{4,5},{5,4},{6,7},{7,6},{8,9},{9,8},{10,11... | collective-permute-start | bytes 2359304 | tf_op jit(solution)/shard_map/ppermute | solution.py:68
  405.1 56.2 %collective-permute-start.9 = (bf16[256,1536]{1,0:T(8,128)(2,1)}, bf16[256,1536]{1,0:T(8,128)(2,1)}, u32[]{:S(2)}, u32[]{:S(2)}) collective-permute-start(bf16[256,1536]{1,0:T(8,128)(2,1)} %collective-permute-done.8.refs_2_), channel_id=1, source_target_pairs={{0,1},{1,0},{2,3},{3,2},{4,5},{5,4},{6,7},{7,6},{8,9},{9,8},{10,11... | collective-permute-start | bytes 2359304 | tf_op jit(solution)/shard_map/ppermute | solution.py:68
  406.7 71.5 %collective-permute-start.7 = (bf16[256,1536]{1,0:T(8,128)(2,1)}, bf16[256,1536]{1,0:T(8,128)(2,1)}, u32[]{:S(2)}, u32[]{:S(2)}) collective-permute-start(bf16[256,1536]{1,0:T(8,128)(2,1)} %collective-permute-done.6.refs_0_), channel_id=1, source_target_pairs={{0,1},{1,0},{2,3},{3,2},{4,5},{5,4},{6,7},{7,6},{8,9},{9,8},{10,11... | collective-permute-start | bytes 2359304 | tf_op jit(solution)/shard_map/ppermute | solution.py:68
  430.4 71.3 %collective-permute-start.3 = (bf16[256,1536]{1,0:T(8,128)(2,1)}, bf16[256,1536]{1,0:T(8,128)(2,1)S(1)}, u32[]{:S(2)}, u32[]{:S(2)}) collective-permute-start(bf16[256,1536]{1,0:T(8,128)(2,1)} %multiply_convert_fusion.refs_0_), channel_id=1, source_target_pairs={{0,1},{1,0},{2,3},{3,2},{4,5},{5,4},{6,7},{7,6},{8,9},{9,8},{10,11... | collective-permute-start | bytes 2359304 | tf_op jit(solution)/shard_map/ppermute | solution.py:68
  565.4 415.9 %reduce-scatter.5.cloned.1.call-start = ((), (), s32[]{:S(2)}) async-start(), calls=%async_computation.22 | async-start | bytes 15728640 | tf_op jit(solution)/shard_map/reduce_scatter | solution.py:624
  565.9 37.6 %copy-start.47 = (bf16[256,1536]{1,0:T(8,128)(2,1)S(1)}, bf16[256,1536]{1,0:T(8,128)(2,1)}, u32[]{:S(2)}) copy-start(bf16[256,1536]{1,0:T(8,128)(2,1)} %get-tuple-element.104) | copy-start | bytes 2359300
  566.0 20.8 %collective-permute-start.22 = (bf16[256,1536]{1,0:T(8,128)(2,1)}, bf16[256,1536]{1,0:T(8,128)(2,1)S(1)}, u32[]{:S(2)}, u32[]{:S(2)}) collective-permute-start(bf16[256,1536]{1,0:T(8,128)(2,1)} %get-tuple-element.107), channel_id=1, source_target_pairs={{0,1},{1,0},{2,3},{3,2},{4,5},{5,4},{6,7},{7,6},{8,9},{9,8},{10,11... | collective-permute-start | bytes 2359304 | tf_op jit(solution)/shard_map/ppermute | solution.py:68
  568.0 35.5 %collective-permute-start.16 = (bf16[256,1536]{1,0:T(8,128)(2,1)}, bf16[256,1536]{1,0:T(8,128)(2,1)S(1)}, u32[]{:S(2)}, u32[]{:S(2)}) collective-permute-start(bf16[256,1536]{1,0:T(8,128)(2,1)} %get-tuple-element.105), channel_id=1, source_target_pairs={{0,1},{1,0},{2,3},{3,2},{4,5},{5,4},{6,7},{7,6},{8,9},{9,8},{10,11... | collective-permute-start | bytes 2359304 | tf_op jit(solution)/shard_map/ppermute | solution.py:68
  568.2 50.7 %collective-permute-start.10 = (bf16[256,1536]{1,0:T(8,128)(2,1)}, bf16[256,1536]{1,0:T(8,128)(2,1)S(1)}, u32[]{:S(2)}, u32[]{:S(2)}) collective-permute-start(bf16[256,1536]{1,0:T(8,128)(2,1)} %get-tuple-element.103), channel_id=1, source_target_pairs={{0,1},{1,0},{2,3},{3,2},{4,5},{5,4},{6,7},{7,6},{8,9},{9,8},{10,11... | collective-permute-start | bytes 2359304 | tf_op jit(solution)/shard_map/ppermute | solution.py:68
  570.2 77.8 %collective-permute-start.5 = (bf16[256,1536]{1,0:T(8,128)(2,1)}, bf16[256,1536]{1,0:T(8,128)(2,1)}, u32[]{:S(2)}, u32[]{:S(2)}) collective-permute-start(bf16[256,1536]{1,0:T(8,128)(2,1)} %get-tuple-element.101), channel_id=1, source_target_pairs={{0,1},{1,0},{2,3},{3,2},{4,5},{5,4},{6,7},{7,6},{8,9},{9,8},{10,11... | collective-permute-start | bytes 2359304 | tf_op jit(solution)/shard_map/ppermute | solution.py:68
  586.7 32.2 %copy-start.48 = (bf16[256,1536]{1,0:T(8,128)(2,1)S(1)}, bf16[256,1536]{1,0:T(8,128)(2,1)}, u32[]{:S(2)}) copy-start(bf16[256,1536]{1,0:T(8,128)(2,1)} %get-tuple-element.102) | copy-start | bytes 2359300
  589.2 58.8 %collective-permute-start.23 = (bf16[256,1536]{1,0:T(8,128)(2,1)}, bf16[256,1536]{1,0:T(8,128)(2,1)}, u32[]{:S(2)}, u32[]{:S(2)}) collective-permute-start(bf16[256,1536]{1,0:T(8,128)(2,1)} %add_convert_fusion.4), channel_id=1, source_target_pairs={{0,24},{8,16},{16,8},{24,0},{1,25},{9,17},{17,9},{25,1},{2,26},{10... | collective-permute-start | bytes 2359304 | tf_op jit(solution)/shard_map/ppermute | solution.py:68
  604.6 43.4 %collective-permute-start.17 = (bf16[256,1536]{1,0:T(8,128)(2,1)}, bf16[256,1536]{1,0:T(8,128)(2,1)}, u32[]{:S(2)}, u32[]{:S(2)}) collective-permute-start(bf16[256,1536]{1,0:T(8,128)(2,1)} %add_convert_fusion.5), channel_id=1, source_target_pairs={{0,16},{8,24},{16,0},{24,8},{1,17},{9,25},{17,1},{25,9},{2,18},{10... | collective-permute-start | bytes 2359304 | tf_op jit(solution)/shard_map/ppermute | solution.py:68
  620.0 28.1 %collective-permute-start.11 = (bf16[256,1536]{1,0:T(8,128)(2,1)}, bf16[256,1536]{1,0:T(8,128)(2,1)}, u32[]{:S(2)}, u32[]{:S(2)}) collective-permute-start(bf16[256,1536]{1,0:T(8,128)(2,1)} %add_convert_fusion.6), channel_id=1, source_target_pairs={{0,8},{8,0},{16,24},{24,16},{1,9},{9,1},{17,25},{25,17},{2,10},{10... | collective-permute-start | bytes 2359304 | tf_op jit(solution)/shard_map/ppermute | solution.py:68
  660.2 23.9 %all-to-all-start.7 = ((bf16[8,256,192]{1,2,0:T(8,128)(2,1)}), bf16[8,256,192]{1,2,0:T(8,128)(2,1)S(1)}, u32[]{:S(2)}, u32[]{:S(2)}) async-start(bf16[8,256,192]{1,2,0:T(8,128)(2,1)} %bitcast.68), calls=%async_computation.7 | async-start | bytes 1572864 | tf_op jit(solution)/shard_map/all_to_all | solution.py:38
  684.0 15.3 %all-to-all-start.9 = ((bf16[2,256,768]{1,2,0:T(8,128)(2,1)}), bf16[2,256,768]{1,2,0:T(8,128)(2,1)}, u32[]{:S(2)}, u32[]{:S(2)}) async-start(bf16[2,256,768]{1,2,0:T(8,128)(2,1)} %bitcast.89), calls=%async_computation.9 | async-start | bytes 1572864 | tf_op jit(solution)/shard_map/all_to_all | solution.py:38
  701.2 41.1 %all-to-all-start.11 = ((f32[32,33,96]{2,1,0:T(8,128)}), f32[32,33,96]{2,1,0:T(8,128)}, u32[]{:S(2)}, u32[]{:S(2)}) async-start(f32[32,33,96]{2,1,0:T(8,128)} %bitcast.94), calls=%async_computation.11 | async-start | bytes 1310720 | tf_op jit(solution)/shard_map/all_to_all | solution.py:38
  742.3 31.2 %all-to-all-start.13 = ((bf16[16,96,320]{2,1,0:T(8,128)(2,1)}), bf16[16,96,320]{2,1,0:T(8,128)(2,1)S(1)}, u32[]{:S(2)}, u32[]{:S(2)}) async-start(bf16[16,96,320]{2,1,0:T(8,128)(2,1)} %bitcast.104), calls=%async_computation.13 | async-start | bytes 2359296 | tf_op jit(solution)/shard_map/all_to_all | solution.py:38
  757.7 27.0 %collective-permute-start.29 = (bf16[256,1536]{1,0:T(8,128)(2,1)}, bf16[256,1536]{1,0:T(8,128)(2,1)}, u32[]{:S(2)}, u32[]{:S(2)}) collective-permute-start(bf16[256,1536]{1,0:T(8,128)(2,1)} %get-tuple-element.126), channel_id=1, source_target_pairs={{0,1},{1,0},{2,3},{3,2},{4,5},{5,4},{6,7},{7,6},{8,9},{9,8},{10,11... | collective-permute-start | bytes 2359304 | tf_op jit(solution)/shard_map/ppermute | solution.py:68
  759.2 111.5 %collective-permute-start.27 = (bf16[256,1536]{1,0:T(8,128)(2,1)}, bf16[256,1536]{1,0:T(8,128)(2,1)}, u32[]{:S(2)}, u32[]{:S(2)}) collective-permute-start(bf16[256,1536]{1,0:T(8,128)(2,1)} %get-tuple-element.122), channel_id=1, source_target_pairs={{0,1},{1,0},{2,3},{3,2},{4,5},{5,4},{6,7},{7,6},{8,9},{9,8},{10,11... | collective-permute-start | bytes 2359304 | tf_op jit(solution)/shard_map/ppermute | solution.py:68
  759.7 115.8 %collective-permute-start.25 = (bf16[256,1536]{1,0:T(8,128)(2,1)}, bf16[256,1536]{1,0:T(8,128)(2,1)}, u32[]{:S(2)}, u32[]{:S(2)}) collective-permute-start(bf16[256,1536]{1,0:T(8,128)(2,1)} %get-tuple-element.118), channel_id=1, source_target_pairs={{0,1},{1,0},{2,3},{3,2},{4,5},{5,4},{6,7},{7,6},{8,9},{9,8},{10,11... | collective-permute-start | bytes 2359304 | tf_op jit(solution)/shard_map/ppermute | solution.py:68
  761.2 149.9 %collective-permute-start.24 = (bf16[256,1536]{1,0:T(8,128)(2,1)}, bf16[256,1536]{1,0:T(8,128)(2,1)}, u32[]{:S(2)}, u32[]{:S(2)}) collective-permute-start(bf16[256,1536]{1,0:T(8,128)(2,1)} %get-tuple-element.114), channel_id=1, source_target_pairs={{0,1},{1,0},{2,3},{3,2},{4,5},{5,4},{6,7},{7,6},{8,9},{9,8},{10,11... | collective-permute-start | bytes 2359304 | tf_op jit(solution)/shard_map/ppermute | solution.py:68
  767.5 111.7 %collective-permute-start.31 = (f32[1,256,1536]{2,1,0:T(8,128)}, f32[1,256,1536]{2,1,0:T(8,128)}, u32[]{:S(2)}, u32[]{:S(2)}) collective-permute-start(f32[1,256,1536]{2,1,0:T(8,128)} %bitcast.69), channel_id=1, source_target_pairs={{0,1},{1,0},{2,3},{3,2},{4,5},{5,4},{6,7},{7,6},{8,9},{9,8},{10,11... | collective-permute-start | bytes 4718600 | tf_op jit(solution)/shard_map/ppermute | solution.py:68
  775.0 89.1 %copy-start.21 = (bf16[4,512,320]{1,2,0:T(8,128)(2,1)S(1)}, bf16[4,512,320]{1,2,0:T(8,128)(2,1)}, u32[]{:S(2)}) copy-start(bf16[4,512,320]{1,2,0:T(8,128)(2,1)} %copy.504) | copy-start | bytes 3932164
  777.3 86.9 %all-to-all-start.14 = ((f32[32,1,1472]{2,1,0:T(1,128)}), f32[32,1,1472]{2,1,0:T(1,128)S(1)}, u32[]{:S(2)}, u32[]{:S(2)}) async-start(f32[32,1,1472]{2,1,0:T(1,128)} %broadcast_in_dim.65), calls=%async_computation.15 | async-start | bytes 393216 | tf_op jit(solution)/shard_map/all_to_all | solution.py:38
  787.1 124.0 %collective-permute-start.30 = (bf16[256,1536]{1,0:T(8,128)(2,1)}, bf16[256,1536]{1,0:T(8,128)(2,1)}, u32[]{:S(2)}, u32[]{:S(2)}) collective-permute-start(bf16[256,1536]{1,0:T(8,128)(2,1)} %add_convert_fusion.1), channel_id=1, source_target_pairs={{0,24},{8,16},{16,8},{24,0},{1,25},{9,17},{17,9},{25,1},{2,26},{10... | collective-permute-start | bytes 2359304 | tf_op jit(solution)/shard_map/ppermute | solution.py:68
  865.9 36.1 %all-to-all-start.8 = ((bf16[8,512,320]{1,2,0:T(8,128)(2,1)}), bf16[8,512,320]{1,2,0:T(8,128)(2,1)}, u32[]{:S(2)}, u32[]{:S(2)}) async-start(bf16[8,512,320]{1,2,0:T(8,128)(2,1)} %bitcast.288), calls=%async_computation.8 | async-start | bytes 5242880 | tf_op jit(solution)/shard_map/all_to_all | solution.py:38
  872.9 38.2 %collective-permute-start.28 = (bf16[256,1536]{1,0:T(8,128)(2,1)}, bf16[256,1536]{1,0:T(8,128)(2,1)}, u32[]{:S(2)}, u32[]{:S(2)}) collective-permute-start(bf16[256,1536]{1,0:T(8,128)(2,1)} %add_convert_fusion.2), channel_id=1, source_target_pairs={{0,16},{8,24},{16,0},{24,8},{1,17},{9,25},{17,1},{25,9},{2,18},{10... | collective-permute-start | bytes 2359304 | tf_op jit(solution)/shard_map/ppermute | solution.py:68
  877.7 43.7 %collective-permute-start.26 = (bf16[256,1536]{1,0:T(8,128)(2,1)}, bf16[256,1536]{1,0:T(8,128)(2,1)}, u32[]{:S(2)}, u32[]{:S(2)}) collective-permute-start(bf16[256,1536]{1,0:T(8,128)(2,1)} %add_convert_fusion.3), channel_id=1, source_target_pairs={{0,8},{8,0},{16,24},{24,16},{1,9},{9,1},{17,25},{25,17},{2,10},{10... | collective-permute-start | bytes 2359304 | tf_op jit(solution)/shard_map/ppermute | solution.py:68
  902.0 51.3 %all-to-all-start.10 = ((bf16[16,96,768]{2,1,0:T(8,128)(2,1)}), bf16[16,96,768]{2,1,0:T(8,128)(2,1)}, u32[]{:S(2)}, u32[]{:S(2)}) async-start(bf16[16,96,768]{2,1,0:T(8,128)(2,1)} %bitcast.312), calls=%async_computation.10 | async-start | bytes 4718592 | tf_op jit(solution)/shard_map/all_to_all | solution.py:38
  911.1 18.6 %copy-start.33 = (f32[96,4,64]{0,2,1:T(8,128)S(1)}, f32[96,4,64]{0,2,1:T(8,128)}, u32[]{:S(2)}) copy-start(f32[96,4,64]{0,2,1:T(8,128)} %copy-done.32) | copy-start | bytes 294916
  959.6 29.0 %all-to-all-start.12 = ((f32[32,1,1031]{2,1,0:T(1,128)}), f32[32,1,1031]{2,1,0:T(1,128)}, u32[]{:S(2)}, u32[]{:S(2)}) async-start(f32[32,1,1031]{2,1,0:T(1,128)} %broadcast_in_dim.64), calls=%async_computation.12 | async-start | bytes 294912 | tf_op jit(solution)/shard_map/all_to_all | solution.py:38
  981.2 110.2 %copy-start.7 = (f32[4,512,384]{2,1,0:T(8,128)}, f32[4,512,384]{2,1,0:T(8,128)S(1)}, u32[]{:S(2)}) copy-start(f32[4,512,384]{2,1,0:T(8,128)S(1)} %get-tuple-element.535) | copy-start | bytes 9437188
  990.5 40.6 %all-to-all-start.15 = ((f32[32,4,2304]{2,1,0:T(4,128)}), f32[32,4,2304]{2,1,0:T(4,128)}, u32[]{:S(2)}, u32[]{:S(2)}) async-start(f32[32,4,2304]{2,1,0:T(4,128)} %broadcast_in_dim.66), calls=%async_computation.16 | async-start | bytes 2359296 | tf_op jit(solution)/shard_map/all_to_all | solution.py:38
  996.6 29.3 %copy-start.52 = (f32[96,32]{0,1:T(8,128)S(1)}, f32[96,32]{0,1:T(8,128)}, u32[]{:S(2)}) copy-start(f32[96,32]{0,1:T(8,128)} %get-tuple-element.542) | copy-start | bytes 36868
  1055.4 13.0 %all-to-all-start.16 = ((f32[32,1,7]{2,1,0:T(1,128)}), f32[32,1,7]{2,1,0:T(1,128)}, u32[]{:S(2)}, u32[]{:S(2)}) async-start(f32[32,1,7]{2,1,0:T(1,128)} %broadcast_in_dim.67), calls=%async_computation.17 | async-start | bytes 32768 | tf_op jit(solution)/shard_map/all_to_all | solution.py:38
  (93 other events, 515.8 us)
Sparse Core Ops, SparseCore 0:
  45.1 60.4 all-gather.5
  107.7 96.7 all-gather.3
  208.0 130.5 all-gather.7
  565.5 58.7 reduce-scatter.6
  626.9 114.4 reduce-scatter.4

commit v3 on v2

v3 whole, which is shorter than its diff:
```python
import functools

import jax
import jax.numpy as jnp
from jax import lax
from jax.experimental import pallas as pl
from jax.experimental.pallas import tpu as pltpu
from jax.sharding import PartitionSpec as P

D = 1536
HEADS = 24
KV_HEADS = 8
HEAD = 64
FFE = 512
TOPK = 8
EXPERTS = 32
NSEG = 13

norm_eps = 1e-05
decay = 0.5
floor_sq = 1e-30
rate = 0.25
clip_rms = 0.05
aux_weight = 1.0
bf16 = jnp.bfloat16
f32 = jnp.float32
EVERY = ("fsdp", "ctx", "tp")
EXTRA = 128

def lasting(microseconds):
    flops = int(microseconds * 1.15e9)
    return pl.CostEstimate(flops=flops, bytes_accessed=1, transcendentals=0)
NT = (((1,), (1,)), ((), ()))
NN = (((1,), (0,)), ((), ()))
TN = (((0,), (0,)), ((), ()))


def dot(spec, left, right):
    return jnp.einsum(spec, left, right, preferred_element_type=f32)


def exchange(values, axes):
    return lax.all_to_all(values, axes, split_axis=0, concat_axis=0, tiled=True)


def share(vector, count):
    return exchange(jnp.broadcast_to(vector[None], (count,) + vector.shape), EVERY)


def inv_rms(values):
    return lax.rsqrt(jnp.mean(values * values, axis=-1, keepdims=True) + norm_eps)


def norm_backward(values, inv, gain, d_out):
    normed = values * inv
    scaled = d_out * gain
    d_values = inv * (scaled - normed * jnp.mean(scaled * normed, axis=-1, keepdims=True))
    return d_values, normed


def ancestry(parent_row):
    seg_labels = jnp.arange(NSEG, dtype=jnp.int32)
    table = jnp.maximum(
        (seg_labels[:, None] == seg_labels[None, :]).astype(f32),
        (parent_row[:, None] == seg_labels[None, :]).astype(f32),
    )
    for sweep in range(NSEG.bit_length()):
        table = jnp.max(table[:, :, None] * table[None, :, :], axis=1)
    return table


def partner(values, axis, bits, count):
    return lax.ppermute(values, axis, [(i, i ^ bits) for i in range(count)])


def after(values, *others):
    return lax.optimization_barrier((values,) + others)[0]


def in_order(mine, other, bit, axis):
    first = jnp.where(bit == 0, mine, other)
    second = jnp.where(bit == 0, other, mine)
    return jnp.stack([first, second], axis=axis)


def mm(left, right, dims):
    return lax.dot_general(left, right, dims, preferred_element_type=f32)


def project_kernel(
    count, index_ref, *refs
):
    block_refs = refs[:count]
    w_ref, gain_ref, barred_ref, seg_ref = refs[count : count + 4]
    act_ref, q_ref, k_ref, kt_ref, v_ref, vt_ref = refs[count + 4 :]
    heads = q_ref.shape[0]
    place = pl.program_id(0) // (pl.num_programs(0) // count) ^ index_ref[0]
    block = block_refs[0][...]
    for j in range(1, count):
        block = jnp.where(place == j, block_refs[j][...], block)
    block = block.astype(f32)
    inv = lax.rsqrt(jnp.mean(block * block, axis=-1, keepdims=True) + norm_eps)
    act = (block * inv * gain_ref[...]).astype(bf16)
    act_ref[...] = act
    qkv = mm(act, w_ref[...], NN).astype(bf16).astype(f32)
    barred = barred_ref[...].astype(f32)
    for h in range(heads):
        query = qkv[:, h * HEAD : (h + 1) * HEAD] * HEAD ** (-0.5)
        q_ref[h] = jnp.concatenate([query, barred], axis=1).astype(bf16)
    key = qkv[:, heads * HEAD : (heads + 1) * HEAD]
    value = qkv[:, (heads + 1) * HEAD : (heads + 2) * HEAD]
    k_ref[...] = jnp.concatenate([key, seg_ref[...].astype(f32)], axis=1).astype(bf16)
    kt_ref[...] = key.T.astype(bf16)
    v_ref[...] = value.astype(bf16)
    vt_ref[...] = value.T.astype(bf16)


def project(blocks, index, weights, gain, barred, seg_hot, heads, rows):
    count = len(blocks)
    tok_rows, width = blocks[0].shape
    per = tok_rows // rows
    length = count * tok_rows
    wide = 2 * HEAD

    def place(j):
        def at(i, s):
            return (jnp.where((i // per ^ s[0]) == j, i % per, 0), 0)

        return at

    whole = lambda a: pl.BlockSpec(a.shape, lambda i, s: (0,) * a.ndim)
    by_rows = lambda columns: pl.BlockSpec((rows, columns), lambda i, s: (i, 0))
    return pl.pallas_call(
        functools.partial(project_kernel, count),
        out_shape=(
            jax.ShapeDtypeStruct((length, width), bf16),
            jax.ShapeDtypeStruct((heads, length, wide), bf16),
            jax.ShapeDtypeStruct((length, wide), bf16),
            jax.ShapeDtypeStruct((HEAD, length), bf16),
            jax.ShapeDtypeStruct((length, HEAD), bf16),
            jax.ShapeDtypeStruct((HEAD, length), bf16),
        ),
        grid_spec=pltpu.PrefetchScalarGridSpec(
            num_scalar_prefetch=1,
            grid=(length // rows,),
            in_specs=[pl.BlockSpec((rows, width), place(j)) for j in range(count)]
            + [whole(weights), whole(gain), by_rows(HEAD), by_rows(HEAD)],
            out_specs=(
                by_rows(width),
                pl.BlockSpec((heads, rows, wide), lambda i, s: (0, i, 0)),
                by_rows(wide),
                pl.BlockSpec((HEAD, rows), lambda i, s: (0, i)),
                by_rows(HEAD),
                pl.BlockSpec((HEAD, rows), lambda i, s: (0, i)),
            ),
        ),
        compiler_params=pltpu.CompilerParams(vmem_limit_bytes=40 * 2**20),
        cost_estimate=lasting(3.3),
    )(index, *blocks, weights, gain, barred, seg_hot)


def forward_kernel(q_ref, k_ref, vt_ref, out_ref, log_ref, acc_ref, top_ref, sum_ref):
    step = pl.program_id(0)
    heads, rows, wide = q_ref.shape
    query = q_ref[...].reshape(heads * rows, wide)
    acc_ref[...] = jnp.zeros_like(acc_ref)
    top_ref[...] = jnp.full(top_ref.shape, -3e38, f32)
    sum_ref[...] = jnp.zeros_like(sum_ref)

    def chunk(j, diagonal):
        at = pl.ds(pl.multiple_of(j * rows, rows), rows)
        scores = mm(k_ref[at, :], query, NT)
        if diagonal:
            key_at = lax.broadcasted_iota(jnp.int32, (rows, rows), 0)
            query_at = lax.broadcasted_iota(jnp.int32, (rows, rows), 1)
            later = jnp.where(key_at > query_at, -1e30, 0.0)
            scores = scores + jnp.concatenate([later] * heads, axis=1)
        top_old = top_ref[...]
        top = jnp.maximum(top_old, jnp.max(scores, axis=0, keepdims=True))
        probs = jnp.exp(scores - top)
        shrink = jnp.exp(top_old - top)
        sum_ref[...] = sum_ref[...] * shrink + jnp.sum(probs, axis=0, keepdims=True)
        acc_ref[...] = acc_ref[...] * shrink + mm(vt_ref[:, at], probs.astype(bf16), NN)
        top_ref[...] = top

    chunk(step, True)

    @pl.loop(0, step)
    def _(j):
        chunk(j, False)

    total = sum_ref[...]
    log_ref[...] = (top_ref[...] + jnp.log(total))[None]
    out = acc_ref[...] / total
    for h in range(heads):
        out_ref[0, h * HEAD : (h + 1) * HEAD, :] = out[:, h * rows : (h + 1) * rows].astype(bf16)


def attention_forward(query, key, value_t, rows):
    heads, length, wide = query.shape
    steps = length // rows
    return pl.pallas_call(
        forward_kernel,
        out_shape=(
            jax.ShapeDtypeStruct((steps, heads * HEAD, rows), bf16),
            jax.ShapeDtypeStruct((steps, 1, heads * rows), f32),
        ),
        grid=(steps,),
        in_specs=[
            pl.BlockSpec((heads, rows, wide), lambda i: (0, i, 0)),
            pl.BlockSpec((length, wide), lambda i: (0, 0)),
            pl.BlockSpec((HEAD, length), lambda i: (0, 0)),
        ],
        out_specs=(
            pl.BlockSpec((1, heads * HEAD, rows), lambda i: (i, 0, 0)),
            pl.BlockSpec((1, 1, heads * rows), lambda i: (i, 0, 0)),
        ),
        scratch_shapes=[
            pltpu.VMEM((HEAD, heads * rows), f32),
            pltpu.VMEM((1, heads * rows), f32),
            pltpu.VMEM((1, heads * rows), f32),
        ],
        compiler_params=pltpu.CompilerParams(vmem_limit_bytes=40 * 2**20),
        cost_estimate=lasting(7.5),
    )(query, key, value_t)


def backward_kernel(
    q_ref, k_ref, kt_ref, v_ref, do_ref, out_ref, log_ref, dq_ref, dkv_ref, acc_ref, dk_ref, dv_ref
):
    step = pl.program_id(0)
    heads, rows, wide = q_ref.shape
    query = q_ref[...].reshape(heads * rows, wide)
    side_by_side = lambda a: jnp.concatenate(
        [a[h * HEAD : (h + 1) * HEAD] for h in range(heads)], axis=1
    )
    d_out = side_by_side(do_ref[0])
    products = side_by_side(do_ref[0].astype(f32) * out_ref[0].astype(f32))
    delta = jnp.sum(products, axis=0, keepdims=True)
    logs = log_ref[0]

    @pl.when(step == 0)
    def _():
        dk_ref[...] = jnp.zeros_like(dk_ref)
        dv_ref[...] = jnp.zeros_like(dv_ref)

    acc_ref[...] = jnp.zeros_like(acc_ref)

    def chunk(j, diagonal):
        at = pl.ds(pl.multiple_of(j * rows, rows), rows)
        scores = mm(k_ref[at, :], query, NT)
        if diagonal:
            key_at = lax.broadcasted_iota(jnp.int32, (rows, rows), 0)
            query_at = lax.broadcasted_iota(jnp.int32, (rows, rows), 1)
            later = jnp.where(key_at > query_at, -1e30, 0.0)
            scores = scores + jnp.concatenate([later] * heads, axis=1)
        probs = jnp.exp(scores - logs)
        d_probs = mm(v_ref[at, :], d_out, NN)
        d_scores = (probs * (d_probs - delta)).astype(bf16)
        dv_ref[at, :] += mm(probs.astype(bf16), d_out, NT)
        dk_ref[at, :] += mm(d_scores, query, NN)
        acc_ref[...] += mm(kt_ref[:, at], d_scores, NN)

    chunk(step, True)

    @pl.loop(0, step)
    def _(j):
        chunk(j, False)

    out = acc_ref[...] * HEAD ** (-0.5)
    out = jnp.concatenate([out[:, h * rows : (h + 1) * rows] for h in range(heads)], axis=0)
    dq_ref[...] = out.T.astype(bf16)

    @pl.when(step == pl.num_programs(0) - 1)
    def _():
        dkv_ref[...] = jnp.concatenate([dk_ref[:, :HEAD], dv_ref[...]], axis=1).astype(bf16)


def attention_backward(query, key, key_t, value, d_out, out, logs):
    heads, length, wide = query.shape
    steps = logs.shape[0]
    rows = length // steps
    by_rows = pl.BlockSpec((rows, heads * HEAD), lambda i: (i, 0))
    return pl.pallas_call(
        backward_kernel,
        out_shape=(
            jax.ShapeDtypeStruct((length, heads * HEAD), bf16),
            jax.ShapeDtypeStruct((length, 2 * HEAD), bf16),
        ),
        grid=(steps,),
        in_specs=[
            pl.BlockSpec((heads, rows, wide), lambda i: (0, i, 0)),
            pl.BlockSpec((length, wide), lambda i: (0, 0)),
            pl.BlockSpec((HEAD, length), lambda i: (0, 0)),
            pl.BlockSpec((length, HEAD), lambda i: (0, 0)),
            pl.BlockSpec((1, heads * HEAD, rows), lambda i: (i, 0, 0)),
            pl.BlockSpec((1, heads * HEAD, rows), lambda i: (i, 0, 0)),
            pl.BlockSpec((1, 1, heads * rows), lambda i: (i, 0, 0)),
        ],
        out_specs=(by_rows, pl.BlockSpec((length, 2 * HEAD), lambda i: (0, 0))),
        scratch_shapes=[
            pltpu.VMEM((HEAD, heads * rows), f32),
            pltpu.VMEM((length, wide), f32),
            pltpu.VMEM((length, HEAD), f32),
        ],
        compiler_params=pltpu.CompilerParams(vmem_limit_bytes=40 * 2**20),
        cost_estimate=lasting(7.5),
    )(query, key, key_t, value, d_out, out, logs)


def slot_kernel(sources, unread, place_in_ref, *refs):
    row_refs, cot_refs = refs[:sources], refs[sources : 2 * sources]
    router_ref, w_ref = refs[2 * sources : 2 * sources + 2]
    refs = refs[2 * sources + 2 + unread :]
    x_ref, hid_ref, ds_ref, dgu_ref, moe_ref = refs[:5]
    dsum_refs = refs[5 : 5 + sources]
    moe_acc, dsum_acc, combine_ref, place_ref = refs[5 + sources :]
    expert = pl.program_id(0)
    tokens, width = row_refs[0].shape
    cap = x_ref.shape[1] // sources
    named = place_in_ref[0] + expert

    @pl.when(expert == 0)
    def _():
        moe_acc[...] = jnp.zeros_like(moe_acc)
        dsum_acc[...] = jnp.zeros_like(dsum_acc)
        for s in range(sources):
            place = cot_refs[s][:, width:].astype(f32).T[:EXPERTS]
            place_ref[s] = place
            hit = place >= 0.0
            logits = mm(router_ref[...], row_refs[s][...], NT)
            top = jnp.max(jnp.where(hit, logits, -3e38), axis=0, keepdims=True)
            grown = jnp.where(hit, jnp.exp(jnp.minimum(logits - top, 0.0)), 0.0)
            combine_ref[s] = grown / jnp.sum(grown, axis=0, keepdims=True)

    slots = lax.broadcasted_iota(jnp.int32, (cap, tokens), 0).astype(f32)
    picks, cots, slot_weights = [], [], []
    for s in range(sources):
        hit = place_ref[s, pl.ds(named, 1), :] == slots
        pick = jnp.where(hit, 1.0, 0.0).astype(bf16)
        picks.append(pick)
        x_ref[0, s * cap : (s + 1) * cap, :] = mm(pick, row_refs[s][...], NN).astype(bf16)
        cots.append(mm(pick, cot_refs[s][:, :width], NN))
        slot_weights.append(
            jnp.sum(
                jnp.where(hit, combine_ref[s, pl.ds(named, 1), :], 0.0), axis=1, keepdims=True
            )
        )
    x_rows = x_ref[0]
    cot = jnp.concatenate(cots, axis=0)
    slot_weight = jnp.concatenate(slot_weights, axis=0)
    gate_up_w = w_ref[0, :, : 2 * FFE]
    down_t = w_ref[0, :, 2 * FFE :]
    gate_up = mm(x_rows, gate_up_w, NN)
    gate = gate_up[:, :FFE]
    up = gate_up[:, FFE:]
    sig = 1.0 / (1.0 + jnp.exp(-gate))
    silu = gate * sig
    hidden = (silu * up).astype(bf16)
    hid_ref[0] = hidden
    expert_out = mm(hidden, down_t, NT).astype(bf16).astype(f32)
    d_slot = (slot_weight * cot).astype(bf16)
    ds_ref[0] = d_slot
    d_comb = jnp.sum(cot * expert_out, axis=1, keepdims=True)
    d_comb_high = d_comb.astype(bf16).astype(f32)
    lane = lax.broadcasted_iota(jnp.int32, (d_comb.shape[0], EXTRA), 1)
    extra = jnp.where(lane == named, d_comb_high, 0.0)
    extra = jnp.where(lane == named + EXPERTS, d_comb - d_comb_high, extra).astype(bf16)
    weighted = (slot_weight * expert_out).astype(bf16)
    d_hidden = mm(d_slot, down_t, NN)
    d_gate = (d_hidden * up * sig * (1.0 + gate * (1.0 - sig))).astype(bf16)
    d_up = (d_hidden * silu).astype(bf16)
    dgu_ref[0, :, :FFE] = d_gate
    dgu_ref[0, :, FFE:] = d_up
    d_row = mm(dgu_ref[0], gate_up_w, NT).astype(bf16)
    for s in range(sources):
        part = slice(s * cap, (s + 1) * cap)
        moe_acc[s] += mm(picks[s], weighted[part], TN)
        dsum_acc[s, :, :width] += mm(picks[s], d_row[part], TN)
        dsum_acc[s, :, width:] += mm(picks[s], extra[part], TN)

    @pl.when(expert == pl.num_programs(0) - 1)
    def _():
        for s in range(sources):
            moe_ref[0, place_in_ref[2] ^ s] = moe_acc[s].astype(bf16)
            dsum_refs[s][...] = dsum_acc[s].astype(bf16)


def expert_slot(place, rows, cots, router_t, weights, cap, slots, moe, needed):
    sources = len(rows)
    tokens, width = rows[0].shape
    experts = weights.shape[0]
    held = sources * cap
    carried = ([] if moe is None else [moe]) + needed
    each = lambda *shape: pl.BlockSpec((1,) + shape, lambda e, s: (e,) + (0,) * len(shape))
    fixed = lambda *shape: pl.BlockSpec(shape, lambda e, s: (0,) * len(shape))
    got = pl.pallas_call(
        functools.partial(slot_kernel, sources, len(carried)),
        out_shape=(
            jax.ShapeDtypeStruct((experts, held, width), bf16),
            jax.ShapeDtypeStruct((experts, held, FFE), bf16),
            jax.ShapeDtypeStruct((experts, held, width), bf16),
            jax.ShapeDtypeStruct((experts, held, 2 * FFE), bf16),
        )
        + (jax.ShapeDtypeStruct((slots, sources, tokens, width), bf16),)
        + (jax.ShapeDtypeStruct((tokens, width + EXTRA), bf16),) * sources,
        grid_spec=pltpu.PrefetchScalarGridSpec(
            num_scalar_prefetch=1,
            grid=(experts,),
            in_specs=[fixed(tokens, width)] * sources
            + [fixed(tokens, width + EXTRA)] * sources
            + [fixed(EXPERTS, width), each(width, 3 * FFE)]
            + [pl.BlockSpec(memory_space=pl.ANY)] * len(carried),
            out_specs=(each(held, width), each(held, FFE), each(held, width), each(held, 2 * FFE))
            + (pl.BlockSpec((1, sources, tokens, width), lambda e, s: (s[1], 0, 0, 0)),)
            + (fixed(tokens, width + EXTRA),) * sources,
            scratch_shapes=[
                pltpu.VMEM((sources, tokens, width), f32),
                pltpu.VMEM((sources, tokens, width + EXTRA), f32),
                pltpu.VMEM((sources, EXPERTS, tokens), f32),
                pltpu.VMEM((sources, EXPERTS, tokens), f32),
            ],
        ),
        compiler_params=pltpu.CompilerParams(vmem_limit_bytes=56 * 2**20),
        cost_estimate=lasting(7.5),
        input_output_aliases={2 * sources + 3: 4} if moe is not None else {},
    )(place, *rows, *cots, router_t, weights, *carried)
    return got[:4], got[4], got[5:]


def middle_kernel(
    tp_ref, got_ref, in_ref, out_ref, gain_ref, router_ref, rank_ref,
    x_ref, act_ref, mine_ref, theirs_ref, combine_ref, probs_ref, total_ref,
):
    tp = tp_ref[0]
    count = got_ref.shape[0] // 2
    gathered = lambda t: jnp.concatenate([got_ref[2 * c + t] for c in range(count)], axis=0)
    mine = gathered(tp).astype(f32).T.astype(bf16)
    theirs = gathered(tp ^ 1).astype(f32).T.astype(bf16)
    mine_ref[...] = mine
    theirs_ref[...] = theirs
    x_one = in_ref[...].astype(f32) + (mm(mine, out_ref[tp], NT) + mm(theirs, out_ref[tp ^ 1], NT))
    x_ref[...] = x_one
    inv = lax.rsqrt(jnp.mean(x_one * x_one, axis=-1, keepdims=True) + norm_eps)
    act = (x_one * inv * gain_ref[...]).astype(bf16)
    act_ref[...] = act
    logits = mm(router_ref[...], act, NT)
    grown = jnp.exp(logits - jnp.max(logits, axis=0, keepdims=True))
    probs = grown / jnp.sum(grown, axis=0, keepdims=True)
    probs_ref[...] = probs
    total_ref[...] = jnp.sum(probs, axis=1, keepdims=True)
    hit = rank_ref[...].astype(f32) >= 0.0
    top = jnp.max(jnp.where(hit, logits, -3e38), axis=0, keepdims=True)
    grown = jnp.where(hit, jnp.exp(jnp.minimum(logits - top, 0.0)), 0.0)
    combine_ref[...] = grown / jnp.sum(grown, axis=0, keepdims=True)


def middle(tp, got, inputs, out_t, gain, router_t, rank):
    rows, width = inputs.shape
    held = got.shape[0] // 2 * got.shape[1]
    shapes = [
        ((rows, width), f32),
        ((rows, width), bf16),
        ((rows, held), bf16),
        ((rows, held), bf16),
        ((EXPERTS, rows), f32),
        ((EXPERTS, rows), f32),
        ((EXPERTS, 1), f32),
    ]
    return pl.pallas_call(
        middle_kernel,
        out_shape=tuple(jax.ShapeDtypeStruct(s, d) for s, d in shapes),
        in_specs=[pl.BlockSpec(memory_space=pltpu.SMEM)]
        + [pl.BlockSpec(memory_space=pltpu.VMEM)] * 6,
        out_specs=(pl.BlockSpec(memory_space=pltpu.VMEM),) * 7,
        compiler_params=pltpu.CompilerParams(vmem_limit_bytes=40 * 2**20),
        cost_estimate=lasting(4),
    )(tp, got, inputs, out_t, gain, router_t, rank)


def return_kernel(slots, tp_ref, *refs):
    part_refs = refs[:slots]
    (
        x_ref, act_ref, combine_ref, probs_ref, aux_ref, cot_ref, gain_ref, router_ref, out_ref,
        low_ref, rest_ref, small_ref, att_ref,
    ) = refs[slots:]
    tp = tp_ref[0]
    width = x_ref.shape[1]
    total = part_refs[0][...].astype(f32)
    for part in part_refs[1:]:
        total = total + part[...].astype(f32)
    extra = total[:, width:].T
    d_combine = extra[:EXPERTS] + extra[EXPERTS : 2 * EXPERTS]
    combine = combine_ref[...]
    probs = probs_ref[...]
    aux = aux_ref[...]
    d_logits = combine * (d_combine - jnp.sum(combine * d_combine, axis=0, keepdims=True))
    d_logits = d_logits + probs * (aux - jnp.sum(probs * aux, axis=0, keepdims=True))
    d_logits = d_logits.astype(bf16)
    d_act = total[:, :width] + mm(d_logits, router_ref[...], TN)
    x_one = x_ref[...]
    inv = lax.rsqrt(jnp.mean(x_one * x_one, axis=-1, keepdims=True) + norm_eps)
    normed = x_one * inv
    scaled = d_act * gain_ref[...]
    d_x = inv * (scaled - normed * jnp.mean(scaled * normed, axis=-1, keepdims=True))
    d_x = d_x + cot_ref[...].astype(f32)
    low = d_x.astype(bf16)
    low_ref[...] = low
    rest_ref[...] = (d_x - low.astype(f32)).astype(bf16)
    mine = mm(low, out_ref[tp], NN).T.astype(bf16)
    theirs = mm(low, out_ref[tp ^ 1], NN).T.astype(bf16)
    cut = att_ref.shape[1]
    for c in range(att_ref.shape[0] // 2):
        att_ref[2 * c + tp] = mine[c * cut : (c + 1) * cut]
        att_ref[2 * c + (tp ^ 1)] = theirs[c * cut : (c + 1) * cut]
    d_router = mm(d_logits, act_ref[...], NN)
    d_gain = jnp.sum(d_act * normed, axis=0, keepdims=True)
    small = jnp.concatenate([d_router, d_gain, jnp.zeros((HEAD - EXPERTS - 1, width), f32)], axis=0)
    small = small.T
    high = small.astype(bf16).astype(f32)
    small_ref[...] = jnp.concatenate([high, small - high], axis=1).astype(bf16)


def expert_return(tp, parts, x_one, act, combine, probs, aux, cot, gain, router_t, out_t, cuts):
    rows, width = x_one.shape
    slots = len(parts)
    shapes = [
        ((rows, width), bf16),
        ((rows, width), bf16),
        ((width, 2 * HEAD), bf16),
        ((cuts, width // cuts, rows), bf16),
    ]
    return pl.pallas_call(
        functools.partial(return_kernel, slots),
        out_shape=tuple(jax.ShapeDtypeStruct(s, d) for s, d in shapes),
        in_specs=[pl.BlockSpec(memory_space=pltpu.SMEM)]
        + [pl.BlockSpec(memory_space=pltpu.VMEM)] * (slots + 9),
        out_specs=(pl.BlockSpec(memory_space=pltpu.VMEM),) * 4,
        compiler_params=pltpu.CompilerParams(vmem_limit_bytes=48 * 2**20),
        cost_estimate=lasting(7),
    )(tp, *parts, x_one, act, combine, probs, aux, cot, gain, router_t, out_t)


def out_grad_kernel(low_ref, other_low_ref, att_ref, other_att_ref, small_ref, other_small_ref, out_ref):
    held = att_ref.shape[1]
    grad = mm(low_ref[...], att_ref[...], TN) + mm(other_low_ref[...], other_att_ref[...], TN)
    out_ref[:, :held] = grad.astype(bf16)
    small = small_ref[...].astype(f32) + other_small_ref[...].astype(f32)
    small = small[:, :HEAD] + small[:, HEAD:]
    high = small.astype(bf16).astype(f32)
    out_ref[:, held:] = jnp.concatenate([high, small - high], axis=1).astype(bf16)


def out_grad(low, other_low, att, other_att, small, other_small):
    rows, width = low.shape
    held = att.shape[1]
    return pl.pallas_call(
        out_grad_kernel,
        out_shape=jax.ShapeDtypeStruct((width, held + small.shape[1]), bf16),
        in_specs=[pl.BlockSpec(memory_space=pltpu.VMEM)] * 6,
        out_specs=pl.BlockSpec(memory_space=pltpu.VMEM),
        compiler_params=pltpu.CompilerParams(vmem_limit_bytes=40 * 2**20),
        cost_estimate=lasting(3),
    )(low, other_low, att, other_att, small, other_small)


def grads_kernel(parts, *refs):
    join = lambda n: jnp.concatenate([r[0] for r in refs[n * parts : (n + 1) * parts]], axis=0)
    out_ref = refs[-1]
    out_ref[0, :, : 2 * FFE] = mm(join(0), join(1), TN).astype(bf16)
    out_ref[0, :, 2 * FFE :] = mm(join(2), join(3), TN).astype(bf16)


def expert_grads(xs, dgus, dss, hids):
    parts = len(xs)
    experts, _, width = xs[0].shape
    spec = lambda a: pl.BlockSpec((1,) + a.shape[1:], lambda e: (e, 0, 0))
    many = [*xs, *dgus, *dss, *hids]
    return pl.pallas_call(
        functools.partial(grads_kernel, parts),
        out_shape=jax.ShapeDtypeStruct((experts, width, 3 * FFE), bf16),
        grid=(experts,),
        in_specs=[spec(a) for a in many],
        out_specs=pl.BlockSpec((1, width, 3 * FFE), lambda e: (e, 0, 0)),
        compiler_params=pltpu.CompilerParams(vmem_limit_bytes=56 * 2**20),
        cost_estimate=lasting(6.6),
    )(*many)


def split_kernel(grad_ref, gu_ref, down_ref, sums_ref):
    wide = gu_ref.shape[2]
    grad = grad_ref[0].astype(f32)
    gate_up = grad[:, :wide]
    down_t = grad[:, wide:]
    gu_ref[0] = gate_up
    down = down_t.T
    down_ref[0] = down
    squares = gate_up * gate_up
    lanes = sum(squares[:, i : i + 128] for i in range(0, wide, 128))
    rows = squares.shape[0]
    sums_ref[0, :, :rows] = jnp.sum(lanes.T, axis=0, keepdims=True)
    sums_ref[0, :, rows : 2 * rows] = jnp.sum(down * down, axis=0, keepdims=True)
    sums_ref[0, :, 2 * rows : 2 * rows + wide] = jnp.sum(squares, axis=0, keepdims=True)
    sums_ref[0, :, 2 * rows + wide :] = jnp.sum(down_t * down_t, axis=0, keepdims=True)


def split(grads):
    experts, rows, wide = grads.shape
    each = lambda *shape: pl.BlockSpec((1,) + shape, lambda e: (e, 0, 0))
    return pl.pallas_call(
        split_kernel,
        out_shape=(
            jax.ShapeDtypeStruct((experts, rows, 2 * FFE), f32),
            jax.ShapeDtypeStruct((experts, FFE, rows), f32),
            jax.ShapeDtypeStruct((experts, 1, 2 * rows + 3 * FFE), f32),
        ),
        grid=(experts,),
        in_specs=[each(rows, wide)],
        out_specs=(each(rows, 2 * FFE), each(FFE, rows), each(1, 2 * rows + 3 * FFE)),
        compiler_params=pltpu.CompilerParams(vmem_limit_bytes=40 * 2**20),
        cost_estimate=lasting(4),
    )(grads)


def half_sum(parts, count):
    total = parts[0].astype(f32)
    for y in range(1, count):
        total = total + partner(parts[y], "tp", y, count).astype(f32)
    return total.astype(bf16)


def per_device(
    inputs,
    cotangent,
    routes,
    segment_ids,
    parents,
    w_qkv,
    w_out,
    w_router,
    w_gate_up,
    w_down,
    gain_attn,
    gain_moe,
    row_qkv,
    col_qkv,
    row_out,
    col_out,
    row_router,
    col_router,
    row_gate_up,
    col_gate_up,
    row_down,
    col_down,
    second_attn,
    second_moe,
):
    tp_count = lax.axis_size("tp")
    ctx_count = lax.axis_size("ctx")
    fsdp_count = lax.axis_size("fsdp")
    count = tp_count * ctx_count * fsdp_count
    tp_index = lax.axis_index("tp")
    ctx_index = lax.axis_index("ctx")
    fsdp_index = lax.axis_index("fsdp")
    flat_index = fsdp_index * ctx_count + ctx_index
    owner_index = fsdp_index * tp_count + tp_index
    keep_once = (tp_index == 0).astype(f32)
    tok_rows = inputs.shape[0]
    half_rows = tok_rows // tp_count
    tree_len = segment_ids.shape[1]
    tokens_all = tok_rows * fsdp_count * ctx_count
    capacity = half_rows * TOPK * 3 // (2 * EXPERTS)
    local_experts = EXPERTS // (fsdp_count * tp_count)
    q_own = HEADS // (tp_count * ctx_count)
    kv_own = KV_HEADS // (tp_count * ctx_count)
    assert kv_own == 1 and tp_count == 2
    q_cols = q_own * HEAD
    kv_cols = kv_own * HEAD
    own_cols = q_cols + 2 * kv_cols
    dense_rows = w_qkv.shape[0]
    qkv_cols = w_qkv.shape[1]
    dense_parts = fsdp_count * ctx_count
    ctx_rows = w_gate_up.shape[1]
    labels = jnp.arange(EXPERTS, dtype=jnp.int32)

    def by_ctx(columns):
        q_end = ctx_count * q_cols
        k_end = q_end + ctx_count * kv_cols
        lead = columns.shape[:-1]
        return jnp.concatenate(
            [
                columns[..., :q_end].reshape(lead + (ctx_count, q_cols)),
                columns[..., q_end:k_end].reshape(lead + (ctx_count, kv_cols)),
                columns[..., k_end:].reshape(lead + (ctx_count, kv_cols)),
            ],
            axis=-1,
        )

    def from_ctx(columns):
        lead = columns.shape[:-2]
        return jnp.concatenate(
            [
                columns[..., :q_cols].reshape(lead + (-1,)),
                columns[..., q_cols : q_cols + kv_cols].reshape(lead + (-1,)),
                columns[..., q_cols + kv_cols :].reshape(lead + (-1,)),
            ],
            axis=-1,
        )

    w_qkv_low = w_qkv.astype(bf16)
    extras = jnp.concatenate(
        [gain_attn.astype(bf16)[:, None], gain_moe.astype(bf16)[:, None], w_router.astype(bf16)],
        axis=1,
    )
    w_send = jnp.concatenate(
        [
            jnp.moveaxis(by_ctx(w_qkv_low), 1, 0),
            jnp.broadcast_to(extras[None], (ctx_count,) + extras.shape),
        ],
        axis=-1,
    )
    w_send = jnp.broadcast_to(w_send[None], (fsdp_count,) + w_send.shape)
    w_got = exchange(w_send.reshape((dense_parts,) + w_send.shape[2:]), ("fsdp", "ctx"))
    w_got = w_got.reshape(D, own_cols + 2 + EXPERTS)
    def spread(block):
        bit = fsdp_count // 2
        blocks = {0: block}
        while bit:
            for j in list(blocks):
                blocks[j ^ bit] = partner(blocks[j], "fsdp", bit, fsdp_count)
            bit //= 2
        near = [blocks[j] for j in range(fsdp_count)]
        return [[b] + [partner(b, "tp", y, tp_count) for y in range(1, tp_count)] for b in near]

    my_routes = lax.dynamic_slice_in_dim(routes, tp_index * half_rows, half_rows, 0)
    hit = jnp.sum((my_routes[..., None] == labels).astype(f32), axis=1)
    before = (
        jnp.arange(half_rows, dtype=jnp.int32)[:, None]
        < jnp.arange(half_rows, dtype=jnp.int32)[None, :]
    ).astype(bf16)
    rank = dot("te,tu->eu", hit.astype(bf16), before)
    rank = jnp.where(hit.T > 0.5, rank, -1.0).astype(bf16)
    riders = jnp.concatenate(
        [rank.T, jnp.broadcast_to(jnp.sum(hit, axis=0).astype(bf16), (half_rows, EXPERTS))], axis=1
    )
    riders = jnp.pad(riders, ((0, 0), (0, EXTRA - 2 * EXPERTS)))
    cot_rows = jnp.concatenate([cotangent, riders], axis=1)
    cot_near = [cot_rows]
    for j in range(1, fsdp_count):
        if fsdp_count == 4 and j == 3:
            cot_near.append(cot_rows)
        else:
            cot_near.append(partner(cot_rows, "fsdp", j, fsdp_count))

    blocks = {0: inputs}
    bit = ctx_count // 2
    while bit:
        for j in list(blocks):
            blocks[j ^ bit] = partner(blocks[j], "ctx", bit, ctx_count)
        if bit == ctx_count // 2:
            arrived = blocks[bit] = after(blocks[bit], w_got)
        bit //= 2
    blocks = [blocks[j] for j in range(ctx_count)]
    gain_one = w_got[:, own_cols].astype(f32)[None]
    gain_two = w_got[:, own_cols + 1].astype(f32)[None]
    router_t = w_got[:, own_cols + 2 :].T
    tp_at = jnp.asarray(tp_index, jnp.int32).reshape(1)

    master_sums = jnp.stack(
        [
            jnp.sum(w_qkv * w_qkv),
            jnp.sum(w_out * w_out),
            keep_once * jnp.sum(w_router * w_router),
            jnp.sum(w_gate_up * w_gate_up),
            jnp.sum(w_down * w_down),
            keep_once * jnp.sum(gain_attn * gain_attn),
            keep_once * jnp.sum(gain_moe * gain_moe),
        ]
    )
    out_rows = w_out.shape[0]
    out_t = lax.all_gather(w_out.astype(bf16).T, ("tp", "fsdp", "ctx"), axis=0, tiled=True)
    out_t = out_t.reshape(tp_count, D, out_rows)
    expert_w = jnp.concatenate(
        [w_gate_up.astype(bf16), w_down.astype(bf16).transpose(0, 2, 1)], axis=2
    )
    expert_w = lax.all_gather(after(expert_w, arrived), "ctx", axis=1, tiled=True)

    seg_hot = (segment_ids[0][:, None] == jnp.arange(HEAD, dtype=jnp.int32)).astype(bf16)
    hidden_from = jnp.pad((1.0 - ancestry(parents[0])) * -1e30, ((0, HEAD - NSEG),) * 2)
    barred = dot("qs,su->qu", seg_hot, hidden_from.astype(bf16)).astype(bf16)
    query_tie = cot_near[1:3]
    act1, query, key, key_t, value, value_t = project(
        blocks,
        jnp.asarray(ctx_index, jnp.int32).reshape(1),
        w_got,
        gain_one,
        barred,
        seg_hot,
        q_own,
        half_rows,
    )
    after_project = [after(c, key) for c in cot_near]
    if fsdp_count == 4:
        after_project[3] = partner(after_project[2], "fsdp", 1, fsdp_count)
    cot_far = [partner(c, "tp", 1, tp_count) for c in after_project]
    grad_slots = [[c, f] for c, f in zip(after_project, cot_far)]
    attended_own, logs = attention_forward(after(query, *query_tie), key, value_t, half_rows)
    counts = sum(
        c[:1, D + EXPERTS : D + 2 * EXPERTS].astype(f32) for pair in grad_slots for c in pair
    )
    bit = 1
    while bit < ctx_count:
        counts = counts + partner(counts, "ctx", bit, ctx_count)
        bit *= 2
    fraction = counts[0] / (tokens_all * TOPK)
    attended_own = after(attended_own, *cot_far[:2], after_project[3])
    attended = exchange(attended_own, ("ctx", "tp"))
    attended = after(attended, *cot_far[2:])
    inputs_half = lax.dynamic_slice_in_dim(inputs, tp_index * half_rows, half_rows, 0)
    x_one, act2, heads_own, heads_other, combine, router_probs, prob_sums = middle(
        tp_at, attended, inputs_half, out_t, gain_two, router_t, rank
    )
    w_tree = lax.all_gather(after(w_got, act2)[:, :own_cols], "ctx", axis=0, tiled=False)
    row_slots = spread(after(act2, *[pair[1] for pair in grad_slots]))

    kept, d_sums, moe_sums = [], [], None
    for j in range(fsdp_count):
        rows = list(row_slots[j])
        if j == 0:
            rows[0] = after(rows[0], row_slots[1][0])
        if j == 1:
            rows[0] = after(rows[0], row_slots[2][0])
        if j >= 2:
            rows[0] = after(rows[0], d_sums[j - 2], *(pair[0] for pair in row_slots[3:]))
        if j == 3:
            rows[0] = after(rows[0], fraction)
        place = jnp.stack([owner_index * local_experts, fsdp_index ^ j, tp_index])
        held, moe_sums, d_out = expert_slot(
            place.astype(jnp.int32),
            rows,
            grad_slots[j],
            router_t,
            expert_w,
            capacity,
            fsdp_count,
            moe_sums,
            [w_tree] if j == fsdp_count - 1 else [],
        )
        kept.append(held)
        d_sums.append(half_sum(d_out, tp_count))
    d_parts = [d_sums[0]] + [partner(d_sums[j], "fsdp", j, fsdp_count) for j in range(1, fsdp_count)]
    other_heads = partner(after(heads_other, d_sums[-1]), "tp", 1, tp_count)
    d_parts[0] = after(d_parts[0], other_heads)
    xs, hids, dss, dgus = (list(part) for part in zip(*kept))
    xs[0] = after(xs[0], *d_sums[-2:])
    g_experts = expert_grads(xs, dgus, dss, hids)
    d_parts[0] = after(d_parts[0], g_experts)
    low, rest, small, d_attended = expert_return(
        tp_at,
        d_parts,
        x_one,
        act2,
        combine,
        router_probs,
        (aux_weight * EXPERTS * fraction)[:, None],
        cotangent,
        gain_two,
        router_t,
        out_t,
        ctx_count * tp_count,
    )
    d_attended = exchange(d_attended, ("ctx", "tp"))
    g_experts = lax.psum_scatter(after(g_experts, low), "ctx", scatter_dimension=1, tiled=True)
    g_gate_up, g_down, expert_sums = split(g_experts)
    expert_sums = expert_sums[:, 0]
    other_low = partner(low, "tp", 1, tp_count)
    other_small = partner(small, "tp", 1, tp_count)
    g_out_part = out_grad(low, other_low, heads_own, other_heads, small, other_small)
    d_attended = after(d_attended, g_out_part)
    g_out_got = exchange(g_out_part.reshape(dense_parts, dense_rows, -1), ("fsdp", "ctx"))
    g_out_got = jnp.sum(g_out_got.astype(f32), axis=0)
    g_out = g_out_got[:, :out_rows].T
    g_small = g_out_got[:, out_rows : out_rows + HEAD] + g_out_got[:, out_rows + HEAD :]
    g_router = g_small[:, :EXPERTS]
    g_gain2 = g_small[:, EXPERTS]

    d_q, d_kv = attention_backward(query, key, key_t, value, d_attended, attended_own, logs)
    moe_sums = after(moe_sums, d_q)
    moe = lax.psum_scatter(
        moe_sums.reshape(-1, D), ("fsdp", "tp"), scatter_dimension=0, tiled=True
    )
    d_qkv = jnp.concatenate([d_q, d_kv], axis=1)
    g_qkv_part = after(dot("td,tc->dc", act1, d_qkv).astype(bf16), g_out_got)
    g_qkv_got = exchange(g_qkv_part.reshape(dense_parts, dense_rows, own_cols), ("fsdp", "ctx"))
    g_qkv_got = g_qkv_got.reshape(fsdp_count, ctx_count, dense_rows, own_cols).astype(f32)
    g_qkv = from_ctx(jnp.moveaxis(jnp.sum(g_qkv_got, axis=0), 0, 1))
    sq_qkv = g_qkv * g_qkv
    sq_out = g_out * g_out
    sq_router = g_router * g_router
    gain_part = jnp.sum(g_qkv * w_qkv_low.astype(f32), axis=1) / gain_attn.astype(bf16).astype(f32)
    d_qkv_send = after(d_qkv, g_qkv_got)
    d_qkv_all = exchange(d_qkv_send.reshape(ctx_count, tok_rows, own_cols), "ctx")
    d_act1_low = dot("crk,cdk->rd", d_qkv_all, w_tree).astype(bf16)
    d_act1_other = partner(d_act1_low, "tp", 1, tp_count)
    pieces = [
        jnp.sum(sq_qkv, axis=0),
        jnp.sum(sq_out, axis=1),
        jnp.sum(sq_qkv, axis=1),
        gain_part,
        jnp.sum(sq_out, axis=0),
        jnp.sum(sq_router, axis=1),
        jnp.concatenate([jnp.sum(sq_router, axis=0), prob_sums[:, 0], master_sums]),
    ]
    sizes = [p.shape[0] for p in pieces]
    padded = [-(-s // 128) * 128 for s in sizes]
    message = jnp.concatenate([jnp.pad(p, (0, n - p.shape[0])) for p, n in zip(pieces, padded)])
    message = after(message, d_qkv_all)
    got = share(message, count).reshape(dense_parts, tp_count, -1)
    shares, at = [], 0
    for size, room in zip(sizes, padded):
        shares.append(got[..., at : at + size])
        at += room
    tot_col_qkv = jnp.sum(shares[0], axis=0).reshape(-1)
    tot_row_out = jnp.sum(shares[1], axis=0).reshape(-1)
    tot_row_qkv = jnp.sum(shares[2], axis=1).reshape(-1)
    g_gain1 = lax.dynamic_index_in_dim(jnp.sum(shares[3], axis=1), flat_index, 0, keepdims=False)
    tot_col_out = jnp.sum(shares[4], axis=1).reshape(-1)
    tot_row_router = shares[5][:, 0].reshape(-1)
    tot_col_router = jnp.sum(shares[6][:, 0, :EXPERTS], axis=0)
    last_totals = jnp.sum(shares[6][..., EXPERTS:], axis=(0, 1))
    prob_totals = last_totals[:EXPERTS]
    master_totals = last_totals[EXPERTS:]

    own_row_gu = expert_sums[:, :ctx_rows]
    start = (owner_index * local_experts, ctx_index * ctx_rows)
    start = tuple(jnp.asarray(s, jnp.int32) for s in start)
    rows_gu = lax.dynamic_slice(row_gate_up, start, (local_experts, ctx_rows))
    rows_gu = decay * rows_gu + (1.0 - decay) * (own_row_gu / (2 * FFE) + floor_sq)
    gu_sum = jnp.pad(jnp.sum(rows_gu, axis=1, keepdims=True), ((0, 0), (0, 127)))
    over_ctx = jnp.concatenate([expert_sums[:, 2 * ctx_rows :], gu_sum], axis=1)
    over_ctx = jnp.broadcast_to(over_ctx[None], (ctx_count,) + over_ctx.shape)
    over_ctx = jnp.sum(exchange(after(over_ctx, got), "ctx"), axis=0)
    mean_gu = over_ctx[:, 3 * FFE] / D
    own_col_gu = over_ctx[:, : 2 * FFE]
    own_row_down = over_ctx[:, 2 * FFE : 3 * FFE]
    own_col_down = expert_sums[:, ctx_rows : 2 * ctx_rows]
    first_row = (start[0], jnp.asarray(0, jnp.int32))
    cols_gu = lax.dynamic_slice(col_gate_up, first_row, (local_experts, 2 * FFE))
    cols_gu = decay * cols_gu + (1.0 - decay) * (own_col_gu / D + floor_sq)
    rows_dn = lax.dynamic_slice(row_down, first_row, (local_experts, FFE))
    rows_dn = decay * rows_dn + (1.0 - decay) * (own_row_down / D + floor_sq)
    cols_dn = lax.dynamic_slice(col_down, start, (local_experts, ctx_rows))
    cols_dn = decay * cols_dn + (1.0 - decay) * (own_col_down / FFE + floor_sq)
    mean_dn = jnp.mean(rows_dn, axis=-1)
    change_gate_up = g_gate_up * lax.rsqrt(
        rows_gu[:, :, None] * cols_gu[:, None, :] / mean_gu[:, None, None]
    )
    change_down = g_down * lax.rsqrt(
        rows_dn[:, :, None] * cols_dn[:, None, :] / mean_dn[:, None, None]
    )
    squares_gu = jnp.sum(change_gate_up * change_gate_up)
    squares_dn = jnp.sum(change_down * change_down)
    d_act1 = d_act1_low.astype(f32) + after(d_act1_other, over_ctx).astype(f32)
    own_inputs = inputs.astype(f32)
    d_inputs_attn, _ = norm_backward(own_inputs, inv_rms(own_inputs), gain_one, d_act1)
    rest = after(rest, d_qkv)
    d_x1 = low.astype(f32) + rest.astype(f32)
    other_x1 = other_low.astype(f32) + partner(rest, "tp", 1, tp_count).astype(f32)
    d_x1 = in_order(d_x1, other_x1, tp_index, 0).reshape(tok_rows, D)
    grad_inputs = d_x1 + d_inputs_attn

    qkv_width = (HEADS + 2 * KV_HEADS) * HEAD
    row_qkv_new = decay * row_qkv + (1.0 - decay) * (tot_row_qkv / qkv_width + floor_sq)
    col_qkv_new = decay * col_qkv + (1.0 - decay) * (tot_col_qkv / D + floor_sq)
    row_out_new = decay * row_out + (1.0 - decay) * (tot_row_out / D + floor_sq)
    col_out_new = decay * col_out + (1.0 - decay) * (tot_col_out / (HEADS * HEAD) + floor_sq)
    row_router_new = decay * row_router + (1.0 - decay) * (tot_row_router / EXPERTS + floor_sq)
    col_router_new = decay * col_router + (1.0 - decay) * (tot_col_router / D + floor_sq)
    aux_loss = EXPERTS * jnp.sum(fraction * prob_totals / tokens_all)

    rows_here = lax.dynamic_slice_in_dim(row_qkv_new, flat_index * dense_rows, dense_rows, 0)
    cols_here = lax.dynamic_slice_in_dim(col_qkv_new, tp_index * qkv_cols, qkv_cols, 0)
    change_qkv = g_qkv * lax.rsqrt(rows_here[:, None] * cols_here[None, :] / jnp.mean(row_qkv_new))
    rows_here = lax.dynamic_slice_in_dim(row_out_new, tp_index * out_rows, out_rows, 0)
    cols_here = lax.dynamic_slice_in_dim(col_out_new, flat_index * dense_rows, dense_rows, 0)
    change_out = g_out * lax.rsqrt(rows_here[:, None] * cols_here[None, :] / jnp.mean(row_out_new))
    rows_here = lax.dynamic_slice_in_dim(row_router_new, flat_index * dense_rows, dense_rows, 0)
    change_router = g_router * lax.rsqrt(
        rows_here[:, None] * col_router_new[None, :] / jnp.mean(row_router_new)
    )
    second_attn_new = decay * second_attn + (1.0 - decay) * (g_gain1 * g_gain1 + floor_sq)
    second_moe_new = decay * second_moe + (1.0 - decay) * (g_gain2 * g_gain2 + floor_sq)
    change_gain1 = g_gain1 * lax.rsqrt(second_attn_new)
    change_gain2 = g_gain2 * lax.rsqrt(second_moe_new)
    square_sums = jnp.stack(
        [
            jnp.sum(change_qkv * change_qkv),
            jnp.sum(change_out * change_out),
            keep_once * jnp.sum(change_router * change_router),
            squares_gu,
            squares_dn,
            keep_once * jnp.sum(change_gain1 * change_gain1),
            keep_once * jnp.sum(change_gain2 * change_gain2),
        ]
    )
    square_totals = jnp.sum(share(square_sums, count), axis=0)
    quarter = lambda a: lax.dynamic_slice_in_dim(
        a, ctx_index * (a.shape[1] // ctx_count), a.shape[1] // ctx_count, 1
    )
    moments = jnp.concatenate([rows_gu, cols_dn, quarter(cols_gu), quarter(rows_dn)], axis=1)
    moments = share(after(moments, square_totals).reshape(-1), count)
    moments = moments.reshape(fsdp_count, ctx_count, tp_count, local_experts, -1)
    moments = moments.transpose(0, 2, 3, 1, 4).reshape(EXPERTS, ctx_count, -1)
    cut_at = (ctx_rows, 2 * ctx_rows, 2 * ctx_rows + 2 * FFE // ctx_count)
    row_gu_new = moments[..., : cut_at[0]].reshape(EXPERTS, D)
    col_down_new = moments[..., cut_at[0] : cut_at[1]].reshape(EXPERTS, D)
    col_gu_new = moments[..., cut_at[1] : cut_at[2]].reshape(EXPERTS, 2 * FFE)
    row_down_new = moments[..., cut_at[2] :].reshape(EXPERTS, FFE)

    entries = jnp.array(
        [
            D * qkv_width,
            HEADS * HEAD * D,
            D * EXPERTS,
            EXPERTS * D * 2 * FFE,
            EXPERTS * FFE * D,
            D,
            D,
        ],
        f32,
    )
    update_rms = jnp.sqrt(square_totals / entries)
    weight_rms = jnp.sqrt(master_totals / entries)
    step_scale = rate * weight_rms / jnp.maximum(clip_rms, update_rms)
    new_qkv = w_qkv - step_scale[0] * change_qkv
    new_out = w_out - step_scale[1] * change_out
    new_router = w_router - step_scale[2] * change_router
    new_gate_up = w_gate_up - step_scale[3] * change_gate_up
    new_down = w_down - step_scale[4] * change_down
    new_gain1 = gain_attn - step_scale[5] * change_gain1
    new_gain2 = gain_moe - step_scale[6] * change_gain2
    layer_out = (x_one + after(moe, update_rms, new_gate_up, grad_inputs).astype(f32)).astype(bf16)
    return (
        layer_out,
        grad_inputs,
        aux_loss,
        g_qkv,
        g_out,
        g_router,
        g_gate_up,
        g_down,
        g_gain1,
        g_gain2,
        new_qkv,
        new_out,
        new_router,
        new_gate_up,
        new_down,
        new_gain1,
        new_gain2,
        new_qkv.astype(bf16),
        new_out.astype(bf16),
        new_router.astype(bf16),
        new_gate_up.astype(bf16),
        new_down.astype(bf16),
        new_gain1.astype(bf16),
        new_gain2.astype(bf16),
        row_qkv_new,
        col_qkv_new,
        row_out_new,
        col_out_new,
        row_router_new,
        col_router_new,
        row_gu_new,
        col_gu_new,
        row_down_new,
        col_down_new,
        second_attn_new,
        second_moe_new,
        update_rms,
    )


def solution(mesh):
    placed = (
        P(("fsdp", "ctx"), None),
        P(("fsdp", "ctx", "tp"), None),
        P(("fsdp", "ctx"), None),
        P("fsdp", None),
        P("fsdp", None),
        P(("fsdp", "ctx"), "tp"),
        P("tp", ("fsdp", "ctx")),
        P(("fsdp", "ctx"), None),
        P(("fsdp", "tp"), "ctx", None),
        P(("fsdp", "tp"), None, "ctx"),
        P(("fsdp", "ctx")),
        P(("fsdp", "ctx")),
        P(),
        P(),
        P(),
        P(),
        P(),
        P(),
        P(),
        P(),
        P(),
        P(),
        P(("fsdp", "ctx")),
        P(("fsdp", "ctx")),
    )
    return jax.shard_map(
        per_device,
        mesh=mesh,
        in_specs=placed,
        out_specs=(
            P(("fsdp", "ctx", "tp"), None),
            P(("fsdp", "ctx"), None),
            P(),
            P(("fsdp", "ctx"), "tp"),
            P("tp", ("fsdp", "ctx")),
            P(("fsdp", "ctx"), None),
            P(("fsdp", "tp"), "ctx", None),
            P(("fsdp", "tp"), None, "ctx"),
            P(("fsdp", "ctx")),
            P(("fsdp", "ctx")),
            P(("fsdp", "ctx"), "tp"),
            P("tp", ("fsdp", "ctx")),
            P(("fsdp", "ctx"), None),
            P(("fsdp", "tp"), "ctx", None),
            P(("fsdp", "tp"), None, "ctx"),
            P(("fsdp", "ctx")),
            P(("fsdp", "ctx")),
            P(("fsdp", "ctx"), "tp"),
            P("tp", ("fsdp", "ctx")),
            P(("fsdp", "ctx"), None),
            P(("fsdp", "tp"), "ctx", None),
            P(("fsdp", "tp"), None, "ctx"),
            P(("fsdp", "ctx")),
            P(("fsdp", "ctx")),
            P(),
            P(),
            P(),
            P(),
            P(),
            P(),
            P(),
            P(),
            P(),
            P(),
            P(("fsdp", "ctx")),
            P(("fsdp", "ctx")),
            P(),
        ),
        check_vma=False,
    )
```

time: 1110 us -> 838 us (0.75)
  waiting for transfers between devices: 426 us -> 299 us
  other arithmetic: 164 us -> 109 us
  local copies, waits for them, and re-layouts: 117 us -> 72.6 us
  starting transfers between devices: 149 us -> 110 us
  Pallas kernels: 162 us -> 197 us
  blocking collectives: 25.1 us -> 0 us
  matrix products: 38.8 us -> 15.7 us
    all_to_all x16 -> x10, waiting for transfers between devices: 284 us -> 79.9 us  [exchange(): return lax.all_to_all(values, axes, split_axis=0, concat_axis=0, tiled=True)]
    ppermute x32 -> x31, waiting for transfers between devices: 141 us -> 184 us  [partner(): return lax.ppermute(values, axis, [(i, i ^ bits) for i in range(count)])]
    pallas_call x7 -> x12, Pallas kernels: 162 us -> 197 us  [the longest x4 97.8 us: expert_slot(): pl.pallas_call(functools.partial(slot_kernel, sources, len(carried)), out...]
    reduce_scatter x1 -> x2, waiting for transfers between devices: 0.02 us -> 34.5 us  [the longest x1 34.4 us: per_device(): lax.psum_scatter(moe_sums.reshape(-1, D), ('fsdp', 'tp'), scatter_dimensi...]
    all_to_all x1 -> x0, blocking collectives: 25.1 us -> none  [exchange(): return lax.all_to_all(values, axes, split_axis=0, concat_axis=0, tiled=True)]
    dot_general x11 -> x4, matrix products: 38.8 us -> 15.7 us  [dot(): return jnp.einsum(spec, left, right, preferred_element_type=f32)]
    all_to_all x16 -> x10, starting transfers between devices: 98.7 us -> 75.8 us  [exchange(): return lax.all_to_all(values, axes, split_axis=0, concat_axis=0, tiled=True)]
    convert_element_type x13 -> x9, other arithmetic: 34.2 us -> 11.9 us  [the longest x4 4.68 us: half_sum(): return total.astype(bf16)]
  transfers between devices with their start and end apart: 53 -> 46, of which waited for: 21 -> 21; matrix products, arithmetic and copies ran while one was open for 23% -> 19% of each run, Pallas kernels for 15% -> 23%
where the time goes in v3:
time: 838 us; the launch traced here: 827 us
  waiting for transfers between devices  299 us (36%)
  Pallas kernels  197 us (24%)
  starting transfers between devices  110 us (13%)
  other arithmetic  109 us (13%)
  local copies, waits for them, and re-layouts  72.6 us (9%)
  between operations  23.2 us (3%)
  matrix products  15.7 us (2%)
    ppermute x31, waiting for transfers between devices, partner(): return lax.ppermute(values, axis, [(i, i ^ bits) for i in range(count)])  184 us
    pallas_call x4, Pallas kernels, expert_slot(): pl.pallas_call(functools.partial(slot_kernel, sources, len(carried)), out...  97.8 us
    all_to_all x10, waiting for transfers between devices, exchange(): return lax.all_to_all(values, axes, split_axis=0, concat_axis=0, tiled=True)  79.9 us
    all_to_all x10, starting transfers between devices, exchange(): return lax.all_to_all(values, axes, split_axis=0, concat_axis=0, tiled=True)  75.8 us
    unnamed x215, local copies, waits for them, and re-layouts  45.5 us
    reduce_scatter x1, waiting for transfers between devices, per_device(): lax.psum_scatter(moe_sums.reshape(-1, D), ('fsdp', 'tp'), scatter_dimensi...  34.4 us
    ppermute x31, starting transfers between devices, partner(): return lax.ppermute(values, axis, [(i, i ^ bits) for i in range(count)])  34.1 us
    pallas_call x1, Pallas kernels, attention_backward(): pl.pallas_call(backward_kernel, out_shape=(jax.ShapeDtypeStruct((length,...  25 us
  transfers between devices with their start and end apart: 46, of which 21 were waited for; matrix products, arithmetic and copies ran while one was open for 19% of the time, Pallas kernels for 23%

profile of v3, /device:TPU:0, one launch (start us, length us, event | category | flops | bytes accessed | tf_op | source)
XLA Modules:
  0.0 826.8 jit_solution(4678326523908674741)
XLA Ops:
  7.3 2.4 multiply_reduce_fusion.10
  16.9 7.4 all-to-all-start
  26.3 3.0 copy.313
  29.3 7.0 multiply_reduce_fusion.1
  36.3 2.6 pad_maximum_fusion
  38.9 46.5 %collective-permute-done.1.refs_2_ = bf16[512,1536]{1,0:T(8,128)(2,1)} collective-permute-done((bf16[512,1536]{1,0:T(8,128)(2,1)S(1)}, bf16[512,1536]{1,0:T(8,128)(2,1)}, u32[]{:S(2)}, u32[]{:S(2)}) %collective-permute-start.1) | collective-permute-done | bytes 1572896 | tf_op jit(solution)/shard_map/ppermute | solution.py:73
  92.1 2.3 collective-permute-start.4
  100.5 11.8 %shard_map.528 = (bf16[2048,1536]{1,0:T(8,128)(2,1)}, bf16[3,2048,128]{2,1,0:T(8,128)(2,1)S(1)}, bf16[2048,128]{1,0:T(8,128)(2,1)S(1)}, bf16[64,2048]{1,0:T(8,12...) custom-call(s32[1]{0:T(128)} %bitcast.1.index_ref, bf16[512,1536]{1,0:T(8,128)(2,1)S(1)} %copy-done.2, ...), custom_call_target="tpu_custom_call" | custom-call | flops 3795000064 | bytes 1 | tf_op jit(solution)/shard_map/pallas_call | solution.py:133
  112.3 15.9 %collective-permute-done.4.refs_2_ = bf16[256,1664]{1,0:T(8,128)(2,1)} collective-permute-done((bf16[256,1664]{1,0:T(8,128)(2,1)}, bf16[256,1664]{1,0:T(8,128)(2,1)}, u32[]{:S(2)}, u32[]{:S(2)}) %collective-permute-start.4) | collective-permute-done | bytes 852000 | tf_op jit(solution)/shard_map/ppermute | solution.py:73
  128.2 4.2 collective-permute-start.7
  136.0 15.0 %collective-permute-done.7.refs_2_ = bf16[256,1664]{1,0:T(8,128)(2,1)} collective-permute-done((bf16[256,1664]{1,0:T(8,128)(2,1)}, bf16[256,1664]{1,0:T(8,128)(2,1)}, u32[]{:S(2)}, u32[]{:S(2)}) %collective-permute-start.7) | collective-permute-done | bytes 852000 | tf_op jit(solution)/shard_map/ppermute | solution.py:73
  152.5 24.8 %shard_map.529 = (bf16[8,192,256]{2,1,0:T(8,128)(2,1)}, f32[8,1,768]{2,1,0:T(1,128)S(1)}) custom-call(bf16[3,2048,128]{2,1,0:T(8,128)(2,1)S(1)} %get-tuple-element.121.q_ref, bf16[2048,128]{1,0:T(8,128)(2,1)S(1)} %get-tuple-element.122.k_ref, bf16[64,2048]{1,0:T(8,128)(2,1)S(1)} %get-tuple-element.123.vt_ref), custom_call_target="tpu_custom_call" | custom-call | flops 8625000448 | bytes 1 | tf_op jit(solution)/shard_map/pallas_call | solution.py:202
  179.7 3.5 all-to-all-start.1
  187.9 5.3 collective-permute-done.8.refs_3_
  193.3 21.4 %all-to-all-done.1.got_ref = bf16[8,192,256]{2,1,0:T(8,128)(2,1)S(1)} async-done(((bf16[8,192,256]{2,1,0:T(8,128)(2,1)}), bf16[8,192,256]{2,1,0:T(8,128)(2,1)S(1)}, u32[]{:S(2)}, u32[]{:S(2)}) %all-to-all-start.1) | async-done | bytes 786464 | tf_op jit(solution)/shard_map/all_to_all | solution.py:43
  215.8 2.3 copy-done.20
  224.2 2.6 collective-permute-start.14
  230.9 28.3 %collective-permute-done.12.refs_0_ = bf16[256,1536]{1,0:T(8,128)(2,1)} collective-permute-done((bf16[256,1536]{1,0:T(8,128)(2,1)S(1)}, bf16[256,1536]{1,0:T(8,128)(2,1)}, u32[]{:S(2)}, u32[]{:S(2)}) %collective-permute-start.12) | collective-permute-done | bytes 786464 | tf_op jit(solution)/shard_map/ppermute | solution.py:73
  260.1 2.3 collective-permute-done.10.refs_0_
  263.4 24.2 %shard_map.531 = (bf16[4,192,1536]{2,1,0:T(8,128)(2,1)}, bf16[4,192,512]{2,1,0:T(8,128)(2,1)}, bf16[4,192,1536]{2,1,0:T(8,128)(2,1)}, bf16[4,192,1024]{2,1,0:T(8...) custom-call(s32[3]{0:T(128)} %add_add_fusion.2.place_in_ref, ...), custom_call_target="tpu_custom_call" | custom-call | flops 8625000448 | bytes 1 | tf_op jit(solution)/shard_map/pallas_call | solution.py:397
  290.7 24.4 %shard_map.532 = (bf16[4,192,1536]{2,1,0:T(8,128)(2,1)}, bf16[4,192,512]{2,1,0:T(8,128)(2,1)}, bf16[4,192,1536]{2,1,0:T(8,128)(2,1)}, bf16[4,192,1024]{2,1,0:T(8...) custom-call(s32[3]{0:T(128)} %add_add_fusion.1.place_in_ref, ...), custom_call_target="tpu_custom_call", output_to_operand_aliasing={{4}: (7, {})} | custom-call | flops 8625000448 | bytes 1 | tf_op jit(solution)/shard_map/pallas_call | solution.py:397
  316.9 9.6 %collective-permute-done.20.refs_1_ = bf16[256,1536]{1,0:T(8,128)(2,1)S(1)} collective-permute-done((bf16[256,1536]{1,0:T(8,128)(2,1)}, bf16[256,1536]{1,0:T(8,128)(2,1)S(1)}, u32[]{:S(2)}, u32[]{:S(2)}) %collective-permute-start.20) | collective-permute-done | bytes 786464 | tf_op jit(solution)/shard_map/ppermute | solution.py:73
  327.5 24.8 %shard_map.533 = (bf16[4,192,1536]{2,1,0:T(8,128)(2,1)}, bf16[4,192,512]{2,1,0:T(8,128)(2,1)}, bf16[4,192,1536]{2,1,0:T(8,128)(2,1)}, bf16[4,192,1024]{2,1,0:T(8...) custom-call(s32[3]{0:T(128)} %add_add_fusion.3.place_in_ref, ...), custom_call_target="tpu_custom_call", output_to_operand_aliasing={{4}: (7, {})} | custom-call | flops 8625000448 | bytes 1 | tf_op jit(solution)/shard_map/pallas_call | solution.py:397
  352.8 8.9 %collective-permute-done.15 = bf16[256,1664]{1,0:T(8,128)(2,1)S(1)} collective-permute-done((bf16[256,1664]{1,0:T(8,128)(2,1)}, bf16[256,1664]{1,0:T(8,128)(2,1)S(1)}, u32[]{:S(2)}, u32[]{:S(2)}) %collective-permute-start.15) | collective-permute-done | bytes 852000 | tf_op jit(solution)/shard_map/ppermute | solution.py:73
  363.7 24.4 %shard_map.534 = (bf16[4,192,1536]{2,1,0:T(8,128)(2,1)}, bf16[4,192,512]{2,1,0:T(8,128)(2,1)}, bf16[4,192,1536]{2,1,0:T(8,128)(2,1)}, bf16[4,192,1024]{2,1,0:T(8...) custom-call(s32[3]{0:T(128)} %add_add_fusion.place_in_ref, ...), custom_call_target="tpu_custom_call", output_to_operand_aliasing={{4}: (7, {})} | custom-call | flops 8625000448 | bytes 1 | tf_op jit(solution)/shard_map/pallas_call | solution.py:397
  393.3 14.3 %collective-permute-done.21 = bf16[256,1664]{1,0:T(8,128)(2,1)S(1)} collective-permute-done((bf16[256,1664]{1,0:T(8,128)(2,1)}, bf16[256,1664]{1,0:T(8,128)(2,1)S(1)}, u32[]{:S(2)}, u32[]{:S(2)}) %collective-permute-start.21) | collective-permute-done | bytes 852000 | tf_op jit(solution)/shard_map/ppermute | solution.py:73
  409.8 21.9 %shard_map.535 = bf16[4,1536,1536]{2,1,0:T(8,128)(2,1)} custom-call(bf16[4,192,1536]{2,1,0:T(8,128)(2,1)} %get-tuple-element.158.refs_0_, bf16[4,192,1536]{2,1,0:T(8,128)(2,1)} %get-tuple-element.159.refs_1_, bf16[4,192,1536]{2,1,0:T(8,128)(2,1)} %get-tuple-element.160.refs_2_, bf16[4,192,1536]{2,1,0:T(8,128)(2,1)} %get-tuple-element.161.refs_3_, ...), custom_call_target="tpu_custom_call" | custom-call | flops 7590000128 | bytes 1 | tf_op jit(solution)/shard_map/pallas_call | solution.py:579
  432.5 20.1 %collective-permute-done.25.refs_2_ = bf16[256,1664]{1,0:T(8,128)(2,1)} collective-permute-done((bf16[256,1664]{1,0:T(8,128)(2,1)}, bf16[256,1664]{1,0:T(8,128)(2,1)}, u32[]{:S(2)}, u32[]{:S(2)}) %collective-permute-start.25) | collective-permute-done | bytes 852000 | tf_op jit(solution)/shard_map/ppermute | solution.py:73
  454.8 6.7 shard_map.536
  465.3 4.2 all-to-all-start.2
  469.6 16.8 %collective-permute-done.28.other_small_ref = bf16[1536,128]{1,0:T(8,128)(2,1)} collective-permute-done((bf16[1536,128]{1,0:T(8,128)(2,1)}, bf16[1536,128]{1,0:T(8,128)(2,1)}, u32[]{:S(2)}, u32[]{:S(2)}) %collective-permute-start.28) | collective-permute-done | bytes 393248 | tf_op jit(solution)/shard_map/ppermute | solution.py:73
  488.7 2.6 shard_map.537
  493.1 23.4 %all-to-all-start.3 = ((bf16[16,96,896]{2,1,0:T(8,128)(2,1)}), bf16[16,96,896]{2,1,0:T(8,128)(2,1)}, u32[]{:S(2)}, u32[]{:S(2)}) async-start(bf16[16,96,896]{2,1,0:T(8,128)(2,1)} %bitcast.111), calls=%async_computation.4 | async-start | bytes 5505024 | tf_op jit(solution)/shard_map/all_to_all | solution.py:43
  520.4 3.3 multiply_reduce_fusion.3
  528.3 25.0 %shard_map.538 = (bf16[2048,192]{1,0:T(8,128)(2,1)S(1)}, bf16[2048,128]{1,0:T(8,128)(2,1)S(1)}) custom-call(bf16[3,2048,128]{2,1,0:T(8,128)(2,1)S(1)} %copy-done.31, bf16[2048,128]{1,0:T(8,128)(2,1)S(1)} %copy-done.33, bf16[64,2048]{1,0:T(8,128)(2,1)S(1)} %copy-done.37, bf16[2048,64]{1,0:T(8,128)(2,1)S(1)} %copy-done.35, ...), custom_call_target="tpu_custom_call" | custom-call | flops 8625000448 | bytes 1 | tf_op jit(solution)/shard_map/pallas_call | solution.py:284
  557.6 6.1 convolution_convert_fusion
  563.7 5.7 all-to-all-done.3
  571.6 2.3 copy.315
  573.9 13.7 %all-to-all-start.4 = ((bf16[16,96,320]{2,1,0:T(8,128)(2,1)}), bf16[16,96,320]{2,1,0:T(8,128)(2,1)}, u32[]{:S(2)}, u32[]{:S(2)}) async-start(bf16[16,96,320]{2,1,0:T(8,128)(2,1)} %bitcast.126), calls=%async_computation.5 | async-start | bytes 2359296 | tf_op jit(solution)/shard_map/all_to_all | solution.py:43
  593.7 19.2 %all-to-all-done.4 = bf16[16,96,320]{2,1,0:T(8,128)(2,1)} async-done(((bf16[16,96,320]{2,1,0:T(8,128)(2,1)}), bf16[16,96,320]{2,1,0:T(8,128)(2,1)}, u32[]{:S(2)}, u32[]{:S(2)}) %all-to-all-start.4) | async-done | bytes 983072 | tf_op jit(solution)/shard_map/all_to_all | solution.py:43
  612.9 2.9 bitcast_convert_fusion
  618.6 2.6 copy.320
  621.2 4.4 all-to-all-start.5
  628.6 2.7 concatenate.44
  631.3 26.4 %all-to-all-done.5 = bf16[4,512,320]{1,2,0:T(8,128)(2,1)} async-done(((bf16[4,512,320]{1,2,0:T(8,128)(2,1)}), bf16[4,512,320]{1,2,0:T(8,128)(2,1)}, u32[]{:S(2)}, u32[]{:S(2)}) %all-to-all-start.5) | async-done | bytes 1310752 | tf_op jit(solution)/shard_map/all_to_all | solution.py:43
  658.7 7.1 all-to-all-start.6
  665.8 6.6 fusion.7
  674.3 3.6 all-to-all-done.6
  699.6 2.4 copy-done.21
  702.0 4.2 shard_map.539
  707.9 3.3 all-to-all-start.7
  712.0 3.5 all-to-all-done.7
  717.3 3.8 multiply_reduce_fusion.2
  721.1 4.8 multiply_reduce_fusion
  725.9 2.7 stack.111
  729.2 2.5 all-to-all-start.8
  731.8 3.0 fusion.2
  734.9 5.0 fusion.5
  741.1 6.2 all-to-all-start.9
  752.8 2.6 fusion.48
  759.3 2.5 fusion.47
  761.8 8.3 %fusion.45 = (bf16[4,384,1024]{2,1,0:T(8,128)(2,1)}, f32[4,384,1024]{2,1,0:T(8,128)}) fusion(f32[4,384,1024]{2,1,0:T(8,128)} %param.33, f32[4,384,1024]{2,1,0:T(8,128)} %get-tuple-element.540, f32[4]{0:T(128)S(1)} %copy-done.75, f32[4,1024]{1,0:T(4,128)S(1)} %fusion.16, f32[4,384]{1,0:T(4,128)S(1)} %get-tuple-element.609, f32[]{:T(128)} %bitcast.54), kind=kLoop, calls=%fused_computation.190 | loop fusion | flops 9437184 | bytes 22042644 | tf_op jit(solution)/shard_map/convert_element_type | solution.py:1064
  770.2 34.4 %reduce-scatter.3.cloned.1.call-done = bf16[256,1536]{1,0:T(8,128)(2,1)} async-done(((bf16[2048,1536]{1,0:T(8,128)(2,1)}), bf16[256,1536]{1,0:T(8,128)(2,1)}) %reduce-scatter.3.cloned.1.call-update) | async-done | bytes 786448 | tf_op jit(solution)/shard_map/reduce_scatter | solution.py:889
  809.4 4.7 fusion.44
  (412 shorter events, 142.8 us)
Async XLA Ops:
  7.2 78.2 %copy-start = (s32[512,8]{0,1:T(8,128)S(1)}, s32[512,8]{0,1:T(8,128)}, u32[]{:S(2)}) copy-start(s32[512,8]{0,1:T(8,128)} %param.27) | copy-start | bytes 49156
  7.2 207.4 %all-gather.5.cloned.1.call-start = ((), (), s32[]{:S(2)}) async-start(), calls=%async_computation.12 | async-start | bytes 4866048 | tf_op jit(solution)/shard_map/all_gather | solution.py:781
  16.9 68.5 %all-to-all-start = ((bf16[16,96,354]{2,1,0:T(8,128)(2,1)}), bf16[16,96,354]{2,1,0:T(8,128)(2,1)S(1)}, u32[]{:S(2)}, u32[]{:S(2)}) async-start(bf16[16,96,354]{2,1,0:T(8,128)(2,1)} %bitcast.127), calls=%async_computation | async-start | bytes 2359296 | tf_op jit(solution)/shard_map/all_to_all | solution.py:43
  24.2 238.3 %all-gather.7.cloned.1.call-start = ((), (), s32[]{:S(2)}) async-start(), calls=%async_computation.13 | async-start | bytes 23592960 | tf_op jit(solution)/shard_map/all_gather | solution.py:786
  24.3 61.1 %collective-permute-start.1 = (bf16[512,1536]{1,0:T(8,128)(2,1)S(1)}, bf16[512,1536]{1,0:T(8,128)(2,1)}, u32[]{:S(2)}, u32[]{:S(2)}) collective-permute-start(bf16[512,1536]{1,0:T(8,128)(2,1)S(1)} %copy-done.2), channel_id=1, source_target_pairs={{0,4},{2,6},{4,0},{6,2},{1,5},{3,7},{5,1},{7,3},{8,12},{10,14},{12... | collective-permute-start | bytes 4718600 | tf_op jit(solution)/shard_map/ppermute | solution.py:73
  38.9 50.8 %copy-start.11 = (bf16[256,1536]{1,0:T(8,128)(2,1)S(1)}, bf16[256,1536]{1,0:T(8,128)(2,1)}, u32[]{:S(2)}) copy-start(bf16[256,1536]{1,0:T(8,128)(2,1)} %refs_9_.1) | copy-start | bytes 2359300
  85.4 99.7 %copy-start.3 = (bf16[16,96,354]{2,1,0:T(8,128)(2,1)}, bf16[16,96,354]{2,1,0:T(8,128)(2,1)S(1)}, u32[]{:S(2)}) copy-start(bf16[16,96,354]{2,1,0:T(8,128)(2,1)S(1)} %all-to-all-done) | copy-start | bytes 3262468
  90.7 41.8 %collective-permute-start.3 = (bf16[256,1664]{1,0:T(8,128)(2,1)}, bf16[256,1664]{1,0:T(8,128)(2,1)}, u32[]{:S(2)}, u32[]{:S(2)}) collective-permute-start(bf16[256,1664]{1,0:T(8,128)(2,1)} %fusion.10.refs_2_), channel_id=1, source_target_pairs={{0,8},{8,0},{16,24},{24,16},{1,9},{9,1},{17,25},{25,17},{2,10},{10... | collective-permute-start | bytes 2555912 | tf_op jit(solution)/shard_map/ppermute | solution.py:73
  92.1 36.1 %collective-permute-start.4 = (bf16[256,1664]{1,0:T(8,128)(2,1)}, bf16[256,1664]{1,0:T(8,128)(2,1)}, u32[]{:S(2)}, u32[]{:S(2)}) collective-permute-start(bf16[256,1664]{1,0:T(8,128)(2,1)} %fusion.10.refs_2_), channel_id=1, source_target_pairs={{0,16},{8,24},{16,0},{24,8},{1,17},{9,25},{17,1},{25,9},{2,18},{10... | collective-permute-start | bytes 2555912 | tf_op jit(solution)/shard_map/ppermute | solution.py:73
  94.5 5.8 collective-permute-start
  94.5 6.0 collective-permute-start.2
  112.3 64.9 %copy-start.30 = (bf16[3,2048,128]{2,1,0:T(8,128)(2,1)}, bf16[3,2048,128]{2,1,0:T(8,128)(2,1)S(1)}, u32[]{:S(2)}) copy-start(bf16[3,2048,128]{2,1,0:T(8,128)(2,1)S(1)} %get-tuple-element.121.q_ref) | copy-start | bytes 4718596
  112.3 64.9 %copy-start.32 = (bf16[2048,128]{1,0:T(8,128)(2,1)}, bf16[2048,128]{1,0:T(8,128)(2,1)S(1)}, u32[]{:S(2)}) copy-start(bf16[2048,128]{1,0:T(8,128)(2,1)S(1)} %get-tuple-element.122.k_ref) | copy-start | bytes 1572868
  112.3 64.9 %copy-start.34 = (bf16[2048,64]{1,0:T(8,128)(2,1)}, bf16[2048,64]{1,0:T(8,128)(2,1)S(1)}, u32[]{:S(2)}) copy-start(bf16[2048,64]{1,0:T(8,128)(2,1)S(1)} %get-tuple-element.149.v_ref) | copy-start | bytes 786436
  112.3 64.9 %copy-start.36 = (bf16[64,2048]{1,0:T(8,128)(2,1)}, bf16[64,2048]{1,0:T(8,128)(2,1)S(1)}, u32[]{:S(2)}) copy-start(bf16[64,2048]{1,0:T(8,128)(2,1)S(1)} %get-tuple-element.148.kt_ref) | copy-start | bytes 786436
  128.2 22.8 %collective-permute-start.7 = (bf16[256,1664]{1,0:T(8,128)(2,1)}, bf16[256,1664]{1,0:T(8,128)(2,1)}, u32[]{:S(2)}, u32[]{:S(2)}) collective-permute-start(bf16[256,1664]{1,0:T(8,128)(2,1)} %collective-permute-done.4.refs_2_), channel_id=1, source_target_pairs={{0,8},{8,0},{16,24},{24,16},{1,9},{9,1},{17,25},{25,17},{2,10},{10... | collective-permute-start | bytes 2555912 | tf_op jit(solution)/shard_map/ppermute | solution.py:73
  132.5 45.4 %collective-permute-start.6 = (bf16[256,1664]{1,0:T(8,128)(2,1)}, bf16[256,1664]{1,0:T(8,128)(2,1)S(1)}, u32[]{:S(2)}, u32[]{:S(2)}) collective-permute-start(bf16[256,1664]{1,0:T(8,128)(2,1)} %collective-permute-done.3.refs_2_), channel_id=1, source_target_pairs={{0,1},{1,0},{2,3},{3,2},{4,5},{5,4},{6,7},{7,6},{8,9},{9,8},{10,11... | collective-permute-start | bytes 2555912 | tf_op jit(solution)/shard_map/ppermute | solution.py:73
  134.0 44.8 %collective-permute-start.5 = (bf16[256,1664]{1,0:T(8,128)(2,1)}, bf16[256,1664]{1,0:T(8,128)(2,1)S(1)}, u32[]{:S(2)}, u32[]{:S(2)}) collective-permute-start(bf16[256,1664]{1,0:T(8,128)(2,1)} %fusion.10.refs_2_), channel_id=1, source_target_pairs={{0,1},{1,0},{2,3},{3,2},{4,5},{5,4},{6,7},{7,6},{8,9},{9,8},{10,11... | collective-permute-start | bytes 2555912 | tf_op jit(solution)/shard_map/ppermute | solution.py:73
  134.5 58.8 %collective-permute-start.8 = (bf16[256,1664]{1,0:T(8,128)(2,1)}, bf16[256,1664]{1,0:T(8,128)(2,1)}, u32[]{:S(2)}, u32[]{:S(2)}) collective-permute-start(bf16[256,1664]{1,0:T(8,128)(2,1)} %collective-permute-done.4.refs_2_), channel_id=1, source_target_pairs={{0,1},{1,0},{2,3},{3,2},{4,5},{5,4},{6,7},{7,6},{8,9},{9,8},{10,11... | collective-permute-start | bytes 2555912 | tf_op jit(solution)/shard_map/ppermute | solution.py:73
  151.0 63.7 %collective-permute-start.9 = (bf16[256,1664]{1,0:T(8,128)(2,1)}, bf16[256,1664]{1,0:T(8,128)(2,1)}, u32[]{:S(2)}, u32[]{:S(2)}) collective-permute-start(bf16[256,1664]{1,0:T(8,128)(2,1)} %collective-permute-done.7.refs_2_), channel_id=1, source_target_pairs={{0,1},{1,0},{2,3},{3,2},{4,5},{5,4},{6,7},{7,6},{8,9},{9,8},{10,11... | collective-permute-start | bytes 2555912 | tf_op jit(solution)/shard_map/ppermute | solution.py:73
  179.7 35.0 %all-to-all-start.1 = ((bf16[8,192,256]{2,1,0:T(8,128)(2,1)}), bf16[8,192,256]{2,1,0:T(8,128)(2,1)S(1)}, u32[]{:S(2)}, u32[]{:S(2)}) async-start(bf16[8,192,256]{2,1,0:T(8,128)(2,1)} %get-tuple-element.128.out_ref), calls=%async_computation.1 | async-start | bytes 1572864 | tf_op jit(solution)/shard_map/all_to_all | solution.py:43
  183.2 179.6 %all-gather.9.cloned.1.call-start = ((), (), s32[]{:S(2)}) async-start(), calls=%async_computation.16 | async-start | bytes 5898240 | tf_op jit(solution)/shard_map/all_gather | solution.py:823
  223.5 64.1 %copy-start.40 = (f32[32,256]{1,0:T(8,128)}, f32[32,256]{1,0:T(8,128)S(1)}, u32[]{:S(2)}) copy-start(f32[32,256]{1,0:T(8,128)S(1)} %get-tuple-element.175.refs_6_) | copy-start | bytes 98308
  223.5 64.1 %copy-start.42 = (f32[32,256]{1,0:T(8,128)}, f32[32,256]{1,0:T(8,128)S(1)}, u32[]{:S(2)}) copy-start(f32[32,256]{1,0:T(8,128)S(1)} %get-tuple-element.176.refs_7_) | copy-start | bytes 98308
  223.6 476.0 %reduce-scatter.5.cloned.1.call-start = ((), (), s32[]{:S(2)}) async-start(), calls=%async_computation.15 | async-start | bytes 23592960 | tf_op jit(solution)/shard_map/reduce_scatter | solution.py:873
  223.8 35.4 %collective-permute-start.12 = (bf16[256,1536]{1,0:T(8,128)(2,1)S(1)}, bf16[256,1536]{1,0:T(8,128)(2,1)}, u32[]{:S(2)}, u32[]{:S(2)}) collective-permute-start(bf16[256,1536]{1,0:T(8,128)(2,1)S(1)} %get-tuple-element.135.refs_0_.refs_5_), channel_id=1, source_target_pairs={{0,8},{8,0},{16,24},{24,16},{1,9},{9,1},{17,25},{25,17},{2,10},{10... | collective-permute-start | bytes 2359304 | tf_op jit(solution)/shard_map/ppermute | solution.py:73
  224.2 38.3 %collective-permute-start.10 = (bf16[256,1536]{1,0:T(8,128)(2,1)S(1)}, bf16[256,1536]{1,0:T(8,128)(2,1)}, u32[]{:S(2)}, u32[]{:S(2)}) collective-permute-start(bf16[256,1536]{1,0:T(8,128)(2,1)S(1)} %get-tuple-element.135.refs_0_.refs_5_), channel_id=1, source_target_pairs={{0,16},{8,24},{16,0},{24,8},{1,17},{9,25},{17,1},{25,9},{2,18},{10... | collective-permute-start | bytes 2359304 | tf_op jit(solution)/shard_map/ppermute | solution.py:73
  224.2 38.2 %collective-permute-start.14 = (bf16[256,1536]{1,0:T(8,128)(2,1)S(1)}, bf16[256,1536]{1,0:T(8,128)(2,1)S(1)}, u32[]{:S(2)}, u32[]{:S(2)}) collective-permute-start(bf16[256,1536]{1,0:T(8,128)(2,1)S(1)} %get-tuple-element.135.refs_0_.refs_5_), channel_id=1, source_target_pairs={{0,1},{1,0},{2,3},{3,2},{4,5},{5,4},{6,7},{7,6},{8,9},{9,8},{10,11... | collective-permute-start | bytes 2359304 | tf_op jit(solution)/shard_map/ppermute | solution.py:73
  229.4 1.2 collective-permute-start.16
  230.6 57.5 %collective-permute-start.17 = (f32[1,32]{1,0:T(1,128)S(1)}, f32[1,32]{1,0:T(1,128)S(1)}, u32[]{:S(2)}, u32[]{:S(2)}) collective-permute-start(f32[1,32]{1,0:T(1,128)S(1)} %add.250), channel_id=1, source_target_pairs={{0,4},{2,6},{4,0},{6,2},{1,5},{3,7},{5,1},{7,3},{8,12},{10,14},{12... | collective-permute-start | bytes 392 | tf_op jit(solution)/shard_map/ppermute | solution.py:73
  259.2 31.5 %collective-permute-start.13 = (bf16[256,1536]{1,0:T(8,128)(2,1)}, bf16[256,1536]{1,0:T(8,128)(2,1)}, u32[]{:S(2)}, u32[]{:S(2)}) collective-permute-start(bf16[256,1536]{1,0:T(8,128)(2,1)} %collective-permute-done.12.refs_0_), channel_id=1, source_target_pairs={{0,1},{1,0},{2,3},{3,2},{4,5},{5,4},{6,7},{7,6},{8,9},{9,8},{10,11... | collective-permute-start | bytes 2359304 | tf_op jit(solution)/shard_map/ppermute | solution.py:73
  262.4 27.8 %collective-permute-start.11 = (bf16[256,1536]{1,0:T(8,128)(2,1)}, bf16[256,1536]{1,0:T(8,128)(2,1)}, u32[]{:S(2)}, u32[]{:S(2)}) collective-permute-start(bf16[256,1536]{1,0:T(8,128)(2,1)} %collective-permute-done.10.refs_0_), channel_id=1, source_target_pairs={{0,8},{8,0},{16,24},{24,16},{1,9},{9,1},{17,25},{25,17},{2,10},{10... | collective-permute-start | bytes 2359304 | tf_op jit(solution)/shard_map/ppermute | solution.py:73
  287.7 29.1 %collective-permute-start.19 = (bf16[256,1664]{1,0:T(8,128)(2,1)}, bf16[256,1664]{1,0:T(8,128)(2,1)S(1)}, u32[]{:S(2)}, u32[]{:S(2)}) collective-permute-start(bf16[256,1664]{1,0:T(8,128)(2,1)} %get-tuple-element.142), channel_id=1, source_target_pairs={{0,1},{1,0},{2,3},{3,2},{4,5},{5,4},{6,7},{7,6},{8,9},{9,8},{10,11... | collective-permute-start | bytes 2555912 | tf_op jit(solution)/shard_map/ppermute | solution.py:73
  288.6 38.0 %collective-permute-start.20 = (bf16[256,1536]{1,0:T(8,128)(2,1)}, bf16[256,1536]{1,0:T(8,128)(2,1)S(1)}, u32[]{:S(2)}, u32[]{:S(2)}) collective-permute-start(bf16[256,1536]{1,0:T(8,128)(2,1)} %collective-permute-done.10.refs_0_), channel_id=1, source_target_pairs={{0,1},{1,0},{2,3},{3,2},{4,5},{5,4},{6,7},{7,6},{8,9},{9,8},{10,11... | collective-permute-start | bytes 2359304 | tf_op jit(solution)/shard_map/ppermute | solution.py:73
  290.3 72.5 %collective-permute-start.18 = (bf16[256,1536]{1,0:T(8,128)(2,1)}, bf16[256,1536]{1,0:T(8,128)(2,1)S(1)}, u32[]{:S(2)}, u32[]{:S(2)}) collective-permute-start(bf16[256,1536]{1,0:T(8,128)(2,1)} %collective-permute-done.11.refs_0_), channel_id=1, source_target_pairs={{0,1},{1,0},{2,3},{3,2},{4,5},{5,4},{6,7},{7,6},{8,9},{9,8},{10,11... | collective-permute-start | bytes 2359304 | tf_op jit(solution)/shard_map/ppermute | solution.py:73
  315.0 46.7 %collective-permute-start.15 = (bf16[256,1664]{1,0:T(8,128)(2,1)}, bf16[256,1664]{1,0:T(8,128)(2,1)S(1)}, u32[]{:S(2)}, u32[]{:S(2)}) collective-permute-start(bf16[256,1664]{1,0:T(8,128)(2,1)} %get-tuple-element.138), channel_id=1, source_target_pairs={{0,1},{1,0},{2,3},{3,2},{4,5},{5,4},{6,7},{7,6},{8,9},{9,8},{10,11... | collective-permute-start | bytes 2555912 | tf_op jit(solution)/shard_map/ppermute | solution.py:73
  352.3 38.4 %collective-permute-start.23 = (bf16[256,1664]{1,0:T(8,128)(2,1)}, bf16[256,1664]{1,0:T(8,128)(2,1)}, u32[]{:S(2)}, u32[]{:S(2)}) collective-permute-start(bf16[256,1664]{1,0:T(8,128)(2,1)} %get-tuple-element.157), channel_id=1, source_target_pairs={{0,1},{1,0},{2,3},{3,2},{4,5},{5,4},{6,7},{7,6},{8,9},{9,8},{10,11... | collective-permute-start | bytes 2555912 | tf_op jit(solution)/shard_map/ppermute | solution.py:73
  388.1 19.4 %collective-permute-start.21 = (bf16[256,1664]{1,0:T(8,128)(2,1)}, bf16[256,1664]{1,0:T(8,128)(2,1)S(1)}, u32[]{:S(2)}, u32[]{:S(2)}) collective-permute-start(bf16[256,1664]{1,0:T(8,128)(2,1)} %get-tuple-element.152), channel_id=1, source_target_pairs={{0,1},{1,0},{2,3},{3,2},{4,5},{5,4},{6,7},{7,6},{8,9},{9,8},{10,11... | collective-permute-start | bytes 2555912 | tf_op jit(solution)/shard_map/ppermute | solution.py:73
  388.6 43.9 %collective-permute-start.24 = (bf16[256,1664]{1,0:T(8,128)(2,1)}, bf16[256,1664]{1,0:T(8,128)(2,1)}, u32[]{:S(2)}, u32[]{:S(2)}) collective-permute-start(bf16[256,1664]{1,0:T(8,128)(2,1)} %add_convert_fusion.3), channel_id=1, source_target_pairs={{0,8},{8,0},{16,24},{24,16},{1,9},{9,1},{17,25},{25,17},{2,10},{10... | collective-permute-start | bytes 2555912 | tf_op jit(solution)/shard_map/ppermute | solution.py:73
  392.9 59.6 %collective-permute-start.25 = (bf16[256,1664]{1,0:T(8,128)(2,1)}, bf16[256,1664]{1,0:T(8,128)(2,1)}, u32[]{:S(2)}, u32[]{:S(2)}) collective-permute-start(bf16[256,1664]{1,0:T(8,128)(2,1)} %add_convert_fusion), channel_id=1, source_target_pairs={{0,16},{8,24},{16,0},{24,8},{1,17},{9,25},{17,1},{25,9},{2,18},{10... | collective-permute-start | bytes 2555912 | tf_op jit(solution)/shard_map/ppermute | solution.py:73
  408.7 43.9 %collective-permute-start.26 = (bf16[256,1664]{1,0:T(8,128)(2,1)}, bf16[256,1664]{1,0:T(8,128)(2,1)}, u32[]{:S(2)}, u32[]{:S(2)}) collective-permute-start(bf16[256,1664]{1,0:T(8,128)(2,1)} %add_convert_fusion.1), channel_id=1, source_target_pairs={{0,24},{8,16},{16,8},{24,0},{1,25},{9,17},{17,9},{25,1},{2,26},{10... | collective-permute-start | bytes 2555912 | tf_op jit(solution)/shard_map/ppermute | solution.py:73
  409.5 22.2 %collective-permute-start.22 = (bf16[256,768]{1,0:T(8,128)(2,1)S(1)}, bf16[256,768]{1,0:T(8,128)(2,1)S(1)}, u32[]{:S(2)}, u32[]{:S(2)}) collective-permute-start(bf16[256,768]{1,0:T(8,128)(2,1)S(1)} %copy-done.25), channel_id=1, source_target_pairs={{0,1},{1,0},{2,3},{3,2},{4,5},{5,4},{6,7},{7,6},{8,9},{9,8},{10,11... | collective-permute-start | bytes 1179656 | tf_op jit(solution)/shard_map/ppermute | solution.py:73
  463.2 23.1 %collective-permute-start.27 = (bf16[256,1536]{1,0:T(8,128)(2,1)S(1)}, bf16[256,1536]{1,0:T(8,128)(2,1)S(1)}, u32[]{:S(2)}, u32[]{:S(2)}) collective-permute-start(bf16[256,1536]{1,0:T(8,128)(2,1)S(1)} %get-tuple-element.178.low_ref), channel_id=1, source_target_pairs={{0,1},{1,0},{2,3},{3,2},{4,5},{5,4},{6,7},{7,6},{8,9},{9,8},{10,11... | collective-permute-start | bytes 2359304 | tf_op jit(solution)/shard_map/ppermute | solution.py:73
  464.9 21.4 %collective-permute-start.28 = (bf16[1536,128]{1,0:T(8,128)(2,1)}, bf16[1536,128]{1,0:T(8,128)(2,1)}, u32[]{:S(2)}, u32[]{:S(2)}) collective-permute-start(bf16[1536,128]{1,0:T(8,128)(2,1)} %copy-done.28), channel_id=1, source_target_pairs={{0,1},{1,0},{2,3},{3,2},{4,5},{5,4},{6,7},{7,6},{8,9},{9,8},{10,11... | collective-permute-start | bytes 1179656 | tf_op jit(solution)/shard_map/ppermute | solution.py:73
  465.3 27.8 %all-to-all-start.2 = ((bf16[8,192,256]{2,1,0:T(8,128)(2,1)}), bf16[8,192,256]{2,1,0:T(8,128)(2,1)}, u32[]{:S(2)}, u32[]{:S(2)}) async-start(bf16[8,192,256]{2,1,0:T(8,128)(2,1)} %copy-done.9), calls=%async_computation.2 | async-start | bytes 1572864 | tf_op jit(solution)/shard_map/all_to_all | solution.py:43
  493.1 76.2 %all-to-all-start.3 = ((bf16[16,96,896]{2,1,0:T(8,128)(2,1)}), bf16[16,96,896]{2,1,0:T(8,128)(2,1)}, u32[]{:S(2)}, u32[]{:S(2)}) async-start(bf16[16,96,896]{2,1,0:T(8,128)(2,1)} %bitcast.111), calls=%async_computation.4 | async-start | bytes 5505024 | tf_op jit(solution)/shard_map/all_to_all | solution.py:43
  516.6 288.1 %reduce-scatter.3.cloned.1.call-start = ((), (), s32[]{:S(2)}) async-start(), calls=%async_computation.14 | async-start | bytes 7077888 | tf_op jit(solution)/shard_map/reduce_scatter | solution.py:889
  555.8 31.9 %collective-permute-start.29 = (bf16[256,1536]{1,0:T(8,128)(2,1)}, bf16[256,1536]{1,0:T(8,128)(2,1)}, u32[]{:S(2)}, u32[]{:S(2)}) collective-permute-start(bf16[256,1536]{1,0:T(8,128)(2,1)} %get-tuple-element.197), channel_id=1, source_target_pairs={{0,1},{1,0},{2,3},{3,2},{4,5},{5,4},{6,7},{7,6},{8,9},{9,8},{10,11... | collective-permute-start | bytes 2359304 | tf_op jit(solution)/shard_map/ppermute | solution.py:73
  573.9 39.0 %all-to-all-start.4 = ((bf16[16,96,320]{2,1,0:T(8,128)(2,1)}), bf16[16,96,320]{2,1,0:T(8,128)(2,1)}, u32[]{:S(2)}, u32[]{:S(2)}) async-start(bf16[16,96,320]{2,1,0:T(8,128)(2,1)} %bitcast.126), calls=%async_computation.5 | async-start | bytes 2359296 | tf_op jit(solution)/shard_map/all_to_all | solution.py:43
  593.7 165.6 %copy-start.51 = (f32[768,96]{0,1:T(8,128)}, f32[768,96]{0,1:T(8,128)S(1)}, u32[]{:S(2)}) copy-start(f32[768,96]{0,1:T(8,128)S(1)} %get-tuple-element.616) | copy-start | bytes 884740
  621.2 36.5 %all-to-all-start.5 = ((bf16[4,512,320]{1,2,0:T(8,128)(2,1)}), bf16[4,512,320]{1,2,0:T(8,128)(2,1)}, u32[]{:S(2)}, u32[]{:S(2)}) async-start(bf16[4,512,320]{1,2,0:T(8,128)(2,1)} %copy.320), calls=%async_computation.6 | async-start | bytes 2621440 | tf_op jit(solution)/shard_map/all_to_all | solution.py:43
  626.9 71.8 %copy-start.52 = (f32[96,4,64]{0,2,1:T(8,128)}, f32[96,4,64]{0,2,1:T(8,128)S(1)}, u32[]{:S(2)}) copy-start(f32[96,4,64]{0,2,1:T(8,128)S(1)} %copy.317) | copy-start | bytes 294916
  627.0 71.7 %copy-start.53 = (f32[96,4,64]{0,2,1:T(8,128)}, f32[96,4,64]{0,2,1:T(8,128)S(1)}, u32[]{:S(2)}) copy-start(f32[96,4,64]{0,2,1:T(8,128)S(1)} %copy.318) | copy-start | bytes 294916
  658.7 19.2 %all-to-all-start.6 = ((f32[32,1,2688]{2,1,0:T(1,128)}), f32[32,1,2688]{2,1,0:T(1,128)S(1)}, u32[]{:S(2)}, u32[]{:S(2)}) async-start(f32[32,1,2688]{2,1,0:T(1,128)} %broadcast_in_dim.35), calls=%async_computation.7 | async-start | bytes 688128 | tf_op jit(solution)/shard_map/all_to_all | solution.py:43
  672.4 59.4 %collective-permute-start.30 = (bf16[512,1536]{1,0:T(8,128)(2,1)}, bf16[512,1536]{1,0:T(8,128)(2,1)}, u32[]{:S(2)}, u32[]{:S(2)}) collective-permute-start(bf16[512,1536]{1,0:T(8,128)(2,1)} %fusion.7), channel_id=1, source_target_pairs={{0,1},{1,0},{2,3},{3,2},{4,5},{5,4},{6,7},{7,6},{8,9},{9,8},{10,11... | collective-permute-start | bytes 4718600 | tf_op jit(solution)/shard_map/ppermute | solution.py:73
  707.9 7.7 all-to-all-start.7
  729.2 10.7 %all-to-all-start.8 = ((f32[32,1,7]{2,1,0:T(1,128)}), f32[32,1,7]{2,1,0:T(1,128)S(1)}, u32[]{:S(2)}, u32[]{:S(2)}) async-start(f32[32,1,7]{2,1,0:T(1,128)} %broadcast_in_dim.38), calls=%async_computation.10 | async-start | bytes 32768 | tf_op jit(solution)/shard_map/all_to_all | solution.py:43
  741.1 72.9 %all-to-all-start.9 = ((f32[32,1,4608]{2,1,0:T(1,128)}), f32[32,1,4608]{2,1,0:T(1,128)S(1)}, u32[]{:S(2)}, u32[]{:S(2)}) async-start(f32[32,1,4608]{2,1,0:T(1,128)} %broadcast_in_dim.40), calls=%async_computation.11 | async-start | bytes 1179648 | tf_op jit(solution)/shard_map/all_to_all | solution.py:43
  761.8 42.9 %copy-start.88 = (f32[96]{0:T(128)S(1)}, f32[96]{0:T(128)}, u32[]{:S(2)}) copy-start(f32[96]{0:T(128)} %get-tuple-element.602) | copy-start | bytes 1156
  761.8 42.9 %copy-start.92 = (f32[96]{0:T(128)S(1)}, f32[96]{0:T(128)}, u32[]{:S(2)}) copy-start(f32[96]{0:T(128)} %param.36) | copy-start | bytes 1156
  761.8 44.2 %copy-start.87 = (f32[96]{0:T(128)S(1)}, f32[96]{0:T(128)}, u32[]{:S(2)}) copy-start(f32[96]{0:T(128)} %param.35) | copy-start | bytes 1156
  761.8 44.2 %copy-start.89 = (f32[96]{0:T(128)S(1)}, f32[96]{0:T(128)}, u32[]{:S(2)}) copy-start(f32[96]{0:T(128)} %get-tuple-element.604) | copy-start | bytes 1156
  761.8 44.2 %copy-start.90 = (f32[96]{0:T(128)S(1)}, f32[96]{0:T(128)}, u32[]{:S(2)}) copy-start(f32[96]{0:T(128)} %get-tuple-element.605) | copy-start | bytes 1156
  761.8 45.3 %copy-start.6 = (f32[256,1536]{1,0:T(8,128)S(1)}, f32[256,1536]{1,0:T(8,128)}, u32[]{:S(2)}) copy-start(f32[256,1536]{1,0:T(8,128)} %copy-done.5) | copy-start | bytes 4718596
  (79 other events, 915.9 us)
Sparse Core Ops, SparseCore 0:
  11.5 84.4 all-gather.4
  98.2 129.7 all-gather.6
  229.5 37.4 all-gather.8
  463.4 208.3 reduce-scatter.4
  675.6 128.9 reduce-scatter.2

commit v4 on v3

--- a/solution.py
+++ b/solution.py
@@ -312,9 +312,10 @@
     row_refs, cot_refs = refs[:sources], refs[sources : 2 * sources]
     router_ref, w_ref = refs[2 * sources : 2 * sources + 2]
     refs = refs[2 * sources + 2 + unread :]
-    x_ref, hid_ref, ds_ref, dgu_ref, moe_ref = refs[:5]
-    dsum_refs = refs[5 : 5 + sources]
-    moe_acc, dsum_acc, combine_ref, place_ref = refs[5 + sources :]
+    x_ref, hid_ref, ds_ref, dgu_ref = refs[:4]
+    moe_refs = refs[4 : 4 + sources]
+    dsum_refs = refs[4 + sources : 4 + 2 * sources]
+    moe_acc, dsum_acc, combine_ref, place_ref = refs[4 + 2 * sources :]
     expert = pl.program_id(0)
     tokens, width = row_refs[0].shape
     cap = x_ref.shape[1] // sources
@@ -382,7 +383,7 @@
     @pl.when(expert == pl.num_programs(0) - 1)
     def _():
         for s in range(sources):
-            moe_ref[0, place_in_ref[2] ^ s] = moe_acc[s].astype(bf16)
+            moe_refs[s][0] = moe_acc[s].astype(bf16)
             dsum_refs[s][...] = dsum_acc[s].astype(bf16)
 
 
@@ -391,7 +392,7 @@
     tokens, width = rows[0].shape
     experts = weights.shape[0]
     held = sources * cap
-    carried = ([] if moe is None else [moe]) + needed
+    carried = [*moe, *needed]
     each = lambda *shape: pl.BlockSpec((1,) + shape, lambda e, s: (e,) + (0,) * len(shape))
     fixed = lambda *shape: pl.BlockSpec(shape, lambda e, s: (0,) * len(shape))
     got = pl.pallas_call(
@@ -402,7 +403,7 @@
             jax.ShapeDtypeStruct((experts, held, width), bf16),
             jax.ShapeDtypeStruct((experts, held, 2 * FFE), bf16),
         )
-        + (jax.ShapeDtypeStruct((slots, sources, tokens, width), bf16),)
+        + (jax.ShapeDtypeStruct((slots, tokens, width), bf16),) * sources
         + (jax.ShapeDtypeStruct((tokens, width + EXTRA), bf16),) * sources,
         grid_spec=pltpu.PrefetchScalarGridSpec(
             num_scalar_prefetch=1,
@@ -412,7 +413,7 @@
             + [fixed(EXPERTS, width), each(width, 3 * FFE)]
             + [pl.BlockSpec(memory_space=pl.ANY)] * len(carried),
             out_specs=(each(held, width), each(held, FFE), each(held, width), each(held, 2 * FFE))
-            + (pl.BlockSpec((1, sources, tokens, width), lambda e, s: (s[1], 0, 0, 0)),)
+            + (pl.BlockSpec((1, tokens, width), lambda e, s: (s[1], 0, 0)),) * sources
             + (fixed(tokens, width + EXTRA),) * sources,
             scratch_shapes=[
                 pltpu.VMEM((sources, tokens, width), f32),
@@ -423,9 +424,9 @@
         ),
         compiler_params=pltpu.CompilerParams(vmem_limit_bytes=56 * 2**20),
         cost_estimate=lasting(7.5),
-        input_output_aliases={2 * sources + 3: 4} if moe is not None else {},
+        input_output_aliases={2 * sources + 3 + n: 4 + n for n in range(len(moe))},
     )(place, *rows, *cots, router_t, weights, *carried)
-    return got[:4], got[4], got[5:]
+    return got[:4], got[4 : 4 + sources], got[4 + sources :]
 
 
 def middle_kernel(
@@ -620,6 +621,78 @@
         compiler_params=pltpu.CompilerParams(vmem_limit_bytes=40 * 2**20),
         cost_estimate=lasting(4),
     )(grads)
+
+
+def dense_kernel(
+    at_ref, mean_ref, got_ref, qkv_ref, out_ref, router_ref, gain_ref, old_ref, colq_ref, rowo_ref, colr_ref,
+    rows_tot, colq_tot, rowo_tot, last_tot, squares_ref,
+):
+    flat, tp = at_ref[0], at_ref[1]
+    devices = got_ref.shape[0] // 2
+    got = got_ref[...]
+    even, odd = (
+        jnp.concatenate([got[2 * n + t : 2 * n + t + 1] for n in range(devices)], axis=0)
+        for t in range(2)
+    )
+    both = even + odd
+    wide_q, wide_o = colq_tot.shape[1], rowo_tot.shape[1]
+    start = wide_q + wide_o
+    cut = lambda a, n: a[:, start + n * 128 : start + (n + 1) * 128]
+    down = lambda a: jnp.sum(a, axis=0, keepdims=True)
+    blend = lambda old, total, n: decay * old + (1.0 - decay) * (total / n + floor_sq)
+    for row, half in enumerate((even, odd)):
+        colq_tot[row : row + 1] = down(half[:, :wide_q])
+        rowo_tot[row : row + 1] = down(half[:, wide_q:start])
+    rows_tot[...] = jnp.concatenate([cut(both, 0), cut(both, 1), cut(both, 2), cut(even, 3)], axis=1)
+    lane = lax.broadcasted_iota(jnp.int32, (1, 128), 1)
+    last = jnp.where(lane < EXPERTS, down(cut(even, 4)), down(cut(both, 4)))
+    last_tot[...] = last
+    own = rows_tot[pl.ds(flat, 1), :]
+    high = qkv_ref.shape[0]
+    stand = lambda v: jnp.broadcast_to(v, (8, 128)).T[:high, :1]
+    old = old_ref[...]
+    qkv_width = (HEADS + 2 * KV_HEADS) * HEAD
+
+    row = blend(old[0:1], own[:, :128], qkv_width)
+    col = blend(colq_ref[...], colq_tot[pl.ds(tp, 1), :], D)
+    mean = blend(mean_ref[0], jnp.sum(cut(both, 0)) / D, qkv_width)
+    change = qkv_ref[...] * lax.rsqrt(stand(row) * col / mean)
+    square_qkv = jnp.sum(change * change)
+    row = blend(rowo_ref[...], rowo_tot[pl.ds(tp, 1), :], D)
+    col = blend(old[1:2], own[:, 256:384], HEADS * HEAD)
+    mean = blend(mean_ref[1], jnp.sum(rowo_tot[...]) / (HEADS * HEAD), D)
+    change = out_ref[...] * lax.rsqrt(stand(col) * row / mean)
+    square_out = jnp.sum(change * change)
+    row = blend(old[2:3], own[:, 384:], EXPERTS)
+    col = blend(colr_ref[...], last[:, :EXPERTS], D)
+    mean = blend(mean_ref[2], jnp.sum(cut(even, 3)) / D, EXPERTS)
+    change = router_ref[...] * lax.rsqrt(stand(row) * col / mean)
+    square_router = jnp.sum(change * change)
+    gain = own[:, 128:256]
+    change = gain * lax.rsqrt(blend(old[3:4], gain * gain, 1.0))
+    square_one = jnp.sum(change * change)
+    gain = gain_ref[...]
+    change = gain * lax.rsqrt(blend(old[4:5], gain * gain, 1.0))
+    square_two = jnp.sum(change * change)
+    once = jnp.where(tp == 0, 1.0, 0.0)
+    squares = jnp.where(lane == 0, square_qkv, 0.0) + jnp.where(lane == 1, square_out, 0.0)
+    for n, square in ((2, square_router), (3, square_one), (4, square_two)):
+        squares = squares + jnp.where(lane == n, square * once, 0.0)
+    squares_ref[...] = squares
+
+
+def dense_moments(at, means, got, qkv, out_t, router, gain, old, col_qkv, row_out, col_router):
+    devices = got.shape[0] // 2
+    shapes = [(devices, 512), (2, col_qkv.shape[1]), (2, row_out.shape[1]), (1, 128), (1, 128)]
+    return pl.pallas_call(
+        dense_kernel,
+        out_shape=tuple(jax.ShapeDtypeStruct(s, f32) for s in shapes),
+        in_specs=[pl.BlockSpec(memory_space=pltpu.SMEM)] * 2
+        + [pl.BlockSpec(memory_space=pltpu.VMEM)] * 9,
+        out_specs=(pl.BlockSpec(memory_space=pltpu.VMEM),) * 5,
+        compiler_params=pltpu.CompilerParams(vmem_limit_bytes=24 * 2**20),
+        cost_estimate=lasting(4),
+    )(at, means, got, qkv, out_t, router, gain, old, col_qkv, row_out, col_router)
 
 
 def half_sum(parts, count):
@@ -823,7 +896,7 @@
     w_tree = lax.all_gather(after(w_got, act2)[:, :own_cols], "ctx", axis=0, tiled=False)
     row_slots = spread(after(act2, *[pair[1] for pair in grad_slots]))
 
-    kept, d_sums, moe_sums = [], [], None
+    kept, d_sums, moe_sums = [], [], []
     for j in range(fsdp_count):
         rows = list(row_slots[j])
         if j == 0:
@@ -834,7 +907,7 @@
             rows[0] = after(rows[0], d_sums[j - 2], *(pair[0] for pair in row_slots[3:]))
         if j == 3:
             rows[0] = after(rows[0], fraction)
-        place = jnp.stack([owner_index * local_experts, fsdp_index ^ j, tp_index])
+        place = jnp.stack([owner_index * local_experts, fsdp_index ^ j])
         held, moe_sums, d_out = expert_slot(
             place.astype(jnp.int32),
             rows,
@@ -879,16 +952,17 @@
     d_attended = after(d_attended, g_out_part)
     g_out_got = exchange(g_out_part.reshape(dense_parts, dense_rows, -1), ("fsdp", "ctx"))
     g_out_got = jnp.sum(g_out_got.astype(f32), axis=0)
-    g_out = g_out_got[:, :out_rows].T
+    g_out_t = g_out_got[:, :out_rows]
+    g_out = g_out_t.T
     g_small = g_out_got[:, out_rows : out_rows + HEAD] + g_out_got[:, out_rows + HEAD :]
     g_router = g_small[:, :EXPERTS]
     g_gain2 = g_small[:, EXPERTS]
 
+    moe_theirs = partner(after(moe_sums[1], d_attended), "tp", 1, tp_count)
     d_q, d_kv = attention_backward(query, key, key_t, value, d_attended, attended_own, logs)
-    moe_sums = after(moe_sums, d_q)
-    moe = lax.psum_scatter(
-        moe_sums.reshape(-1, D), ("fsdp", "tp"), scatter_dimension=0, tiled=True
-    )
+    moe = moe_sums[0].astype(f32) + moe_theirs.astype(f32)
+    moe = after(moe.astype(bf16), d_q)
+    moe_rows = lax.psum_scatter(moe.reshape(-1, D), "fsdp", scatter_dimension=0, tiled=True)
     d_qkv = jnp.concatenate([d_q, d_kv], axis=1)
     g_qkv_part = after(dot("td,tc->dc", act1, d_qkv).astype(bf16), g_out_got)
     g_qkv_got = exchange(g_qkv_part.reshape(dense_parts, dense_rows, own_cols), ("fsdp", "ctx"))
@@ -914,23 +988,8 @@
     sizes = [p.shape[0] for p in pieces]
     padded = [-(-s // 128) * 128 for s in sizes]
     message = jnp.concatenate([jnp.pad(p, (0, n - p.shape[0])) for p, n in zip(pieces, padded)])
-    message = after(message, d_qkv_all)
-    got = share(message, count).reshape(dense_parts, tp_count, -1)
-    shares, at = [], 0
-    for size, room in zip(sizes, padded):
-        shares.append(got[..., at : at + size])
-        at += room
-    tot_col_qkv = jnp.sum(shares[0], axis=0).reshape(-1)
-    tot_row_out = jnp.sum(shares[1], axis=0).reshape(-1)
-    tot_row_qkv = jnp.sum(shares[2], axis=1).reshape(-1)
-    g_gain1 = lax.dynamic_index_in_dim(jnp.sum(shares[3], axis=1), flat_index, 0, keepdims=False)
-    tot_col_out = jnp.sum(shares[4], axis=1).reshape(-1)
-    tot_row_router = shares[5][:, 0].reshape(-1)
-    tot_col_router = jnp.sum(shares[6][:, 0, :EXPERTS], axis=0)
-    last_totals = jnp.sum(shares[6][..., EXPERTS:], axis=(0, 1))
-    prob_totals = last_totals[:EXPERTS]
-    master_totals = last_totals[EXPERTS:]
-
+    message = after(message, d_qkv_all, moe)
+    got = after(share(message, count), expert_sums)
     own_row_gu = expert_sums[:, :ctx_rows]
     start = (owner_index * local_experts, ctx_index * ctx_rows)
     start = tuple(jnp.asarray(s, jnp.int32) for s in start)
@@ -939,7 +998,7 @@
     gu_sum = jnp.pad(jnp.sum(rows_gu, axis=1, keepdims=True), ((0, 0), (0, 127)))
     over_ctx = jnp.concatenate([expert_sums[:, 2 * ctx_rows :], gu_sum], axis=1)
     over_ctx = jnp.broadcast_to(over_ctx[None], (ctx_count,) + over_ctx.shape)
-    over_ctx = jnp.sum(exchange(after(over_ctx, got), "ctx"), axis=0)
+    over_ctx = jnp.sum(exchange(over_ctx, "ctx"), axis=0)
     mean_gu = over_ctx[:, 3 * FFE] / D
     own_col_gu = over_ctx[:, : 2 * FFE]
     own_row_down = over_ctx[:, 2 * FFE : 3 * FFE]
@@ -960,12 +1019,47 @@
     )
     squares_gu = jnp.sum(change_gate_up * change_gate_up)
     squares_dn = jnp.sum(change_down * change_down)
+    at_own = lambda a: lax.dynamic_slice_in_dim(a, flat_index * dense_rows, dense_rows, 0)
+    lanes_of = lambda a: jnp.pad(a, (0, 128 - dense_rows))
+    old_own = [at_own(row_qkv), at_own(col_out), at_own(row_router), second_attn, second_moe]
+    old_own = jnp.pad(jnp.stack([lanes_of(a) for a in old_own]), ((0, 3), (0, 0)))
+    tot_rows, tot_colq, tot_rowo, tot_last, dense_squares = dense_moments(
+        jnp.stack([flat_index, tp_index]).astype(jnp.int32),
+        jnp.stack([jnp.mean(row_qkv), jnp.mean(row_out), jnp.mean(row_router)]),
+        got,
+        g_qkv,
+        g_out_t,
+        g_router,
+        lanes_of(g_gain2)[None],
+        old_own,
+        lax.dynamic_slice_in_dim(col_qkv, tp_index * qkv_cols, qkv_cols, 0)[None],
+        lax.dynamic_slice_in_dim(row_out, tp_index * out_rows, out_rows, 0)[None],
+        col_router[None],
+    )
+    square_sums = jnp.concatenate(
+        [dense_squares[0, :3], squares_gu[None], squares_dn[None], dense_squares[0, 3:5]]
+    )
+    square_totals = jnp.sum(share(square_sums, count), axis=0)
+    tot_rows, tot_colq, tot_rowo, tot_last = (
+        after(t, square_totals) for t in (tot_rows, tot_colq, tot_rowo, tot_last)
+    )
+    piece = lambda n: tot_rows[:, n * 128 : n * 128 + dense_rows].reshape(-1)
+    tot_row_qkv, tot_col_out, tot_row_router = piece(0), piece(2), piece(3)
+    g_gain1 = lax.dynamic_slice_in_dim(piece(1), flat_index * dense_rows, dense_rows, 0)
+    tot_col_qkv = tot_colq.reshape(-1)
+    tot_row_out = tot_rowo.reshape(-1)
+    tot_col_router = tot_last[0, :EXPERTS]
+    last_totals = tot_last[0, EXPERTS : 2 * EXPERTS + 7]
+    prob_totals = last_totals[:EXPERTS]
+    master_totals = last_totals[EXPERTS:]
+
     d_act1 = d_act1_low.astype(f32) + after(d_act1_other, over_ctx).astype(f32)
     own_inputs = inputs.astype(f32)
     d_inputs_attn, _ = norm_backward(own_inputs, inv_rms(own_inputs), gain_one, d_act1)
-    rest = after(rest, d_qkv)
+    rest = after(rest, d_qkv_all)
     d_x1 = low.astype(f32) + rest.astype(f32)
-    other_x1 = other_low.astype(f32) + partner(rest, "tp", 1, tp_count).astype(f32)
+    other_rest = after(partner(rest, "tp", 1, tp_count), over_ctx)
+    other_x1 = other_low.astype(f32) + other_rest.astype(f32)
     d_x1 = in_order(d_x1, other_x1, tp_index, 0).reshape(tok_rows, D)
     grad_inputs = d_x1 + d_inputs_attn
 
@@ -992,18 +1086,6 @@
     second_moe_new = decay * second_moe + (1.0 - decay) * (g_gain2 * g_gain2 + floor_sq)
     change_gain1 = g_gain1 * lax.rsqrt(second_attn_new)
     change_gain2 = g_gain2 * lax.rsqrt(second_moe_new)
-    square_sums = jnp.stack(
-        [
-            jnp.sum(change_qkv * change_qkv),
-            jnp.sum(change_out * change_out),
-            keep_once * jnp.sum(change_router * change_router),
-            squares_gu,
-            squares_dn,
-            keep_once * jnp.sum(change_gain1 * change_gain1),
-            keep_once * jnp.sum(change_gain2 * change_gain2),
-        ]
-    )
-    square_totals = jnp.sum(share(square_sums, count), axis=0)
     quarter = lambda a: lax.dynamic_slice_in_dim(
         a, ctx_index * (a.shape[1] // ctx_count), a.shape[1] // ctx_count, 1
     )
@@ -1039,7 +1121,7 @@
     new_down = w_down - step_scale[4] * change_down
     new_gain1 = gain_attn - step_scale[5] * change_gain1
     new_gain2 = gain_moe - step_scale[6] * change_gain2
-    layer_out = (x_one + after(moe, update_rms, new_gate_up, grad_inputs).astype(f32)).astype(bf16)
+    layer_out = (x_one + after(moe_rows, update_rms, new_gate_up, grad_inputs).astype(f32)).astype(bf16)
     return (
         layer_out,
         grad_inputs,

time: 838 us -> 805 us (0.961)
  waiting for transfers between devices: 299 us -> 244 us
  local copies, waits for them, and re-layouts: 72.6 us -> 89.4 us
    reduce_scatter x1, waiting for transfers between devices: 34.4 us -> 0.02 us  [per_device(): lax.psum_scatter(moe.reshape(-1, D), 'fsdp', scatter_dimension=0, tiled=T...]
    all_to_all x10, waiting for transfers between devices: 79.9 us -> 48.1 us  [exchange(): return lax.all_to_all(values, axes, split_axis=0, concat_axis=0, tiled=True)]
    ppermute x31 -> x32, waiting for transfers between devices: 184 us -> 196 us  [partner(): return lax.ppermute(values, axis, [(i, i ^ bits) for i in range(count)])]
    unnamed x215 -> x242, local copies, waits for them, and re-layouts: 45.5 us -> 53.7 us
    ppermute x31 -> x32, starting transfers between devices: 34.1 us -> 34.7 us  [partner(): return lax.ppermute(values, axis, [(i, i ^ bits) for i in range(count)])]
  transfers between devices with their start and end apart: 46 -> 47, of which waited for: 21 -> 21; matrix products, arithmetic and copies ran while one was open for 19% -> 22% of each run, Pallas kernels for 23% -> 24%
where the time goes in v4:
time: 805 us; the launch traced here: 793 us
  waiting for transfers between devices  244 us (30%)
  Pallas kernels  198 us (25%)
  starting transfers between devices  112 us (14%)
  other arithmetic  110 us (14%)
  local copies, waits for them, and re-layouts  89.4 us (11%)
  between operations  23.4 us (3%)
  matrix products  15.7 us (2%)
    ppermute x32, waiting for transfers between devices, partner(): return lax.ppermute(values, axis, [(i, i ^ bits) for i in range(count)])  196 us
    pallas_call x4, Pallas kernels, expert_slot(): pl.pallas_call(functools.partial(slot_kernel, sources, len(carried)), out...  97.6 us
    all_to_all x10, starting transfers between devices, exchange(): return lax.all_to_all(values, axes, split_axis=0, concat_axis=0, tiled=True)  77.1 us
    unnamed x242, local copies, waits for them, and re-layouts  53.7 us
    all_to_all x10, waiting for transfers between devices, exchange(): return lax.all_to_all(values, axes, split_axis=0, concat_axis=0, tiled=True)  48.1 us
    ppermute x32, starting transfers between devices, partner(): return lax.ppermute(values, axis, [(i, i ^ bits) for i in range(count)])  34.7 us
    pallas_call x1, Pallas kernels, attention_backward(): pl.pallas_call(backward_kernel, out_shape=(jax.ShapeDtypeStruct((length,...  24.8 us
    pallas_call x1, Pallas kernels, attention_forward(): pl.pallas_call(forward_kernel, out_shape=(jax.ShapeDtypeStruct((steps, he...  24.8 us
  transfers between devices with their start and end apart: 47, of which 21 were waited for; matrix products, arithmetic and copies ran while one was open for 22% of the time, Pallas kernels for 24%

profile of v4, /device:TPU:0, one launch (start us, length us, event | category | flops | bytes accessed | tf_op | source)
XLA Modules:
  0.0 792.9 jit_solution(6878805326772761039)
XLA Ops:
  7.3 2.4 multiply_reduce_fusion.8
  18.1 7.4 all-to-all-start
  27.5 3.0 copy.263
  30.5 7.0 multiply_reduce_fusion.1
  37.5 2.6 pad_maximum_fusion
  40.1 46.6 %collective-permute-done.1.refs_2_ = bf16[512,1536]{1,0:T(8,128)(2,1)} collective-permute-done((bf16[512,1536]{1,0:T(8,128)(2,1)S(1)}, bf16[512,1536]{1,0:T(8,128)(2,1)}, u32[]{:S(2)}, u32[]{:S(2)}) %collective-permute-start.1) | collective-permute-done | bytes 1572896 | tf_op jit(solution)/shard_map/ppermute | solution.py:73
  93.4 2.3 collective-permute-start.4
  101.7 11.8 %shard_map.528 = (bf16[2048,1536]{1,0:T(8,128)(2,1)}, bf16[3,2048,128]{2,1,0:T(8,128)(2,1)S(1)}, bf16[2048,128]{1,0:T(8,128)(2,1)S(1)}, bf16[64,2048]{1,0:T(8,12...) custom-call(s32[1]{0:T(128)} %bitcast.1.index_ref, bf16[512,1536]{1,0:T(8,128)(2,1)S(1)} %copy-done.2, ...), custom_call_target="tpu_custom_call" | custom-call | flops 3795000064 | bytes 1 | tf_op jit(solution)/shard_map/pallas_call | solution.py:133
  113.6 15.9 %collective-permute-done.4.refs_2_ = bf16[256,1664]{1,0:T(8,128)(2,1)} collective-permute-done((bf16[256,1664]{1,0:T(8,128)(2,1)}, bf16[256,1664]{1,0:T(8,128)(2,1)}, u32[]{:S(2)}, u32[]{:S(2)}) %collective-permute-start.4) | collective-permute-done | bytes 852000 | tf_op jit(solution)/shard_map/ppermute | solution.py:73
  129.5 4.2 collective-permute-start.7
  137.3 14.9 %collective-permute-done.7.refs_2_ = bf16[256,1664]{1,0:T(8,128)(2,1)} collective-permute-done((bf16[256,1664]{1,0:T(8,128)(2,1)}, bf16[256,1664]{1,0:T(8,128)(2,1)}, u32[]{:S(2)}, u32[]{:S(2)}) %collective-permute-start.7) | collective-permute-done | bytes 852000 | tf_op jit(solution)/shard_map/ppermute | solution.py:73
  153.7 24.8 %shard_map.529 = (bf16[8,192,256]{2,1,0:T(8,128)(2,1)}, f32[8,1,768]{2,1,0:T(1,128)S(1)}) custom-call(bf16[3,2048,128]{2,1,0:T(8,128)(2,1)S(1)} %get-tuple-element.136.q_ref, bf16[2048,128]{1,0:T(8,128)(2,1)S(1)} %get-tuple-element.137.k_ref, bf16[64,2048]{1,0:T(8,128)(2,1)S(1)} %get-tuple-element.138.vt_ref), custom_call_target="tpu_custom_call" | custom-call | flops 8625000448 | bytes 1 | tf_op jit(solution)/shard_map/pallas_call | solution.py:202
  180.9 3.5 all-to-all-start.1
  189.2 5.3 collective-permute-done.8.refs_3_
  194.5 21.4 %all-to-all-done.1.got_ref = bf16[8,192,256]{2,1,0:T(8,128)(2,1)S(1)} async-done(((bf16[8,192,256]{2,1,0:T(8,128)(2,1)}), bf16[8,192,256]{2,1,0:T(8,128)(2,1)S(1)}, u32[]{:S(2)}, u32[]{:S(2)}) %all-to-all-start.1) | async-done | bytes 786464 | tf_op jit(solution)/shard_map/all_to_all | solution.py:43
  217.0 2.3 copy-done.33
  225.4 2.5 collective-permute-start.14
  232.1 28.3 %collective-permute-done.12.refs_0_ = bf16[256,1536]{1,0:T(8,128)(2,1)} collective-permute-done((bf16[256,1536]{1,0:T(8,128)(2,1)S(1)}, bf16[256,1536]{1,0:T(8,128)(2,1)}, u32[]{:S(2)}, u32[]{:S(2)}) %collective-permute-start.12) | collective-permute-done | bytes 786464 | tf_op jit(solution)/shard_map/ppermute | solution.py:73
  261.3 2.3 collective-permute-done.10.refs_0_
  264.5 24.3 %shard_map.531 = (bf16[4,192,1536]{2,1,0:T(8,128)(2,1)}, bf16[4,192,512]{2,1,0:T(8,128)(2,1)}, bf16[4,192,1536]{2,1,0:T(8,128)(2,1)}, bf16[4,192,1024]{2,1,0:T(8...) custom-call(s32[2]{0:T(128)} %pad_add_fusion.2.place_in_ref, ...), custom_call_target="tpu_custom_call" | custom-call | flops 8625000448 | bytes 1 | tf_op jit(solution)/shard_map/pallas_call | solution.py:398
  291.9 24.3 %shard_map.532 = (bf16[4,192,1536]{2,1,0:T(8,128)(2,1)}, bf16[4,192,512]{2,1,0:T(8,128)(2,1)}, bf16[4,192,1536]{2,1,0:T(8,128)(2,1)}, bf16[4,192,1024]{2,1,0:T(8...) custom-call(s32[2]{0:T(128)} %pad_add_fusion.1.place_in_ref, ...), custom_call_target="tpu_custom_call", output_to_operand_aliasing={{4}: (7, {}), {5}: (8, {})} | custom-call | flops 8625000448 | bytes 1 | tf_op jit(solution)/shard_map/pallas_call | solution.py:398
  318.1 9.7 %collective-permute-done.20.refs_1_ = bf16[256,1536]{1,0:T(8,128)(2,1)S(1)} collective-permute-done((bf16[256,1536]{1,0:T(8,128)(2,1)}, bf16[256,1536]{1,0:T(8,128)(2,1)S(1)}, u32[]{:S(2)}, u32[]{:S(2)}) %collective-permute-start.20) | collective-permute-done | bytes 786464 | tf_op jit(solution)/shard_map/ppermute | solution.py:73
  328.7 24.7 %shard_map.533 = (bf16[4,192,1536]{2,1,0:T(8,128)(2,1)}, bf16[4,192,512]{2,1,0:T(8,128)(2,1)}, bf16[4,192,1536]{2,1,0:T(8,128)(2,1)}, bf16[4,192,1024]{2,1,0:T(8...) custom-call(s32[2]{0:T(128)} %pad_add_fusion.3.place_in_ref, ...), custom_call_target="tpu_custom_call", output_to_operand_aliasing={{4}: (7, {}), {5}: (8, {})} | custom-call | flops 8625000448 | bytes 1 | tf_op jit(solution)/shard_map/pallas_call | solution.py:398
  353.9 8.9 %collective-permute-done.15 = bf16[256,1664]{1,0:T(8,128)(2,1)S(1)} collective-permute-done((bf16[256,1664]{1,0:T(8,128)(2,1)}, bf16[256,1664]{1,0:T(8,128)(2,1)S(1)}, u32[]{:S(2)}, u32[]{:S(2)}) %collective-permute-start.15) | collective-permute-done | bytes 852000 | tf_op jit(solution)/shard_map/ppermute | solution.py:73
  364.9 24.3 %shard_map.534 = (bf16[4,192,1536]{2,1,0:T(8,128)(2,1)}, bf16[4,192,512]{2,1,0:T(8,128)(2,1)}, bf16[4,192,1536]{2,1,0:T(8,128)(2,1)}, bf16[4,192,1024]{2,1,0:T(8...) custom-call(s32[2]{0:T(128)} %pad_add_fusion.place_in_ref, ...), custom_call_target="tpu_custom_call", output_to_operand_aliasing={{4}: (7, {}), {5}: (8, {})} | custom-call | flops 8625000448 | bytes 1 | tf_op jit(solution)/shard_map/pallas_call | solution.py:398
  394.5 14.1 %collective-permute-done.21 = bf16[256,1664]{1,0:T(8,128)(2,1)S(1)} collective-permute-done((bf16[256,1664]{1,0:T(8,128)(2,1)}, bf16[256,1664]{1,0:T(8,128)(2,1)S(1)}, u32[]{:S(2)}, u32[]{:S(2)}) %collective-permute-start.21) | collective-permute-done | bytes 852000 | tf_op jit(solution)/shard_map/ppermute | solution.py:73
  411.2 21.8 %shard_map.535 = bf16[4,1536,1536]{2,1,0:T(8,128)(2,1)} custom-call(bf16[4,192,1536]{2,1,0:T(8,128)(2,1)} %get-tuple-element.175.refs_0_, bf16[4,192,1536]{2,1,0:T(8,128)(2,1)} %get-tuple-element.176.refs_1_, bf16[4,192,1536]{2,1,0:T(8,128)(2,1)} %get-tuple-element.177.refs_2_, bf16[4,192,1536]{2,1,0:T(8,128)(2,1)} %get-tuple-element.178.refs_3_, ...), custom_call_target="tpu_custom_call" | custom-call | flops 7590000128 | bytes 1 | tf_op jit(solution)/shard_map/pallas_call | solution.py:580
  433.7 20.0 %collective-permute-done.25.refs_2_ = bf16[256,1664]{1,0:T(8,128)(2,1)} collective-permute-done((bf16[256,1664]{1,0:T(8,128)(2,1)}, bf16[256,1664]{1,0:T(8,128)(2,1)}, u32[]{:S(2)}, u32[]{:S(2)}) %collective-permute-start.25) | collective-permute-done | bytes 852000 | tf_op jit(solution)/shard_map/ppermute | solution.py:73
  456.0 6.8 shard_map.536
  466.5 4.2 all-to-all-start.2
  470.7 16.9 %collective-permute-done.28.other_small_ref = bf16[1536,128]{1,0:T(8,128)(2,1)} collective-permute-done((bf16[1536,128]{1,0:T(8,128)(2,1)}, bf16[1536,128]{1,0:T(8,128)(2,1)}, u32[]{:S(2)}, u32[]{:S(2)}) %collective-permute-start.28) | collective-permute-done | bytes 393248 | tf_op jit(solution)/shard_map/ppermute | solution.py:73
  490.0 2.5 shard_map.537
  494.3 23.5 %all-to-all-start.3 = ((bf16[16,96,896]{2,1,0:T(8,128)(2,1)}), bf16[16,96,896]{2,1,0:T(8,128)(2,1)}, u32[]{:S(2)}, u32[]{:S(2)}) async-start(bf16[16,96,896]{2,1,0:T(8,128)(2,1)} %bitcast.136), calls=%async_computation.4 | async-start | bytes 5505024 | tf_op jit(solution)/shard_map/all_to_all | solution.py:43
  530.5 3.3 multiply_reduce_fusion.3
  538.9 24.8 %shard_map.538 = (bf16[2048,192]{1,0:T(8,128)(2,1)S(1)}, bf16[2048,128]{1,0:T(8,128)(2,1)S(1)}) custom-call(bf16[3,2048,128]{2,1,0:T(8,128)(2,1)S(1)} %copy-done.46, bf16[2048,128]{1,0:T(8,128)(2,1)S(1)} %copy-done.48, bf16[64,2048]{1,0:T(8,128)(2,1)S(1)} %copy-done.52, bf16[2048,64]{1,0:T(8,128)(2,1)S(1)} %copy-done.50, ...), custom_call_target="tpu_custom_call" | custom-call | flops 8625000448 | bytes 1 | tf_op jit(solution)/shard_map/pallas_call | solution.py:284
  564.5 6.0 convolution_convert_fusion
  570.6 2.9 convert_reduce_fusion
  573.5 2.3 copy.265
  575.9 13.7 %all-to-all-start.4 = ((bf16[16,96,320]{2,1,0:T(8,128)(2,1)}), bf16[16,96,320]{2,1,0:T(8,128)(2,1)}, u32[]{:S(2)}, u32[]{:S(2)}) async-start(bf16[16,96,320]{2,1,0:T(8,128)(2,1)} %bitcast.150), calls=%async_computation.5 | async-start | bytes 2359296 | tf_op jit(solution)/shard_map/all_to_all | solution.py:43
  589.7 2.8 pad_maximum_fusion.2
  593.0 4.4 add_convert_fusion
  601.8 13.1 %all-to-all-done.4 = bf16[16,96,320]{2,1,0:T(8,128)(2,1)} async-done(((bf16[16,96,320]{2,1,0:T(8,128)(2,1)}), bf16[16,96,320]{2,1,0:T(8,128)(2,1)}, u32[]{:S(2)}, u32[]{:S(2)}) %all-to-all-start.4) | async-done | bytes 983072 | tf_op jit(solution)/shard_map/all_to_all | solution.py:43
  614.9 2.9 bitcast_convert_fusion
  617.8 2.7 reduce_sum.303
  623.4 2.5 copy.271
  625.9 4.4 all-to-all-start.5
  639.9 3.2 concatenate.47
  652.2 10.3 %all-to-all-done.5 = bf16[4,512,320]{1,2,0:T(8,128)(2,1)} async-done(((bf16[4,512,320]{1,2,0:T(8,128)(2,1)}), bf16[4,512,320]{1,2,0:T(8,128)(2,1)}, u32[]{:S(2)}, u32[]{:S(2)}) %all-to-all-start.5) | async-done | bytes 1310752 | tf_op jit(solution)/shard_map/all_to_all | solution.py:43
  664.1 7.2 all-to-all-start.6
  671.3 6.6 fusion.7
  680.0 3.4 all-to-all-done.6
  684.4 2.3 copy-done.34
  686.8 4.2 shard_map.539
  694.5 3.9 all-to-all-start.7
  707.6 5.0 multiply_reduce_fusion
  717.2 3.8 all-to-all-start.8
  721.1 11.5 %collective-permute-done.30 = bf16[256,1536]{1,0:T(8,128)(2,1)} collective-permute-done((bf16[256,1536]{1,0:T(8,128)(2,1)}, bf16[256,1536]{1,0:T(8,128)(2,1)}, u32[]{:S(2)}, u32[]{:S(2)}) %collective-permute-start.30) | collective-permute-done | bytes 786464 | tf_op jit(solution)/shard_map/ppermute | solution.py:73
  732.6 2.8 fusion.2
  737.6 5.0 fusion.5
  743.9 5.4 all-to-all-start.9
  757.2 8.3 %fusion.43 = (bf16[4,384,1024]{2,1,0:T(8,128)(2,1)}, f32[4,384,1024]{2,1,0:T(8,128)}) fusion(f32[4,384,1024]{2,1,0:T(8,128)} %param.33, f32[4,384,1024]{2,1,0:T(8,128)} %get-tuple-element.496, f32[4]{0:T(128)S(1)} %fusion.28, f32[4,1024]{1,0:T(4,128)S(1)} %fusion.16, f32[4,384]{1,0:T(4,128)S(1)} %copy-done.79, f32[]{:T(128)} %bitcast.59), kind=kLoop, calls=%fused_computation.184 | loop fusion | flops 9437184 | bytes 22042644 | tf_op jit(solution)/shard_map/convert_element_type | solution.py:1146
  765.7 2.2 add_convert_fusion.5
  770.5 2.6 fusion.45
  774.8 5.3 fusion.42
  (458 shorter events, 155.7 us)
Async XLA Ops:
  7.2 79.5 %copy-start = (s32[512,8]{0,1:T(8,128)S(1)}, s32[512,8]{0,1:T(8,128)}, u32[]{:S(2)}) copy-start(s32[512,8]{0,1:T(8,128)} %param.27) | copy-start | bytes 49156
  7.2 208.7 %all-gather.5.cloned.1.call-start = ((), (), s32[]{:S(2)}) async-start(), calls=%async_computation.12 | async-start | bytes 4866048 | tf_op jit(solution)/shard_map/all_gather | solution.py:854
  18.1 68.6 %all-to-all-start = ((bf16[16,96,354]{2,1,0:T(8,128)(2,1)}), bf16[16,96,354]{2,1,0:T(8,128)(2,1)S(1)}, u32[]{:S(2)}, u32[]{:S(2)}) async-start(bf16[16,96,354]{2,1,0:T(8,128)(2,1)} %bitcast.151), calls=%async_computation | async-start | bytes 2359296 | tf_op jit(solution)/shard_map/all_to_all | solution.py:43
  25.4 238.2 %all-gather.7.cloned.1.call-start = ((), (), s32[]{:S(2)}) async-start(), calls=%async_computation.13 | async-start | bytes 23592960 | tf_op jit(solution)/shard_map/all_gather | solution.py:859
  25.5 61.2 %collective-permute-start.1 = (bf16[512,1536]{1,0:T(8,128)(2,1)S(1)}, bf16[512,1536]{1,0:T(8,128)(2,1)}, u32[]{:S(2)}, u32[]{:S(2)}) collective-permute-start(bf16[512,1536]{1,0:T(8,128)(2,1)S(1)} %copy-done.2), channel_id=1, source_target_pairs={{0,4},{2,6},{4,0},{6,2},{1,5},{3,7},{5,1},{7,3},{8,12},{10,14},{12... | collective-permute-start | bytes 4718600 | tf_op jit(solution)/shard_map/ppermute | solution.py:73
  40.1 50.9 %copy-start.12 = (bf16[256,1536]{1,0:T(8,128)(2,1)S(1)}, bf16[256,1536]{1,0:T(8,128)(2,1)}, u32[]{:S(2)}) copy-start(bf16[256,1536]{1,0:T(8,128)(2,1)} %refs_9_.1) | copy-start | bytes 2359300
  86.7 99.7 %copy-start.3 = (bf16[16,96,354]{2,1,0:T(8,128)(2,1)}, bf16[16,96,354]{2,1,0:T(8,128)(2,1)S(1)}, u32[]{:S(2)}) copy-start(bf16[16,96,354]{2,1,0:T(8,128)(2,1)S(1)} %all-to-all-done) | copy-start | bytes 3262468
  91.9 41.7 %collective-permute-start.3 = (bf16[256,1664]{1,0:T(8,128)(2,1)}, bf16[256,1664]{1,0:T(8,128)(2,1)}, u32[]{:S(2)}, u32[]{:S(2)}) collective-permute-start(bf16[256,1664]{1,0:T(8,128)(2,1)} %fusion.10.refs_2_), channel_id=1, source_target_pairs={{0,8},{8,0},{16,24},{24,16},{1,9},{9,1},{17,25},{25,17},{2,10},{10... | collective-permute-start | bytes 2555912 | tf_op jit(solution)/shard_map/ppermute | solution.py:73
  93.4 36.1 %collective-permute-start.4 = (bf16[256,1664]{1,0:T(8,128)(2,1)}, bf16[256,1664]{1,0:T(8,128)(2,1)}, u32[]{:S(2)}, u32[]{:S(2)}) collective-permute-start(bf16[256,1664]{1,0:T(8,128)(2,1)} %fusion.10.refs_2_), channel_id=1, source_target_pairs={{0,16},{8,24},{16,0},{24,8},{1,17},{9,25},{17,1},{25,9},{2,18},{10... | collective-permute-start | bytes 2555912 | tf_op jit(solution)/shard_map/ppermute | solution.py:73
  95.7 5.8 collective-permute-start
  95.7 6.0 collective-permute-start.2
  113.6 64.9 %copy-start.45 = (bf16[3,2048,128]{2,1,0:T(8,128)(2,1)}, bf16[3,2048,128]{2,1,0:T(8,128)(2,1)S(1)}, u32[]{:S(2)}) copy-start(bf16[3,2048,128]{2,1,0:T(8,128)(2,1)S(1)} %get-tuple-element.136.q_ref) | copy-start | bytes 4718596
  113.6 64.9 %copy-start.47 = (bf16[2048,128]{1,0:T(8,128)(2,1)}, bf16[2048,128]{1,0:T(8,128)(2,1)S(1)}, u32[]{:S(2)}) copy-start(bf16[2048,128]{1,0:T(8,128)(2,1)S(1)} %get-tuple-element.137.k_ref) | copy-start | bytes 1572868
  113.6 64.9 %copy-start.49 = (bf16[2048,64]{1,0:T(8,128)(2,1)}, bf16[2048,64]{1,0:T(8,128)(2,1)S(1)}, u32[]{:S(2)}) copy-start(bf16[2048,64]{1,0:T(8,128)(2,1)S(1)} %get-tuple-element.201.v_ref) | copy-start | bytes 786436
  113.6 64.9 %copy-start.51 = (bf16[64,2048]{1,0:T(8,128)(2,1)}, bf16[64,2048]{1,0:T(8,128)(2,1)S(1)}, u32[]{:S(2)}) copy-start(bf16[64,2048]{1,0:T(8,128)(2,1)S(1)} %get-tuple-element.200.kt_ref) | copy-start | bytes 786436
  129.5 22.7 %collective-permute-start.7 = (bf16[256,1664]{1,0:T(8,128)(2,1)}, bf16[256,1664]{1,0:T(8,128)(2,1)}, u32[]{:S(2)}, u32[]{:S(2)}) collective-permute-start(bf16[256,1664]{1,0:T(8,128)(2,1)} %collective-permute-done.4.refs_2_), channel_id=1, source_target_pairs={{0,8},{8,0},{16,24},{24,16},{1,9},{9,1},{17,25},{25,17},{2,10},{10... | collective-permute-start | bytes 2555912 | tf_op jit(solution)/shard_map/ppermute | solution.py:73
  133.7 45.4 %collective-permute-start.6 = (bf16[256,1664]{1,0:T(8,128)(2,1)}, bf16[256,1664]{1,0:T(8,128)(2,1)S(1)}, u32[]{:S(2)}, u32[]{:S(2)}) collective-permute-start(bf16[256,1664]{1,0:T(8,128)(2,1)} %collective-permute-done.3.refs_2_), channel_id=1, source_target_pairs={{0,1},{1,0},{2,3},{3,2},{4,5},{5,4},{6,7},{7,6},{8,9},{9,8},{10,11... | collective-permute-start | bytes 2555912 | tf_op jit(solution)/shard_map/ppermute | solution.py:73
  135.2 44.8 %collective-permute-start.5 = (bf16[256,1664]{1,0:T(8,128)(2,1)}, bf16[256,1664]{1,0:T(8,128)(2,1)S(1)}, u32[]{:S(2)}, u32[]{:S(2)}) collective-permute-start(bf16[256,1664]{1,0:T(8,128)(2,1)} %fusion.10.refs_2_), channel_id=1, source_target_pairs={{0,1},{1,0},{2,3},{3,2},{4,5},{5,4},{6,7},{7,6},{8,9},{9,8},{10,11... | collective-permute-start | bytes 2555912 | tf_op jit(solution)/shard_map/ppermute | solution.py:73
  135.7 58.8 %collective-permute-start.8 = (bf16[256,1664]{1,0:T(8,128)(2,1)}, bf16[256,1664]{1,0:T(8,128)(2,1)}, u32[]{:S(2)}, u32[]{:S(2)}) collective-permute-start(bf16[256,1664]{1,0:T(8,128)(2,1)} %collective-permute-done.4.refs_2_), channel_id=1, source_target_pairs={{0,1},{1,0},{2,3},{3,2},{4,5},{5,4},{6,7},{7,6},{8,9},{9,8},{10,11... | collective-permute-start | bytes 2555912 | tf_op jit(solution)/shard_map/ppermute | solution.py:73
  152.2 63.7 %collective-permute-start.9 = (bf16[256,1664]{1,0:T(8,128)(2,1)}, bf16[256,1664]{1,0:T(8,128)(2,1)}, u32[]{:S(2)}, u32[]{:S(2)}) collective-permute-start(bf16[256,1664]{1,0:T(8,128)(2,1)} %collective-permute-done.7.refs_2_), channel_id=1, source_target_pairs={{0,1},{1,0},{2,3},{3,2},{4,5},{5,4},{6,7},{7,6},{8,9},{9,8},{10,11... | collective-permute-start | bytes 2555912 | tf_op jit(solution)/shard_map/ppermute | solution.py:73
  180.9 35.0 %all-to-all-start.1 = ((bf16[8,192,256]{2,1,0:T(8,128)(2,1)}), bf16[8,192,256]{2,1,0:T(8,128)(2,1)S(1)}, u32[]{:S(2)}, u32[]{:S(2)}) async-start(bf16[8,192,256]{2,1,0:T(8,128)(2,1)} %get-tuple-element.143.out_ref), calls=%async_computation.1 | async-start | bytes 1572864 | tf_op jit(solution)/shard_map/all_to_all | solution.py:43
  184.5 179.6 %all-gather.9.cloned.1.call-start = ((), (), s32[]{:S(2)}) async-start(), calls=%async_computation.16 | async-start | bytes 5898240 | tf_op jit(solution)/shard_map/all_gather | solution.py:896
  188.4 33.1 %copy-start.15 = (bf16[1536,32]{0,1:T(8,128)(2,1)}, bf16[1536,32]{0,1:T(8,128)(2,1)S(1)}, u32[]{:S(2)}) copy-start(bf16[1536,32]{0,1:T(8,128)(2,1)S(1)} %copy.285) | copy-start | bytes 294916
  224.8 38.9 %copy-start.35 = (bf16[256,1536]{1,0:T(8,128)(2,1)}, bf16[256,1536]{1,0:T(8,128)(2,1)S(1)}, u32[]{:S(2)}) copy-start(bf16[256,1536]{1,0:T(8,128)(2,1)S(1)} %get-tuple-element.150.refs_0_.refs_5_) | copy-start | bytes 2359300
  224.8 64.1 %copy-start.55 = (f32[32,256]{1,0:T(8,128)}, f32[32,256]{1,0:T(8,128)S(1)}, u32[]{:S(2)}) copy-start(f32[32,256]{1,0:T(8,128)S(1)} %get-tuple-element.192.refs_6_) | copy-start | bytes 98308
  224.8 64.1 %copy-start.57 = (f32[32,256]{1,0:T(8,128)}, f32[32,256]{1,0:T(8,128)S(1)}, u32[]{:S(2)}) copy-start(f32[32,256]{1,0:T(8,128)S(1)} %get-tuple-element.193.refs_7_) | copy-start | bytes 98308
  224.8 459.6 %reduce-scatter.5.cloned.1.call-start = ((), (), s32[]{:S(2)}) async-start(), calls=%async_computation.15 | async-start | bytes 23592960 | tf_op jit(solution)/shard_map/reduce_scatter | solution.py:946
  225.1 35.4 %collective-permute-start.12 = (bf16[256,1536]{1,0:T(8,128)(2,1)S(1)}, bf16[256,1536]{1,0:T(8,128)(2,1)}, u32[]{:S(2)}, u32[]{:S(2)}) collective-permute-start(bf16[256,1536]{1,0:T(8,128)(2,1)S(1)} %get-tuple-element.150.refs_0_.refs_5_), channel_id=1, source_target_pairs={{0,8},{8,0},{16,24},{24,16},{1,9},{9,1},{17,25},{25,17},{2,10},{10... | collective-permute-start | bytes 2359304 | tf_op jit(solution)/shard_map/ppermute | solution.py:73
  225.4 38.2 %collective-permute-start.10 = (bf16[256,1536]{1,0:T(8,128)(2,1)S(1)}, bf16[256,1536]{1,0:T(8,128)(2,1)}, u32[]{:S(2)}, u32[]{:S(2)}) collective-permute-start(bf16[256,1536]{1,0:T(8,128)(2,1)S(1)} %get-tuple-element.150.refs_0_.refs_5_), channel_id=1, source_target_pairs={{0,16},{8,24},{16,0},{24,8},{1,17},{9,25},{17,1},{25,9},{2,18},{10... | collective-permute-start | bytes 2359304 | tf_op jit(solution)/shard_map/ppermute | solution.py:73
  225.4 38.2 %collective-permute-start.14 = (bf16[256,1536]{1,0:T(8,128)(2,1)S(1)}, bf16[256,1536]{1,0:T(8,128)(2,1)S(1)}, u32[]{:S(2)}, u32[]{:S(2)}) collective-permute-start(bf16[256,1536]{1,0:T(8,128)(2,1)S(1)} %get-tuple-element.150.refs_0_.refs_5_), channel_id=1, source_target_pairs={{0,1},{1,0},{2,3},{3,2},{4,5},{5,4},{6,7},{7,6},{8,9},{9,8},{10,11... | collective-permute-start | bytes 2359304 | tf_op jit(solution)/shard_map/ppermute | solution.py:73
  230.4 1.2 collective-permute-start.16
  231.6 57.7 %collective-permute-start.17 = (f32[1,32]{1,0:T(1,128)S(1)}, f32[1,32]{1,0:T(1,128)S(1)}, u32[]{:S(2)}, u32[]{:S(2)}) collective-permute-start(f32[1,32]{1,0:T(1,128)S(1)} %add.272), channel_id=1, source_target_pairs={{0,4},{2,6},{4,0},{6,2},{1,5},{3,7},{5,1},{7,3},{8,12},{10,14},{12... | collective-permute-start | bytes 392 | tf_op jit(solution)/shard_map/ppermute | solution.py:73
  260.5 31.4 %collective-permute-start.13 = (bf16[256,1536]{1,0:T(8,128)(2,1)}, bf16[256,1536]{1,0:T(8,128)(2,1)}, u32[]{:S(2)}, u32[]{:S(2)}) collective-permute-start(bf16[256,1536]{1,0:T(8,128)(2,1)} %collective-permute-done.12.refs_0_), channel_id=1, source_target_pairs={{0,1},{1,0},{2,3},{3,2},{4,5},{5,4},{6,7},{7,6},{8,9},{9,8},{10,11... | collective-permute-start | bytes 2359304 | tf_op jit(solution)/shard_map/ppermute | solution.py:73
  263.6 27.8 %collective-permute-start.11 = (bf16[256,1536]{1,0:T(8,128)(2,1)}, bf16[256,1536]{1,0:T(8,128)(2,1)}, u32[]{:S(2)}, u32[]{:S(2)}) collective-permute-start(bf16[256,1536]{1,0:T(8,128)(2,1)} %collective-permute-done.10.refs_0_), channel_id=1, source_target_pairs={{0,8},{8,0},{16,24},{24,16},{1,9},{9,1},{17,25},{25,17},{2,10},{10... | collective-permute-start | bytes 2359304 | tf_op jit(solution)/shard_map/ppermute | solution.py:73
  288.8 29.0 %collective-permute-start.19 = (bf16[256,1664]{1,0:T(8,128)(2,1)}, bf16[256,1664]{1,0:T(8,128)(2,1)S(1)}, u32[]{:S(2)}, u32[]{:S(2)}) collective-permute-start(bf16[256,1664]{1,0:T(8,128)(2,1)} %get-tuple-element.158), channel_id=1, source_target_pairs={{0,1},{1,0},{2,3},{3,2},{4,5},{5,4},{6,7},{7,6},{8,9},{9,8},{10,11... | collective-permute-start | bytes 2555912 | tf_op jit(solution)/shard_map/ppermute | solution.py:73
  289.9 37.9 %collective-permute-start.20 = (bf16[256,1536]{1,0:T(8,128)(2,1)}, bf16[256,1536]{1,0:T(8,128)(2,1)S(1)}, u32[]{:S(2)}, u32[]{:S(2)}) collective-permute-start(bf16[256,1536]{1,0:T(8,128)(2,1)} %collective-permute-done.10.refs_0_), channel_id=1, source_target_pairs={{0,1},{1,0},{2,3},{3,2},{4,5},{5,4},{6,7},{7,6},{8,9},{9,8},{10,11... | collective-permute-start | bytes 2359304 | tf_op jit(solution)/shard_map/ppermute | solution.py:73
  291.5 72.6 %collective-permute-start.18 = (bf16[256,1536]{1,0:T(8,128)(2,1)}, bf16[256,1536]{1,0:T(8,128)(2,1)S(1)}, u32[]{:S(2)}, u32[]{:S(2)}) collective-permute-start(bf16[256,1536]{1,0:T(8,128)(2,1)} %collective-permute-done.11.refs_0_), channel_id=1, source_target_pairs={{0,1},{1,0},{2,3},{3,2},{4,5},{5,4},{6,7},{7,6},{8,9},{9,8},{10,11... | collective-permute-start | bytes 2359304 | tf_op jit(solution)/shard_map/ppermute | solution.py:73
  316.2 46.7 %collective-permute-start.15 = (bf16[256,1664]{1,0:T(8,128)(2,1)}, bf16[256,1664]{1,0:T(8,128)(2,1)S(1)}, u32[]{:S(2)}, u32[]{:S(2)}) collective-permute-start(bf16[256,1664]{1,0:T(8,128)(2,1)} %get-tuple-element.154), channel_id=1, source_target_pairs={{0,1},{1,0},{2,3},{3,2},{4,5},{5,4},{6,7},{7,6},{8,9},{9,8},{10,11... | collective-permute-start | bytes 2555912 | tf_op jit(solution)/shard_map/ppermute | solution.py:73
  328.7 34.2 %copy-start.70 = (bf16[256,1664]{1,0:T(8,128)(2,1)S(1)}, bf16[256,1664]{1,0:T(8,128)(2,1)}, u32[]{:S(2)}) copy-start(bf16[256,1664]{1,0:T(8,128)(2,1)} %get-tuple-element.153) | copy-start | bytes 2555908
  353.4 38.4 %collective-permute-start.23 = (bf16[256,1664]{1,0:T(8,128)(2,1)}, bf16[256,1664]{1,0:T(8,128)(2,1)}, u32[]{:S(2)}, u32[]{:S(2)}) collective-permute-start(bf16[256,1664]{1,0:T(8,128)(2,1)} %get-tuple-element.174), channel_id=1, source_target_pairs={{0,1},{1,0},{2,3},{3,2},{4,5},{5,4},{6,7},{7,6},{8,9},{9,8},{10,11... | collective-permute-start | bytes 2555912 | tf_op jit(solution)/shard_map/ppermute | solution.py:73
  389.3 19.3 %collective-permute-start.21 = (bf16[256,1664]{1,0:T(8,128)(2,1)}, bf16[256,1664]{1,0:T(8,128)(2,1)S(1)}, u32[]{:S(2)}, u32[]{:S(2)}) collective-permute-start(bf16[256,1664]{1,0:T(8,128)(2,1)} %get-tuple-element.169), channel_id=1, source_target_pairs={{0,1},{1,0},{2,3},{3,2},{4,5},{5,4},{6,7},{7,6},{8,9},{9,8},{10,11... | collective-permute-start | bytes 2555912 | tf_op jit(solution)/shard_map/ppermute | solution.py:73
  389.8 43.9 %collective-permute-start.24 = (bf16[256,1664]{1,0:T(8,128)(2,1)}, bf16[256,1664]{1,0:T(8,128)(2,1)}, u32[]{:S(2)}, u32[]{:S(2)}) collective-permute-start(bf16[256,1664]{1,0:T(8,128)(2,1)} %add_convert_fusion.4), channel_id=1, source_target_pairs={{0,8},{8,0},{16,24},{24,16},{1,9},{9,1},{17,25},{25,17},{2,10},{10... | collective-permute-start | bytes 2555912 | tf_op jit(solution)/shard_map/ppermute | solution.py:73
  394.1 59.6 %collective-permute-start.25 = (bf16[256,1664]{1,0:T(8,128)(2,1)}, bf16[256,1664]{1,0:T(8,128)(2,1)}, u32[]{:S(2)}, u32[]{:S(2)}) collective-permute-start(bf16[256,1664]{1,0:T(8,128)(2,1)} %add_convert_fusion.1), channel_id=1, source_target_pairs={{0,16},{8,24},{16,0},{24,8},{1,17},{9,25},{17,1},{25,9},{2,18},{10... | collective-permute-start | bytes 2555912 | tf_op jit(solution)/shard_map/ppermute | solution.py:73
  409.7 43.9 %collective-permute-start.26 = (bf16[256,1664]{1,0:T(8,128)(2,1)}, bf16[256,1664]{1,0:T(8,128)(2,1)}, u32[]{:S(2)}, u32[]{:S(2)}) collective-permute-start(bf16[256,1664]{1,0:T(8,128)(2,1)} %add_convert_fusion.2), channel_id=1, source_target_pairs={{0,24},{8,16},{16,8},{24,0},{1,25},{9,17},{17,9},{25,1},{2,26},{10... | collective-permute-start | bytes 2555912 | tf_op jit(solution)/shard_map/ppermute | solution.py:73
  410.9 22.1 %collective-permute-start.22 = (bf16[256,768]{1,0:T(8,128)(2,1)S(1)}, bf16[256,768]{1,0:T(8,128)(2,1)S(1)}, u32[]{:S(2)}, u32[]{:S(2)}) collective-permute-start(bf16[256,768]{1,0:T(8,128)(2,1)S(1)} %copy-done.38), channel_id=1, source_target_pairs={{0,1},{1,0},{2,3},{3,2},{4,5},{5,4},{6,7},{7,6},{8,9},{9,8},{10,11... | collective-permute-start | bytes 1179656 | tf_op jit(solution)/shard_map/ppermute | solution.py:73
  411.1 42.6 %copy-start.16 = (bf16[1536,32]{0,1:T(8,128)(2,1)S(1)}, bf16[1536,32]{0,1:T(8,128)(2,1)}, u32[]{:S(2)}) copy-start(bf16[1536,32]{0,1:T(8,128)(2,1)} %copy-done.15) | copy-start | bytes 294916
  411.1 42.6 %copy-start.22 = (f32[1,1536]{1,0:T(1,128)S(1)}, f32[1,1536]{1,0:T(1,128)}, u32[]{:S(2)}) copy-start(f32[1,1536]{1,0:T(1,128)} %copy-done.21) | copy-start | bytes 18436
  411.1 42.6 %copy-start.56 = (f32[32,256]{1,0:T(8,128)S(1)}, f32[32,256]{1,0:T(8,128)}, u32[]{:S(2)}) copy-start(f32[32,256]{1,0:T(8,128)} %copy-done.55) | copy-start | bytes 98308
  411.1 42.6 %copy-start.58 = (f32[32,256]{1,0:T(8,128)S(1)}, f32[32,256]{1,0:T(8,128)}, u32[]{:S(2)}) copy-start(f32[32,256]{1,0:T(8,128)} %copy-done.57) | copy-start | bytes 98308
  464.4 23.2 %collective-permute-start.27 = (bf16[256,1536]{1,0:T(8,128)(2,1)S(1)}, bf16[256,1536]{1,0:T(8,128)(2,1)S(1)}, u32[]{:S(2)}, u32[]{:S(2)}) collective-permute-start(bf16[256,1536]{1,0:T(8,128)(2,1)S(1)} %get-tuple-element.195.low_ref), channel_id=1, source_target_pairs={{0,1},{1,0},{2,3},{3,2},{4,5},{5,4},{6,7},{7,6},{8,9},{9,8},{10,11... | collective-permute-start | bytes 2359304 | tf_op jit(solution)/shard_map/ppermute | solution.py:73
  466.1 21.5 %collective-permute-start.28 = (bf16[1536,128]{1,0:T(8,128)(2,1)}, bf16[1536,128]{1,0:T(8,128)(2,1)}, u32[]{:S(2)}, u32[]{:S(2)}) collective-permute-start(bf16[1536,128]{1,0:T(8,128)(2,1)} %copy-done.41), channel_id=1, source_target_pairs={{0,1},{1,0},{2,3},{3,2},{4,5},{5,4},{6,7},{7,6},{8,9},{9,8},{10,11... | collective-permute-start | bytes 1179656 | tf_op jit(solution)/shard_map/ppermute | solution.py:73
  466.5 27.8 %all-to-all-start.2 = ((bf16[8,192,256]{2,1,0:T(8,128)(2,1)}), bf16[8,192,256]{2,1,0:T(8,128)(2,1)}, u32[]{:S(2)}, u32[]{:S(2)}) async-start(bf16[8,192,256]{2,1,0:T(8,128)(2,1)} %copy-done.10), calls=%async_computation.2 | async-start | bytes 1572864 | tf_op jit(solution)/shard_map/all_to_all | solution.py:43
  494.3 76.3 %all-to-all-start.3 = ((bf16[16,96,896]{2,1,0:T(8,128)(2,1)}), bf16[16,96,896]{2,1,0:T(8,128)(2,1)}, u32[]{:S(2)}, u32[]{:S(2)}) async-start(bf16[16,96,896]{2,1,0:T(8,128)(2,1)} %bitcast.136), calls=%async_computation.4 | async-start | bytes 5505024 | tf_op jit(solution)/shard_map/all_to_all | solution.py:43
  522.1 70.9 %collective-permute-start.29 = (bf16[4,256,1536]{2,1,0:T(8,128)(2,1)}, bf16[4,256,1536]{2,1,0:T(8,128)(2,1)}, u32[]{:S(2)}, u32[]{:S(2)}) collective-permute-start(bf16[4,256,1536]{2,1,0:T(8,128)(2,1)} %get-tuple-element.199), channel_id=1, source_target_pairs={{0,1},{1,0},{2,3},{3,2},{4,5},{5,4},{6,7},{7,6},{8,9},{9,8},{10,11... | collective-permute-start | bytes 9437192 | tf_op jit(solution)/shard_map/ppermute | solution.py:73
  575.9 39.0 %all-to-all-start.4 = ((bf16[16,96,320]{2,1,0:T(8,128)(2,1)}), bf16[16,96,320]{2,1,0:T(8,128)(2,1)}, u32[]{:S(2)}, u32[]{:S(2)}) async-start(bf16[16,96,320]{2,1,0:T(8,128)(2,1)} %bitcast.150), calls=%async_computation.5 | async-start | bytes 2359296 | tf_op jit(solution)/shard_map/all_to_all | solution.py:43
  589.6 176.0 %reduce-scatter.3.cloned.1.call-start = ((), (), s32[]{:S(2)}) async-start(), calls=%async_computation.14 | async-start | bytes 3932160 | tf_op jit(solution)/shard_map/reduce_scatter | solution.py:965
  625.9 36.6 %all-to-all-start.5 = ((bf16[4,512,320]{1,2,0:T(8,128)(2,1)}), bf16[4,512,320]{1,2,0:T(8,128)(2,1)}, u32[]{:S(2)}, u32[]{:S(2)}) async-start(bf16[4,512,320]{1,2,0:T(8,128)(2,1)} %copy.271), calls=%async_computation.6 | async-start | bytes 2621440 | tf_op jit(solution)/shard_map/all_to_all | solution.py:43
  637.9 135.2 %copy-start.5 = (f32[96,1280]{1,0:T(8,128)}, f32[96,1280]{1,0:T(8,128)S(1)}, u32[]{:S(2)}) copy-start(f32[96,1280]{1,0:T(8,128)S(1)} %get-tuple-element.568.qkv_ref) | copy-start | bytes 1474564
  664.1 19.3 %all-to-all-start.6 = ((f32[32,1,2688]{2,1,0:T(1,128)}), f32[32,1,2688]{2,1,0:T(1,128)}, u32[]{:S(2)}, u32[]{:S(2)}) async-start(f32[32,1,2688]{2,1,0:T(1,128)} %broadcast_in_dim.47), calls=%async_computation.7 | async-start | bytes 688128 | tf_op jit(solution)/shard_map/all_to_all | solution.py:43
  677.9 43.1 %collective-permute-start.31 = (bf16[512,1536]{1,0:T(8,128)(2,1)}, bf16[512,1536]{1,0:T(8,128)(2,1)}, u32[]{:S(2)}, u32[]{:S(2)}) collective-permute-start(bf16[512,1536]{1,0:T(8,128)(2,1)} %fusion.7), channel_id=1, source_target_pairs={{0,1},{1,0},{2,3},{3,2},{4,5},{5,4},{6,7},{7,6},{8,9},{9,8},{10,11... | collective-permute-start | bytes 4718600 | tf_op jit(solution)/shard_map/ppermute | solution.py:73
  679.8 52.8 %collective-permute-start.30 = (bf16[256,1536]{1,0:T(8,128)(2,1)}, bf16[256,1536]{1,0:T(8,128)(2,1)}, u32[]{:S(2)}, u32[]{:S(2)}) collective-permute-start(bf16[256,1536]{1,0:T(8,128)(2,1)} %get-tuple-element.220), channel_id=1, source_target_pairs={{0,1},{1,0},{2,3},{3,2},{4,5},{5,4},{6,7},{7,6},{8,9},{9,8},{10,11... | collective-permute-start | bytes 2359304 | tf_op jit(solution)/shard_map/ppermute | solution.py:73
  694.5 11.2 %all-to-all-start.7 = ((f32[4,4,1664]{2,1,0:T(4,128)}), f32[4,4,1664]{2,1,0:T(4,128)}, u32[]{:S(2)}, u32[]{:S(2)}) async-start(f32[4,4,1664]{2,1,0:T(4,128)} %broadcast_in_dim.53), calls=%async_computation.9 | async-start | bytes 212992 | tf_op jit(solution)/shard_map/all_to_all | solution.py:43
  717.2 25.4 %all-to-all-start.8 = ((f32[32,1,7]{2,1,0:T(1,128)}), f32[32,1,7]{2,1,0:T(1,128)S(1)}, u32[]{:S(2)}, u32[]{:S(2)}) async-start(f32[32,1,7]{2,1,0:T(1,128)} %broadcast_in_dim.56), calls=%async_computation.10 | async-start | bytes 32768 | tf_op jit(solution)/shard_map/all_to_all | solution.py:43
  743.9 36.3 %all-to-all-start.9 = ((f32[32,1,4608]{2,1,0:T(1,128)}), f32[32,1,4608]{2,1,0:T(1,128)S(1)}, u32[]{:S(2)}, u32[]{:S(2)}) async-start(f32[32,1,4608]{2,1,0:T(1,128)} %broadcast_in_dim.58), calls=%async_computation.11 | async-start | bytes 1179648 | tf_op jit(solution)/shard_map/all_to_all | solution.py:43
  (95 other events, 890.5 us)
Sparse Core Ops, SparseCore 0:
  11.5 85.6 all-gather.4
  99.4 129.8 all-gather.6
  230.8 37.5 all-gather.8
  464.5 207.2 reduce-scatter.4
  674.7 60.5 reduce-scatter.2

commit v5 on v4

--- a/solution.py
+++ b/solution.py
@@ -943,13 +943,12 @@
         ctx_count * tp_count,
     )
     d_attended = exchange(d_attended, ("ctx", "tp"))
-    g_experts = lax.psum_scatter(after(g_experts, low), "ctx", scatter_dimension=1, tiled=True)
+    g_experts = lax.psum_scatter(after(g_experts, d_parts[2]), "ctx", scatter_dimension=1, tiled=True)
     g_gate_up, g_down, expert_sums = split(g_experts)
     expert_sums = expert_sums[:, 0]
     other_low = partner(low, "tp", 1, tp_count)
     other_small = partner(small, "tp", 1, tp_count)
     g_out_part = out_grad(low, other_low, heads_own, other_heads, small, other_small)
-    d_attended = after(d_attended, g_out_part)
     g_out_got = exchange(g_out_part.reshape(dense_parts, dense_rows, -1), ("fsdp", "ctx"))
     g_out_got = jnp.sum(g_out_got.astype(f32), axis=0)
     g_out_t = g_out_got[:, :out_rows]

time: 805 us -> 800 us (level)
  starting transfers between devices: 112 us -> 98.1 us
  waiting for transfers between devices: 244 us -> 254 us
    all_to_all x10, starting transfers between devices: 77.1 us -> 61.6 us  [exchange(): return lax.all_to_all(values, axes, split_axis=0, concat_axis=0, tiled=True)]
    ppermute x32, waiting for transfers between devices: 196 us -> 208 us  [partner(): return lax.ppermute(values, axis, [(i, i ^ bits) for i in range(count)])]
    unnamed x242 -> x238, local copies, waits for them, and re-layouts: 53.7 us -> 53.1 us
  transfers between devices with their start and end apart: 47 -> 47, of which waited for: 21 -> 21; matrix products, arithmetic and copies ran while one was open for 22% -> 22% of each run, Pallas kernels for 24% -> 25%
where the time goes in v5:
time: 800 us; the launch traced here: 789 us
  waiting for transfers between devices  254 us (32%)
  Pallas kernels  199 us (25%)
  other arithmetic  110 us (14%)
  starting transfers between devices  98.1 us (12%)
  local copies, waits for them, and re-layouts  88.9 us (11%)
  between operations  23.3 us (3%)
  matrix products  15.8 us (2%)
    ppermute x32, waiting for transfers between devices, partner(): return lax.ppermute(values, axis, [(i, i ^ bits) for i in range(count)])  208 us
    pallas_call x4, Pallas kernels, expert_slot(): pl.pallas_call(functools.partial(slot_kernel, sources, len(carried)), out...  97.7 us
    all_to_all x10, starting transfers between devices, exchange(): return lax.all_to_all(values, axes, split_axis=0, concat_axis=0, tiled=True)  61.6 us
    unnamed x238, local copies, waits for them, and re-layouts  53.1 us
    all_to_all x10, waiting for transfers between devices, exchange(): return lax.all_to_all(values, axes, split_axis=0, concat_axis=0, tiled=True)  45.8 us
    ppermute x32, starting transfers between devices, partner(): return lax.ppermute(values, axis, [(i, i ^ bits) for i in range(count)])  36 us
    pallas_call x1, Pallas kernels, attention_backward(): pl.pallas_call(backward_kernel, out_shape=(jax.ShapeDtypeStruct((length,...  24.8 us
    pallas_call x1, Pallas kernels, attention_forward(): pl.pallas_call(forward_kernel, out_shape=(jax.ShapeDtypeStruct((steps, he...  24.8 us
  transfers between devices with their start and end apart: 47, of which 21 were waited for; matrix products, arithmetic and copies ran while one was open for 22% of the time, Pallas kernels for 25%

profile of v5, /device:TPU:0, one launch (start us, length us, event | category | flops | bytes accessed | tf_op | source)
XLA Modules:
  0.0 788.6 jit_solution(8340572511524138952)
XLA Ops:
  7.3 2.4 multiply_reduce_fusion.8
  18.1 7.4 all-to-all-start
  27.5 3.0 copy.263
  30.5 7.0 multiply_reduce_fusion.1
  37.5 2.6 pad_maximum_fusion
  40.1 46.6 %collective-permute-done.1.refs_2_ = bf16[512,1536]{1,0:T(8,128)(2,1)} collective-permute-done((bf16[512,1536]{1,0:T(8,128)(2,1)S(1)}, bf16[512,1536]{1,0:T(8,128)(2,1)}, u32[]{:S(2)}, u32[]{:S(2)}) %collective-permute-start.1) | collective-permute-done | bytes 1572896 | tf_op jit(solution)/shard_map/ppermute | solution.py:73
  93.4 2.3 collective-permute-start.4
  101.7 11.8 %shard_map.528 = (bf16[2048,1536]{1,0:T(8,128)(2,1)}, bf16[3,2048,128]{2,1,0:T(8,128)(2,1)S(1)}, bf16[2048,128]{1,0:T(8,128)(2,1)S(1)}, bf16[64,2048]{1,0:T(8,12...) custom-call(s32[1]{0:T(128)} %bitcast.1.index_ref, bf16[512,1536]{1,0:T(8,128)(2,1)S(1)} %copy-done.2, ...), custom_call_target="tpu_custom_call" | custom-call | flops 3795000064 | bytes 1 | tf_op jit(solution)/shard_map/pallas_call | solution.py:133
  113.6 15.9 %collective-permute-done.4.refs_2_ = bf16[256,1664]{1,0:T(8,128)(2,1)} collective-permute-done((bf16[256,1664]{1,0:T(8,128)(2,1)}, bf16[256,1664]{1,0:T(8,128)(2,1)}, u32[]{:S(2)}, u32[]{:S(2)}) %collective-permute-start.4) | collective-permute-done | bytes 852000 | tf_op jit(solution)/shard_map/ppermute | solution.py:73
  129.5 4.2 collective-permute-start.7
  137.3 14.9 %collective-permute-done.7.refs_2_ = bf16[256,1664]{1,0:T(8,128)(2,1)} collective-permute-done((bf16[256,1664]{1,0:T(8,128)(2,1)}, bf16[256,1664]{1,0:T(8,128)(2,1)}, u32[]{:S(2)}, u32[]{:S(2)}) %collective-permute-start.7) | collective-permute-done | bytes 852000 | tf_op jit(solution)/shard_map/ppermute | solution.py:73
  153.7 24.8 %shard_map.529 = (bf16[8,192,256]{2,1,0:T(8,128)(2,1)}, f32[8,1,768]{2,1,0:T(1,128)S(1)}) custom-call(bf16[3,2048,128]{2,1,0:T(8,128)(2,1)S(1)} %get-tuple-element.135.q_ref, bf16[2048,128]{1,0:T(8,128)(2,1)S(1)} %get-tuple-element.136.k_ref, bf16[64,2048]{1,0:T(8,128)(2,1)S(1)} %get-tuple-element.137.vt_ref), custom_call_target="tpu_custom_call" | custom-call | flops 8625000448 | bytes 1 | tf_op jit(solution)/shard_map/pallas_call | solution.py:202
  180.9 3.5 all-to-all-start.1
  189.2 5.3 collective-permute-done.8.refs_3_
  194.5 21.4 %all-to-all-done.1.got_ref = bf16[8,192,256]{2,1,0:T(8,128)(2,1)S(1)} async-done(((bf16[8,192,256]{2,1,0:T(8,128)(2,1)}), bf16[8,192,256]{2,1,0:T(8,128)(2,1)S(1)}, u32[]{:S(2)}, u32[]{:S(2)}) %all-to-all-start.1) | async-done | bytes 786464 | tf_op jit(solution)/shard_map/all_to_all | solution.py:43
  217.0 2.3 copy-done.33
  226.6 2.5 collective-permute-start.14
  233.4 28.3 %collective-permute-done.12.refs_0_ = bf16[256,1536]{1,0:T(8,128)(2,1)S(1)} collective-permute-done((bf16[256,1536]{1,0:T(8,128)(2,1)S(1)}, bf16[256,1536]{1,0:T(8,128)(2,1)S(1)}, u32[]{:S(2)}, u32[]{:S(2)}) %collective-permute-start.12) | collective-permute-done | bytes 786464 | tf_op jit(solution)/shard_map/ppermute | solution.py:73
  262.5 2.4 collective-permute-done.10.refs_0_
  264.9 24.3 %shard_map.531 = (bf16[4,192,1536]{2,1,0:T(8,128)(2,1)}, bf16[4,192,512]{2,1,0:T(8,128)(2,1)}, bf16[4,192,1536]{2,1,0:T(8,128)(2,1)}, bf16[4,192,1024]{2,1,0:T(8...) custom-call(s32[2]{0:T(128)} %pad_add_fusion.2.place_in_ref, ...), custom_call_target="tpu_custom_call" | custom-call | flops 8625000448 | bytes 1 | tf_op jit(solution)/shard_map/pallas_call | solution.py:398
  292.2 24.3 %shard_map.532 = (bf16[4,192,1536]{2,1,0:T(8,128)(2,1)}, bf16[4,192,512]{2,1,0:T(8,128)(2,1)}, bf16[4,192,1536]{2,1,0:T(8,128)(2,1)}, bf16[4,192,1024]{2,1,0:T(8...) custom-call(s32[2]{0:T(128)} %pad_add_fusion.1.place_in_ref, ...), custom_call_target="tpu_custom_call", output_to_operand_aliasing={{4}: (7, {}), {5}: (8, {})} | custom-call | flops 8625000448 | bytes 1 | tf_op jit(solution)/shard_map/pallas_call | solution.py:398
  318.4 9.7 %collective-permute-done.20.refs_1_ = bf16[256,1536]{1,0:T(8,128)(2,1)S(1)} collective-permute-done((bf16[256,1536]{1,0:T(8,128)(2,1)}, bf16[256,1536]{1,0:T(8,128)(2,1)S(1)}, u32[]{:S(2)}, u32[]{:S(2)}) %collective-permute-start.20) | collective-permute-done | bytes 786464 | tf_op jit(solution)/shard_map/ppermute | solution.py:73
  329.0 24.7 %shard_map.533 = (bf16[4,192,1536]{2,1,0:T(8,128)(2,1)}, bf16[4,192,512]{2,1,0:T(8,128)(2,1)}, bf16[4,192,1536]{2,1,0:T(8,128)(2,1)}, bf16[4,192,1024]{2,1,0:T(8...) custom-call(s32[2]{0:T(128)} %pad_add_fusion.3.place_in_ref, ...), custom_call_target="tpu_custom_call", output_to_operand_aliasing={{4}: (7, {}), {5}: (8, {})} | custom-call | flops 8625000448 | bytes 1 | tf_op jit(solution)/shard_map/pallas_call | solution.py:398
  354.3 9.0 %collective-permute-done.15 = bf16[256,1664]{1,0:T(8,128)(2,1)S(1)} collective-permute-done((bf16[256,1664]{1,0:T(8,128)(2,1)}, bf16[256,1664]{1,0:T(8,128)(2,1)S(1)}, u32[]{:S(2)}, u32[]{:S(2)}) %collective-permute-start.15) | collective-permute-done | bytes 852000 | tf_op jit(solution)/shard_map/ppermute | solution.py:73
  365.2 24.3 %shard_map.534 = (bf16[4,192,1536]{2,1,0:T(8,128)(2,1)}, bf16[4,192,512]{2,1,0:T(8,128)(2,1)}, bf16[4,192,1536]{2,1,0:T(8,128)(2,1)}, bf16[4,192,1024]{2,1,0:T(8...) custom-call(s32[2]{0:T(128)} %pad_add_fusion.place_in_ref, ...), custom_call_target="tpu_custom_call", output_to_operand_aliasing={{4}: (7, {}), {5}: (8, {})} | custom-call | flops 8625000448 | bytes 1 | tf_op jit(solution)/shard_map/pallas_call | solution.py:398
  394.4 14.5 %collective-permute-done.21 = bf16[256,1664]{1,0:T(8,128)(2,1)S(1)} collective-permute-done((bf16[256,1664]{1,0:T(8,128)(2,1)}, bf16[256,1664]{1,0:T(8,128)(2,1)S(1)}, u32[]{:S(2)}, u32[]{:S(2)}) %collective-permute-start.21) | collective-permute-done | bytes 852000 | tf_op jit(solution)/shard_map/ppermute | solution.py:73
  410.0 21.8 %shard_map.535 = bf16[4,1536,1536]{2,1,0:T(8,128)(2,1)} custom-call(bf16[4,192,1536]{2,1,0:T(8,128)(2,1)} %get-tuple-element.174.refs_0_, bf16[4,192,1536]{2,1,0:T(8,128)(2,1)} %get-tuple-element.175.refs_1_, bf16[4,192,1536]{2,1,0:T(8,128)(2,1)} %get-tuple-element.176.refs_2_, bf16[4,192,1536]{2,1,0:T(8,128)(2,1)} %get-tuple-element.177.refs_3_, ...), custom_call_target="tpu_custom_call" | custom-call | flops 7590000128 | bytes 1 | tf_op jit(solution)/shard_map/pallas_call | solution.py:580
  435.2 7.4 collective-permute-done.22.other_att_ref
  443.4 11.6 %collective-permute-done.24.refs_1_ = bf16[256,1664]{1,0:T(8,128)(2,1)} collective-permute-done((bf16[256,1664]{1,0:T(8,128)(2,1)}, bf16[256,1664]{1,0:T(8,128)(2,1)}, u32[]{:S(2)}, u32[]{:S(2)}) %collective-permute-start.24) | collective-permute-done | bytes 852000 | tf_op jit(solution)/shard_map/ppermute | solution.py:73
  455.0 14.3 %collective-permute-done.26.refs_3_ = bf16[256,1664]{1,0:T(8,128)(2,1)} collective-permute-done((bf16[256,1664]{1,0:T(8,128)(2,1)}, bf16[256,1664]{1,0:T(8,128)(2,1)}, u32[]{:S(2)}, u32[]{:S(2)}) %collective-permute-start.26) | collective-permute-done | bytes 852000 | tf_op jit(solution)/shard_map/ppermute | solution.py:73
  471.6 7.6 shard_map.536
  482.1 4.2 all-to-all-start.2
  486.3 23.6 %collective-permute-done.29.other_small_ref = bf16[1536,128]{1,0:T(8,128)(2,1)S(1)} collective-permute-done((bf16[1536,128]{1,0:T(8,128)(2,1)}, bf16[1536,128]{1,0:T(8,128)(2,1)S(1)}, u32[]{:S(2)}, u32[]{:S(2)}) %collective-permute-start.29) | collective-permute-done | bytes 393248 | tf_op jit(solution)/shard_map/ppermute | solution.py:73
  512.2 2.4 shard_map.538
  516.2 5.0 all-to-all-start.3
  534.0 3.4 multiply_reduce_fusion.3
  542.4 24.8 %shard_map.537 = (bf16[2048,192]{1,0:T(8,128)(2,1)S(1)}, bf16[2048,128]{1,0:T(8,128)(2,1)S(1)}) custom-call(bf16[3,2048,128]{2,1,0:T(8,128)(2,1)S(1)} %copy-done.44, bf16[2048,128]{1,0:T(8,128)(2,1)S(1)} %copy-done.46, bf16[64,2048]{1,0:T(8,128)(2,1)S(1)} %copy-done.50, bf16[2048,64]{1,0:T(8,128)(2,1)S(1)} %copy-done.48, ...), custom_call_target="tpu_custom_call" | custom-call | flops 8625000448 | bytes 1 | tf_op jit(solution)/shard_map/pallas_call | solution.py:284
  568.1 6.1 convolution_convert_fusion
  574.2 2.9 convert_reduce_fusion
  577.1 2.3 copy.265
  579.4 13.8 %all-to-all-start.4 = ((bf16[16,96,320]{2,1,0:T(8,128)(2,1)}), bf16[16,96,320]{2,1,0:T(8,128)(2,1)}, u32[]{:S(2)}, u32[]{:S(2)}) async-start(bf16[16,96,320]{2,1,0:T(8,128)(2,1)} %bitcast.150), calls=%async_computation.5 | async-start | bytes 2359296 | tf_op jit(solution)/shard_map/all_to_all | solution.py:43
  593.3 2.9 pad_maximum_fusion.2
  596.4 4.4 add_convert_fusion
  605.2 13.2 %all-to-all-done.4 = bf16[16,96,320]{2,1,0:T(8,128)(2,1)} async-done(((bf16[16,96,320]{2,1,0:T(8,128)(2,1)}), bf16[16,96,320]{2,1,0:T(8,128)(2,1)}, u32[]{:S(2)}, u32[]{:S(2)}) %all-to-all-start.4) | async-done | bytes 983072 | tf_op jit(solution)/shard_map/all_to_all | solution.py:43
  618.4 2.9 bitcast_convert_fusion
  621.3 2.7 reduce_sum.303
  626.9 2.5 copy.271
  629.4 4.5 all-to-all-start.5
  643.5 3.3 concatenate.47
  657.5 9.0 %all-to-all-start.6 = ((f32[32,1,2688]{2,1,0:T(1,128)}), f32[32,1,2688]{2,1,0:T(1,128)}, u32[]{:S(2)}, u32[]{:S(2)}) async-start(f32[32,1,2688]{2,1,0:T(1,128)} %broadcast_in_dim.47), calls=%async_computation.7 | async-start | bytes 688128 | tf_op jit(solution)/shard_map/all_to_all | solution.py:43
  666.5 6.7 fusion.7
  675.2 11.2 %all-to-all-done.6 = f32[32,1,2688]{2,1,0:T(1,128)} async-done(((f32[32,1,2688]{2,1,0:T(1,128)}), f32[32,1,2688]{2,1,0:T(1,128)}, u32[]{:S(2)}, u32[]{:S(2)}) %all-to-all-start.6) | async-done | bytes 344096 | tf_op jit(solution)/shard_map/all_to_all | solution.py:43
  687.5 2.3 copy-done.34
  689.8 4.2 shard_map.539
  697.6 3.9 all-to-all-start.7
  710.7 5.0 multiply_reduce_fusion
  720.3 5.2 all-to-all-start.8
  725.6 3.1 collective-permute-done.30
  728.6 2.8 fusion.2
  733.7 5.0 fusion.5
  739.9 5.0 all-to-all-start.9
  752.9 8.3 %fusion.43 = (bf16[4,384,1024]{2,1,0:T(8,128)(2,1)}, f32[4,384,1024]{2,1,0:T(8,128)}) fusion(f32[4,384,1024]{2,1,0:T(8,128)} %param.33, f32[4,384,1024]{2,1,0:T(8,128)} %get-tuple-element.494, f32[4]{0:T(128)S(1)} %fusion.28, f32[4,1024]{1,0:T(4,128)S(1)} %fusion.16, f32[4,384]{1,0:T(4,128)S(1)} %copy-done.77, f32[]{:T(128)} %bitcast.59), kind=kLoop, calls=%fused_computation.184 | loop fusion | flops 9437184 | bytes 22042644 | tf_op jit(solution)/shard_map/convert_element_type | solution.py:1145
  766.2 2.6 fusion.45
  770.5 5.3 fusion.42
  (454 shorter events, 158.4 us)
Async XLA Ops:
  7.2 79.5 %copy-start = (s32[512,8]{0,1:T(8,128)S(1)}, s32[512,8]{0,1:T(8,128)}, u32[]{:S(2)}) copy-start(s32[512,8]{0,1:T(8,128)} %param.27) | copy-start | bytes 49156
  7.2 208.7 %all-gather.5.cloned.1.call-start = ((), (), s32[]{:S(2)}) async-start(), calls=%async_computation.12 | async-start | bytes 4866048 | tf_op jit(solution)/shard_map/all_gather | solution.py:854
  18.1 68.6 %all-to-all-start = ((bf16[16,96,354]{2,1,0:T(8,128)(2,1)}), bf16[16,96,354]{2,1,0:T(8,128)(2,1)S(1)}, u32[]{:S(2)}, u32[]{:S(2)}) async-start(bf16[16,96,354]{2,1,0:T(8,128)(2,1)} %bitcast.151), calls=%async_computation | async-start | bytes 2359296 | tf_op jit(solution)/shard_map/all_to_all | solution.py:43
  25.4 239.4 %all-gather.7.cloned.1.call-start = ((), (), s32[]{:S(2)}) async-start(), calls=%async_computation.13 | async-start | bytes 23592960 | tf_op jit(solution)/shard_map/all_gather | solution.py:859
  25.5 61.2 %collective-permute-start.1 = (bf16[512,1536]{1,0:T(8,128)(2,1)S(1)}, bf16[512,1536]{1,0:T(8,128)(2,1)}, u32[]{:S(2)}, u32[]{:S(2)}) collective-permute-start(bf16[512,1536]{1,0:T(8,128)(2,1)S(1)} %copy-done.2), channel_id=1, source_target_pairs={{0,4},{2,6},{4,0},{6,2},{1,5},{3,7},{5,1},{7,3},{8,12},{10,14},{12... | collective-permute-start | bytes 4718600 | tf_op jit(solution)/shard_map/ppermute | solution.py:73
  40.1 50.9 %copy-start.12 = (bf16[256,1536]{1,0:T(8,128)(2,1)S(1)}, bf16[256,1536]{1,0:T(8,128)(2,1)}, u32[]{:S(2)}) copy-start(bf16[256,1536]{1,0:T(8,128)(2,1)} %refs_9_.1) | copy-start | bytes 2359300
  86.7 99.7 %copy-start.3 = (bf16[16,96,354]{2,1,0:T(8,128)(2,1)}, bf16[16,96,354]{2,1,0:T(8,128)(2,1)S(1)}, u32[]{:S(2)}) copy-start(bf16[16,96,354]{2,1,0:T(8,128)(2,1)S(1)} %all-to-all-done) | copy-start | bytes 3262468
  92.0 41.7 %collective-permute-start.3 = (bf16[256,1664]{1,0:T(8,128)(2,1)}, bf16[256,1664]{1,0:T(8,128)(2,1)}, u32[]{:S(2)}, u32[]{:S(2)}) collective-permute-start(bf16[256,1664]{1,0:T(8,128)(2,1)} %fusion.10.refs_2_), channel_id=1, source_target_pairs={{0,8},{8,0},{16,24},{24,16},{1,9},{9,1},{17,25},{25,17},{2,10},{10... | collective-permute-start | bytes 2555912 | tf_op jit(solution)/shard_map/ppermute | solution.py:73
  93.4 36.1 %collective-permute-start.4 = (bf16[256,1664]{1,0:T(8,128)(2,1)}, bf16[256,1664]{1,0:T(8,128)(2,1)}, u32[]{:S(2)}, u32[]{:S(2)}) collective-permute-start(bf16[256,1664]{1,0:T(8,128)(2,1)} %fusion.10.refs_2_), channel_id=1, source_target_pairs={{0,16},{8,24},{16,0},{24,8},{1,17},{9,25},{17,1},{25,9},{2,18},{10... | collective-permute-start | bytes 2555912 | tf_op jit(solution)/shard_map/ppermute | solution.py:73
  95.7 5.8 collective-permute-start
  95.7 6.0 collective-permute-start.2
  113.6 64.9 %copy-start.43 = (bf16[3,2048,128]{2,1,0:T(8,128)(2,1)}, bf16[3,2048,128]{2,1,0:T(8,128)(2,1)S(1)}, u32[]{:S(2)}) copy-start(bf16[3,2048,128]{2,1,0:T(8,128)(2,1)S(1)} %get-tuple-element.135.q_ref) | copy-start | bytes 4718596
  113.6 64.9 %copy-start.45 = (bf16[2048,128]{1,0:T(8,128)(2,1)}, bf16[2048,128]{1,0:T(8,128)(2,1)S(1)}, u32[]{:S(2)}) copy-start(bf16[2048,128]{1,0:T(8,128)(2,1)S(1)} %get-tuple-element.136.k_ref) | copy-start | bytes 1572868
  113.6 64.9 %copy-start.47 = (bf16[2048,64]{1,0:T(8,128)(2,1)}, bf16[2048,64]{1,0:T(8,128)(2,1)S(1)}, u32[]{:S(2)}) copy-start(bf16[2048,64]{1,0:T(8,128)(2,1)S(1)} %get-tuple-element.196.v_ref) | copy-start | bytes 786436
  113.6 64.9 %copy-start.49 = (bf16[64,2048]{1,0:T(8,128)(2,1)}, bf16[64,2048]{1,0:T(8,128)(2,1)S(1)}, u32[]{:S(2)}) copy-start(bf16[64,2048]{1,0:T(8,128)(2,1)S(1)} %get-tuple-element.195.kt_ref) | copy-start | bytes 786436
  129.5 22.7 %collective-permute-start.7 = (bf16[256,1664]{1,0:T(8,128)(2,1)}, bf16[256,1664]{1,0:T(8,128)(2,1)}, u32[]{:S(2)}, u32[]{:S(2)}) collective-permute-start(bf16[256,1664]{1,0:T(8,128)(2,1)} %collective-permute-done.4.refs_2_), channel_id=1, source_target_pairs={{0,8},{8,0},{16,24},{24,16},{1,9},{9,1},{17,25},{25,17},{2,10},{10... | collective-permute-start | bytes 2555912 | tf_op jit(solution)/shard_map/ppermute | solution.py:73
  133.7 45.4 %collective-permute-start.6 = (bf16[256,1664]{1,0:T(8,128)(2,1)}, bf16[256,1664]{1,0:T(8,128)(2,1)S(1)}, u32[]{:S(2)}, u32[]{:S(2)}) collective-permute-start(bf16[256,1664]{1,0:T(8,128)(2,1)} %collective-permute-done.3.refs_2_), channel_id=1, source_target_pairs={{0,1},{1,0},{2,3},{3,2},{4,5},{5,4},{6,7},{7,6},{8,9},{9,8},{10,11... | collective-permute-start | bytes 2555912 | tf_op jit(solution)/shard_map/ppermute | solution.py:73
  135.2 44.8 %collective-permute-start.5 = (bf16[256,1664]{1,0:T(8,128)(2,1)}, bf16[256,1664]{1,0:T(8,128)(2,1)S(1)}, u32[]{:S(2)}, u32[]{:S(2)}) collective-permute-start(bf16[256,1664]{1,0:T(8,128)(2,1)} %fusion.10.refs_2_), channel_id=1, source_target_pairs={{0,1},{1,0},{2,3},{3,2},{4,5},{5,4},{6,7},{7,6},{8,9},{9,8},{10,11... | collective-permute-start | bytes 2555912 | tf_op jit(solution)/shard_map/ppermute | solution.py:73
  135.7 58.8 %collective-permute-start.8 = (bf16[256,1664]{1,0:T(8,128)(2,1)}, bf16[256,1664]{1,0:T(8,128)(2,1)}, u32[]{:S(2)}, u32[]{:S(2)}) collective-permute-start(bf16[256,1664]{1,0:T(8,128)(2,1)} %collective-permute-done.4.refs_2_), channel_id=1, source_target_pairs={{0,1},{1,0},{2,3},{3,2},{4,5},{5,4},{6,7},{7,6},{8,9},{9,8},{10,11... | collective-permute-start | bytes 2555912 | tf_op jit(solution)/shard_map/ppermute | solution.py:73
  152.2 63.7 %collective-permute-start.9 = (bf16[256,1664]{1,0:T(8,128)(2,1)}, bf16[256,1664]{1,0:T(8,128)(2,1)}, u32[]{:S(2)}, u32[]{:S(2)}) collective-permute-start(bf16[256,1664]{1,0:T(8,128)(2,1)} %collective-permute-done.7.refs_2_), channel_id=1, source_target_pairs={{0,1},{1,0},{2,3},{3,2},{4,5},{5,4},{6,7},{7,6},{8,9},{9,8},{10,11... | collective-permute-start | bytes 2555912 | tf_op jit(solution)/shard_map/ppermute | solution.py:73
  180.9 35.0 %all-to-all-start.1 = ((bf16[8,192,256]{2,1,0:T(8,128)(2,1)}), bf16[8,192,256]{2,1,0:T(8,128)(2,1)S(1)}, u32[]{:S(2)}, u32[]{:S(2)}) async-start(bf16[8,192,256]{2,1,0:T(8,128)(2,1)} %get-tuple-element.142.out_ref), calls=%async_computation.1 | async-start | bytes 1572864 | tf_op jit(solution)/shard_map/all_to_all | solution.py:43
  184.5 179.9 %all-gather.9.cloned.1.call-start = ((), (), s32[]{:S(2)}) async-start(), calls=%async_computation.16 | async-start | bytes 5898240 | tf_op jit(solution)/shard_map/all_gather | solution.py:896
  188.4 33.1 %copy-start.15 = (bf16[1536,32]{0,1:T(8,128)(2,1)}, bf16[1536,32]{0,1:T(8,128)(2,1)S(1)}, u32[]{:S(2)}) copy-start(bf16[1536,32]{0,1:T(8,128)(2,1)S(1)} %copy.285) | copy-start | bytes 294916
  189.2 32.3 %copy-start.21 = (f32[1,1536]{1,0:T(1,128)}, f32[1,1536]{1,0:T(1,128)S(1)}, u32[]{:S(2)}) copy-start(f32[1,1536]{1,0:T(1,128)S(1)} %reshape.379.gain_ref.refs_10_) | copy-start | bytes 18436
  226.0 38.9 %copy-start.35 = (bf16[256,1536]{1,0:T(8,128)(2,1)}, bf16[256,1536]{1,0:T(8,128)(2,1)S(1)}, u32[]{:S(2)}) copy-start(bf16[256,1536]{1,0:T(8,128)(2,1)S(1)} %get-tuple-element.149.refs_0_.refs_5_) | copy-start | bytes 2359300
  226.0 461.5 %reduce-scatter.5.cloned.1.call-start = ((), (), s32[]{:S(2)}) async-start(), calls=%async_computation.15 | async-start | bytes 23592960 | tf_op jit(solution)/shard_map/reduce_scatter | solution.py:946
  226.3 35.4 %collective-permute-start.12 = (bf16[256,1536]{1,0:T(8,128)(2,1)S(1)}, bf16[256,1536]{1,0:T(8,128)(2,1)S(1)}, u32[]{:S(2)}, u32[]{:S(2)}) collective-permute-start(bf16[256,1536]{1,0:T(8,128)(2,1)S(1)} %get-tuple-element.149.refs_0_.refs_5_), channel_id=1, source_target_pairs={{0,8},{8,0},{16,24},{24,16},{1,9},{9,1},{17,25},{25,17},{2,10},{10... | collective-permute-start | bytes 2359304 | tf_op jit(solution)/shard_map/ppermute | solution.py:73
  226.6 38.2 %collective-permute-start.10 = (bf16[256,1536]{1,0:T(8,128)(2,1)S(1)}, bf16[256,1536]{1,0:T(8,128)(2,1)}, u32[]{:S(2)}, u32[]{:S(2)}) collective-permute-start(bf16[256,1536]{1,0:T(8,128)(2,1)S(1)} %get-tuple-element.149.refs_0_.refs_5_), channel_id=1, source_target_pairs={{0,16},{8,24},{16,0},{24,8},{1,17},{9,25},{17,1},{25,9},{2,18},{10... | collective-permute-start | bytes 2359304 | tf_op jit(solution)/shard_map/ppermute | solution.py:73
  226.6 38.2 %collective-permute-start.14 = (bf16[256,1536]{1,0:T(8,128)(2,1)S(1)}, bf16[256,1536]{1,0:T(8,128)(2,1)}, u32[]{:S(2)}, u32[]{:S(2)}) collective-permute-start(bf16[256,1536]{1,0:T(8,128)(2,1)S(1)} %get-tuple-element.149.refs_0_.refs_5_), channel_id=1, source_target_pairs={{0,1},{1,0},{2,3},{3,2},{4,5},{5,4},{6,7},{7,6},{8,9},{9,8},{10,11... | collective-permute-start | bytes 2359304 | tf_op jit(solution)/shard_map/ppermute | solution.py:73
  231.7 1.2 collective-permute-start.16
  232.8 56.8 %collective-permute-start.17 = (f32[1,32]{1,0:T(1,128)S(1)}, f32[1,32]{1,0:T(1,128)S(1)}, u32[]{:S(2)}, u32[]{:S(2)}) collective-permute-start(f32[1,32]{1,0:T(1,128)S(1)} %add.272), channel_id=1, source_target_pairs={{0,4},{2,6},{4,0},{6,2},{1,5},{3,7},{5,1},{7,3},{8,12},{10,14},{12... | collective-permute-start | bytes 392 | tf_op jit(solution)/shard_map/ppermute | solution.py:73
  261.6 27.5 %copy-start.108 = (bf16[256,1536]{1,0:T(8,128)(2,1)}, bf16[256,1536]{1,0:T(8,128)(2,1)S(1)}, u32[]{:S(2)}) copy-start(bf16[256,1536]{1,0:T(8,128)(2,1)S(1)} %collective-permute-done.12.refs_0_) | copy-start | bytes 2359300
  261.6 30.6 %collective-permute-start.13 = (bf16[256,1536]{1,0:T(8,128)(2,1)S(1)}, bf16[256,1536]{1,0:T(8,128)(2,1)}, u32[]{:S(2)}, u32[]{:S(2)}) collective-permute-start(bf16[256,1536]{1,0:T(8,128)(2,1)S(1)} %collective-permute-done.12.refs_0_), channel_id=1, source_target_pairs={{0,1},{1,0},{2,3},{3,2},{4,5},{5,4},{6,7},{7,6},{8,9},{9,8},{10,11... | collective-permute-start | bytes 2359304 | tf_op jit(solution)/shard_map/ppermute | solution.py:73
  264.8 27.0 %collective-permute-start.11 = (bf16[256,1536]{1,0:T(8,128)(2,1)}, bf16[256,1536]{1,0:T(8,128)(2,1)}, u32[]{:S(2)}, u32[]{:S(2)}) collective-permute-start(bf16[256,1536]{1,0:T(8,128)(2,1)} %collective-permute-done.10.refs_0_), channel_id=1, source_target_pairs={{0,8},{8,0},{16,24},{24,16},{1,9},{9,1},{17,25},{25,17},{2,10},{10... | collective-permute-start | bytes 2359304 | tf_op jit(solution)/shard_map/ppermute | solution.py:73
  289.2 29.0 %collective-permute-start.19 = (bf16[256,1664]{1,0:T(8,128)(2,1)}, bf16[256,1664]{1,0:T(8,128)(2,1)S(1)}, u32[]{:S(2)}, u32[]{:S(2)}) collective-permute-start(bf16[256,1664]{1,0:T(8,128)(2,1)} %get-tuple-element.157), channel_id=1, source_target_pairs={{0,1},{1,0},{2,3},{3,2},{4,5},{5,4},{6,7},{7,6},{8,9},{9,8},{10,11... | collective-permute-start | bytes 2555912 | tf_op jit(solution)/shard_map/ppermute | solution.py:73
  290.2 37.9 %collective-permute-start.20 = (bf16[256,1536]{1,0:T(8,128)(2,1)}, bf16[256,1536]{1,0:T(8,128)(2,1)S(1)}, u32[]{:S(2)}, u32[]{:S(2)}) collective-permute-start(bf16[256,1536]{1,0:T(8,128)(2,1)} %collective-permute-done.10.refs_0_), channel_id=1, source_target_pairs={{0,1},{1,0},{2,3},{3,2},{4,5},{5,4},{6,7},{7,6},{8,9},{9,8},{10,11... | collective-permute-start | bytes 2359304 | tf_op jit(solution)/shard_map/ppermute | solution.py:73
  291.8 72.6 %collective-permute-start.18 = (bf16[256,1536]{1,0:T(8,128)(2,1)}, bf16[256,1536]{1,0:T(8,128)(2,1)S(1)}, u32[]{:S(2)}, u32[]{:S(2)}) collective-permute-start(bf16[256,1536]{1,0:T(8,128)(2,1)} %collective-permute-done.11.refs_0_), channel_id=1, source_target_pairs={{0,1},{1,0},{2,3},{3,2},{4,5},{5,4},{6,7},{7,6},{8,9},{9,8},{10,11... | collective-permute-start | bytes 2359304 | tf_op jit(solution)/shard_map/ppermute | solution.py:73
  316.5 46.7 %collective-permute-start.15 = (bf16[256,1664]{1,0:T(8,128)(2,1)}, bf16[256,1664]{1,0:T(8,128)(2,1)S(1)}, u32[]{:S(2)}, u32[]{:S(2)}) collective-permute-start(bf16[256,1664]{1,0:T(8,128)(2,1)} %get-tuple-element.153), channel_id=1, source_target_pairs={{0,1},{1,0},{2,3},{3,2},{4,5},{5,4},{6,7},{7,6},{8,9},{9,8},{10,11... | collective-permute-start | bytes 2555912 | tf_op jit(solution)/shard_map/ppermute | solution.py:73
  329.0 34.2 %copy-start.68 = (bf16[256,1664]{1,0:T(8,128)(2,1)S(1)}, bf16[256,1664]{1,0:T(8,128)(2,1)}, u32[]{:S(2)}) copy-start(bf16[256,1664]{1,0:T(8,128)(2,1)} %get-tuple-element.152) | copy-start | bytes 2555908
  353.8 36.4 %collective-permute-start.23 = (bf16[256,1664]{1,0:T(8,128)(2,1)}, bf16[256,1664]{1,0:T(8,128)(2,1)}, u32[]{:S(2)}, u32[]{:S(2)}) collective-permute-start(bf16[256,1664]{1,0:T(8,128)(2,1)} %get-tuple-element.173), channel_id=1, source_target_pairs={{0,1},{1,0},{2,3},{3,2},{4,5},{5,4},{6,7},{7,6},{8,9},{9,8},{10,11... | collective-permute-start | bytes 2555912 | tf_op jit(solution)/shard_map/ppermute | solution.py:73
  389.6 19.3 %collective-permute-start.21 = (bf16[256,1664]{1,0:T(8,128)(2,1)}, bf16[256,1664]{1,0:T(8,128)(2,1)S(1)}, u32[]{:S(2)}, u32[]{:S(2)}) collective-permute-start(bf16[256,1664]{1,0:T(8,128)(2,1)} %get-tuple-element.168), channel_id=1, source_target_pairs={{0,1},{1,0},{2,3},{3,2},{4,5},{5,4},{6,7},{7,6},{8,9},{9,8},{10,11... | collective-permute-start | bytes 2555912 | tf_op jit(solution)/shard_map/ppermute | solution.py:73
  392.4 39.5 %collective-permute-start.25 = (bf16[256,1664]{1,0:T(8,128)(2,1)}, bf16[256,1664]{1,0:T(8,128)(2,1)}, u32[]{:S(2)}, u32[]{:S(2)}) collective-permute-start(bf16[256,1664]{1,0:T(8,128)(2,1)} %add_convert_fusion.1), channel_id=1, source_target_pairs={{0,16},{8,24},{16,0},{24,8},{1,17},{9,25},{17,1},{25,9},{2,18},{10... | collective-permute-start | bytes 2555912 | tf_op jit(solution)/shard_map/ppermute | solution.py:73
  431.8 37.5 %copy-start.16 = (bf16[1536,32]{0,1:T(8,128)(2,1)S(1)}, bf16[1536,32]{0,1:T(8,128)(2,1)}, u32[]{:S(2)}) copy-start(bf16[1536,32]{0,1:T(8,128)(2,1)} %copy-done.15) | copy-start | bytes 294916
  431.8 37.5 %copy-start.22 = (f32[1,1536]{1,0:T(1,128)S(1)}, f32[1,1536]{1,0:T(1,128)}, u32[]{:S(2)}) copy-start(f32[1,1536]{1,0:T(1,128)} %copy-done.21) | copy-start | bytes 18436
  431.9 37.4 %copy-start.54 = (f32[32,256]{1,0:T(8,128)S(1)}, f32[32,256]{1,0:T(8,128)}, u32[]{:S(2)}) copy-start(f32[32,256]{1,0:T(8,128)} %copy-done.53) | copy-start | bytes 98308
  431.9 37.4 %copy-start.56 = (f32[32,256]{1,0:T(8,128)S(1)}, f32[32,256]{1,0:T(8,128)}, u32[]{:S(2)}) copy-start(f32[32,256]{1,0:T(8,128)} %copy-done.55) | copy-start | bytes 98308
  431.9 23.0 %collective-permute-start.24 = (bf16[256,1664]{1,0:T(8,128)(2,1)}, bf16[256,1664]{1,0:T(8,128)(2,1)}, u32[]{:S(2)}, u32[]{:S(2)}) collective-permute-start(bf16[256,1664]{1,0:T(8,128)(2,1)} %add_convert_fusion.4), channel_id=1, source_target_pairs={{0,8},{8,0},{16,24},{24,16},{1,9},{9,1},{17,25},{25,17},{2,10},{10... | collective-permute-start | bytes 2555912 | tf_op jit(solution)/shard_map/ppermute | solution.py:73
  433.4 35.9 %collective-permute-start.26 = (bf16[256,1664]{1,0:T(8,128)(2,1)}, bf16[256,1664]{1,0:T(8,128)(2,1)}, u32[]{:S(2)}, u32[]{:S(2)}) collective-permute-start(bf16[256,1664]{1,0:T(8,128)(2,1)} %add_convert_fusion.2), channel_id=1, source_target_pairs={{0,24},{8,16},{16,8},{24,0},{1,25},{9,17},{17,9},{25,1},{2,26},{10... | collective-permute-start | bytes 2555912 | tf_op jit(solution)/shard_map/ppermute | solution.py:73
  434.8 7.8 collective-permute-start.22
  480.0 29.9 %collective-permute-start.28 = (bf16[256,1536]{1,0:T(8,128)(2,1)S(1)}, bf16[256,1536]{1,0:T(8,128)(2,1)S(1)}, u32[]{:S(2)}, u32[]{:S(2)}) collective-permute-start(bf16[256,1536]{1,0:T(8,128)(2,1)S(1)} %get-tuple-element.202.low_ref), channel_id=1, source_target_pairs={{0,1},{1,0},{2,3},{3,2},{4,5},{5,4},{6,7},{7,6},{8,9},{9,8},{10,11... | collective-permute-start | bytes 2359304 | tf_op jit(solution)/shard_map/ppermute | solution.py:73
  481.6 28.4 %collective-permute-start.29 = (bf16[1536,128]{1,0:T(8,128)(2,1)}, bf16[1536,128]{1,0:T(8,128)(2,1)S(1)}, u32[]{:S(2)}, u32[]{:S(2)}) collective-permute-start(bf16[1536,128]{1,0:T(8,128)(2,1)} %get-tuple-element.204.small_ref), channel_id=1, source_target_pairs={{0,1},{1,0},{2,3},{3,2},{4,5},{5,4},{6,7},{7,6},{8,9},{9,8},{10,11... | collective-permute-start | bytes 1179656 | tf_op jit(solution)/shard_map/ppermute | solution.py:73
  482.1 34.2 %all-to-all-start.2 = ((bf16[8,192,256]{2,1,0:T(8,128)(2,1)}), bf16[8,192,256]{2,1,0:T(8,128)(2,1)}, u32[]{:S(2)}, u32[]{:S(2)}) async-start(bf16[8,192,256]{2,1,0:T(8,128)(2,1)} %copy-done.10), calls=%async_computation.2 | async-start | bytes 1572864 | tf_op jit(solution)/shard_map/all_to_all | solution.py:43
  516.2 57.9 %all-to-all-start.3 = ((bf16[16,96,896]{2,1,0:T(8,128)(2,1)}), bf16[16,96,896]{2,1,0:T(8,128)(2,1)}, u32[]{:S(2)}, u32[]{:S(2)}) async-start(bf16[16,96,896]{2,1,0:T(8,128)(2,1)} %bitcast.136), calls=%async_computation.4 | async-start | bytes 5505024 | tf_op jit(solution)/shard_map/all_to_all | solution.py:43
  525.5 70.9 %collective-permute-start.27 = (bf16[4,256,1536]{2,1,0:T(8,128)(2,1)}, bf16[4,256,1536]{2,1,0:T(8,128)(2,1)}, u32[]{:S(2)}, u32[]{:S(2)}) collective-permute-start(bf16[4,256,1536]{2,1,0:T(8,128)(2,1)} %get-tuple-element.194), channel_id=1, source_target_pairs={{0,1},{1,0},{2,3},{3,2},{4,5},{5,4},{6,7},{7,6},{8,9},{9,8},{10,11... | collective-permute-start | bytes 9437192 | tf_op jit(solution)/shard_map/ppermute | solution.py:73
  579.4 39.0 %all-to-all-start.4 = ((bf16[16,96,320]{2,1,0:T(8,128)(2,1)}), bf16[16,96,320]{2,1,0:T(8,128)(2,1)}, u32[]{:S(2)}, u32[]{:S(2)}) async-start(bf16[16,96,320]{2,1,0:T(8,128)(2,1)} %bitcast.150), calls=%async_computation.5 | async-start | bytes 2359296 | tf_op jit(solution)/shard_map/all_to_all | solution.py:43
  593.2 168.1 %reduce-scatter.3.cloned.1.call-start = ((), (), s32[]{:S(2)}) async-start(), calls=%async_computation.14 | async-start | bytes 3932160 | tf_op jit(solution)/shard_map/reduce_scatter | solution.py:964
  629.4 26.5 %all-to-all-start.5 = ((bf16[4,512,320]{1,2,0:T(8,128)(2,1)}), bf16[4,512,320]{1,2,0:T(8,128)(2,1)}, u32[]{:S(2)}, u32[]{:S(2)}) async-start(bf16[4,512,320]{1,2,0:T(8,128)(2,1)} %copy.271), calls=%async_computation.6 | async-start | bytes 2621440 | tf_op jit(solution)/shard_map/all_to_all | solution.py:43
  641.5 127.3 %copy-start.5 = (f32[96,1280]{1,0:T(8,128)}, f32[96,1280]{1,0:T(8,128)S(1)}, u32[]{:S(2)}) copy-start(f32[96,1280]{1,0:T(8,128)S(1)} %get-tuple-element.566.qkv_ref) | copy-start | bytes 1474564
  657.5 28.9 %all-to-all-start.6 = ((f32[32,1,2688]{2,1,0:T(1,128)}), f32[32,1,2688]{2,1,0:T(1,128)}, u32[]{:S(2)}, u32[]{:S(2)}) async-start(f32[32,1,2688]{2,1,0:T(1,128)} %broadcast_in_dim.47), calls=%async_computation.7 | async-start | bytes 688128 | tf_op jit(solution)/shard_map/all_to_all | solution.py:43
  673.2 52.3 %collective-permute-start.31 = (bf16[512,1536]{1,0:T(8,128)(2,1)}, bf16[512,1536]{1,0:T(8,128)(2,1)}, u32[]{:S(2)}, u32[]{:S(2)}) collective-permute-start(bf16[512,1536]{1,0:T(8,128)(2,1)} %fusion.7), channel_id=1, source_target_pairs={{0,1},{1,0},{2,3},{3,2},{4,5},{5,4},{6,7},{7,6},{8,9},{9,8},{10,11... | collective-permute-start | bytes 4718600 | tf_op jit(solution)/shard_map/ppermute | solution.py:73
  675.1 53.6 %collective-permute-start.30 = (bf16[256,1536]{1,0:T(8,128)(2,1)}, bf16[256,1536]{1,0:T(8,128)(2,1)}, u32[]{:S(2)}, u32[]{:S(2)}) collective-permute-start(bf16[256,1536]{1,0:T(8,128)(2,1)} %get-tuple-element.218), channel_id=1, source_target_pairs={{0,1},{1,0},{2,3},{3,2},{4,5},{5,4},{6,7},{7,6},{8,9},{9,8},{10,11... | collective-permute-start | bytes 2359304 | tf_op jit(solution)/shard_map/ppermute | solution.py:73
  697.6 11.2 %all-to-all-start.7 = ((f32[4,4,1664]{2,1,0:T(4,128)}), f32[4,4,1664]{2,1,0:T(4,128)}, u32[]{:S(2)}, u32[]{:S(2)}) async-start(f32[4,4,1664]{2,1,0:T(4,128)} %broadcast_in_dim.53), calls=%async_computation.9 | async-start | bytes 212992 | tf_op jit(solution)/shard_map/all_to_all | solution.py:43
  720.3 18.4 %all-to-all-start.8 = ((f32[32,1,7]{2,1,0:T(1,128)}), f32[32,1,7]{2,1,0:T(1,128)S(1)}, u32[]{:S(2)}, u32[]{:S(2)}) async-start(f32[32,1,7]{2,1,0:T(1,128)} %broadcast_in_dim.56), calls=%async_computation.10 | async-start | bytes 32768 | tf_op jit(solution)/shard_map/all_to_all | solution.py:43
  739.9 35.9 %all-to-all-start.9 = ((f32[32,1,4608]{2,1,0:T(1,128)}), f32[32,1,4608]{2,1,0:T(1,128)S(1)}, u32[]{:S(2)}, u32[]{:S(2)}) async-start(f32[32,1,4608]{2,1,0:T(1,128)} %broadcast_in_dim.58), calls=%async_computation.11 | async-start | bytes 1179648 | tf_op jit(solution)/shard_map/all_to_all | solution.py:43
  (93 other events, 656.6 us)
Sparse Core Ops, SparseCore 0:
  11.5 85.6 all-gather.4
  99.4 129.8 all-gather.6
  230.9 37.4 all-gather.8
  432.0 184.0 reduce-scatter.4
  618.9 67.2 reduce-scatter.2
